TPU v7x, 32 devices: a whole 2x2x4 slice. The times are simulated.
32 devices in a mesh: group: 2 (over y), sess: 4 (over z), head: 2 (over x), dp: 2 (over core).
Axes of the slice: x: 2, y: 2, z: 4, core: 2. Of those that a mesh axis runs over, the one named last changes fastest.
Arguments:
- x_rows: bfloat16 [32, 128, 2048], P(('group', 'sess', 'dp'), None, 'head'), parts along dimension 0, may hold values from -6 to 6
- z_rows: bfloat16 [32, 128, 2048], P(('group', 'sess', 'dp'), None, 'head'), parts along dimension 0, may hold values from -6 to 6
- input_projection_matrix: bfloat16 [32, 128, 256], P(('group', 'sess', 'dp')), parts along dimension 0, may hold values from -6 to 6
- c_rows: bfloat16 [32, 128, 256], P(('group', 'sess', 'dp')), parts along dimension 0, may hold values from -0.375 to 0.375
- dt_raw: float32 [32, 32, 128], P(('group', 'sess', 'dp'), 'head'), parts along dimension 0
- a_log: float32 [32], P('head'), may hold values from -5.8 to -2.3
- dt_bias: float32 [32], P('head'), may hold values from -1 to 1
- d_skip: float32 [32], P('head'), may hold values from 0.5 to 2
- norm_gain: bfloat16 [2048], P('head'), may hold values from 0.25 to 1.75
- cache_state: bfloat16 [16, 32, 64, 256], P(('group', 'sess', 'dp'), 'head'), parts along dimension 0, may hold values from -12 to 12
- lengths: int32 [16], P(('group', 'sess', 'dp')), parts along dimension 0, may hold values from 16 to 192
- slot_owner: int32 [4, 8], P('group'), parts along dimension 0, may hold values from 0 to 3, as said below
- slot_task: int32 [4, 8], P('group'), parts along dimension 0, may hold values from 0 to 1, as said below
Outputs:
- mixed_rows: bfloat16 [32, 128, 2048], P(('group', 'sess', 'dp'), None, 'head'), parts along dimension 0
- final_state: bfloat16 [16, 32, 64, 256], P(('group', 'sess', 'dp'), 'head'), parts along dimension 0
There are 2 independent parts, one for each index of `group`. A program takes and returns all parts, laid end to end along the dimension named above; an argument that names none is the same for every part. Nothing has to cross between parts.
Inputs may be any that keep to these rules, and one draw needn't show every extreme that they name: `slot_owner`: in each dp index, the slots of one device belong to 2 different owners, and the 2 tasks of one owner lie on 2 different devices. `slot_task`: every task of every owner stands in exactly one slot of its dp index.
All inputs are finite; a program needn't handle non-finite values.
Results may differ from a plain program's by a relative error of at most 0.0063.
Values may be sent and summed in bfloat16 or wider, within the bound.
No kernel may reach another device: no remote copies, remote signals or barrier semaphores. Data moves between devices by JAX's collectives and lax.ppermute only.
A program may use at most 64 MiB of HBM per device.

v0:
```python
import jax
import jax.numpy as jnp
from jax import lax
from jax.sharding import PartitionSpec as P


def swapped(block, axis, apart):
    count = lax.axis_size(axis)
    route = []
    for low in range(count):
        high = low | 1 << apart
        if high != low and high < count:
            route += [(low, high), (high, low)]
    return lax.ppermute(block, axis, route)


def feature_decays(got_decay, slice_index, piece, head_count, per_head):
    feature_head = (slice_index * piece + jnp.arange(piece, dtype=jnp.int32)) // per_head
    head_pick = jnp.where(
        feature_head[None, :] == jnp.arange(head_count, dtype=jnp.int32)[:, None], 1.0, 0.0
    ).astype(jnp.bfloat16)
    return jnp.dot(got_decay, head_pick, preferred_element_type=jnp.float32).astype(jnp.bfloat16)


def merge_slices(states, decay_factors, caches, session_of, part_of, session_total):
    sessions = jnp.arange(session_total, dtype=jnp.int32)
    belongs = session_of[None, :] == sessions[:, None]
    pick_first = jnp.where(belongs & (part_of[None, :] == 0), 1.0, 0.0).astype(jnp.bfloat16)
    pick_second = jnp.where(belongs & (part_of[None, :] == 1), 1.0, 0.0).astype(jnp.bfloat16)
    state_first = jnp.dot(pick_first, states, preferred_element_type=jnp.float32)
    state_second = jnp.dot(pick_second, states, preferred_element_type=jnp.float32)
    decay_first = jnp.dot(pick_first, decay_factors, preferred_element_type=jnp.float32)
    decay_second = jnp.dot(pick_second, decay_factors, preferred_element_type=jnp.float32)
    start_late = (decay_first * caches.astype(jnp.float32) + state_first).astype(jnp.bfloat16)
    final_piece = (decay_second * start_late.astype(jnp.float32) + state_second).astype(
        jnp.bfloat16
    )
    slot_pick = jnp.where(belongs.T, 1.0, 0.0).astype(jnp.bfloat16)
    from_cache = jnp.dot(slot_pick, caches, preferred_element_type=jnp.float32)
    from_late = jnp.dot(slot_pick, start_late, preferred_element_type=jnp.float32)
    slot_start = jnp.where((part_of == 0)[:, None], from_cache, from_late).astype(jnp.bfloat16)
    return (final_piece, slot_start)


def per_device(
    x_rows,
    z_rows,
    input_projection_matrix,
    c_rows,
    dt_raw,
    a_log,
    dt_bias,
    d_skip,
    norm_gain,
    cache_state,
    lengths,
    slot_owner,
    slot_task,
):
    slot_count, block_len, width = x_rows.shape
    head_count = dt_raw.shape[1]
    head_size = width // head_count
    state_size = cache_state.shape[3]
    sess_count = lengths.shape[0]
    peer_count = lax.axis_size("sess")
    sess_index = lax.axis_index("sess")
    dp_index = lax.axis_index("dp")
    group_index = lax.axis_index("head") // 2
    per_head = head_size * state_size
    features = head_count * per_head
    all_lengths = lax.all_gather(lengths, "sess", axis=0, tiled=True)
    owner_row = lax.dynamic_index_in_dim(slot_owner, dp_index, 0, keepdims=False)
    task_row = lax.dynamic_index_in_dim(slot_task, dp_index, 0, keepdims=False)
    owner_ids = lax.dynamic_slice_in_dim(owner_row, sess_index * slot_count, slot_count)
    job_identifiers = lax.dynamic_slice_in_dim(task_row, sess_index * slot_count, slot_count)
    block_part = job_identifiers % 2
    session_len = jnp.take(all_lengths, owner_ids * sess_count + job_identifiers // 2)
    valid = jnp.clip(session_len - block_part * block_len, 0, block_len)
    b_mine = lax.dynamic_slice_in_dim(
        input_projection_matrix, group_index * state_size, state_size, 2
    )
    c_mine = lax.dynamic_slice_in_dim(c_rows, group_index * state_size, state_size, 2)
    row_index = jnp.arange(block_len)
    live_rows = row_index[None, :] < valid[:, None]
    step_lengths = jnp.where(
        live_rows[:, None, :], jax.nn.softplus(dt_raw + dt_bias[None, :, None]), 0.0
    )
    log_decay = jnp.cumsum(-jnp.exp(a_log)[None, :, None] * step_lengths, axis=2)
    scores = jnp.einsum("srn,sun->sru", c_mine, b_mine, preferred_element_type=jnp.float32)
    lower = row_index[:, None] >= row_index[None, :]
    gap_log = jnp.where(
        lower[None, None], log_decay[:, :, :, None] - log_decay[:, :, None, :], -jnp.inf
    )
    weights = (jnp.exp(gap_log) * step_lengths[:, :, None, :] * scores[:, None]).astype(
        jnp.bfloat16
    )
    x_heads = x_rows.reshape(slot_count, block_len, head_count, head_size)
    in_block = jnp.einsum("shru,suhp->srhp", weights, x_heads, preferred_element_type=jnp.float32)
    trailing_share = jnp.exp(log_decay[:, :, -1:] - log_decay) * step_lengths
    scaled = (x_heads * jnp.transpose(trailing_share, (0, 2, 1))[:, :, :, None]).astype(
        jnp.bfloat16
    )
    local_state = jnp.einsum(
        "suhp,sun->shpn", scaled, b_mine, preferred_element_type=jnp.float32
    ).astype(jnp.bfloat16)
    block_decay = jnp.exp(log_decay[:, :, -1]).astype(jnp.bfloat16)
    local_flat = local_state.reshape(slot_count, features)
    cache_flat = cache_state.reshape(sess_count, features)
    piece = features // peer_count
    decay_send = jnp.broadcast_to(block_decay[:, None, :], (slot_count, peer_count, head_count))
    got_states, got_decay, got_cache = (
        lax.all_to_all(
            local_flat.reshape(slot_count, peer_count, piece),
            "sess",
            split_axis=1,
            concat_axis=0,
            tiled=True,
        ),
        lax.all_to_all(decay_send, "sess", split_axis=1, concat_axis=0, tiled=True),
        lax.all_to_all(
            cache_flat.reshape(sess_count, peer_count, piece),
            "sess",
            split_axis=1,
            concat_axis=0,
            tiled=True,
        ),
    )
    session_of = owner_row * sess_count + task_row // 2
    part_of = task_row % 2
    decay_factors = feature_decays(got_decay[:, 0], sess_index, piece, head_count, per_head)
    final_piece, slot_piece = merge_slices(
        got_states[:, 0],
        decay_factors,
        got_cache[:, 0],
        session_of,
        part_of,
        peer_count * sess_count,
    )
    final_flat, start_flat = (
        lax.all_to_all(final_piece, "sess", split_axis=0, concat_axis=1, tiled=True),
        lax.all_to_all(slot_piece, "sess", split_axis=0, concat_axis=1, tiled=True),
    )
    final_state = final_flat.reshape(sess_count, head_count, head_size, state_size)
    slot_start = start_flat.reshape(slot_count, head_count, head_size, state_size)
    carried = jnp.einsum("srn,shpn->srhp", c_mine, slot_start, preferred_element_type=jnp.float32)
    carried = carried * jnp.exp(jnp.transpose(log_decay, (0, 2, 1)))[:, :, :, None]
    y_total = in_block + carried + d_skip[None, None, :, None] * x_heads
    gated_rows = y_total.reshape(slot_count, block_len, width) * jax.nn.silu(
        z_rows.astype(jnp.float32)
    )
    own_squares = jnp.sum(gated_rows * gated_rows, axis=2)
    other_squares = swapped(own_squares, "head", 0)
    inv_rms = lax.rsqrt((own_squares + other_squares) / (2.0 * width) + 1e-05)
    normed = gated_rows * inv_rms[:, :, None] * norm_gain.astype(jnp.float32)
    mixed_rows = jnp.where(live_rows[:, :, None], normed, 0.0).astype(jnp.bfloat16)
    return (mixed_rows, final_state)


def solution(mesh):
    in_specs = (
        P(("group", "sess", "dp"), None, "head"),
        P(("group", "sess", "dp"), None, "head"),
        P(("group", "sess", "dp"), None, None),
        P(("group", "sess", "dp"), None, None),
        P(("group", "sess", "dp"), "head", None),
        P("head"),
        P("head"),
        P("head"),
        P("head"),
        P(("group", "sess", "dp"), "head", None, None),
        P(("group", "sess", "dp")),
        P("group", None),
        P("group", None),
    )
    out_specs = (
        P(("group", "sess", "dp"), None, "head"),
        P(("group", "sess", "dp"), "head", None, None),
    )
    return jax.shard_map(
        per_device, mesh=mesh, in_specs=in_specs, out_specs=out_specs, check_vma=False
    )
```

profile of v0, /device:TPU:0, one launch (start us, length us, event | category | flops | bytes accessed | tf_op | source)
XLA Modules:
  0.0 133.8 jit_solution(8201821026581378483)
XLA Ops:
  1.4 1.2 dynamic-slice.2
  4.2 9.9 %all-reduce = s32[4]{0:T(128)S(1)} all-reduce(s32[4]{0:T(128)S(1)} %dynamic-update-slice), channel_id=1, replica_groups=mesh['group'=2,'sess'=4,'head'=2,'dp'=2] {'sess'}, use_global_device_ids=true, to_apply=%add | all-reduce | flops 4 | bytes 32
  16.3 0.8 broadcast_multiply_fusion
  18.4 3.2 %all-to-all-start.1 = ((bf16[2,4,16]{2,0,1:T(2,128)(2,1)}), bf16[2,4,16]{2,0,1:T(2,128)(2,1)S(1)}, u32[]{:S(2)}, u32[]{:S(2)}) async-start(bf16[2,4,16]{2,0,1:T(2,128)(2,1)} %broadcast_in_dim.110), calls=%async_computation.1 | async-start | bytes 4096 | tf_op jit(solution)/shard_map/all_to_all | solution.py:119
  23.0 4.0 %reduce.3 = bf16[4,65536]{1,0:T(4,128)(2,1)S(1)} reduce(bf16[4,1,65536]{2,1,0:T(2,128)(2,1)S(1)} %bitcast.111, bf16[]{:T(256)} %broadcast.360), dimensions={1}, to_apply=%bitcast.93.reduce_sub_computation | reduce | bytes 1048578
  27.0 1.3 %reshape.305 = bf16[4,2,32768]{2,1,0:T(2,128)(2,1)} reshape(bf16[4,65536]{1,0:T(4,128)(2,1)S(1)} %reduce.3) | data formatting | bytes 1048576
  28.7 5.0 %all-to-all-start = ((bf16[4,2,32768]{2,1,0:T(2,128)(2,1)}), bf16[4,2,32768]{2,1,0:T(2,128)(2,1)S(1)}, u32[]{:S(2)}, u32[]{:S(2)}) async-start(bf16[4,2,32768]{2,1,0:T(2,128)(2,1)} %reshape.305), calls=%async_computation | async-start | bytes 1048576 | tf_op jit(solution)/shard_map/all_to_all | solution.py:120
  35.0 2.1 %copy.35 = bf16[2,4,65536]{2,0,1:T(2,128)(2,1)} copy(bf16[2,4,65536]{2,1,0:T(4,128)(2,1)S(1)} %reshape_reshape.7) | data formatting | bytes 2097152 | tf_op jit(solution)/shard_map/reshape;reshape | solution.py:113
  37.7 8.2 %all-to-all-done = bf16[4,2,32768]{2,1,0:T(2,128)(2,1)S(1)} async-done(((bf16[4,2,32768]{2,1,0:T(2,128)(2,1)}), bf16[4,2,32768]{2,1,0:T(2,128)(2,1)S(1)}, u32[]{:S(2)}, u32[]{:S(2)}) %all-to-all-start) | async-done | bytes 524320 | tf_op jit(solution)/shard_map/all_to_all | solution.py:120
  45.9 4.2 %all-to-all-start.2 = ((bf16[2,4,65536]{2,0,1:T(2,128)(2,1)}), bf16[2,4,65536]{2,0,1:T(2,128)(2,1)}, u32[]{:S(2)}, u32[]{:S(2)}) async-start(bf16[2,4,65536]{2,0,1:T(2,128)(2,1)} %copy.35), calls=%async_computation.2 | async-start | bytes 2097152 | tf_op jit(solution)/shard_map/all_to_all | solution.py:112
  51.3 1.8 %fusion.22 = bf16[8,65536]{1,0:T(8,128)(2,1)} fusion(bf16[1,4,65536]{2,0,1:T(2,128)(2,1)S(1)} %bitcast.109, s32[8]{0:T(128)S(1)} %add_bitcast_fusion), kind=kOutput, calls=%fused_computation.40 | convolution fusion | flops 4194400 | bytes 1572896 | tf_op jit(solution)/shard_map/dot_general | solution.py:39
  53.1 1.8 %convolution_multiply_fusion.1 = f32[4,65536]{1,0:T(4,128)} fusion(bf16[8,65536]{1,0:T(8,128)(2,1)S(1)} %convolution_convert_fusion, bf16[1,4,65536]{2,0,1:T(2,128)(2,1)S(1)} %bitcast.110, s32[8]{0:T(128)S(1)} %add_bitcast_fusion, pred[8]{0:T(512)(128)(4,1)S(1)} %compare_bitcast_fusion.1), kind=kOutput, calls=%fused_computation.7 | convolution fusion | flops 4718720 | bytes 2621480 | tf_op jit(solution)/shard_map/dot_general | solution.py:32
  54.9 18.1 %all-to-all-done.2 = bf16[2,4,65536]{2,0,1:T(2,128)(2,1)} async-done(((bf16[2,4,65536]{2,0,1:T(2,128)(2,1)}), bf16[2,4,65536]{2,0,1:T(2,128)(2,1)}, u32[]{:S(2)}, u32[]{:S(2)}) %all-to-all-start.2) | async-done | bytes 1048608 | tf_op jit(solution)/shard_map/all_to_all | solution.py:112
  73.0 1.6 %squeeze.21 = bf16[8,65536]{1,0:T(8,128)(2,1)S(1)} reshape(bf16[4,2,1,65536]{3,1,0,2:T(2,128)(2,1)} %bitcast.18) | data formatting | bytes 2097152 | tf_op jit(solution)/shard_map/squeeze | solution.py:132
  74.6 1.7 %fusion.1 = bf16[4,65536]{1,0:T(4,128)(2,1)S(1)} fusion(f32[4,65536]{1,0:T(4,128)} %convolution_multiply_fusion.1, bf16[8,65536]{1,0:T(8,128)(2,1)S(1)} %squeeze.21, s32[8]{0:T(128)S(1)} %add_bitcast_fusion, pred[8]{0:T(512)(128)(4,1)S(1)} %compare_bitcast_fusion.1), kind=kOutput, calls=%fused_computation.8 | convolution fusion | flops 4718720 | bytes 2621480 | tf_op jit(solution)/shard_map/dot_general | solution.py:30
  76.4 1.5 %fusion = bf16[8,65536]{1,0:T(8,128)(2,1)} fusion(bf16[8,65536]{1,0:T(8,128)(2,1)S(1)} %copy-done.1, bf16[4,65536]{1,0:T(4,128)(2,1)S(1)} %fusion.1, pred[8]{0:T(512)(128)(4,1)S(1)} %fusion.42, s32[8]{0:T(128)S(1)} %add_bitcast_fusion), kind=kOutput, calls=%fused_computation.2 | convolution fusion | flops 4718688 | bytes 2621480 | tf_op jit(solution)/shard_map/dot_general | solution.py:40
  77.8 2.9 %all_to_all.58 = bf16[4,2,65536]{2,1,0:T(2,128)(2,1)} reshape(bf16[8,65536]{1,0:T(8,128)(2,1)} %fusion) | data formatting | bytes 2097152 | tf_op jit(solution)/shard_map/all_to_all | solution.py:141
  80.7 4.5 %all-to-all-start.3 = ((bf16[4,2,65536]{2,1,0:T(2,128)(2,1)}), bf16[4,2,65536]{2,1,0:T(2,128)(2,1)}, u32[]{:S(2)}, u32[]{:S(2)}) async-start(bf16[4,2,65536]{2,1,0:T(2,128)(2,1)} %all_to_all.58), calls=%async_computation.3 | async-start | bytes 2097152 | tf_op jit(solution)/shard_map/all_to_all | solution.py:141
  86.1 1.2 convolution_multiply_fusion
  87.7 1.3 reduce.4
  89.0 1.3 %reshape.307 = bf16[4,2,32768]{2,1,0:T(2,128)(2,1)} reshape(bf16[4,65536]{1,0:T(4,128)(2,1)S(1)} %reduce.4) | data formatting | bytes 1048576
  90.3 19.6 %all-to-all-done.3 = bf16[4,2,65536]{2,1,0:T(2,128)(2,1)} async-done(((bf16[4,2,65536]{2,1,0:T(2,128)(2,1)}), bf16[4,2,65536]{2,1,0:T(2,128)(2,1)}, u32[]{:S(2)}, u32[]{:S(2)}) %all-to-all-start.3) | async-done | bytes 1048608 | tf_op jit(solution)/shard_map/all_to_all | solution.py:141
  110.0 3.5 %all-to-all-start.4 = ((bf16[4,2,32768]{2,1,0:T(2,128)(2,1)}), bf16[4,2,32768]{2,1,0:T(2,128)(2,1)S(1)}, u32[]{:S(2)}, u32[]{:S(2)}) async-start(bf16[4,2,32768]{2,1,0:T(2,128)(2,1)} %reshape.307), calls=%async_computation.4 | async-start | bytes 1048576 | tf_op jit(solution)/shard_map/all_to_all | solution.py:140
  113.5 1.9 %convolution_bitcast_fusion.1 = f32[2,128,16,64]{1,3,2,0:T(8,128)} fusion(bf16[2,128,16,64]{1,3,2,0:T(8,128)(2,1)S(1)} %bitcast.107, f32[2,128,128]{2,1,0:T(8,128)S(1)} %fusion.62, f32[2,16,128]{2,1,0:T(8,128)S(1)} %copy-done.9, f32[2,16,128]{2,1,0:T(8,128)S(1)} %reduce_window_sum.11, pred[128,128]{1,0:T(8,128)(4,1)S(1)} %copy-done.12), kind=kOutput, calls=%fused_computation.22 | convolution fusion | flops 69730304 | bytes 1753088 | tf_op jit(solution)/shard_map/shru,suhp->srhp/dot_general | solution.py:98
  115.4 2.0 %copy.36 = bf16[2,4,65536]{2,1,0:T(4,128)(2,1)S(1)} copy(bf16[2,4,65536]{2,0,1:T(2,128)(2,1)} %bitcast.19) | data formatting | bytes 2097152 | tf_op jit(solution)/shard_map/all_to_all | solution.py:141
  117.5 0.9 reshape.285
  118.3 1.7 %fusion.9 = f32[2,128,16,64]{1,3,2,0:T(8,128)S(1)} fusion(f32[2,128,16,64]{1,3,2,0:T(8,128)} %convolution_bitcast_fusion.1, bf16[2,16,64,256]{3,2,1,0:T(8,128)(2,1)S(1)} %reshape.285, bf16[2,128,16,64]{1,3,2,0:T(8,128)(2,1)S(1)} %bitcast.108, f32[16]{0:T(128)S(1)} %copy-done.19, f32[2,128,16]{1,2,0:T(8,128)S(1)} %copy-done.7, ...), kind=kOutput, calls=%fused_computation.21 | convolution fusion | flops 135528448 | bytes 3817536 | tf_op jit(solution)/shard_map/srn,shpn->srhp/dot_general | solution.py:145
  121.5 1.5 %collective-permute-start = (f32[2,128]{1,0:T(2,128)S(1)}, f32[2,128]{1,0:T(2,128)S(1)}, u32[]{:S(2)}, u32[]{:S(2)}) collective-permute-start(f32[2,128]{1,0:T(2,128)S(1)} %multiply_reduce_fusion), channel_id=1, source_target_pairs={{0,2},{2,0},{1,3},{3,1},{4,6},{6,4},{5,7},{7,5},{8,10},{10,8},{9,1... | collective-permute-start | bytes 3080 | tf_op jit(solution)/shard_map/ppermute | solution.py:14
  123.0 4.4 %all-to-all-done.4 = bf16[4,2,32768]{2,1,0:T(2,128)(2,1)S(1)} async-done(((bf16[4,2,32768]{2,1,0:T(2,128)(2,1)}), bf16[4,2,32768]{2,1,0:T(2,128)(2,1)S(1)}, u32[]{:S(2)}, u32[]{:S(2)}) %all-to-all-start.4) | async-done | bytes 524320 | tf_op jit(solution)/shard_map/all_to_all | solution.py:140
  128.0 3.4 %reduce.1 = bf16[4,65536]{1,0:T(4,128)(2,1)S(1)} reduce(bf16[4,1,65536]{2,1,0:T(2,128)(2,1)S(1)} %reshape.308, bf16[]{:T(256)} %constant.165), dimensions={1}, to_apply=%all_to_all.62.reduce_sub_computation | reduce | bytes 1048578 | tf_op jit(solution)/shard_map/all_to_all | solution.py:140
  131.3 1.2 reshape.287
  132.6 1.3 select_convert_fusion.2
  (77 shorter events, 13.0 us)
Async XLA Ops:
  0.6 33.1 %copy-start = (bf16[2,128,256]{2,1,0:T(8,128)(2,1)S(1)}, bf16[2,128,256]{2,1,0:T(8,128)(2,1)}, u32[]{:S(2)}) copy-start(bf16[2,128,256]{2,1,0:T(8,128)(2,1)} %param.15) | copy-start | bytes 393220
  0.6 21.0 %copy-start.4 = (bf16[1,16,64,256]{3,2,1,0:T(8,128)(2,1)S(1)}, bf16[1,16,64,256]{3,2,1,0:T(8,128)(2,1)}, u32[]{:S(2)}) copy-start(bf16[1,16,64,256]{3,2,1,0:T(8,128)(2,1)} %param.22) | copy-start | bytes 1572868
  15.6 2.8 %copy-start.16 = (pred[2,128]{1,0:T(4,128)(4,1)}, pred[2,128]{1,0:T(4,128)(4,1)S(1)}, u32[]{:S(2)}) copy-start(pred[2,128]{1,0:T(4,128)(4,1)S(1)} %iota_compare_fusion.4) | copy-start | bytes 772
  17.1 10.0 %copy-start.8 = (f32[2,16,128]{2,1,0:T(8,128)}, f32[2,16,128]{2,1,0:T(8,128)S(1)}, u32[]{:S(2)}) copy-start(f32[2,16,128]{2,1,0:T(8,128)S(1)} %get-tuple-element.5) | copy-start | bytes 49156
  18.4 10.2 %all-to-all-start.1 = ((bf16[2,4,16]{2,0,1:T(2,128)(2,1)}), bf16[2,4,16]{2,0,1:T(2,128)(2,1)S(1)}, u32[]{:S(2)}, u32[]{:S(2)}) async-start(bf16[2,4,16]{2,0,1:T(2,128)(2,1)} %broadcast_in_dim.110), calls=%async_computation.1 | async-start | bytes 4096 | tf_op jit(solution)/shard_map/all_to_all | solution.py:119
  23.0 5.4 %copy-start.6 = (bf16[2,128,1024]{2,1,0:T(8,128)(2,1)S(1)}, bf16[2,128,1024]{2,1,0:T(8,128)(2,1)}, u32[]{:S(2)}) copy-start(bf16[2,128,1024]{2,1,0:T(8,128)(2,1)} %param.13) | copy-start | bytes 1572868
  28.7 17.2 %all-to-all-start = ((bf16[4,2,32768]{2,1,0:T(2,128)(2,1)}), bf16[4,2,32768]{2,1,0:T(2,128)(2,1)S(1)}, u32[]{:S(2)}, u32[]{:S(2)}) async-start(bf16[4,2,32768]{2,1,0:T(2,128)(2,1)} %reshape.305), calls=%async_computation | async-start | bytes 1048576 | tf_op jit(solution)/shard_map/all_to_all | solution.py:120
  35.0 2.1 %copy-start.14 = (s32[2,8]{1,0:T(2,128)S(1)}, s32[2,8]{1,0:T(2,128)}, u32[]{:S(2)}) copy-start(s32[2,8]{1,0:T(2,128)} %param.25) | copy-start | bytes 196
  35.0 2.7 %copy-start.15 = (s32[2,8]{1,0:T(2,128)S(1)}, s32[2,8]{1,0:T(2,128)}, u32[]{:S(2)}) copy-start(s32[2,8]{1,0:T(2,128)} %param.24) | copy-start | bytes 196
  37.7 38.7 %copy-start.10 = (s32[8]{0:T(128)}, s32[8]{0:T(128)S(1)}, u32[]{:S(2)}) copy-start(s32[8]{0:T(128)S(1)} %add_bitcast_fusion) | copy-start | bytes 100
  45.9 27.1 %all-to-all-start.2 = ((bf16[2,4,65536]{2,0,1:T(2,128)(2,1)}), bf16[2,4,65536]{2,0,1:T(2,128)(2,1)}, u32[]{:S(2)}, u32[]{:S(2)}) async-start(bf16[2,4,65536]{2,0,1:T(2,128)(2,1)} %copy.35), calls=%async_computation.2 | async-start | bytes 2097152 | tf_op jit(solution)/shard_map/all_to_all | solution.py:112
  74.6 1.8 %copy-start.1 = (bf16[8,65536]{1,0:T(8,128)(2,1)S(1)}, bf16[8,65536]{1,0:T(8,128)(2,1)}, u32[]{:S(2)}) copy-start(bf16[8,65536]{1,0:T(8,128)(2,1)} %fusion.22) | copy-start | bytes 3145732
  80.7 5.2 %copy-start.5 = (bf16[2,128,256]{2,1,0:T(8,128)(2,1)S(1)}, bf16[2,128,256]{2,1,0:T(8,128)(2,1)}, u32[]{:S(2)}) copy-start(bf16[2,128,256]{2,1,0:T(8,128)(2,1)} %param.16) | copy-start | bytes 393220
  80.7 29.3 %all-to-all-start.3 = ((bf16[4,2,65536]{2,1,0:T(2,128)(2,1)}), bf16[4,2,65536]{2,1,0:T(2,128)(2,1)}, u32[]{:S(2)}, u32[]{:S(2)}) async-start(bf16[4,2,65536]{2,1,0:T(2,128)(2,1)} %all_to_all.58), calls=%async_computation.3 | async-start | bytes 2097152 | tf_op jit(solution)/shard_map/all_to_all | solution.py:141
  86.1 1.2 copy-start.11
  86.1 1.2 copy-start.13
  89.0 24.5 %copy-start.9 = (f32[2,16,128]{2,1,0:T(8,128)S(1)}, f32[2,16,128]{2,1,0:T(8,128)}, u32[]{:S(2)}) copy-start(f32[2,16,128]{2,1,0:T(8,128)} %copy-done.8) | copy-start | bytes 49156
  89.0 24.5 %copy-start.12 = (pred[128,128]{1,0:T(8,128)(4,1)S(1)}, pred[128,128]{1,0:T(8,128)(4,1)}, u32[]{:S(2)}) copy-start(pred[128,128]{1,0:T(8,128)(4,1)} %iota_compare_fusion.1) | copy-start | bytes 49156
  110.0 17.4 %all-to-all-start.4 = ((bf16[4,2,32768]{2,1,0:T(2,128)(2,1)}), bf16[4,2,32768]{2,1,0:T(2,128)(2,1)S(1)}, u32[]{:S(2)}, u32[]{:S(2)}) async-start(bf16[4,2,32768]{2,1,0:T(2,128)(2,1)} %reshape.307), calls=%async_computation.4 | async-start | bytes 1048576 | tf_op jit(solution)/shard_map/all_to_all | solution.py:140
  117.4 0.9 copy-start.7
  117.5 0.9 copy-start.19
  120.0 1.0 copy-start.2
  121.1 2.0 %copy-start.18 = (bf16[1024]{0:T(1024)(128)(2,1)S(1)}, bf16[1024]{0:T(1024)(128)(2,1)}, u32[]{:S(2)}) copy-start(bf16[1024]{0:T(1024)(128)(2,1)} %param.21) | copy-start | bytes 6148
  121.5 11.1 %collective-permute-start = (f32[2,128]{1,0:T(2,128)S(1)}, f32[2,128]{1,0:T(2,128)S(1)}, u32[]{:S(2)}, u32[]{:S(2)}) collective-permute-start(f32[2,128]{1,0:T(2,128)S(1)} %multiply_reduce_fusion), channel_id=1, source_target_pairs={{0,2},{2,0},{1,3},{3,1},{4,6},{6,4},{5,7},{7,5},{8,10},{10,8},{9,1... | collective-permute-start | bytes 3080 | tf_op jit(solution)/shard_map/ppermute | solution.py:14
  127.9 4.6 %copy-start.3 = (bf16[2,128,1024]{2,1,0:T(8,128)(2,1)S(1)}, bf16[2,128,1024]{2,1,0:T(8,128)(2,1)}, u32[]{:S(2)}) copy-start(bf16[2,128,1024]{2,1,0:T(8,128)(2,1)} %param.14) | copy-start | bytes 1572868
  127.9 4.6 %copy-start.17 = (pred[2,128]{1,0:T(4,128)(4,1)S(1)}, pred[2,128]{1,0:T(4,128)(4,1)}, u32[]{:S(2)}) copy-start(pred[2,128]{1,0:T(4,128)(4,1)} %copy-done.16) | copy-start | bytes 772
where the time goes:
time: 135 us; the launch traced here: 134 us
  waiting for transfers between devices  50.3 us (37%)
  starting transfers between devices  22 us (16%)
  local copies, waits for them, and re-layouts  20.7 us (15%)
  other arithmetic  16.1 us (12%)
  matrix products  13 us (10%)
  blocking collectives  9.92 us (7%)
  between operations  1.83 us (1%)
    all_to_all x1, waiting for transfers between devices, per_device(): lax.all_to_all(slot_piece, 'sess', split_axis=0, concat_axis=1, tiled=True)  19.6 us
    all_to_all x1, waiting for transfers between devices, per_device(): lax.all_to_all(local_flat.reshape(slot_count, peer_count, piece), 'sess',...  18.1 us
    unnamed x1, blocking collectives  9.92 us
    all_to_all x1, waiting for transfers between devices, per_device(): lax.all_to_all(cache_flat.reshape(sess_count, peer_count, piece), 'sess',...  8.19 us
    unnamed x49, local copies, waits for them, and re-layouts  7.32 us
    all_to_all x1, starting transfers between devices, per_device(): lax.all_to_all(cache_flat.reshape(sess_count, peer_count, piece), 'sess',...  5.04 us
    all_to_all x2, local copies, waits for them, and re-layouts, per_device(): lax.all_to_all(slot_piece, 'sess', split_axis=0, concat_axis=1, tiled=True)  4.91 us
    all_to_all x2, other arithmetic, per_device(): lax.all_to_all(final_piece, 'sess', split_axis=0, concat_axis=1, tiled=True)  4.63 us
  transfers between devices with their start and end apart: 6, of which 4 were waited for; matrix products, arithmetic and copies ran while one was open for 25% of the time, Pallas kernels for 0%

commit v1 on v0

v1 whole, which is shorter than its diff:
```python
import functools

import jax
import jax.numpy as jnp
from jax import lax
from jax.experimental import pallas as pl
from jax.experimental.pallas import tpu as pltpu
from jax.sharding import PartitionSpec as P

F32 = jnp.float32
BF16 = jnp.bfloat16
HALF = 64
VMEM = pl.BlockSpec(memory_space=pltpu.VMEM)
SMEM = pl.BlockSpec(memory_space=pltpu.SMEM)
ANY = pl.BlockSpec(memory_space=pl.ANY)
PARAMS = pltpu.CompilerParams(vmem_limit_bytes=24 * 1024 * 1024)


def dot(a, b, dims, precision=None):
    return lax.dot_general(
        a, b, ((dims[:1], dims[1:]), ((), ())), precision=precision, preferred_element_type=F32
    )


def iota(shape, dim):
    return lax.broadcasted_iota(jnp.int32, shape, dim)


def softplus(v):
    return jnp.maximum(v, 0.0) + jnp.log1p(jnp.exp(-jnp.abs(v)))


def running(v):
    rows = v.shape[1]
    upto = jnp.where(iota((rows, rows), 0) <= iota((rows, rows), 1), 1.0, 0.0).astype(F32)
    return dot(v, upto, (1, 0), lax.Precision.HIGHEST)


def silu(v):
    return v * (1.0 / (1.0 + jnp.exp(-v)))


def choose(index, values):
    out = values[0]
    for k in range(1, len(values)):
        out = jnp.where(index == k, values[k], out)
    return out


def slot_for(ids, owner, k, slots):
    me, dp = ids[0], ids[1]
    pick = jnp.int32(0)
    for j in range(1, slots):
        pick = jnp.where(owner[dp, me * slots + j] == me ^ k, j, pick)
    return pick


def sources(ids, owner, task, slots):
    me, dp = ids[0], ids[1]
    first = jnp.int32(0)
    second = jnp.int32(0)
    for i in range(owner.shape[1]):
        mine = owner[dp, i] == me
        late = task[dp, i] % 2 == 1
        first = jnp.where(mine & ~late, me ^ (i // slots), first)
        second = jnp.where(mine & late, me ^ (i // slots), second)
    return first, second


def small_send(peers, ids, owner, lens, dt, b, c, *outs):
    slots, heads = dt.shape[:2]
    dtls, bcs = outs[:peers], outs[peers:]
    own_len = lens[0].astype(F32)
    for k in range(peers):
        j = slot_for(ids, owner, k, slots)
        dtls[k][:heads] = dt[j]
        dtls[k][heads:] = jnp.full((8, dt.shape[2]), own_len, F32)

        @pl.when(ids[2] == 0)
        def _():
            bcs[k][...] = b[j]

        @pl.when(ids[2] != 0)
        def _():
            bcs[k][...] = c[j]


def x_send(peers, ids, owner, x, *rest):
    outs, sem = rest[:peers], rest[peers]
    slots = x.shape[0]
    copies = []
    for k in range(peers):
        j = slot_for(ids, owner, k, slots)
        copies.append(pltpu.make_async_copy(x.at[j], outs[k], sem.at[k]))
        copies[-1].start()
    for copy in copies:
        copy.wait()


def bc_pick(peers, slots, ids, owner, task, *rest):
    bcs, out = rest[:peers], rest[peers]
    k0, k1 = sources(ids, owner, task, slots)
    rows = bcs[0].shape[0]
    for k in range(peers):

        @pl.when(k0 == k)
        def _():
            out[:rows] = bcs[k][...]

        @pl.when(k1 == k)
        def _():
            out[rows:] = bcs[k][:HALF]


def block_part(ids, x, z, b, c, dt, alog, bias, skip, yz, ez):
    slots, rows, width = x.shape
    heads = dt.shape[1]
    size = width // heads
    per = 128 // size
    causal = iota((rows, rows), 0) >= iota((rows, rows), 1)
    lane = iota((rows, 128), 1) // size
    rate = -jnp.exp(alog[...])
    for s in range(slots):
        step = softplus(dt[s] + bias[...])
        log_decay = running(rate * step)
        log_col = jnp.transpose(log_decay)
        decay_col = jnp.exp(log_col)
        scores = jnp.where(causal, dot(c[s], b[s], (1, 1)), 0.0)
        for p in range(width // 128):
            lanes = slice(p * 128, (p + 1) * 128)
            xp = x[s, :, lanes]
            weights = []
            blocks = []
            decay = decay_col[:, p * per : p * per + 1]
            own_skip = skip[p * per : p * per + 1]
            for q in range(per):
                h = p * per + q
                gap = jnp.minimum(log_col[:, h : h + 1] - log_decay[h : h + 1], 0.0)
                weights.append((jnp.exp(gap) * step[h : h + 1] * scores).astype(BF16))
                blocks.append(jnp.where(lane == q, xp, jnp.zeros_like(xp)))
                if q:
                    decay = jnp.where(lane == q, decay_col[:, h : h + 1], decay)
                    own_skip = jnp.where(lane[:1] == q, skip[h : h + 1], own_skip)
            inner = dot(
                jnp.concatenate(weights, axis=1), jnp.concatenate(blocks, axis=0), (1, 0)
            )
            gate = silu(z[s, :, lanes].astype(F32))
            yz[s, :, lanes] = (inner + own_skip * xp.astype(F32)) * gate
            ez[s, :, lanes] = decay * gate


def owner_part(peers, slots, ids, owner, task, lens, cache, alog, bias, mine, other, *rest):
    dtls, xs = rest[:peers], rest[peers : 2 * peers]
    final = rest[2 * peers]
    cars = rest[2 * peers + 1 : 3 * peers + 1]
    x0, x1, car0, car1, bs, cs, sem = rest[3 * peers + 1 :]
    rows, width = x0.shape
    heads = alog.shape[0]
    size = width // heads
    k0, k1 = sources(ids, owner, task, slots)

    def load(k):
        return (
            (k0 == k, pltpu.make_async_copy(xs[k], x0, sem.at[0])),
            (k1 == k, pltpu.make_async_copy(xs[k].at[:HALF], x1, sem.at[1])),
        )

    for k in range(peers):
        for pred, copy in load(k):
            pl.when(pred)(copy.start)

    @pl.when(ids[2] == 0)
    def _():
        bs[...] = mine[...]
        cs[...] = other[...]

    @pl.when(ids[2] != 0)
    def _():
        bs[...] = other[...]
        cs[...] = mine[...]

    length = lens[0]
    rate = -jnp.exp(alog[...])
    col = iota((heads, rows), 1)

    def shares(dt, valid):
        step = jnp.where(col < valid, softplus(dt + bias[...]), 0.0)
        log_decay = running(rate * step)
        total = log_decay[:, rows - 1 :]
        share = jnp.exp(total - log_decay) * step
        return jnp.transpose(share), jnp.exp(total).astype(BF16).astype(F32)

    share0, decay0 = shares(choose(k0, [d[:heads] for d in dtls]), length)
    share1, decay1 = shares(choose(k1, [d[:heads] for d in dtls]), length - rows)
    per = 128 // size
    lane = iota((rows, 128), 1) // size

    def scaled(xv, share, p):
        factor = share[:, p * per : p * per + 1]
        for q in range(1, per):
            factor = jnp.where(lane[: xv.shape[0]] == q, share[:, p * per + q : p * per + q + 1], factor)
        return (xv.astype(F32) * factor).astype(BF16)

    for k in range(peers):
        for pred, copy in load(k):
            pl.when(pred)(copy.wait)

    for g in range(width // 256):
        lanes = slice(g * 256, (g + 1) * 256)
        old = cache[lanes]
        car0[:, lanes] = dot(cs[:rows], old, (1, 1)).astype(BF16)
        s0 = jnp.concatenate(
            [scaled(x0[:, p * 128 : (p + 1) * 128], share0, p) for p in (2 * g, 2 * g + 1)], axis=1
        )
        s1 = jnp.concatenate(
            [scaled(x1[:, p * 128 : (p + 1) * 128], share1[:HALF], p) for p in (2 * g, 2 * g + 1)],
            axis=1,
        )
        local0 = dot(s0, bs[:rows], (0, 0)).astype(BF16).astype(F32)
        local1 = dot(s1, bs[rows:], (0, 0)).astype(BF16).astype(F32)
        late = []
        for q in range(256 // size):
            h = g * (256 // size) + q
            part = slice(q * size, (q + 1) * size)
            start = decay0[h : h + 1] * old[part].astype(F32) + local0[part]
            late.append(start.astype(BF16))
            final[h * size : (h + 1) * size] = (
                decay1[h : h + 1] * late[-1].astype(F32) + local1[part]
            ).astype(BF16)
        late = jnp.concatenate(late, axis=0)
        car1[:, lanes] = dot(cs[rows:], late, (1, 1)).astype(BF16)

    def store(k):
        return (
            (k0 == k, pltpu.make_async_copy(car0, cars[k], sem.at[0])),
            (k1 == k, pltpu.make_async_copy(car1, cars[k].at[:HALF], sem.at[1])),
        )

    for k in range(peers):
        for pred, copy in store(k):
            pl.when(pred)(copy.start)
    for k in range(peers):
        for pred, copy in store(k):
            pl.when(pred)(copy.wait)


def gate_part(peers, ids, owner, yz, ez, *rest):
    cars = rest[:peers]
    gated, squares, got, sem = rest[peers:]
    slots, rows, width = yz.shape
    me, dp = ids[0], ids[1]

    def load(j, k):
        far = me ^ owner[dp, me * slots + j]
        return far == k, pltpu.make_async_copy(cars[k], got.at[j], sem.at[j])

    for j in range(slots):
        for k in range(peers):
            pred, copy = load(j, k)
            pl.when(pred)(copy.start)
    for j in range(slots):
        for k in range(peers):
            pred, copy = load(j, k)
            pl.when(pred)(copy.wait)
        total = jnp.zeros((rows, 128), F32)
        for p in range(width // 128):
            lanes = slice(p * 128, (p + 1) * 128)
            value = yz[j, :, lanes] + ez[j, :, lanes] * got[j, :, lanes].astype(F32)
            gated[j, :, lanes] = value
            total = total + value * value
        squares[j : j + 1] = jnp.sum(jnp.transpose(total), axis=0, keepdims=True)


def norm_part(peers, ids, owner, task, gated, own, other, gain, *rest):
    dtls, mixed = rest[:peers], rest[peers]
    slots, rows, width = gated.shape
    heads = dtls[0].shape[0] - 8
    me, dp = ids[0], ids[1]
    row = iota((rows, 128), 0).astype(F32)
    for j in range(slots):
        far = me ^ owner[dp, me * slots + j]
        late = task[dp, me * slots + j] % 2
        length = choose(far, [d[heads : heads + 1] for d in dtls])
        live = row + (late * rows).astype(F32) < length
        mean = (own[j : j + 1] + other[j : j + 1]) / (2.0 * width)
        inverse = jnp.transpose(jnp.broadcast_to(lax.rsqrt(mean + 1e-05), (rows, rows)))
        for p in range(width // 128):
            lanes = slice(p * 128, (p + 1) * 128)
            value = gated[j, :, lanes] * inverse * gain[:, lanes].astype(F32)
            mixed[j, :, lanes] = jnp.where(live, value, 0.0).astype(BF16)


def call(kernel, outs, in_specs, out_specs=None, scratch=(), flops=0, moved=0):
    return pl.pallas_call(
        kernel,
        out_shape=outs,
        in_specs=in_specs,
        out_specs=out_specs if out_specs is not None else jax.tree.map(lambda _: VMEM, outs),
        scratch_shapes=scratch,
        compiler_params=PARAMS,
        cost_estimate=pl.CostEstimate(flops=flops, bytes_accessed=moved, transcendentals=0),
    )


def per_device(
    x_rows,
    z_rows,
    input_projection_matrix,
    c_rows,
    dt_raw,
    a_log,
    dt_bias,
    d_skip,
    norm_gain,
    cache_state,
    lengths,
    slot_owner,
    slot_task,
):
    slots, rows, width = x_rows.shape
    heads = dt_raw.shape[1]
    state = cache_state.shape[3]
    peers = lax.axis_size("sess")
    head = lax.axis_index("head")
    groups = input_projection_matrix.shape[2] // state
    if groups > 1:
        at = head // 2 * state
        b = lax.dynamic_slice_in_dim(input_projection_matrix, at, state, 2)
        c = lax.dynamic_slice_in_dim(c_rows, at, state, 2)
    else:
        b, c = input_projection_matrix, c_rows
    ids = jnp.stack([lax.axis_index("sess"), lax.axis_index("dp"), head % 2]).astype(jnp.int32)
    alog = a_log[:, None]
    bias = dt_bias[:, None]
    skip = d_skip[:, None]
    gain = norm_gain[None]
    cache = cache_state.reshape(width, state)

    def exchange(values):
        return [values[0]] + [
            lax.ppermute(values[k], "sess", [(i, i ^ k) for i in range(peers)])
            for k in range(1, peers)
        ]

    def swapped(value):
        count = lax.axis_size("head")
        return lax.ppermute(value, "head", [(i, i ^ 1) for i in range(count)])

    shape = jax.ShapeDtypeStruct
    small = call(
        functools.partial(small_send, peers),
        [shape((heads + 8, rows), F32)] * peers + [shape((rows, state), BF16)] * peers,
        [SMEM, SMEM, SMEM, VMEM, VMEM, VMEM],
    )(ids, slot_owner, lengths, dt_raw, b, c)
    dtls = exchange(small[:peers])
    bcs = exchange(small[peers:])
    xs = exchange(
        call(
            functools.partial(x_send, peers),
            [shape((rows, width), BF16)] * peers,
            [SMEM, SMEM, ANY],
            [ANY] * peers,
            [pltpu.SemaphoreType.DMA((peers,))],
        )(ids, slot_owner, x_rows)
    )
    mine = call(
        functools.partial(bc_pick, peers, slots),
        shape((rows + HALF, state), BF16),
        [SMEM, SMEM, SMEM] + [VMEM] * peers,
    )(ids, slot_owner, slot_task, *bcs)
    other = swapped(mine)
    yz, ez = call(
        block_part,
        [shape(x_rows.shape, F32)] * 2,
        [SMEM] + [VMEM] * 8,
        flops=2 * slots * rows * rows * width * 2,
        moved=16 * 1024 * 1024,
    )(ids, x_rows, z_rows, b, c, dt_raw, alog, bias, skip)
    out = call(
        functools.partial(owner_part, peers, slots),
        [shape((width, state), BF16)] + [shape((rows, width), BF16)] * peers,
        [SMEM] * 4 + [VMEM] * 5 + [VMEM] * peers + [ANY] * peers,
        [VMEM] + [ANY] * peers,
        [
            pltpu.VMEM((rows, width), BF16),
            pltpu.VMEM((HALF, width), BF16),
            pltpu.VMEM((rows, width), BF16),
            pltpu.VMEM((HALF, width), BF16),
            pltpu.VMEM((rows + HALF, state), BF16),
            pltpu.VMEM((rows + HALF, state), BF16),
            pltpu.SemaphoreType.DMA((2,)),
        ],
    )(ids, slot_owner, slot_task, lengths, cache, alog, bias, mine, other, *dtls, *xs)
    final_state = out[0].reshape(cache_state.shape)
    cars = exchange(out[1:])
    gated, own = call(
        functools.partial(gate_part, peers),
        [shape(x_rows.shape, F32), shape((slots, rows), F32)],
        [SMEM, SMEM, VMEM, VMEM] + [ANY] * peers,
        scratch=[pltpu.VMEM((slots, rows, width), BF16), pltpu.SemaphoreType.DMA((slots,))],
    )(ids, slot_owner, yz, ez, *cars)
    mixed_rows = call(
        functools.partial(norm_part, peers),
        shape(x_rows.shape, BF16),
        [SMEM] * 3 + [VMEM] * 4 + [VMEM] * peers,
    )(ids, slot_owner, slot_task, gated, own, swapped(own), gain, *dtls)
    return (mixed_rows, final_state)


def solution(mesh):
    in_specs = (
        P(("group", "sess", "dp"), None, "head"),
        P(("group", "sess", "dp"), None, "head"),
        P(("group", "sess", "dp"), None, None),
        P(("group", "sess", "dp"), None, None),
        P(("group", "sess", "dp"), "head", None),
        P("head"),
        P("head"),
        P("head"),
        P("head"),
        P(("group", "sess", "dp"), "head", None, None),
        P(("group", "sess", "dp")),
        P("group", None),
        P("group", None),
    )
    out_specs = (
        P(("group", "sess", "dp"), None, "head"),
        P(("group", "sess", "dp"), "head", None, None),
    )
    return jax.shard_map(
        per_device, mesh=mesh, in_specs=in_specs, out_specs=out_specs, check_vma=False
    )
```

time: 135 us -> 82.1 us (0.61)
  local copies, waits for them, and re-layouts: 20.7 us -> 2.59 us
  other arithmetic: 16.1 us -> 0.08 us
  matrix products: 13 us -> 0 us
  Pallas kernels: 0 us -> 12 us
  waiting for transfers between devices: 50.3 us -> 40 us
  blocking collectives: 9.92 us -> 0 us
  starting transfers between devices: 22 us -> 25.4 us
    all_to_all x5 -> x0, waiting for transfers between devices: 50.3 us -> none  [the longest x1 19.6 us: per_device(): lax.all_to_all(slot_piece, 'sess', split_axis=0, concat_axis=1, tiled=True)]
    ppermute x1 -> x14, waiting for transfers between devices: 0.01 us -> 40 us  [the longest x12 37 us: exchange(): lax.ppermute(values[k], 'sess', [(i, i ^ k) for i in range(peers)])]
    ppermute x1 -> x14, starting transfers between devices: 1.55 us -> 25.4 us  [the longest x12 23.3 us: exchange(): lax.ppermute(values[k], 'sess', [(i, i ^ k) for i in range(peers)])]
    all_to_all x5 -> x0, starting transfers between devices: 20.5 us -> none  [the longest x1 5.04 us: per_device(): lax.all_to_all(cache_flat.reshape(sess_count, peer_count, piece), 'sess',...]
    dot_general x11 -> x0, matrix products: 13 us -> none  [the longest x1 1.93 us: per_device(): jnp.einsum('shru,suhp->srhp', weights, x_heads, preferred_element_type=jn...]
    pallas_call x0 -> x7, Pallas kernels: none -> 12 us  [the longest x1 4.4 us: per_device(): call(functools.partial(owner_part, peers, slots), [shape((width, state),...]
    unnamed x1 -> x0, blocking collectives: 9.92 us -> none
    unnamed x49 -> x26, local copies, waits for them, and re-layouts: 7.32 us -> 2.33 us
  transfers between devices with their start and end apart: 6 -> 14, of which waited for: 4 -> 8; matrix products, arithmetic and copies ran while one was open for 25% -> 0% of each run, Pallas kernels for 0% -> 5%
where the time goes in v1:
time: 82.1 us; the launch traced here: 81.5 us
  waiting for transfers between devices  40 us (49%)
  starting transfers between devices  25.4 us (31%)
  Pallas kernels  12 us (15%)
  local copies, waits for them, and re-layouts  2.59 us (3%)
  between operations  1.45 us (2%)
    ppermute x12, waiting for transfers between devices, exchange(): lax.ppermute(values[k], 'sess', [(i, i ^ k) for i in range(peers)])  37 us
    ppermute x12, starting transfers between devices, exchange(): lax.ppermute(values[k], 'sess', [(i, i ^ k) for i in range(peers)])  23.3 us
    pallas_call x1, Pallas kernels, per_device(): call(functools.partial(owner_part, peers, slots), [shape((width, state),...  4.4 us
    ppermute x2, waiting for transfers between devices, swapped(): return lax.ppermute(value, 'head', [(i, i ^ 1) for i in range(count)])  3.03 us
    pallas_call x1, Pallas kernels, per_device(): call(block_part, [shape(x_rows.shape, F32)] * 2, [SMEM] + [VMEM] * 8, flo...  2.93 us
    unnamed x26, local copies, waits for them, and re-layouts  2.33 us
    ppermute x2, starting transfers between devices, swapped(): return lax.ppermute(value, 'head', [(i, i ^ 1) for i in range(count)])  2.16 us
  transfers between devices with their start and end apart: 14, of which 8 were waited for; matrix products, arithmetic and copies ran while one was open for 0% of the time, Pallas kernels for 5%

profile of v1, /device:TPU:0, one launch (start us, length us, event | category | flops | bytes accessed | tf_op | source)
XLA Modules:
  0.0 81.5 jit_solution(3937168869530525133)
XLA Ops:
  0.7 0.6 copy-done.7
  1.3 1.0 %copy-done = bf16[2,128,1024]{2,1,0:T(8,128)(2,1)S(1)} copy-done((bf16[2,128,1024]{2,1,0:T(8,128)(2,1)S(1)}, bf16[2,128,1024]{2,1,0:T(8,128)(2,1)}, u32[]{:S(2)}) %copy-start) | copy-done | bytes 524312
  2.4 0.7 shard_map.143
  3.1 3.1 %collective-permute-start.7 = (bf16[128,1024]{1,0:T(8,128)(2,1)S(1)}, bf16[128,1024]{1,0:T(8,128)(2,1)S(1)}, u32[]{:S(2)}, u32[]{:S(2)}) collective-permute-start(bf16[128,1024]{1,0:T(8,128)(2,1)S(1)} %get-tuple-element.34), channel_id=1, source_target_pairs={{0,4},{4,0},{8,12},{12,8},{1,5},{5,1},{9,13},{13,9},{2,6},{6,2},{1... | collective-permute-start | bytes 786440 | tf_op jit(solution)/shard_map/ppermute | solution.py:341
  6.2 2.6 %collective-permute-start.8 = (bf16[128,1024]{1,0:T(8,128)(2,1)S(1)}, bf16[128,1024]{1,0:T(8,128)(2,1)S(1)}, u32[]{:S(2)}, u32[]{:S(2)}) collective-permute-start(bf16[128,1024]{1,0:T(8,128)(2,1)S(1)} %get-tuple-element.35), channel_id=1, source_target_pairs={{0,8},{4,12},{8,0},{12,4},{1,9},{5,13},{9,1},{13,5},{2,10},{6,14},... | collective-permute-start | bytes 786440 | tf_op jit(solution)/shard_map/ppermute | solution.py:341
  9.5 0.7 shard_map.141
  10.1 1.0 %collective-permute-start = (bf16[128,256]{1,0:T(8,128)(2,1)S(1)}, bf16[128,256]{1,0:T(8,128)(2,1)S(1)}, u32[]{:S(2)}, u32[]{:S(2)}) collective-permute-start(bf16[128,256]{1,0:T(8,128)(2,1)S(1)} %get-tuple-element.26), channel_id=1, source_target_pairs={{0,4},{4,0},{8,12},{12,8},{1,5},{5,1},{9,13},{13,9},{2,6},{6,2},{1... | collective-permute-start | bytes 196616 | tf_op jit(solution)/shard_map/ppermute | solution.py:341
  11.1 3.5 %collective-permute-start.1 = (bf16[128,256]{1,0:T(8,128)(2,1)S(1)}, bf16[128,256]{1,0:T(8,128)(2,1)S(1)}, u32[]{:S(2)}, u32[]{:S(2)}) collective-permute-start(bf16[128,256]{1,0:T(8,128)(2,1)S(1)} %get-tuple-element.27), channel_id=1, source_target_pairs={{0,8},{4,12},{8,0},{12,4},{1,9},{5,13},{9,1},{13,5},{2,10},{6,14},... | collective-permute-start | bytes 196616 | tf_op jit(solution)/shard_map/ppermute | solution.py:341
  14.6 10.6 %collective-permute-done.rest_1_ = bf16[128,256]{1,0:T(8,128)(2,1)S(1)} collective-permute-done((bf16[128,256]{1,0:T(8,128)(2,1)S(1)}, bf16[128,256]{1,0:T(8,128)(2,1)S(1)}, u32[]{:S(2)}, u32[]{:S(2)}) %collective-permute-start) | collective-permute-done | bytes 65568 | tf_op jit(solution)/shard_map/ppermute | solution.py:341
  25.2 2.6 %collective-permute-start.2 = (bf16[128,256]{1,0:T(8,128)(2,1)S(1)}, bf16[128,256]{1,0:T(8,128)(2,1)S(1)}, u32[]{:S(2)}, u32[]{:S(2)}) collective-permute-start(bf16[128,256]{1,0:T(8,128)(2,1)S(1)} %get-tuple-element.28), channel_id=1, source_target_pairs={{0,12},{4,8},{8,4},{12,0},{1,13},{5,9},{9,5},{13,1},{2,14},{6,10},... | collective-permute-start | bytes 196616 | tf_op jit(solution)/shard_map/ppermute | solution.py:341
  27.8 8.9 %collective-permute-done.1.rest_2_ = bf16[128,256]{1,0:T(8,128)(2,1)S(1)} collective-permute-done((bf16[128,256]{1,0:T(8,128)(2,1)S(1)}, bf16[128,256]{1,0:T(8,128)(2,1)S(1)}, u32[]{:S(2)}, u32[]{:S(2)}) %collective-permute-start.1) | collective-permute-done | bytes 65568 | tf_op jit(solution)/shard_map/ppermute | solution.py:341
  36.7 0.7 shard_map.142.mine
  37.3 1.6 %collective-permute-start.3 = (bf16[192,256]{1,0:T(8,128)(2,1)S(1)}, bf16[192,256]{1,0:T(8,128)(2,1)S(1)}, u32[]{:S(2)}, u32[]{:S(2)}) collective-permute-start(bf16[192,256]{1,0:T(8,128)(2,1)S(1)} %shard_map.142.mine), channel_id=1, source_target_pairs={{0,2},{2,0},{1,3},{3,1},{4,6},{6,4},{5,7},{7,5},{8,10},{10,8},{9,1... | collective-permute-start | bytes 294920 | tf_op jit(solution)/shard_map/ppermute | solution.py:347
  38.9 1.3 %collective-permute-start.4 = (f32[24,128]{1,0:T(8,128)S(1)}, f32[24,128]{1,0:T(8,128)S(1)}, u32[]{:S(2)}, u32[]{:S(2)}) collective-permute-start(f32[24,128]{1,0:T(8,128)S(1)} %get-tuple-element.30), channel_id=1, source_target_pairs={{0,4},{4,0},{8,12},{12,8},{1,5},{5,1},{9,13},{13,9},{2,6},{6,2},{1... | collective-permute-start | bytes 36872 | tf_op jit(solution)/shard_map/ppermute | solution.py:341
  40.2 2.4 %collective-permute-done.4.rest_1_ = f32[24,128]{1,0:T(8,128)S(1)} collective-permute-done((f32[24,128]{1,0:T(8,128)S(1)}, f32[24,128]{1,0:T(8,128)S(1)}, u32[]{:S(2)}, u32[]{:S(2)}) %collective-permute-start.4) | collective-permute-done | bytes 12320 | tf_op jit(solution)/shard_map/ppermute | solution.py:341
  42.6 2.3 %collective-permute-start.5 = (f32[24,128]{1,0:T(8,128)S(1)}, f32[24,128]{1,0:T(8,128)S(1)}, u32[]{:S(2)}, u32[]{:S(2)}) collective-permute-start(f32[24,128]{1,0:T(8,128)S(1)} %get-tuple-element.31), channel_id=1, source_target_pairs={{0,8},{4,12},{8,0},{12,4},{1,9},{5,13},{9,1},{13,5},{2,10},{6,14},... | collective-permute-start | bytes 36872 | tf_op jit(solution)/shard_map/ppermute | solution.py:341
  44.9 2.3 %collective-permute-done.5.rest_2_ = f32[24,128]{1,0:T(8,128)S(1)} collective-permute-done((f32[24,128]{1,0:T(8,128)S(1)}, f32[24,128]{1,0:T(8,128)S(1)}, u32[]{:S(2)}, u32[]{:S(2)}) %collective-permute-start.5) | collective-permute-done | bytes 12320 | tf_op jit(solution)/shard_map/ppermute | solution.py:341
  47.2 2.5 %collective-permute-start.6 = (f32[24,128]{1,0:T(8,128)S(1)}, f32[24,128]{1,0:T(8,128)S(1)}, u32[]{:S(2)}, u32[]{:S(2)}) collective-permute-start(f32[24,128]{1,0:T(8,128)S(1)} %get-tuple-element.32), channel_id=1, source_target_pairs={{0,12},{4,8},{8,4},{12,0},{1,13},{5,9},{9,5},{13,1},{2,14},{6,10},... | collective-permute-start | bytes 36872 | tf_op jit(solution)/shard_map/ppermute | solution.py:341
  49.7 0.1 copy.15.alog
  49.8 0.7 copy-done.11
  50.5 2.2 %collective-permute-done.6.rest_3_ = f32[24,128]{1,0:T(8,128)S(1)} collective-permute-done((f32[24,128]{1,0:T(8,128)S(1)}, f32[24,128]{1,0:T(8,128)S(1)}, u32[]{:S(2)}, u32[]{:S(2)}) %collective-permute-start.6) | collective-permute-done | bytes 12320 | tf_op jit(solution)/shard_map/ppermute | solution.py:341
  52.7 4.4 %shard_map.144 = (bf16[1024,256]{1,0:T(8,128)(2,1)}, bf16[128,1024]{1,0:T(8,128)(2,1)S(1)}, bf16[128,1024]{1,0:T(8,128)(2,1)}, bf16[128,1024]{1,0:T(8,128)(2,1)}, bf16[128,1024]{1,0:T(8,128)(2,1)}) custom-call(s32[3]{0:T(128)S(1)} %pad_add_fusion.ids, s32[2,8]{1,0:T(2,128)S(1)} %copy-done.7, s32[2,8]{1,0:T(2,128)S(1)} %copy-done.8, s32[1]{0:T(128)S(6)} %copy.20.lens, ...), custom_call_target="tpu_custom_call" | custom-call | tf_op jit(solution)/shard_map/pallas_call | solution.py:379
  57.2 2.9 %collective-permute-start.11 = (bf16[128,1024]{1,0:T(8,128)(2,1)}, bf16[128,1024]{1,0:T(8,128)(2,1)S(1)}, u32[]{:S(2)}, u32[]{:S(2)}) collective-permute-start(bf16[128,1024]{1,0:T(8,128)(2,1)} %get-tuple-element.39), channel_id=1, source_target_pairs={{0,8},{4,12},{8,0},{12,4},{1,9},{5,13},{9,1},{13,5},{2,10},{6,14},... | collective-permute-start | bytes 786440 | tf_op jit(solution)/shard_map/ppermute | solution.py:341
  60.1 1.5 %collective-permute-start.12 = (bf16[128,1024]{1,0:T(8,128)(2,1)}, bf16[128,1024]{1,0:T(8,128)(2,1)S(1)}, u32[]{:S(2)}, u32[]{:S(2)}) collective-permute-start(bf16[128,1024]{1,0:T(8,128)(2,1)} %get-tuple-element.40), channel_id=1, source_target_pairs={{0,12},{4,8},{8,4},{12,0},{1,13},{5,9},{9,5},{13,1},{2,14},{6,10},... | collective-permute-start | bytes 786440 | tf_op jit(solution)/shard_map/ppermute | solution.py:341
  61.6 0.1 copy.17.skip
  61.7 2.9 %shard_map.140 = (f32[2,128,1024]{2,1,0:T(8,128)S(1)}, f32[2,128,1024]{2,1,0:T(8,128)S(1)}) custom-call(s32[3]{0:T(128)S(1)} %pad_add_fusion.ids, bf16[2,128,1024]{2,1,0:T(8,128)(2,1)S(1)} %copy-done.1, bf16[2,128,1024]{2,1,0:T(8,128)(2,1)S(1)} %copy-done.2, bf16[2,128,256]{2,1,0:T(8,128)(2,1)S(1)} %copy-done.3, bf16[2,128,256]{2,1,0:T(8,128)(2,1)S(1)} %copy-done.4, ...), custom_call_target="tpu_custom_call" | custom-call | flops 134217728 | bytes 16777216 | tf_op jit(solution)/shard_map/pallas_call | solution.py:372
  64.6 3.4 %collective-permute-done.10.rest_1_ = bf16[128,1024]{1,0:T(8,128)(2,1)S(1)} collective-permute-done((bf16[128,1024]{1,0:T(8,128)(2,1)}, bf16[128,1024]{1,0:T(8,128)(2,1)S(1)}, u32[]{:S(2)}, u32[]{:S(2)}) %collective-permute-start.10) | collective-permute-done | bytes 262176 | tf_op jit(solution)/shard_map/ppermute | solution.py:341
  68.1 7.2 %collective-permute-done.11.rest_2_ = bf16[128,1024]{1,0:T(8,128)(2,1)S(1)} collective-permute-done((bf16[128,1024]{1,0:T(8,128)(2,1)}, bf16[128,1024]{1,0:T(8,128)(2,1)S(1)}, u32[]{:S(2)}, u32[]{:S(2)}) %collective-permute-start.11) | collective-permute-done | bytes 262176 | tf_op jit(solution)/shard_map/ppermute | solution.py:341
  75.2 1.1 %shard_map.145 = (f32[2,128,1024]{2,1,0:T(8,128)S(1)}, f32[2,128]{1,0:T(2,128)S(1)}) custom-call(s32[3]{0:T(128)S(1)} %pad_add_fusion.ids, s32[2,8]{1,0:T(2,128)S(1)} %copy-done.7, f32[2,128,1024]{2,1,0:T(8,128)S(1)} %get-tuple-element.23.yz, f32[2,128,1024]{2,1,0:T(8,128)S(1)} %get-tuple-element.24.ez, bf16[128,1024]{1,0:T(8,128)(2,1)S(1)} %get-tuple-element.37.rest_0_, ...), custom_call_target="tpu_custom_call" | custom-call | tf_op jit(solution)/shard_map/pallas_call | solution.py:396
  76.3 0.6 collective-permute-start.13
  76.9 3.0 %collective-permute-done.13.other = f32[2,128]{1,0:T(2,128)S(1)} collective-permute-done((f32[2,128]{1,0:T(2,128)S(1)}, f32[2,128]{1,0:T(2,128)S(1)}, u32[]{:S(2)}, u32[]{:S(2)}) %collective-permute-start.13) | collective-permute-done | bytes 1056 | tf_op jit(solution)/shard_map/ppermute | solution.py:347
  79.9 1.6 %shard_map.146 = bf16[2,128,1024]{2,1,0:T(8,128)(2,1)} custom-call(s32[3]{0:T(128)S(1)} %pad_add_fusion.ids, s32[2,8]{1,0:T(2,128)S(1)} %copy-done.7, s32[2,8]{1,0:T(2,128)S(1)} %copy-done.8, f32[2,128,1024]{2,1,0:T(8,128)S(1)} %get-tuple-element.41.gated, f32[2,128]{1,0:T(2,128)S(1)} %get-tuple-element.42.own, f32[2,128]{1,0:T(2,128)S(1)} %collective-permute-done.13.other, ...), custom_call_target="tpu_custom_call" | custom-call | tf_op jit(solution)/shard_map/pallas_call | solution.py:402
  (34 shorter events, 0.3 us)
Async XLA Ops:
  0.6 8.8 %copy-start.6 = (f32[2,16,128]{2,1,0:T(8,128)S(1)}, f32[2,16,128]{2,1,0:T(8,128)}, u32[]{:S(2)}) copy-start(f32[2,16,128]{2,1,0:T(8,128)} %dt.3) | copy-start | bytes 49156
  0.7 0.7 copy-start.7
  1.3 1.0 %copy-start = (bf16[2,128,1024]{2,1,0:T(8,128)(2,1)S(1)}, bf16[2,128,1024]{2,1,0:T(8,128)(2,1)}, u32[]{:S(2)}) copy-start(bf16[2,128,1024]{2,1,0:T(8,128)(2,1)} %x.3) | copy-start | bytes 1572868
  2.4 7.1 %copy-start.3 = (bf16[2,128,256]{2,1,0:T(8,128)(2,1)S(1)}, bf16[2,128,256]{2,1,0:T(8,128)(2,1)}, u32[]{:S(2)}) copy-start(bf16[2,128,256]{2,1,0:T(8,128)(2,1)} %b.3) | copy-start | bytes 393220
  2.4 7.1 %copy-start.4 = (bf16[2,128,256]{2,1,0:T(8,128)(2,1)S(1)}, bf16[2,128,256]{2,1,0:T(8,128)(2,1)}, u32[]{:S(2)}) copy-start(bf16[2,128,256]{2,1,0:T(8,128)(2,1)} %c.3) | copy-start | bytes 393220
  2.4 50.3 %copy-start.5 = (bf16[1,16,64,256]{3,2,1,0:T(8,128)(2,1)S(1)}, bf16[1,16,64,256]{3,2,1,0:T(8,128)(2,1)}, u32[]{:S(2)}) copy-start(bf16[1,16,64,256]{3,2,1,0:T(8,128)(2,1)} %param.22) | copy-start | bytes 1572868
  3.1 49.6 %collective-permute-start.7 = (bf16[128,1024]{1,0:T(8,128)(2,1)S(1)}, bf16[128,1024]{1,0:T(8,128)(2,1)S(1)}, u32[]{:S(2)}, u32[]{:S(2)}) collective-permute-start(bf16[128,1024]{1,0:T(8,128)(2,1)S(1)} %get-tuple-element.34), channel_id=1, source_target_pairs={{0,4},{4,0},{8,12},{12,8},{1,5},{5,1},{9,13},{13,9},{2,6},{6,2},{1... | collective-permute-start | bytes 786440 | tf_op jit(solution)/shard_map/ppermute | solution.py:341
  6.2 46.5 %collective-permute-start.8 = (bf16[128,1024]{1,0:T(8,128)(2,1)S(1)}, bf16[128,1024]{1,0:T(8,128)(2,1)S(1)}, u32[]{:S(2)}, u32[]{:S(2)}) collective-permute-start(bf16[128,1024]{1,0:T(8,128)(2,1)S(1)} %get-tuple-element.35), channel_id=1, source_target_pairs={{0,8},{4,12},{8,0},{12,4},{1,9},{5,13},{9,1},{13,5},{2,10},{6,14},... | collective-permute-start | bytes 786440 | tf_op jit(solution)/shard_map/ppermute | solution.py:341
  8.8 43.9 %collective-permute-start.9 = (bf16[128,1024]{1,0:T(8,128)(2,1)S(1)}, bf16[128,1024]{1,0:T(8,128)(2,1)S(1)}, u32[]{:S(2)}, u32[]{:S(2)}) collective-permute-start(bf16[128,1024]{1,0:T(8,128)(2,1)S(1)} %get-tuple-element.36), channel_id=1, source_target_pairs={{0,12},{4,8},{8,4},{12,0},{1,13},{5,9},{9,5},{13,1},{2,14},{6,10},... | collective-permute-start | bytes 786440 | tf_op jit(solution)/shard_map/ppermute | solution.py:341
  10.1 15.1 %collective-permute-start = (bf16[128,256]{1,0:T(8,128)(2,1)S(1)}, bf16[128,256]{1,0:T(8,128)(2,1)S(1)}, u32[]{:S(2)}, u32[]{:S(2)}) collective-permute-start(bf16[128,256]{1,0:T(8,128)(2,1)S(1)} %get-tuple-element.26), channel_id=1, source_target_pairs={{0,4},{4,0},{8,12},{12,8},{1,5},{5,1},{9,13},{13,9},{2,6},{6,2},{1... | collective-permute-start | bytes 196616 | tf_op jit(solution)/shard_map/ppermute | solution.py:341
  11.1 25.6 %collective-permute-start.1 = (bf16[128,256]{1,0:T(8,128)(2,1)S(1)}, bf16[128,256]{1,0:T(8,128)(2,1)S(1)}, u32[]{:S(2)}, u32[]{:S(2)}) collective-permute-start(bf16[128,256]{1,0:T(8,128)(2,1)S(1)} %get-tuple-element.27), channel_id=1, source_target_pairs={{0,8},{4,12},{8,0},{12,4},{1,9},{5,13},{9,1},{13,5},{2,10},{6,14},... | collective-permute-start | bytes 196616 | tf_op jit(solution)/shard_map/ppermute | solution.py:341
  25.2 11.5 %copy-start.8 = (s32[2,8]{1,0:T(2,128)S(1)}, s32[2,8]{1,0:T(2,128)}, u32[]{:S(2)}) copy-start(s32[2,8]{1,0:T(2,128)} %task.5) | copy-start | bytes 196
  25.2 11.5 %collective-permute-start.2 = (bf16[128,256]{1,0:T(8,128)(2,1)S(1)}, bf16[128,256]{1,0:T(8,128)(2,1)S(1)}, u32[]{:S(2)}, u32[]{:S(2)}) collective-permute-start(bf16[128,256]{1,0:T(8,128)(2,1)S(1)} %get-tuple-element.28), channel_id=1, source_target_pairs={{0,12},{4,8},{8,4},{12,0},{1,13},{5,9},{9,5},{13,1},{2,14},{6,10},... | collective-permute-start | bytes 196616 | tf_op jit(solution)/shard_map/ppermute | solution.py:341
  37.3 15.3 %collective-permute-start.3 = (bf16[192,256]{1,0:T(8,128)(2,1)S(1)}, bf16[192,256]{1,0:T(8,128)(2,1)S(1)}, u32[]{:S(2)}, u32[]{:S(2)}) collective-permute-start(bf16[192,256]{1,0:T(8,128)(2,1)S(1)} %shard_map.142.mine), channel_id=1, source_target_pairs={{0,2},{2,0},{1,3},{3,1},{4,6},{6,4},{5,7},{7,5},{8,10},{10,8},{9,1... | collective-permute-start | bytes 294920 | tf_op jit(solution)/shard_map/ppermute | solution.py:347
  38.9 3.7 %collective-permute-start.4 = (f32[24,128]{1,0:T(8,128)S(1)}, f32[24,128]{1,0:T(8,128)S(1)}, u32[]{:S(2)}, u32[]{:S(2)}) collective-permute-start(f32[24,128]{1,0:T(8,128)S(1)} %get-tuple-element.30), channel_id=1, source_target_pairs={{0,4},{4,0},{8,12},{12,8},{1,5},{5,1},{9,13},{13,9},{2,6},{6,2},{1... | collective-permute-start | bytes 36872 | tf_op jit(solution)/shard_map/ppermute | solution.py:341
  42.6 4.6 %collective-permute-start.5 = (f32[24,128]{1,0:T(8,128)S(1)}, f32[24,128]{1,0:T(8,128)S(1)}, u32[]{:S(2)}, u32[]{:S(2)}) collective-permute-start(f32[24,128]{1,0:T(8,128)S(1)} %get-tuple-element.31), channel_id=1, source_target_pairs={{0,8},{4,12},{8,0},{12,4},{1,9},{5,13},{9,1},{13,5},{2,10},{6,14},... | collective-permute-start | bytes 36872 | tf_op jit(solution)/shard_map/ppermute | solution.py:341
  47.2 2.5 %copy-start.10 = (f32[16]{0:T(128)S(1)}, f32[16]{0:T(128)}, u32[]{:S(2)}) copy-start(f32[16]{0:T(128)} %param.18) | copy-start | bytes 196
  47.2 5.5 %collective-permute-start.6 = (f32[24,128]{1,0:T(8,128)S(1)}, f32[24,128]{1,0:T(8,128)S(1)}, u32[]{:S(2)}, u32[]{:S(2)}) collective-permute-start(f32[24,128]{1,0:T(8,128)S(1)} %get-tuple-element.32), channel_id=1, source_target_pairs={{0,12},{4,8},{8,4},{12,0},{1,13},{5,9},{9,5},{13,1},{2,14},{6,10},... | collective-permute-start | bytes 36872 | tf_op jit(solution)/shard_map/ppermute | solution.py:341
  49.8 0.7 copy-start.11
  52.7 9.0 %copy-start.1 = (bf16[2,128,1024]{2,1,0:T(8,128)(2,1)S(1)}, bf16[2,128,1024]{2,1,0:T(8,128)(2,1)}, u32[]{:S(2)}) copy-start(bf16[2,128,1024]{2,1,0:T(8,128)(2,1)} %x.3) | copy-start | bytes 1572868
  52.7 9.0 %copy-start.2 = (bf16[2,128,1024]{2,1,0:T(8,128)(2,1)S(1)}, bf16[2,128,1024]{2,1,0:T(8,128)(2,1)}, u32[]{:S(2)}) copy-start(bf16[2,128,1024]{2,1,0:T(8,128)(2,1)} %z.1) | copy-start | bytes 1572868
  57.1 10.9 %collective-permute-start.10 = (bf16[128,1024]{1,0:T(8,128)(2,1)}, bf16[128,1024]{1,0:T(8,128)(2,1)S(1)}, u32[]{:S(2)}, u32[]{:S(2)}) collective-permute-start(bf16[128,1024]{1,0:T(8,128)(2,1)} %get-tuple-element.38), channel_id=1, source_target_pairs={{0,4},{4,0},{8,12},{12,8},{1,5},{5,1},{9,13},{13,9},{2,6},{6,2},{1... | collective-permute-start | bytes 786440 | tf_op jit(solution)/shard_map/ppermute | solution.py:341
  57.2 18.0 %collective-permute-start.11 = (bf16[128,1024]{1,0:T(8,128)(2,1)}, bf16[128,1024]{1,0:T(8,128)(2,1)S(1)}, u32[]{:S(2)}, u32[]{:S(2)}) collective-permute-start(bf16[128,1024]{1,0:T(8,128)(2,1)} %get-tuple-element.39), channel_id=1, source_target_pairs={{0,8},{4,12},{8,0},{12,4},{1,9},{5,13},{9,1},{13,5},{2,10},{6,14},... | collective-permute-start | bytes 786440 | tf_op jit(solution)/shard_map/ppermute | solution.py:341
  60.1 1.5 %copy-start.12 = (f32[16]{0:T(128)S(1)}, f32[16]{0:T(128)}, u32[]{:S(2)}) copy-start(f32[16]{0:T(128)} %param.20) | copy-start | bytes 196
  60.1 15.1 %collective-permute-start.12 = (bf16[128,1024]{1,0:T(8,128)(2,1)}, bf16[128,1024]{1,0:T(8,128)(2,1)S(1)}, u32[]{:S(2)}, u32[]{:S(2)}) collective-permute-start(bf16[128,1024]{1,0:T(8,128)(2,1)} %get-tuple-element.40), channel_id=1, source_target_pairs={{0,12},{4,8},{8,4},{12,0},{1,13},{5,9},{9,5},{13,1},{2,14},{6,10},... | collective-permute-start | bytes 786440 | tf_op jit(solution)/shard_map/ppermute | solution.py:341
  75.2 1.7 %copy-start.9 = (bf16[1024]{0:T(1024)(128)(2,1)S(1)}, bf16[1024]{0:T(1024)(128)(2,1)}, u32[]{:S(2)}) copy-start(bf16[1024]{0:T(1024)(128)(2,1)} %param.21) | copy-start | bytes 6148
  76.3 3.6 %collective-permute-start.13 = (f32[2,128]{1,0:T(2,128)S(1)}, f32[2,128]{1,0:T(2,128)S(1)}, u32[]{:S(2)}, u32[]{:S(2)}) collective-permute-start(f32[2,128]{1,0:T(2,128)S(1)} %get-tuple-element.42.own), channel_id=1, source_target_pairs={{0,2},{2,0},{1,3},{3,1},{4,6},{6,4},{5,7},{7,5},{8,10},{10,8},{9,1... | collective-permute-start | bytes 3080 | tf_op jit(solution)/shard_map/ppermute | solution.py:347

commit v2 on v1

v2 whole, which is shorter than its diff:
```python
import functools

import jax
import jax.numpy as jnp
from jax import lax
from jax.experimental import pallas as pl
from jax.experimental.pallas import tpu as pltpu
from jax.sharding import PartitionSpec as P

F32 = jnp.float32
BF16 = jnp.bfloat16
HALF = 64
VMEM = pl.BlockSpec(memory_space=pltpu.VMEM)
SMEM = pl.BlockSpec(memory_space=pltpu.SMEM)
ANY = pl.BlockSpec(memory_space=pl.ANY)
PARAMS = pltpu.CompilerParams(vmem_limit_bytes=24 * 1024 * 1024)


def dot(a, b, dims, precision=None):
    return lax.dot_general(
        a, b, ((dims[:1], dims[1:]), ((), ())), precision=precision, preferred_element_type=F32
    )


def iota(shape, dim):
    return lax.broadcasted_iota(jnp.int32, shape, dim)


def softplus(v):
    return jnp.maximum(v, 0.0) + jnp.log1p(jnp.exp(-jnp.abs(v)))


def running(v):
    rows = v.shape[1]
    upto = jnp.where(iota((rows, rows), 0) <= iota((rows, rows), 1), 1.0, 0.0).astype(F32)
    return dot(v, upto, (1, 0), lax.Precision.HIGHEST)


def silu(v):
    return v * (1.0 / (1.0 + jnp.exp(-v)))


def choose(index, values):
    out = values[0]
    for k in range(1, len(values)):
        out = jnp.where(index == k, values[k], out)
    return out


def slot_for(ids, owner, k, slots):
    me, dp = ids[0], ids[1]
    pick = jnp.int32(0)
    for j in range(1, slots):
        pick = jnp.where(owner[dp, me * slots + j] == me ^ k, j, pick)
    return pick


def holder(ids, owner, task, slots, k, part):
    me, dp = ids[0], ids[1]
    found = jnp.int32(0)
    for i in range(owner.shape[1]):
        hit = (owner[dp, i] == me ^ k) & (task[dp, i] % 2 == part)
        found = jnp.where(hit, me ^ (i // slots), found)
    return found


def run(choices):
    for pred, copy in choices:
        pl.when(pred)(copy.start)

    def finish():
        for pred, copy in choices:
            pl.when(pred)(copy.wait)

    return finish


def small_send(peers, ids, owner, lens, dt, b, c, *outs):
    slots, heads, rows = dt.shape
    size = jnp.full((heads, rows), lens[0].astype(F32)).astype(BF16)
    for k in range(peers):
        j = slot_for(ids, owner, k, slots)
        out = outs[k]

        @pl.when(ids[2] == 0)
        def _():
            out[:rows] = b[j]

        @pl.when(ids[2] != 0)
        def _():
            out[:rows] = c[j]

        rest = dt[j]
        high = rest.astype(BF16)
        rest = rest - high.astype(F32)
        middle = rest.astype(BF16)
        low = (rest - middle.astype(F32)).astype(BF16)
        out[rows : rows + heads, :rows] = high
        out[rows : rows + heads, rows:] = middle
        out[rows + heads :, :rows] = low
        out[rows + heads :, rows:] = size


def x_send(peers, ids, owner, x, near, *rest):
    far, sem = rest[:-1], rest[-1]
    slots = x.shape[0]
    copies = []

    def move(k, start, out):
        j = slot_for(ids, owner, k, slots)
        copy = pltpu.make_async_copy(x.at[j, pl.ds(start, HALF)], out, sem.at[len(copies)])
        copy.start()
        copies.append(copy)

    for m in range(peers // 2):
        move(1 ^ 2 * m, HALF, near.at[pl.ds((m + 1) * HALF, HALF)])
    for k in range(2, peers):
        move(k, 0, far[k - 2])
    move(1, 0, near.at[pl.ds(0, HALF)])
    for copy in copies:
        copy.wait()


def x_forward(peers, ids, owner, task, x, near, *rest):
    outs, sem = rest[:-1], rest[-1]
    slots = x.shape[0]
    choices = []
    for m in range(1, peers // 2):
        at = holder(ids, owner, task, slots, 2 * m, 0)
        j = slot_for(ids, owner, 2 * m, slots)
        upper = x.at[j, pl.ds(HALF, HALF)]
        passing = near.at[pl.ds((m + 1) * HALF, HALF)]
        for pred, src in ((at == 0, upper), (at == 1, passing)):
            choices.append((pred, pltpu.make_async_copy(src, outs[m - 1], sem.at[m - 1])))
    run(choices)()


def small_pick(peers, slots, heads, ids, owner, task, *rest):
    got = rest[:peers]
    mine, dts, lens = rest[peers:]
    rows = got[0].shape[0] - 2 * heads
    me, dp = ids[0], ids[1]
    for part, count in ((0, rows), (1, HALF)):
        at = holder(ids, owner, task, slots, 0, part)
        for k in range(peers):

            @pl.when(at == k)
            def _():
                mine[part * rows : part * rows + count] = got[k][:count]
                high = got[k][rows : rows + heads, :rows].astype(F32)
                middle = got[k][rows : rows + heads, rows:].astype(F32)
                low = got[k][rows + heads :, :rows].astype(F32)
                dts[part] = high + (middle + low)

    for j in range(slots):
        far = me ^ owner[dp, me * slots + j]
        for k in range(peers):

            @pl.when(far == k)
            def _():
                lens[j] = got[k][rows + heads :, rows:].astype(F32)


def block_part(ids, x, z, b, c, dt, alog, bias, skip, yz, ez):
    slots, rows, width = x.shape
    heads = dt.shape[1]
    size = width // heads
    per = 128 // size
    causal = iota((rows, rows), 0) >= iota((rows, rows), 1)
    lane = iota((rows, 128), 1) // size
    rate = -jnp.exp(alog[...])
    for s in range(slots):
        step = softplus(dt[s] + bias[...])
        log_decay = running(rate * step)
        log_col = jnp.transpose(log_decay)
        decay_col = jnp.exp(log_col)
        scores = jnp.where(causal, dot(c[s], b[s], (1, 1)), 0.0)
        for p in range(width // 128):
            lanes = slice(p * 128, (p + 1) * 128)
            xp = x[s, :, lanes]
            weights = []
            blocks = []
            decay = decay_col[:, p * per : p * per + 1]
            own_skip = skip[p * per : p * per + 1]
            for q in range(per):
                h = p * per + q
                gap = jnp.minimum(log_col[:, h : h + 1] - log_decay[h : h + 1], 0.0)
                weights.append((jnp.exp(gap) * step[h : h + 1] * scores).astype(BF16))
                blocks.append(jnp.where(lane == q, xp, jnp.zeros_like(xp)))
                if q:
                    decay = jnp.where(lane == q, decay_col[:, h : h + 1], decay)
                    own_skip = jnp.where(lane[:1] == q, skip[h : h + 1], own_skip)
            inner = dot(
                jnp.concatenate(weights, axis=1), jnp.concatenate(blocks, axis=0), (1, 0)
            )
            gate = silu(z[s, :, lanes].astype(F32))
            yz[s, :, lanes] = (inner + own_skip * xp.astype(F32)) * gate
            ez[s, :, lanes] = decay * gate


def early_part(ids, cache, mine, other, lower, upper):
    rows = lower.shape[0] + upper.shape[0]

    def work(cs):
        for g in range(cache.shape[0] // 256):
            lanes = slice(g * 256, (g + 1) * 256)
            value = dot(cs[:rows], cache[lanes], (1, 1)).astype(BF16)
            lower[:, lanes] = value[:HALF]
            upper[:, lanes] = value[HALF:]

    @pl.when(ids[2] == 0)
    def _():
        work(other)

    @pl.when(ids[2] != 0)
    def _():
        work(mine)


def owner_part(
    peers, slots, ids, owner, task, lens, cache, alog, bias, mine, other, dts, lower, x, near, *rest
):
    half = peers // 2
    far, onward = rest[: peers - 2], rest[peers - 2 : peers - 3 + half]
    rest = rest[peers - 3 + half :]
    final, cars = rest[0], rest[1 : peers + 1]
    x0, x1, car1, bs, cs, sem = rest[peers + 1 :]
    rows, width = x0.shape
    heads = alog.shape[0]
    size = width // heads
    k0 = holder(ids, owner, task, slots, 0, 0)
    k1 = holder(ids, owner, task, slots, 0, 1)
    j = slot_for(ids, owner, 0, slots)
    loads = []
    for at, out, flag in ((k0, x0.at[pl.ds(0, HALF)], 0), (k1, x1, 1)):
        for k in range(peers):
            src = far[k - 2] if k > 1 else near.at[pl.ds(0, HALF)] if k else x.at[j, pl.ds(0, HALF)]
            loads.append((at == k, pltpu.make_async_copy(src, out, sem.at[flag])))
    out = x0.at[pl.ds(HALF, HALF)]
    for pred, src in [
        (k0 == 0, x.at[j, pl.ds(HALF, HALF)]),
        (k0 == 1, near.at[pl.ds(HALF, HALF)]),
    ] + [(k0 // 2 == m, onward[m - 1]) for m in range(1, half)]:
        loads.append((pred, pltpu.make_async_copy(src, out, sem.at[2])))
    loaded = run(loads)

    @pl.when(ids[2] == 0)
    def _():
        bs[...] = mine[...]
        cs[...] = other[rows:]

    @pl.when(ids[2] != 0)
    def _():
        bs[...] = other[...]
        cs[...] = mine[rows:]

    length = lens[0]
    rate = -jnp.exp(alog[...])
    col = iota((heads, rows), 1)

    def shares(dt, valid):
        step = jnp.where(col < valid, softplus(dt + bias[...]), 0.0)
        log_decay = running(rate * step)
        total = log_decay[:, rows - 1 :]
        share = jnp.exp(total - log_decay) * step
        return jnp.transpose(share), jnp.exp(total).astype(BF16).astype(F32)

    share0, decay0 = shares(dts[0], length)
    share1, decay1 = shares(dts[1], length - rows)
    per = 128 // size
    lane = iota((rows, 128), 1) // size

    def scaled(xv, share, p):
        factor = share[:, p * per : p * per + 1]
        for q in range(1, per):
            factor = jnp.where(
                lane[: xv.shape[0]] == q, share[:, p * per + q : p * per + q + 1], factor
            )
        return (xv.astype(F32) * factor).astype(BF16)

    loaded()
    for g in range(width // 256):
        lanes = slice(g * 256, (g + 1) * 256)
        old = cache[lanes]
        pairs = [(p, slice(p * 128, (p + 1) * 128)) for p in (2 * g, 2 * g + 1)]
        s0 = jnp.concatenate([scaled(x0[:, at], share0, p) for p, at in pairs], axis=1)
        s1 = jnp.concatenate([scaled(x1[:, at], share1[:HALF], p) for p, at in pairs], axis=1)
        local0 = dot(s0, bs[:rows], (0, 0)).astype(BF16).astype(F32)
        local1 = dot(s1, bs[rows:], (0, 0)).astype(BF16).astype(F32)
        late = []
        for q in range(256 // size):
            h = g * (256 // size) + q
            part = slice(q * size, (q + 1) * size)
            start = decay0[h : h + 1] * old[part].astype(F32) + local0[part]
            late.append(start.astype(BF16))
            final[h * size : (h + 1) * size] = (
                decay1[h : h + 1] * late[-1].astype(F32) + local1[part]
            ).astype(BF16)
        late = jnp.concatenate(late, axis=0)
        car1[:, lanes] = dot(cs[...], late, (1, 1)).astype(BF16)

    stores = []
    for k in range(peers):
        stores.append((k0 == k, pltpu.make_async_copy(lower, cars[k], sem.at[0])))
        stores.append((k1 == k, pltpu.make_async_copy(car1, cars[k], sem.at[1])))
    run(stores)()


def gate_part(peers, ids, owner, task, yz, ez, *rest):
    cars, uppers = rest[:peers], rest[peers : 2 * peers]
    gated, squares, got, sem = rest[2 * peers :]
    slots, rows, width = yz.shape
    me, dp = ids[0], ids[1]
    waits = []
    for j in range(slots):
        far = me ^ owner[dp, me * slots + j]
        early = task[dp, me * slots + j] % 2 == 0
        loads = []
        for k in range(peers):
            low = got.at[j, pl.ds(0, HALF)]
            high = got.at[j, pl.ds(HALF, HALF)]
            loads.append((far == k, pltpu.make_async_copy(cars[k], low, sem.at[j, 0])))
            loads.append(
                ((far == k) & early, pltpu.make_async_copy(uppers[k], high, sem.at[j, 1]))
            )
        waits.append(run(loads))
    for j in range(slots):
        waits[j]()
        total = jnp.zeros((rows, 128), F32)
        for p in range(width // 128):
            lanes = slice(p * 128, (p + 1) * 128)
            value = yz[j, :, lanes] + ez[j, :, lanes] * got[j, :, lanes].astype(F32)
            gated[j, :, lanes] = value
            total = total + value * value
        squares[j : j + 1] = jnp.sum(jnp.transpose(total), axis=0, keepdims=True)


def norm_part(ids, task, gated, own, other, gain, lens, mixed):
    slots, rows, width = gated.shape
    me, dp = ids[0], ids[1]
    row = iota((rows, 128), 0).astype(F32)
    for j in range(slots):
        late = task[dp, me * slots + j] % 2
        live = row + (late * rows).astype(F32) < lens[j][:1]
        mean = (own[j : j + 1] + other[j : j + 1]) / (2.0 * width)
        inverse = jnp.transpose(jnp.broadcast_to(lax.rsqrt(mean + 1e-05), (rows, rows)))
        for p in range(width // 128):
            lanes = slice(p * 128, (p + 1) * 128)
            value = gated[j, :, lanes] * inverse * gain[:, lanes].astype(F32)
            mixed[j, :, lanes] = jnp.where(live, value, 0.0).astype(BF16)


def call(kernel, outs, in_specs, out_specs=None, scratch=(), flops=0, moved=0):
    return pl.pallas_call(
        kernel,
        out_shape=outs,
        in_specs=in_specs,
        out_specs=out_specs if out_specs is not None else jax.tree.map(lambda _: VMEM, outs),
        scratch_shapes=scratch,
        compiler_params=PARAMS,
        cost_estimate=pl.CostEstimate(flops=flops, bytes_accessed=moved, transcendentals=0),
    )


def per_device(
    x_rows,
    z_rows,
    input_projection_matrix,
    c_rows,
    dt_raw,
    a_log,
    dt_bias,
    d_skip,
    norm_gain,
    cache_state,
    lengths,
    slot_owner,
    slot_task,
):
    slots, rows, width = x_rows.shape
    heads = dt_raw.shape[1]
    state = cache_state.shape[3]
    peers = lax.axis_size("sess")
    head = lax.axis_index("head")
    groups = input_projection_matrix.shape[2] // state
    if groups > 1:
        at = head // 2 * state
        b = lax.dynamic_slice_in_dim(input_projection_matrix, at, state, 2)
        c = lax.dynamic_slice_in_dim(c_rows, at, state, 2)
    else:
        b, c = input_projection_matrix, c_rows
    ids = jnp.stack([lax.axis_index("sess"), lax.axis_index("dp"), head % 2]).astype(jnp.int32)
    alog = a_log[:, None]
    bias = dt_bias[:, None]
    skip = d_skip[:, None]
    gain = norm_gain[None]
    cache = cache_state.reshape(width, state)

    half = peers // 2

    def far(value, k):
        return lax.ppermute(value, "sess", [(i, i ^ k) for i in range(peers)])

    def swapped(value):
        count = lax.axis_size("head")
        return lax.ppermute(value, "head", [(i, i ^ 1) for i in range(count)])

    shape = jax.ShapeDtypeStruct
    rows_of = lambda count: shape((count, width), BF16)
    dma = lambda *sizes: pltpu.SemaphoreType.DMA(sizes)
    small = call(
        functools.partial(small_send, peers),
        [shape((rows + 2 * heads, state), BF16)] * peers,
        [SMEM, SMEM, SMEM, VMEM, VMEM, VMEM],
    )(ids, slot_owner, lengths, dt_raw, b, c)
    order = list(range(2, peers)) + [1]
    got = {k: far(small[k], k) for k in order}
    near, *sends = call(
        functools.partial(x_send, peers),
        [rows_of((1 + half) * HALF)] + [rows_of(HALF)] * (peers - 2),
        [SMEM, SMEM, ANY],
        [ANY] * (peers - 1),
        [dma(half + peers - 1)],
    )(ids, slot_owner, x_rows)
    near = far(near, 1)
    sends = [far(value, k + 2) for k, value in enumerate(sends)]
    mine, dts, lens = call(
        functools.partial(small_pick, peers, slots, heads),
        [
            shape((rows + HALF, state), BF16),
            shape((2, heads, rows), F32),
            shape((slots, heads, rows), F32),
        ],
        [SMEM, SMEM, SMEM] + [VMEM] * peers,
    )(ids, slot_owner, slot_task, small[0], *[got[k] for k in range(1, peers)])
    other = swapped(mine)
    onward = call(
        functools.partial(x_forward, peers),
        [rows_of(HALF)] * (half - 1),
        [SMEM, SMEM, SMEM, ANY, ANY],
        [ANY] * (half - 1),
        [dma(half - 1)],
    )(ids, slot_owner, slot_task, x_rows, near)
    onward = [far(value, 2 * (m + 1)) for m, value in enumerate(onward)]
    lower, upper = call(
        early_part,
        [rows_of(HALF)] * 2,
        [SMEM, VMEM, VMEM, VMEM],
        flops=2 * rows * width * state,
        moved=2 * 1024 * 1024,
    )(ids, cache, mine, other)
    uppers = {2 * m: far(upper, 2 * m) if m else upper for m in range(half)}
    yz, ez = call(
        block_part,
        [shape(x_rows.shape, F32)] * 2,
        [SMEM] + [VMEM] * 8,
        flops=2 * slots * rows * rows * width * 2,
        moved=9 * 1024 * 1024,
    )(ids, x_rows, z_rows, b, c, dt_raw, alog, bias, skip)
    final, *cars = call(
        functools.partial(owner_part, peers, slots),
        [shape((width, state), BF16)] + [rows_of(HALF)] * peers,
        [SMEM] * 4 + [VMEM] * 6 + [ANY] * (2 + peers - 2 + half),
        [VMEM] + [ANY] * peers,
        [
            pltpu.VMEM((rows, width), BF16),
            pltpu.VMEM((HALF, width), BF16),
            pltpu.VMEM((HALF, width), BF16),
            pltpu.VMEM((rows + HALF, state), BF16),
            pltpu.VMEM((HALF, state), BF16),
            dma(3),
        ],
        flops=4 * rows * width * state,
        moved=9 * 1024 * 1024,
    )(
        ids,
        slot_owner,
        slot_task,
        lengths,
        cache,
        alog,
        bias,
        mine,
        other,
        dts,
        lower,
        x_rows,
        near,
        *sends,
        *onward,
    )
    cars = {0: cars[0]} | {k: far(cars[k], k) for k in order}
    uppers |= {2 * m + 1: far(uppers[2 * m], 1) for m in range(half)}
    gated, own = call(
        functools.partial(gate_part, peers),
        [shape(x_rows.shape, F32), shape((slots, rows), F32)],
        [SMEM, SMEM, SMEM, VMEM, VMEM] + [ANY] * (2 * peers),
        scratch=[pltpu.VMEM((slots, rows, width), BF16), dma(slots, 2)],
    )(
        ids,
        slot_owner,
        slot_task,
        yz,
        ez,
        *[cars[k] for k in range(peers)],
        *[uppers[k] for k in range(peers)],
    )
    mixed_rows = call(
        norm_part,
        shape(x_rows.shape, BF16),
        [SMEM] * 2 + [VMEM] * 5,
    )(ids, slot_task, gated, own, swapped(own), gain, lens)
    return (mixed_rows, final.reshape(cache_state.shape))


def solution(mesh):
    in_specs = (
        P(("group", "sess", "dp"), None, "head"),
        P(("group", "sess", "dp"), None, "head"),
        P(("group", "sess", "dp"), None, None),
        P(("group", "sess", "dp"), None, None),
        P(("group", "sess", "dp"), "head", None),
        P("head"),
        P("head"),
        P("head"),
        P("head"),
        P(("group", "sess", "dp"), "head", None, None),
        P(("group", "sess", "dp")),
        P("group", None),
        P("group", None),
    )
    out_specs = (
        P(("group", "sess", "dp"), None, "head"),
        P(("group", "sess", "dp"), "head", None, None),
    )
    return jax.shard_map(
        per_device, mesh=mesh, in_specs=in_specs, out_specs=out_specs, check_vma=False
    )
```

time: 82.1 us -> 75.1 us (0.915)
  waiting for transfers between devices: 40 us -> 33.3 us
  starting transfers between devices: 25.4 us -> 18.9 us
  local copies, waits for them, and re-layouts: 2.59 us -> 5.95 us
  Pallas kernels: 12 us -> 15.2 us
    ppermute x12 -> x13, waiting for transfers between devices: 37 us -> 27.1 us  [far(): return lax.ppermute(value, 'sess', [(i, i ^ k) for i in range(peers)])]
    ppermute x12 -> x13, starting transfers between devices: 23.3 us -> 16.8 us  [far(): return lax.ppermute(value, 'sess', [(i, i ^ k) for i in range(peers)])]
    unnamed x26 -> x34, local copies, waits for them, and re-layouts: 2.33 us -> 5.69 us
    ppermute x2, waiting for transfers between devices: 3.03 us -> 6.14 us  [swapped(): return lax.ppermute(value, 'head', [(i, i ^ 1) for i in range(count)])]
    pallas_call x4 -> x6, Pallas kernels: 3.62 us -> 5.96 us  [the longest x1 1.57 us: per_device(): call(norm_part, shape(x_rows.shape, BF16), [SMEM] * 2 + [VMEM] * 5)]
  transfers between devices with their start and end apart: 14 -> 15, of which waited for: 8 -> 10; matrix products, arithmetic and copies ran while one was open for 0% -> 0% of each run, Pallas kernels for 5% -> 14%
where the time goes in v2:
time: 75.1 us; the launch traced here: 74.8 us
  waiting for transfers between devices  33.3 us (44%)
  starting transfers between devices  18.9 us (25%)
  Pallas kernels  15.2 us (20%)
  local copies, waits for them, and re-layouts  5.95 us (8%)
  between operations  1.46 us (2%)
    ppermute x13, waiting for transfers between devices, far(): return lax.ppermute(value, 'sess', [(i, i ^ k) for i in range(peers)])  27.1 us
    ppermute x13, starting transfers between devices, far(): return lax.ppermute(value, 'sess', [(i, i ^ k) for i in range(peers)])  16.8 us
    ppermute x2, waiting for transfers between devices, swapped(): return lax.ppermute(value, 'head', [(i, i ^ 1) for i in range(count)])  6.14 us
    unnamed x34, local copies, waits for them, and re-layouts  5.69 us
    pallas_call x1, Pallas kernels, per_device(): call(functools.partial(owner_part, peers, slots), [shape((width, state),...  4.76 us
    pallas_call x1, Pallas kernels, per_device(): call(block_part, [shape(x_rows.shape, F32)] * 2, [SMEM] + [VMEM] * 8, flo...  2.94 us
    ppermute x2, starting transfers between devices, swapped(): return lax.ppermute(value, 'head', [(i, i ^ 1) for i in range(count)])  2.16 us
    pallas_call x1, Pallas kernels, per_device(): call(norm_part, shape(x_rows.shape, BF16), [SMEM] * 2 + [VMEM] * 5)  1.57 us
  transfers between devices with their start and end apart: 15, of which 10 were waited for; matrix products, arithmetic and copies ran while one was open for 0% of the time, Pallas kernels for 14%

profile of v2, /device:TPU:0, one launch (start us, length us, event | category | flops | bytes accessed | tf_op | source)
XLA Modules:
  0.0 74.8 jit_solution(11839847865923759290)
XLA Ops:
  1.3 1.0 %copy-done = bf16[2,128,1024]{2,1,0:T(8,128)(2,1)S(1)} copy-done((bf16[2,128,1024]{2,1,0:T(8,128)(2,1)S(1)}, bf16[2,128,1024]{2,1,0:T(8,128)(2,1)}, u32[]{:S(2)}) %copy-start) | copy-done | bytes 524312
  2.4 1.5 %shard_map.144 = (bf16[192,1024]{1,0:T(8,128)(2,1)S(1)}, bf16[64,1024]{1,0:T(8,128)(2,1)S(1)}, bf16[64,1024]{1,0:T(8,128)(2,1)S(1)}) custom-call(s32[3]{0:T(128)S(1)} %pad_add_fusion.ids, s32[2,8]{1,0:T(2,128)S(1)} %copy-done.11, bf16[2,128,1024]{2,1,0:T(8,128)(2,1)S(1)} %copy-done), custom_call_target="tpu_custom_call" | custom-call | tf_op jit(solution)/shard_map/pallas_call | solution.py:418
  3.9 3.1 %collective-permute-start.4 = (bf16[192,1024]{1,0:T(8,128)(2,1)S(1)}, bf16[192,1024]{1,0:T(8,128)(2,1)S(1)}, u32[]{:S(2)}, u32[]{:S(2)}) collective-permute-start(bf16[192,1024]{1,0:T(8,128)(2,1)S(1)} %get-tuple-element.32), channel_id=1, source_target_pairs={{0,4},{4,0},{8,12},{12,8},{1,5},{5,1},{9,13},{13,9},{2,6},{6,2},{1... | collective-permute-start | bytes 1179656 | tf_op jit(solution)/shard_map/ppermute | solution.py:402
  7.7 0.9 %copy-done.4 = bf16[2,128,256]{2,1,0:T(8,128)(2,1)S(1)} copy-done((bf16[2,128,256]{2,1,0:T(8,128)(2,1)S(1)}, bf16[2,128,256]{2,1,0:T(8,128)(2,1)}, u32[]{:S(2)}) %copy-start.4) | copy-done | bytes 131096
  8.5 0.9 %copy-done.6 = bf16[2,128,256]{2,1,0:T(8,128)(2,1)S(1)} copy-done((bf16[2,128,256]{2,1,0:T(8,128)(2,1)S(1)}, bf16[2,128,256]{2,1,0:T(8,128)(2,1)}, u32[]{:S(2)}) %copy-start.6) | copy-done | bytes 131096
  9.5 0.7 shard_map.141
  10.2 3.0 %collective-permute-start.1 = (bf16[160,256]{1,0:T(8,128)(2,1)S(1)}, bf16[160,256]{1,0:T(8,128)(2,1)S(1)}, u32[]{:S(2)}, u32[]{:S(2)}) collective-permute-start(bf16[160,256]{1,0:T(8,128)(2,1)S(1)} %get-tuple-element.27), channel_id=1, source_target_pairs={{0,8},{4,12},{8,0},{12,4},{1,9},{5,13},{9,1},{13,5},{2,10},{6,14},... | collective-permute-start | bytes 245768 | tf_op jit(solution)/shard_map/ppermute | solution.py:402
  13.2 1.3 %collective-permute-start.2 = (bf16[160,256]{1,0:T(8,128)(2,1)S(1)}, bf16[160,256]{1,0:T(8,128)(2,1)S(1)}, u32[]{:S(2)}, u32[]{:S(2)}) collective-permute-start(bf16[160,256]{1,0:T(8,128)(2,1)S(1)} %get-tuple-element.28), channel_id=1, source_target_pairs={{0,12},{4,8},{8,4},{12,0},{1,13},{5,9},{9,5},{13,1},{2,14},{6,10},... | collective-permute-start | bytes 245768 | tf_op jit(solution)/shard_map/ppermute | solution.py:402
  14.6 5.0 %collective-permute-done.rest_1_ = bf16[160,256]{1,0:T(8,128)(2,1)S(1)} collective-permute-done((bf16[160,256]{1,0:T(8,128)(2,1)S(1)}, bf16[160,256]{1,0:T(8,128)(2,1)S(1)}, u32[]{:S(2)}, u32[]{:S(2)}) %collective-permute-start) | collective-permute-done | bytes 81952 | tf_op jit(solution)/shard_map/ppermute | solution.py:402
  19.7 3.8 %collective-permute-done.2.rest_3_ = bf16[160,256]{1,0:T(8,128)(2,1)S(1)} collective-permute-done((bf16[160,256]{1,0:T(8,128)(2,1)S(1)}, bf16[160,256]{1,0:T(8,128)(2,1)S(1)}, u32[]{:S(2)}, u32[]{:S(2)}) %collective-permute-start.2) | collective-permute-done | bytes 81952 | tf_op jit(solution)/shard_map/ppermute | solution.py:402
  23.6 0.7 shard_map.142
  24.3 1.6 %collective-permute-start.3 = (bf16[192,256]{1,0:T(8,128)(2,1)S(1)}, bf16[192,256]{1,0:T(8,128)(2,1)S(1)}, u32[]{:S(2)}, u32[]{:S(2)}) collective-permute-start(bf16[192,256]{1,0:T(8,128)(2,1)S(1)} %get-tuple-element.29.mine), channel_id=1, source_target_pairs={{0,2},{2,0},{1,3},{3,1},{4,6},{6,4},{5,7},{7,5},{8,10},{10,8},{9,1... | collective-permute-start | bytes 294920 | tf_op jit(solution)/shard_map/ppermute | solution.py:406
  25.9 3.1 %collective-permute-done.3.other = bf16[192,256]{1,0:T(8,128)(2,1)S(1)} collective-permute-done((bf16[192,256]{1,0:T(8,128)(2,1)S(1)}, bf16[192,256]{1,0:T(8,128)(2,1)S(1)}, u32[]{:S(2)}, u32[]{:S(2)}) %collective-permute-start.3) | collective-permute-done | bytes 98336 | tf_op jit(solution)/shard_map/ppermute | solution.py:406
  29.0 0.9 %shard_map.143 = (bf16[64,1024]{1,0:T(8,128)(2,1)S(1)}, bf16[64,1024]{1,0:T(8,128)(2,1)S(1)}) custom-call(s32[3]{0:T(128)S(1)} %pad_add_fusion.ids, bf16[1024,256]{1,0:T(8,128)(2,1)S(1)} %bitcast.8, bf16[192,256]{1,0:T(8,128)(2,1)S(1)} %get-tuple-element.29.mine, bf16[192,256]{1,0:T(8,128)(2,1)S(1)} %collective-permute-done.3.other), custom_call_target="tpu_custom_call" | custom-call | flops 67108864 | bytes 2097152 | tf_op jit(solution)/shard_map/pallas_call | solution.py:445
  29.9 2.0 %collective-permute-start.6 = (bf16[64,1024]{1,0:T(8,128)(2,1)S(1)}, bf16[64,1024]{1,0:T(8,128)(2,1)S(1)}, u32[]{:S(2)}, u32[]{:S(2)}) collective-permute-start(bf16[64,1024]{1,0:T(8,128)(2,1)S(1)} %get-tuple-element.34), channel_id=1, source_target_pairs={{0,12},{4,8},{8,4},{12,0},{1,13},{5,9},{9,5},{13,1},{2,14},{6,10},... | collective-permute-start | bytes 393224 | tf_op jit(solution)/shard_map/ppermute | solution.py:402
  32.6 1.6 %collective-permute-start.7 = (bf16[64,1024]{1,0:T(8,128)(2,1)S(1)}, bf16[64,1024]{1,0:T(8,128)(2,1)S(1)}, u32[]{:S(2)}, u32[]{:S(2)}) collective-permute-start(bf16[64,1024]{1,0:T(8,128)(2,1)S(1)} %shard_map.145), channel_id=1, source_target_pairs={{0,8},{4,12},{8,0},{12,4},{1,9},{5,13},{9,1},{13,5},{2,10},{6,14},... | collective-permute-start | bytes 393224 | tf_op jit(solution)/shard_map/ppermute | solution.py:402
  34.4 0.7 copy-done.15
  35.1 1.0 %collective-permute-start.11 = (bf16[64,1024]{1,0:T(8,128)(2,1)S(1)}, bf16[64,1024]{1,0:T(8,128)(2,1)S(1)}, u32[]{:S(2)}, u32[]{:S(2)}) collective-permute-start(bf16[64,1024]{1,0:T(8,128)(2,1)S(1)} %get-tuple-element.39.rest_4_), channel_id=1, source_target_pairs={{0,4},{4,0},{8,12},{12,8},{1,5},{5,1},{9,13},{13,9},{2,6},{6,2},{1... | collective-permute-start | bytes 393224 | tf_op jit(solution)/shard_map/ppermute | solution.py:402
  36.1 8.7 %collective-permute-done.12.rest_6_ = bf16[64,1024]{1,0:T(8,128)(2,1)S(1)} collective-permute-done((bf16[64,1024]{1,0:T(8,128)(2,1)S(1)}, bf16[64,1024]{1,0:T(8,128)(2,1)S(1)}, u32[]{:S(2)}, u32[]{:S(2)}) %collective-permute-start.12) | collective-permute-done | bytes 131104 | tf_op jit(solution)/shard_map/ppermute | solution.py:402
  44.9 4.3 %collective-permute-done.7.rest_2_ = bf16[64,1024]{1,0:T(8,128)(2,1)S(1)} collective-permute-done((bf16[64,1024]{1,0:T(8,128)(2,1)S(1)}, bf16[64,1024]{1,0:T(8,128)(2,1)S(1)}, u32[]{:S(2)}, u32[]{:S(2)}) %collective-permute-start.7) | collective-permute-done | bytes 131104 | tf_op jit(solution)/shard_map/ppermute | solution.py:402
  49.2 0.7 copy-done.8
  49.8 0.9 %copy-done.9 = bf16[64,1024]{1,0:T(8,128)(2,1)S(1)} copy-done((bf16[64,1024]{1,0:T(8,128)(2,1)S(1)}, bf16[64,1024]{1,0:T(8,128)(2,1)}, u32[]{:S(2)}) %copy-start.9) | copy-done | bytes 131096
  50.8 4.8 %shard_map.146 = (bf16[1024,256]{1,0:T(8,128)(2,1)}, bf16[64,1024]{1,0:T(8,128)(2,1)S(1)}, bf16[64,1024]{1,0:T(8,128)(2,1)}, bf16[64,1024]{1,0:T(8,128)(2,1)}, bf16[64,1024]{1,0:T(8,128)(2,1)}) custom-call(s32[3]{0:T(128)S(1)} %pad_add_fusion.ids, s32[2,8]{1,0:T(2,128)S(1)} %copy-done.11, s32[2,8]{1,0:T(2,128)S(1)} %copy-done.12, s32[1]{0:T(128)S(6)} %copy.20.lens, ...), custom_call_target="tpu_custom_call" | custom-call | flops 134217728 | bytes 9437184 | tf_op jit(solution)/shard_map/pallas_call | solution.py:460
  55.5 2.4 %collective-permute-start.10 = (bf16[64,1024]{1,0:T(8,128)(2,1)}, bf16[64,1024]{1,0:T(8,128)(2,1)S(1)}, u32[]{:S(2)}, u32[]{:S(2)}) collective-permute-start(bf16[64,1024]{1,0:T(8,128)(2,1)} %get-tuple-element.38), channel_id=1, source_target_pairs={{0,12},{4,8},{8,4},{12,0},{1,13},{5,9},{9,5},{13,1},{2,14},{6,10},... | collective-permute-start | bytes 393224 | tf_op jit(solution)/shard_map/ppermute | solution.py:402
  57.9 2.1 %collective-permute-start.9 = (bf16[64,1024]{1,0:T(8,128)(2,1)}, bf16[64,1024]{1,0:T(8,128)(2,1)S(1)}, u32[]{:S(2)}, u32[]{:S(2)}) collective-permute-start(bf16[64,1024]{1,0:T(8,128)(2,1)} %get-tuple-element.37), channel_id=1, source_target_pairs={{0,8},{4,12},{8,0},{12,4},{1,9},{5,13},{9,1},{13,5},{2,10},{6,14},... | collective-permute-start | bytes 393224 | tf_op jit(solution)/shard_map/ppermute | solution.py:402
  60.1 2.9 %shard_map.140 = (f32[2,128,1024]{2,1,0:T(8,128)S(1)}, f32[2,128,1024]{2,1,0:T(8,128)S(1)}) custom-call(s32[3]{0:T(128)S(1)} %pad_add_fusion.ids, bf16[2,128,1024]{2,1,0:T(8,128)(2,1)S(1)} %copy-done.1, bf16[2,128,1024]{2,1,0:T(8,128)(2,1)S(1)} %copy-done.3, bf16[2,128,256]{2,1,0:T(8,128)(2,1)S(1)} %copy-done.5, bf16[2,128,256]{2,1,0:T(8,128)(2,1)S(1)} %copy-done.7, ...), custom_call_target="tpu_custom_call" | custom-call | flops 134217728 | bytes 9437184 | tf_op jit(solution)/shard_map/pallas_call | solution.py:453
  63.0 1.1 %collective-permute-done.10.rest_3_ = bf16[64,1024]{1,0:T(8,128)(2,1)S(1)} collective-permute-done((bf16[64,1024]{1,0:T(8,128)(2,1)}, bf16[64,1024]{1,0:T(8,128)(2,1)S(1)}, u32[]{:S(2)}, u32[]{:S(2)}) %collective-permute-start.10) | collective-permute-done | bytes 131104 | tf_op jit(solution)/shard_map/ppermute | solution.py:402
  64.1 2.5 %collective-permute-done.8.rest_1_ = bf16[64,1024]{1,0:T(8,128)(2,1)S(1)} collective-permute-done((bf16[64,1024]{1,0:T(8,128)(2,1)}, bf16[64,1024]{1,0:T(8,128)(2,1)S(1)}, u32[]{:S(2)}, u32[]{:S(2)}) %collective-permute-start.8) | collective-permute-done | bytes 131104 | tf_op jit(solution)/shard_map/ppermute | solution.py:402
  66.6 1.5 %collective-permute-done.9.rest_2_ = bf16[64,1024]{1,0:T(8,128)(2,1)S(1)} collective-permute-done((bf16[64,1024]{1,0:T(8,128)(2,1)}, bf16[64,1024]{1,0:T(8,128)(2,1)S(1)}, u32[]{:S(2)}, u32[]{:S(2)}) %collective-permute-start.9) | collective-permute-done | bytes 131104 | tf_op jit(solution)/shard_map/ppermute | solution.py:402
  68.1 1.5 %shard_map.147 = (f32[2,128,1024]{2,1,0:T(8,128)S(1)}, f32[2,128]{1,0:T(2,128)S(1)}) custom-call(s32[3]{0:T(128)S(1)} %pad_add_fusion.ids, s32[2,8]{1,0:T(2,128)S(1)} %copy-done.11, s32[2,8]{1,0:T(2,128)S(1)} %copy-done.12, f32[2,128,1024]{2,1,0:T(8,128)S(1)} %get-tuple-element.23.yz, f32[2,128,1024]{2,1,0:T(8,128)S(1)} %get-tuple-element.24.ez, ...), custom_call_target="tpu_custom_call" | custom-call | tf_op jit(solution)/shard_map/pallas_call | solution.py:494
  70.2 3.0 %collective-permute-done.14.other = f32[2,128]{1,0:T(2,128)S(1)} collective-permute-done((f32[2,128]{1,0:T(2,128)S(1)}, f32[2,128]{1,0:T(2,128)S(1)}, u32[]{:S(2)}, u32[]{:S(2)}) %collective-permute-start.14) | collective-permute-done | bytes 1056 | tf_op jit(solution)/shard_map/ppermute | solution.py:406
  73.3 1.6 %shard_map.148 = bf16[2,128,1024]{2,1,0:T(8,128)(2,1)} custom-call(s32[3]{0:T(128)S(1)} %pad_add_fusion.ids, s32[2,8]{1,0:T(2,128)S(1)} %copy-done.12, f32[2,128,1024]{2,1,0:T(8,128)S(1)} %get-tuple-element.40.gated, f32[2,128]{1,0:T(2,128)S(1)} %get-tuple-element.41.own, f32[2,128]{1,0:T(2,128)S(1)} %collective-permute-done.14.other, ...), custom_call_target="tpu_custom_call" | custom-call | tf_op jit(solution)/shard_map/pallas_call | solution.py:508
  (46 shorter events, 2.5 us)
Async XLA Ops:
  0.6 7.0 %copy-start.10 = (f32[2,16,128]{2,1,0:T(8,128)S(1)}, f32[2,16,128]{2,1,0:T(8,128)}, u32[]{:S(2)}) copy-start(f32[2,16,128]{2,1,0:T(8,128)} %dt.3) | copy-start | bytes 49156
  0.7 0.7 copy-start.11
  1.3 1.0 %copy-start = (bf16[2,128,1024]{2,1,0:T(8,128)(2,1)S(1)}, bf16[2,128,1024]{2,1,0:T(8,128)(2,1)}, u32[]{:S(2)}) copy-start(bf16[2,128,1024]{2,1,0:T(8,128)(2,1)} %x.7) | copy-start | bytes 1572868
  2.4 26.6 %copy-start.2 = (bf16[1,16,64,256]{3,2,1,0:T(8,128)(2,1)S(1)}, bf16[1,16,64,256]{3,2,1,0:T(8,128)(2,1)}, u32[]{:S(2)}) copy-start(bf16[1,16,64,256]{3,2,1,0:T(8,128)(2,1)} %param.22) | copy-start | bytes 1572868
  3.9 28.1 %collective-permute-start.4 = (bf16[192,1024]{1,0:T(8,128)(2,1)S(1)}, bf16[192,1024]{1,0:T(8,128)(2,1)S(1)}, u32[]{:S(2)}, u32[]{:S(2)}) collective-permute-start(bf16[192,1024]{1,0:T(8,128)(2,1)S(1)} %get-tuple-element.32), channel_id=1, source_target_pairs={{0,4},{4,0},{8,12},{12,8},{1,5},{5,1},{9,13},{13,9},{2,6},{6,2},{1... | collective-permute-start | bytes 1179656 | tf_op jit(solution)/shard_map/ppermute | solution.py:402
  7.6 0.9 %copy-start.4 = (bf16[2,128,256]{2,1,0:T(8,128)(2,1)S(1)}, bf16[2,128,256]{2,1,0:T(8,128)(2,1)}, u32[]{:S(2)}) copy-start(bf16[2,128,256]{2,1,0:T(8,128)(2,1)} %b.3) | copy-start | bytes 393220
  8.5 0.9 %copy-start.6 = (bf16[2,128,256]{2,1,0:T(8,128)(2,1)S(1)}, bf16[2,128,256]{2,1,0:T(8,128)(2,1)}, u32[]{:S(2)}) copy-start(bf16[2,128,256]{2,1,0:T(8,128)(2,1)} %c.3) | copy-start | bytes 393220
  10.1 9.5 %collective-permute-start = (bf16[160,256]{1,0:T(8,128)(2,1)S(1)}, bf16[160,256]{1,0:T(8,128)(2,1)S(1)}, u32[]{:S(2)}, u32[]{:S(2)}) collective-permute-start(bf16[160,256]{1,0:T(8,128)(2,1)S(1)} %get-tuple-element.26), channel_id=1, source_target_pairs={{0,4},{4,0},{8,12},{12,8},{1,5},{5,1},{9,13},{13,9},{2,6},{6,2},{1... | collective-permute-start | bytes 245768 | tf_op jit(solution)/shard_map/ppermute | solution.py:402
  10.2 9.5 %collective-permute-start.1 = (bf16[160,256]{1,0:T(8,128)(2,1)S(1)}, bf16[160,256]{1,0:T(8,128)(2,1)S(1)}, u32[]{:S(2)}, u32[]{:S(2)}) collective-permute-start(bf16[160,256]{1,0:T(8,128)(2,1)S(1)} %get-tuple-element.27), channel_id=1, source_target_pairs={{0,8},{4,12},{8,0},{12,4},{1,9},{5,13},{9,1},{13,5},{2,10},{6,14},... | collective-permute-start | bytes 245768 | tf_op jit(solution)/shard_map/ppermute | solution.py:402
  13.2 10.3 %copy-start.12 = (s32[2,8]{1,0:T(2,128)S(1)}, s32[2,8]{1,0:T(2,128)}, u32[]{:S(2)}) copy-start(s32[2,8]{1,0:T(2,128)} %task.9) | copy-start | bytes 196
  13.2 10.3 %collective-permute-start.2 = (bf16[160,256]{1,0:T(8,128)(2,1)S(1)}, bf16[160,256]{1,0:T(8,128)(2,1)S(1)}, u32[]{:S(2)}, u32[]{:S(2)}) collective-permute-start(bf16[160,256]{1,0:T(8,128)(2,1)S(1)} %get-tuple-element.28), channel_id=1, source_target_pairs={{0,12},{4,8},{8,4},{12,0},{1,13},{5,9},{9,5},{13,1},{2,14},{6,10},... | collective-permute-start | bytes 245768 | tf_op jit(solution)/shard_map/ppermute | solution.py:402
  23.6 8.4 %copy-start.1 = (bf16[2,128,1024]{2,1,0:T(8,128)(2,1)S(1)}, bf16[2,128,1024]{2,1,0:T(8,128)(2,1)}, u32[]{:S(2)}) copy-start(bf16[2,128,1024]{2,1,0:T(8,128)(2,1)} %x.7) | copy-start | bytes 1572868
  24.3 4.7 %collective-permute-start.3 = (bf16[192,256]{1,0:T(8,128)(2,1)S(1)}, bf16[192,256]{1,0:T(8,128)(2,1)S(1)}, u32[]{:S(2)}, u32[]{:S(2)}) collective-permute-start(bf16[192,256]{1,0:T(8,128)(2,1)S(1)} %get-tuple-element.29.mine), channel_id=1, source_target_pairs={{0,2},{2,0},{1,3},{3,1},{4,6},{6,4},{5,7},{7,5},{8,10},{10,8},{9,1... | collective-permute-start | bytes 294920 | tf_op jit(solution)/shard_map/ppermute | solution.py:406
  25.9 19.0 %collective-permute-start.5 = (bf16[64,1024]{1,0:T(8,128)(2,1)S(1)}, bf16[64,1024]{1,0:T(8,128)(2,1)S(1)}, u32[]{:S(2)}, u32[]{:S(2)}) collective-permute-start(bf16[64,1024]{1,0:T(8,128)(2,1)S(1)} %get-tuple-element.33), channel_id=1, source_target_pairs={{0,8},{4,12},{8,0},{12,4},{1,9},{5,13},{9,1},{13,5},{2,10},{6,14},... | collective-permute-start | bytes 393224 | tf_op jit(solution)/shard_map/ppermute | solution.py:402
  29.8 15.0 %collective-permute-start.12 = (bf16[64,1024]{1,0:T(8,128)(2,1)S(1)}, bf16[64,1024]{1,0:T(8,128)(2,1)S(1)}, u32[]{:S(2)}, u32[]{:S(2)}) collective-permute-start(bf16[64,1024]{1,0:T(8,128)(2,1)S(1)} %get-tuple-element.39.rest_4_), channel_id=1, source_target_pairs={{0,8},{4,12},{8,0},{12,4},{1,9},{5,13},{9,1},{13,5},{2,10},{6,14},... | collective-permute-start | bytes 393224 | tf_op jit(solution)/shard_map/ppermute | solution.py:402
  29.9 14.9 %collective-permute-start.6 = (bf16[64,1024]{1,0:T(8,128)(2,1)S(1)}, bf16[64,1024]{1,0:T(8,128)(2,1)S(1)}, u32[]{:S(2)}, u32[]{:S(2)}) collective-permute-start(bf16[64,1024]{1,0:T(8,128)(2,1)S(1)} %get-tuple-element.34), channel_id=1, source_target_pairs={{0,12},{4,8},{8,4},{12,0},{1,13},{5,9},{9,5},{13,1},{2,14},{6,10},... | collective-permute-start | bytes 393224 | tf_op jit(solution)/shard_map/ppermute | solution.py:402
  32.6 1.7 %copy-start.14 = (f32[16]{0:T(128)S(1)}, f32[16]{0:T(128)}, u32[]{:S(2)}) copy-start(f32[16]{0:T(128)} %param.18) | copy-start | bytes 196
  32.6 16.6 %collective-permute-start.7 = (bf16[64,1024]{1,0:T(8,128)(2,1)S(1)}, bf16[64,1024]{1,0:T(8,128)(2,1)S(1)}, u32[]{:S(2)}, u32[]{:S(2)}) collective-permute-start(bf16[64,1024]{1,0:T(8,128)(2,1)S(1)} %shard_map.145), channel_id=1, source_target_pairs={{0,8},{4,12},{8,0},{12,4},{1,9},{5,13},{9,1},{13,5},{2,10},{6,14},... | collective-permute-start | bytes 393224 | tf_op jit(solution)/shard_map/ppermute | solution.py:402
  34.3 0.7 copy-start.15
  35.1 27.9 %collective-permute-start.11 = (bf16[64,1024]{1,0:T(8,128)(2,1)S(1)}, bf16[64,1024]{1,0:T(8,128)(2,1)S(1)}, u32[]{:S(2)}, u32[]{:S(2)}) collective-permute-start(bf16[64,1024]{1,0:T(8,128)(2,1)S(1)} %get-tuple-element.39.rest_4_), channel_id=1, source_target_pairs={{0,4},{4,0},{8,12},{12,8},{1,5},{5,1},{9,13},{13,9},{2,6},{6,2},{1... | collective-permute-start | bytes 393224 | tf_op jit(solution)/shard_map/ppermute | solution.py:402
  44.8 18.2 %collective-permute-start.13 = (bf16[64,1024]{1,0:T(8,128)(2,1)S(1)}, bf16[64,1024]{1,0:T(8,128)(2,1)S(1)}, u32[]{:S(2)}, u32[]{:S(2)}) collective-permute-start(bf16[64,1024]{1,0:T(8,128)(2,1)S(1)} %collective-permute-done.12.rest_6_), channel_id=1, source_target_pairs={{0,4},{4,0},{8,12},{12,8},{1,5},{5,1},{9,13},{13,9},{2,6},{6,2},{1... | collective-permute-start | bytes 393224 | tf_op jit(solution)/shard_map/ppermute | solution.py:402
  49.2 0.7 copy-start.8
  49.8 0.9 %copy-start.9 = (bf16[64,1024]{1,0:T(8,128)(2,1)S(1)}, bf16[64,1024]{1,0:T(8,128)(2,1)}, u32[]{:S(2)}) copy-start(bf16[64,1024]{1,0:T(8,128)(2,1)} %copy-done.8) | copy-start | bytes 393220
  50.7 9.3 %copy-start.3 = (bf16[2,128,1024]{2,1,0:T(8,128)(2,1)S(1)}, bf16[2,128,1024]{2,1,0:T(8,128)(2,1)}, u32[]{:S(2)}) copy-start(bf16[2,128,1024]{2,1,0:T(8,128)(2,1)} %z.1) | copy-start | bytes 1572868
  50.8 9.3 %copy-start.5 = (bf16[2,128,256]{2,1,0:T(8,128)(2,1)S(1)}, bf16[2,128,256]{2,1,0:T(8,128)(2,1)}, u32[]{:S(2)}) copy-start(bf16[2,128,256]{2,1,0:T(8,128)(2,1)} %b.3) | copy-start | bytes 393220
  50.8 9.3 %copy-start.7 = (bf16[2,128,256]{2,1,0:T(8,128)(2,1)S(1)}, bf16[2,128,256]{2,1,0:T(8,128)(2,1)}, u32[]{:S(2)}) copy-start(bf16[2,128,256]{2,1,0:T(8,128)(2,1)} %c.3) | copy-start | bytes 393220
  55.5 8.6 %collective-permute-start.10 = (bf16[64,1024]{1,0:T(8,128)(2,1)}, bf16[64,1024]{1,0:T(8,128)(2,1)S(1)}, u32[]{:S(2)}, u32[]{:S(2)}) collective-permute-start(bf16[64,1024]{1,0:T(8,128)(2,1)} %get-tuple-element.38), channel_id=1, source_target_pairs={{0,12},{4,8},{8,4},{12,0},{1,13},{5,9},{9,5},{13,1},{2,14},{6,10},... | collective-permute-start | bytes 393224 | tf_op jit(solution)/shard_map/ppermute | solution.py:402
  57.9 8.7 %collective-permute-start.8 = (bf16[64,1024]{1,0:T(8,128)(2,1)}, bf16[64,1024]{1,0:T(8,128)(2,1)S(1)}, u32[]{:S(2)}, u32[]{:S(2)}) collective-permute-start(bf16[64,1024]{1,0:T(8,128)(2,1)} %get-tuple-element.36), channel_id=1, source_target_pairs={{0,4},{4,0},{8,12},{12,8},{1,5},{5,1},{9,13},{13,9},{2,6},{6,2},{1... | collective-permute-start | bytes 393224 | tf_op jit(solution)/shard_map/ppermute | solution.py:402
  57.9 2.1 %copy-start.16 = (f32[16]{0:T(128)S(1)}, f32[16]{0:T(128)}, u32[]{:S(2)}) copy-start(f32[16]{0:T(128)} %param.20) | copy-start | bytes 196
  57.9 10.2 %collective-permute-start.9 = (bf16[64,1024]{1,0:T(8,128)(2,1)}, bf16[64,1024]{1,0:T(8,128)(2,1)S(1)}, u32[]{:S(2)}, u32[]{:S(2)}) collective-permute-start(bf16[64,1024]{1,0:T(8,128)(2,1)} %get-tuple-element.37), channel_id=1, source_target_pairs={{0,8},{4,12},{8,0},{12,4},{1,9},{5,13},{9,1},{13,5},{2,10},{6,14},... | collective-permute-start | bytes 393224 | tf_op jit(solution)/shard_map/ppermute | solution.py:402
  68.1 2.2 %copy-start.13 = (bf16[1024]{0:T(1024)(128)(2,1)S(1)}, bf16[1024]{0:T(1024)(128)(2,1)}, u32[]{:S(2)}) copy-start(bf16[1024]{0:T(1024)(128)(2,1)} %param.21) | copy-start | bytes 6148
  69.6 3.6 %collective-permute-start.14 = (f32[2,128]{1,0:T(2,128)S(1)}, f32[2,128]{1,0:T(2,128)S(1)}, u32[]{:S(2)}, u32[]{:S(2)}) collective-permute-start(f32[2,128]{1,0:T(2,128)S(1)} %get-tuple-element.41.own), channel_id=1, source_target_pairs={{0,2},{2,0},{1,3},{3,1},{4,6},{6,4},{5,7},{7,5},{8,10},{10,8},{9,1... | collective-permute-start | bytes 3080 | tf_op jit(solution)/shard_map/ppermute | solution.py:406

commit v3 on v1

v3 whole, which is shorter than its diff:
```python
import functools

import jax
import jax.numpy as jnp
from jax import lax
from jax.experimental import pallas as pl
from jax.experimental.pallas import tpu as pltpu
from jax.sharding import PartitionSpec as P

F32 = jnp.float32
BF16 = jnp.bfloat16
HALF = 64
VMEM = pl.BlockSpec(memory_space=pltpu.VMEM)
SMEM = pl.BlockSpec(memory_space=pltpu.SMEM)
HBM = pl.BlockSpec(memory_space=pltpu.HBM)
ANY = pl.BlockSpec(memory_space=pl.ANY)


def dot(a, b, dims, precision=None):
    return lax.dot_general(
        a, b, ((dims[:1], dims[1:]), ((), ())), precision=precision, preferred_element_type=F32
    )


def iota(shape, dim):
    return lax.broadcasted_iota(jnp.int32, shape, dim)


def softplus(v):
    return jnp.maximum(v, 0.0) + jnp.log1p(jnp.exp(-jnp.abs(v)))


def running(v):
    rows = v.shape[1]
    upto = jnp.where(iota((rows, rows), 0) <= iota((rows, rows), 1), 1.0, 0.0).astype(F32)
    return dot(v, upto, (1, 0), lax.Precision.HIGHEST)


def silu(v):
    return v * (1.0 / (1.0 + jnp.exp(-v)))


def columns(params):
    heads = params.shape[1]
    eye = iota((heads, heads), 0) == iota((heads, heads), 1)
    return [
        jnp.sum(jnp.where(eye, params[i : i + 1], 0.0), axis=1, keepdims=True)
        for i in range(params.shape[0])
    ]


class Table:
    def __init__(self, tab, peers, slots):
        self.peers, self.slots = peers, slots
        self.me, self.odd, self.length = tab[0], tab[1], tab[2]
        count = peers * slots
        self.owner = lambda i: tab[3 + i]
        self.late = lambda i: tab[3 + count + i] % 2

    def far(self, j):
        return self.me ^ self.owner(self.me * self.slots + j)

    def slot(self, k):
        pick = jnp.int32(0)
        for j in range(1, self.slots):
            pick = jnp.where(self.far(j) == k, j, pick)
        return pick

    def holder(self, k, part):
        found = jnp.int32(0)
        for i in range(self.peers * self.slots):
            hit = (self.owner(i) == self.me ^ k) & (self.late(i) == part)
            found = jnp.where(hit, self.me ^ (i // self.slots), found)
        return found


class Copies:
    def __init__(self, sem):
        self.sem, self.count, self.started = sem, 0, []

    def __call__(self, src, dst, pred=None, again=False):
        self.count += not again
        copy = pltpu.make_async_copy(src, dst, self.sem.at[self.count - 1])
        if pred is None:
            copy.start()
        else:
            pl.when(pred)(copy.start)
        self.started.append((pred, copy))

    def wait(self):
        for pred, copy in self.started:
            if pred is None:
                copy.wait()
            else:
                pl.when(pred)(copy.wait)
        self.started = []


def spans(width):
    return [slice(g * 256, (g + 1) * 256) for g in range(width // 256)]


def chunk(ref, index, width):
    size = width // 256 * HALF
    return ref.at[pl.ds(index * size, size)]


def from_rows(x, j, start, out):
    return [
        (x.at[j, pl.ds(start, HALF), lanes], out.at[pl.ds(g * HALF, HALF)])
        for g, lanes in enumerate(spans(x.shape[2]))
    ]


def tail_of(ref, size, start=0, count=None):
    return ref.at[pl.ds(ref.shape[0] - size + start, size if count is None else count)]


def send_part(peers, tab, x_in, b, c, dt, own, near, *rest):
    far = rest[: peers - 2]
    dtv, packed, x, bc, sem, in_sem = rest[peers - 2 :]
    slots, rows, width = x.shape
    heads = dt.shape[1]
    t = Table(tab, peers, slots)
    copies = Copies(sem)
    first = Copies(in_sem.at[pl.ds(0, 1)])
    first(dt, dtv)
    second = Copies(in_sem.at[pl.ds(1, 2)])
    second(x_in, x)
    second(b, bc, t.odd == 0)
    second(c, bc, t.odd != 0, again=True)
    outs = [own, near] + list(far)
    size = rows + 2 * heads
    first.wait()
    length = jnp.full((heads, rows), t.length.astype(F32)).astype(BF16)
    for j in range(slots):
        value = dtv[j]
        high = value.astype(BF16)
        value = value - high.astype(F32)
        middle = value.astype(BF16)
        low = (value - middle.astype(F32)).astype(BF16)
        packed[j, :heads, :rows] = high
        packed[j, :heads, rows:] = middle
        packed[j, heads:, :rows] = low
        packed[j, heads:, rows:] = length
    second.wait()
    for m in range(peers // 2):
        for src, dst in from_rows(x, t.slot(1 ^ 2 * m), HALF, chunk(near, m + 1, width)):
            copies(src, dst)
    for k in range(peers):
        j = t.slot(k)
        copies(bc.at[j], tail_of(outs[k], size, 0, rows))
        if k:
            for src, dst in from_rows(x, j, 0, chunk(outs[k], 0, width)):
                copies(src, dst)
    for k in range(peers):
        copies(packed.at[t.slot(k)], tail_of(outs[k], size, rows, 2 * heads))
    copies.wait()


def forward_part(peers, slots, tab, x, near, after, *rest):
    outs, sem = rest[:-1], rest[-1]
    rows, width = x.shape[1:]
    t = Table(tab, peers, slots)
    copies = Copies(sem)
    for m in range(1, peers // 2):
        at = t.holder(2 * m, 0)
        copies(chunk(near, m + 1, width), outs[m - 1], at == 1)
        for g, (src, dst) in enumerate(from_rows(x, t.slot(2 * m), HALF, outs[m - 1])):
            copies(src, dst, at == 0, again=not g)
    copies.wait()


def pick_part(peers, slots, heads, tab, *rest):
    got = rest[:peers]
    mine, dts, lens, tails, counts, sem = rest[peers + 1 :]
    rows = mine.shape[0] - HALF
    size = rows + 2 * heads
    t = Table(tab, peers, slots)
    copies = Copies(sem)
    for part in range(2):
        at = t.holder(0, part)
        for k in range(peers):
            copies(tail_of(got[k], size), tails.at[part], at == k, again=k > 0)
    for j in range(slots):
        for k in range(peers):
            copies(
                tail_of(got[k], size, rows + heads, heads), counts.at[j], t.far(j) == k, again=k > 0
            )
    copies.wait()
    mine[:rows] = tails[0, :rows]
    mine[rows:] = tails[1, :HALF]
    for part in range(2):
        first = tails[part, rows : rows + heads].astype(F32)
        second = tails[part, rows + heads :].astype(F32)
        dts[part] = first[:, :rows] + (first[:, rows:] + second[:, :rows])
    for j in range(slots):
        lens[j] = counts[j, :, rows:].astype(F32)


def touch_part(value, out):
    out[...] = jnp.zeros(out.shape, out.dtype)


def share_part(peers, slots, tab, dts, params, share0, share1, decays):
    parts, heads, rows = dts.shape
    width = share0.shape[1]
    size = width // heads
    per = 128 // size
    length = Table(tab, peers, slots).length
    alog, bias, _ = columns(params)
    rate = -jnp.exp(alog)
    col = iota((heads, rows), 1)
    lane = iota((rows, 128), 1) // size
    for part, out in ((0, share0), (1, share1)):
        step = jnp.where(col < length - part * rows, softplus(dts[part] + bias), 0.0)
        log_decay = running(rate * step)
        total = log_decay[:, rows - 1 :]
        share = jnp.transpose(jnp.exp(total - log_decay) * step)
        decays[part] = jnp.broadcast_to(jnp.exp(total).astype(BF16).astype(F32), (heads, 256))
        for p in range(width // 128):
            factor = jnp.broadcast_to(share[:, p * per : p * per + 1], (rows, 128))
            for q in range(1, per):
                factor = jnp.where(lane == q, share[:, p * per + q : p * per + q + 1], factor)
            out[:, p * 128 : (p + 1) * 128] = factor[: out.shape[0]]


def block_part(x_in, z_in, b_in, c_in, dt_in, params, yz, ez, x, z, b, c, dt, sem):
    slots, rows, width = x.shape
    heads = dt.shape[1]
    size = width // heads
    per = 128 // size
    waits = []
    for s in range(slots):
        copies = Copies(sem.at[s])
        for src, dst in ((dt_in, dt), (b_in, b), (c_in, c), (x_in, x), (z_in, z)):
            copies(src.at[s], dst.at[s])
        waits.append(copies)
    causal = iota((rows, rows), 0) >= iota((rows, rows), 1)
    lane = iota((rows, 128), 1) // size
    alog, bias, skip = columns(params)
    rate = -jnp.exp(alog)
    for s in range(slots):
        waits[s].wait()
        step = softplus(dt[s] + bias)
        log_decay = running(rate * step)
        log_col = jnp.transpose(log_decay)
        decay_col = jnp.exp(log_col)
        scores = jnp.where(causal, dot(c[s], b[s], (1, 1)), 0.0)
        for p in range(width // 128):
            lanes = slice(p * 128, (p + 1) * 128)
            xp = x[s, :, lanes]
            weights = []
            parts = []
            decay = decay_col[:, p * per : p * per + 1]
            own_skip = skip[p * per : p * per + 1]
            for q in range(per):
                h = p * per + q
                gap = jnp.minimum(log_col[:, h : h + 1] - log_decay[h : h + 1], 0.0)
                weights.append((jnp.exp(gap) * step[h : h + 1] * scores).astype(BF16))
                parts.append(jnp.where(lane == q, xp, jnp.zeros_like(xp)))
                if q:
                    decay = jnp.where(lane == q, decay_col[:, h : h + 1], decay)
                    own_skip = jnp.where(lane[:1] == q, skip[h : h + 1], own_skip)
            inner = dot(jnp.concatenate(weights, axis=1), jnp.concatenate(parts, axis=0), (1, 0))
            gate = silu(z[s, :, lanes].astype(F32))
            yz[s, :, lanes] = (inner + own_skip * xp.astype(F32)) * gate
            ez[s, :, lanes] = decay * gate


def early_part(peers, slots, tab, cache, mine, other, token, decays, upper):
    def work(cs):
        for lanes in spans(cache.shape[0]):
            upper[:, lanes] = dot(cs[HALF : 2 * HALF], cache[lanes], (1, 1)).astype(BF16)

    odd = Table(tab, peers, slots).odd
    pl.when(odd == 0)(lambda: work(other))
    pl.when(odd != 0)(lambda: work(mine))


def late_part(peers, slots, tab, cache, mine, other, share, decays, x, near, *rest):
    half = peers // 2
    far, onward = rest[: peers - 2], rest[peers - 2 : peers - 3 + half]
    rest = rest[peers - 3 + half :]
    late, second, cars = rest[0], rest[1], rest[2 : peers + 2]
    low, high, car0, car1, bs, cs, sem = rest[peers + 2 :]
    rows, width = share.shape
    heads = decays.shape[1]
    size = width // heads
    t = Table(tab, peers, slots)
    k0, k1, j = t.holder(0, 0), t.holder(0, 1), t.slot(0)
    loads = Copies(sem)
    others = Copies(sem.at[pl.ds(2 * width // 256, width // 256 + 2)])
    straight = [(1, chunk(near, 0, width))] + [
        (k, chunk(far[k - 2], 0, width)) for k in range(2, peers)
    ]
    for g, (src, dst) in enumerate(from_rows(x, j, HALF, high)):
        loads(src, dst, k0 == 0)
    loads(chunk(near, 1, width), high, k0 == 1, again=True)
    for m in range(1, half):
        loads(onward[m - 1], high, k0 // 2 == m, again=True)
    for at, out, use in ((k0, low, loads), (k1, second, others)):
        for g, (src, dst) in enumerate(from_rows(x, j, 0, out)):
            use(src, dst, at == 0)
        for k, src in straight:
            use(src, out, at == k, again=True)

    @pl.when(t.odd == 0)
    def _():
        bs[...] = mine[:rows]
        cs[...] = other[...]

    @pl.when(t.odd != 0)
    def _():
        bs[...] = other[:rows]
        cs[...] = mine[...]

    for lanes in spans(width):
        car0[:, lanes] = dot(cs[:HALF], cache[lanes], (1, 1)).astype(BF16)
    loads.wait()
    for g, lanes in enumerate(spans(width)):
        at = slice(g * HALF, (g + 1) * HALF)
        xv = jnp.concatenate([low[at], high[at]], axis=0).astype(F32)
        local = dot((xv * share[:, lanes]).astype(BF16), bs[...], (0, 0)).astype(BF16).astype(F32)
        for q in range(256 // size):
            h = g * (256 // size) + q
            state = slice(h * size, (h + 1) * size)
            late[state] = (
                decays[0, h : h + 1] * cache[state].astype(F32)
                + local[q * size : (q + 1) * size]
            ).astype(BF16)
        car1[:, lanes] = dot(cs[rows:], late[lanes], (1, 1)).astype(BF16)
    others.wait()
    stores = Copies(sem)
    for at, src in ((k0, car0), (k1, car1)):
        for k in range(peers):
            stores(src, cars[k], at == k, again=k > 0)
    stores.wait()


def final_part(peers, slots, tab, mine, other, share, decays, late, second, final, bs):
    width = share.shape[1]
    heads = decays.shape[1]
    size = width // heads
    rows = mine.shape[0] - HALF
    odd = Table(tab, peers, slots).odd

    @pl.when(odd == 0)
    def _():
        bs[...] = mine[rows:]

    @pl.when(odd != 0)
    def _():
        bs[...] = other[rows:]

    for g, lanes in enumerate(spans(width)):
        xv = second[g * HALF : (g + 1) * HALF].astype(F32)
        local = dot((xv * share[:, lanes]).astype(BF16), bs[...], (0, 0)).astype(BF16).astype(F32)
        for q in range(256 // size):
            h = g * (256 // size) + q
            state = slice(h * size, (h + 1) * size)
            final[state] = (
                decays[1, h : h + 1] * late[state].astype(F32)
                + local[q * size : (q + 1) * size]
            ).astype(BF16)


def gate_part(peers, tab, yz, ez, *rest):
    cars, uppers = rest[:peers], rest[peers : 2 * peers]
    gated, squares, got, sem = rest[2 * peers :]
    slots, rows, width = yz.shape
    t = Table(tab, peers, slots)
    waits = []
    for j in range(slots):
        copies = Copies(sem.at[j])
        early = t.late(t.me * slots + j) == 0
        for k in range(peers):
            copies(cars[k], got.at[j, pl.ds(0, HALF)], t.far(j) == k, again=k > 0)
        for k in range(peers):
            copies(
                uppers[k], got.at[j, pl.ds(HALF, HALF)], (t.far(j) == k) & early, again=k > 0
            )
        waits.append(copies)
    for j in range(slots):
        waits[j].wait()
        total = jnp.zeros((rows, 128), F32)
        for p in range(width // 128):
            lanes = slice(p * 128, (p + 1) * 128)
            value = yz[j, :, lanes] + ez[j, :, lanes] * got[j, :, lanes].astype(F32)
            gated[j, :, lanes] = value
            total = total + value * value
        squares[j : j + 1] = jnp.sum(jnp.transpose(total), axis=0, keepdims=True)


def norm_part(peers, tab, gated, own, other, gain, lens, mixed):
    slots, rows, width = gated.shape
    t = Table(tab, peers, slots)
    row = iota((rows, 128), 0).astype(F32)
    for j in range(slots):
        late = t.late(t.me * slots + j)
        live = row + (late * rows).astype(F32) < lens[j][:1]
        mean = (own[j : j + 1] + other[j : j + 1]) / (2.0 * width)
        inverse = jnp.transpose(jnp.broadcast_to(lax.rsqrt(mean + 1e-05), (rows, rows)))
        for p in range(width // 128):
            lanes = slice(p * 128, (p + 1) * 128)
            value = gated[j, :, lanes] * inverse * gain[:, lanes].astype(F32)
            mixed[j, :, lanes] = jnp.where(live, value, 0.0).astype(BF16)


def call(kernel, outs, in_specs, out_specs=None, scratch=(), limit=24, cost=0):
    return pl.pallas_call(
        kernel,
        out_shape=outs,
        in_specs=in_specs,
        out_specs=out_specs if out_specs is not None else jax.tree.map(lambda _: VMEM, outs),
        scratch_shapes=scratch,
        compiler_params=pltpu.CompilerParams(vmem_limit_bytes=limit * 1024 * 1024),
        cost_estimate=pl.CostEstimate(flops=0, bytes_accessed=cost, transcendentals=0),
    )


def per_device(
    x_rows,
    z_rows,
    input_projection_matrix,
    c_rows,
    dt_raw,
    a_log,
    dt_bias,
    d_skip,
    norm_gain,
    cache_state,
    lengths,
    slot_owner,
    slot_task,
):
    slots, rows, width = x_rows.shape
    heads = dt_raw.shape[1]
    state = cache_state.shape[3]
    peers = lax.axis_size("sess")
    half = peers // 2
    head = lax.axis_index("head")
    groups = input_projection_matrix.shape[2] // state
    if groups > 1:
        at = head // 2 * state
        b = lax.dynamic_slice_in_dim(input_projection_matrix, at, state, 2)
        c = lax.dynamic_slice_in_dim(c_rows, at, state, 2)
    else:
        b, c = input_projection_matrix, c_rows

    def own_row(table):
        mine = iota(table.shape, 0) == lax.axis_index("dp")
        return jnp.sum(jnp.where(mine, table, 0), axis=0)

    ids = jnp.stack([lax.axis_index("sess"), head % 2]).astype(jnp.int32)
    tab = jnp.concatenate([ids, lengths, own_row(slot_owner), own_row(slot_task)])
    params = jnp.stack([a_log, dt_bias, d_skip])
    cache = cache_state.reshape(width, state)

    def far(value, k):
        return lax.ppermute(value, "sess", [(i, i ^ k) for i in range(peers)])

    def swapped(value):
        count = lax.axis_size("head")
        return lax.ppermute(value, "head", [(i, i ^ 1) for i in range(count)])

    def scratch(*sizes, dtype=BF16):
        return pltpu.VMEM(sizes, dtype)

    shape = jax.ShapeDtypeStruct
    dma = lambda *sizes: pltpu.SemaphoreType.DMA(sizes)
    bind = lambda kernel, *more: functools.partial(kernel, peers, *more)
    count = width // 256
    piece = count * HALF
    tail = rows + 2 * heads
    packed = lambda size: shape((size, 256), BF16)
    upper_rows = shape((HALF, width), BF16)
    own, near, *sends = call(
        bind(send_part),
        [packed(tail), packed((1 + half) * piece + tail)] + [packed(piece + tail)] * (peers - 2),
        [SMEM, HBM, HBM, HBM, HBM],
        [ANY] * peers,
        [
            scratch(*dt_raw.shape, dtype=F32),
            scratch(slots, 2 * heads, state),
            scratch(*x_rows.shape),
            scratch(*b.shape),
            dma((half + peers - 1) * count + 2 * peers),
            dma(3),
        ],
        limit=60,
    )(tab, x_rows, b, c, dt_raw)
    near = far(near, 1)
    sends = [far(value, k + 2) for k, value in enumerate(sends)]
    yz, ez = call(
        block_part,
        [shape(x_rows.shape, F32)] * 2,
        [HBM] * 5 + [VMEM],
        scratch=[
            scratch(*x_rows.shape),
            scratch(*x_rows.shape),
            scratch(*b.shape),
            scratch(*b.shape),
            scratch(*dt_raw.shape, dtype=F32),
            dma(slots, 5),
        ],
    )(x_rows, z_rows, b, c, dt_raw, params)
    passing = call(
        bind(forward_part, slots),
        [packed(piece)] * (half - 1),
        [SMEM, HBM, ANY, ANY],
        [ANY] * (half - 1),
        [dma((half - 1) * count)],
    )(tab, x_rows, near, ez)
    onward = [far(value, 2 * (m + 1)) for m, value in enumerate(passing)]
    mine, dts, lens = call(
        bind(pick_part, slots, heads),
        [
            shape((rows + HALF, state), BF16),
            shape((2, heads, rows), F32),
            shape((slots, heads, rows), F32),
        ],
        [SMEM] + [ANY] * (peers + 1),
        scratch=[scratch(2, tail, 256), scratch(slots, heads, 256), dma(2 + slots)],
    )(tab, own, near, *sends, passing[0])
    other = swapped(mine)
    share0, share1, decays = call(
        bind(share_part, slots),
        [shape((rows, width), F32), shape((HALF, width), F32), shape((2, heads, 256), F32)],
        [SMEM, VMEM, VMEM],
    )(tab, dts, params)
    token = call(touch_part, shape((8, 128), F32), [ANY], cost=40_000_000)(onward[0])
    upper = call(
        bind(early_part, slots), upper_rows, [SMEM, VMEM, VMEM, VMEM, ANY, ANY]
    )(tab, cache, mine, other, token, decays)
    uppers = {2 * m: far(upper, 2 * m) if m else upper for m in range(half)}
    late, second, *cars = call(
        bind(late_part, slots),
        [shape((width, state), BF16), packed(piece)] + [upper_rows] * peers,
        [SMEM] + [VMEM] * 5 + [HBM] + [ANY] * (peers + half - 2),
        [VMEM, VMEM] + [ANY] * peers,
        [
            scratch(piece, 256),
            scratch(piece, 256),
            scratch(HALF, width),
            scratch(HALF, width),
            scratch(rows, state),
            scratch(rows + HALF, state),
            dma(3 * count + 2),
        ],
    )(tab, cache, mine, other, share0, decays, x_rows, near, *sends, *onward)
    cars = {0: cars[0]} | {k: far(cars[k], k) for k in list(range(2, peers)) + [1]}
    uppers |= {2 * m + 1: far(uppers[2 * m], 1) for m in range(half)}
    final = call(
        bind(final_part, slots),
        shape((width, state), BF16),
        [SMEM] + [VMEM] * 6,
        scratch=[scratch(HALF, state)],
    )(tab, mine, other, share1, decays, late, second)
    gated, squares = call(
        bind(gate_part),
        [shape(x_rows.shape, F32), shape((slots, rows), F32)],
        [SMEM, VMEM, VMEM] + [ANY] * (2 * peers),
        scratch=[scratch(slots, rows, width), dma(slots, 2)],
    )(
        tab,
        yz,
        ez,
        *[cars[k] for k in range(peers)],
        *[uppers[k] for k in range(peers)],
    )
    mixed_rows = call(bind(norm_part), shape(x_rows.shape, BF16), [SMEM] + [VMEM] * 5)(
        tab, gated, squares, swapped(squares), norm_gain[None], lens
    )
    return (mixed_rows, final.reshape(cache_state.shape))


def solution(mesh):
    in_specs = (
        P(("group", "sess", "dp"), None, "head"),
        P(("group", "sess", "dp"), None, "head"),
        P(("group", "sess", "dp"), None, None),
        P(("group", "sess", "dp"), None, None),
        P(("group", "sess", "dp"), "head", None),
        P("head"),
        P("head"),
        P("head"),
        P("head"),
        P(("group", "sess", "dp"), "head", None, None),
        P(("group", "sess", "dp")),
        P("group", None),
        P("group", None),
    )
    out_specs = (
        P(("group", "sess", "dp"), None, "head"),
        P(("group", "sess", "dp"), "head", None, None),
    )
    return jax.shard_map(
        per_device, mesh=mesh, in_specs=in_specs, out_specs=out_specs, check_vma=False
    )
```

time: 82.1 us -> 64.6 us (0.79)
  waiting for transfers between devices: 40 us -> 22 us
  Pallas kernels: 12 us -> 17.4 us
  starting transfers between devices: 25.4 us -> 20 us
    ppermute x12 -> x10, waiting for transfers between devices: 37 us -> 20.3 us  [far(): return lax.ppermute(value, 'sess', [(i, i ^ k) for i in range(peers)])]
    ppermute x12 -> x10, starting transfers between devices: 23.3 us -> 16.9 us  [far(): return lax.ppermute(value, 'sess', [(i, i ^ k) for i in range(peers)])]
    pallas_call x7 -> x11, Pallas kernels: 12 us -> 17.4 us  [the longest x1 3.06 us: per_device(): call(bind(send_part), [packed(tail), packed((1 + half) * piece + tail)] +...]
    ppermute x2, waiting for transfers between devices: 3.03 us -> 1.72 us  [swapped(): return lax.ppermute(value, 'head', [(i, i ^ 1) for i in range(count)])]
    ppermute x2, starting transfers between devices: 2.16 us -> 3.11 us  [swapped(): return lax.ppermute(value, 'head', [(i, i ^ 1) for i in range(count)])]
    unnamed x26 -> x24, local copies, waits for them, and re-layouts: 2.33 us -> 1.75 us
  transfers between devices with their start and end apart: 14 -> 12, of which waited for: 8 -> 10; matrix products, arithmetic and copies ran while one was open for 0% -> 0% of each run, Pallas kernels for 5% -> 16%
where the time goes in v3:
time: 64.6 us; the launch traced here: 64.1 us
  waiting for transfers between devices  22 us (34%)
  starting transfers between devices  20 us (31%)
  Pallas kernels  17.4 us (27%)
  local copies, waits for them, and re-layouts  2.39 us (4%)
  between operations  1.5 us (2%)
  other arithmetic  0.8 us (1%)
    ppermute x10, waiting for transfers between devices, far(): return lax.ppermute(value, 'sess', [(i, i ^ k) for i in range(peers)])  20.3 us
    ppermute x10, starting transfers between devices, far(): return lax.ppermute(value, 'sess', [(i, i ^ k) for i in range(peers)])  16.9 us
    ppermute x2, starting transfers between devices, swapped(): return lax.ppermute(value, 'head', [(i, i ^ 1) for i in range(count)])  3.11 us
    pallas_call x1, Pallas kernels, per_device(): call(bind(send_part), [packed(tail), packed((1 + half) * piece + tail)] +...  3.06 us
    pallas_call x1, Pallas kernels, per_device(): call(block_part, [shape(x_rows.shape, F32)] * 2, [HBM] * 5 + [VMEM], scra...  2.87 us
    pallas_call x1, Pallas kernels, per_device(): call(bind(late_part, slots), [shape((width, state), BF16), packed(piece)]...  2.65 us
    unnamed x24, local copies, waits for them, and re-layouts  1.75 us
    ppermute x2, waiting for transfers between devices, swapped(): return lax.ppermute(value, 'head', [(i, i ^ 1) for i in range(count)])  1.72 us
  transfers between devices with their start and end apart: 12, of which 10 were waited for; matrix products, arithmetic and copies ran while one was open for 0% of the time, Pallas kernels for 16%

profile of v3, /device:TPU:0, one launch (start us, length us, event | category | flops | bytes accessed | tf_op | source)
XLA Modules:
  0.0 64.1 jit_solution(1711175326098297111)
XLA Ops:
  1.4 0.8 %select_reduce_fusion = (s32[8]{0:T(128)S(1)}, s32[8]{0:T(128)S(1)}) fusion(s32[2,8]{1,0:T(2,128)} %param.25, pred[2]{0:T(512)(128)(4,1)S(1)} %iota_compare_fusion, s32[2,8]{1,0:T(2,128)} %param.24), kind=kLoop, calls=%fused_computation.1 | loop fusion | flops 48 | bytes 194 | tf_op jit(solution)/shard_map/reduce_sum | solution.py:453
  2.2 0.6 concatenate.3.tab
  2.8 3.1 %shard_map.141 = (bf16[160,256]{1,0:T(8,128)(2,1)}, bf16[928,256]{1,0:T(8,128)(2,1)}, bf16[416,256]{1,0:T(8,128)(2,1)}, bf16[416,256]{1,0:T(8,128)(2,1)}) custom-call(s32[19]{0:T(128)} %concatenate.3.tab, bf16[2,128,1024]{2,1,0:T(8,128)(2,1)} %x.3, bf16[2,128,256]{2,1,0:T(8,128)(2,1)} %b.1, bf16[2,128,256]{2,1,0:T(8,128)(2,1)} %c.1, f32[2,16,128]{2,1,0:T(8,128)} %dt.1), custom_call_target="tpu_custom_call" | custom-call | tf_op jit(solution)/shard_map/pallas_call | solution.py:478
  5.9 3.1 %collective-permute-start = (bf16[928,256]{1,0:T(8,128)(2,1)}, bf16[928,256]{1,0:T(8,128)(2,1)S(1)}, u32[]{:S(2)}, u32[]{:S(2)}) collective-permute-start(bf16[928,256]{1,0:T(8,128)(2,1)} %get-tuple-element.25), channel_id=1, source_target_pairs={{0,4},{4,0},{8,12},{12,8},{1,5},{5,1},{9,13},{13,9},{2,6},{6,2},{1... | collective-permute-start | bytes 1425416 | tf_op jit(solution)/shard_map/ppermute | solution.py:461
  9.0 2.6 %collective-permute-start.1 = (bf16[416,256]{1,0:T(8,128)(2,1)}, bf16[416,256]{1,0:T(8,128)(2,1)S(1)}, u32[]{:S(2)}, u32[]{:S(2)}) collective-permute-start(bf16[416,256]{1,0:T(8,128)(2,1)} %get-tuple-element.26), channel_id=1, source_target_pairs={{0,8},{4,12},{8,0},{12,4},{1,9},{5,13},{9,1},{13,5},{2,10},{6,14},... | collective-permute-start | bytes 638984 | tf_op jit(solution)/shard_map/ppermute | solution.py:461
  11.6 0.6 %copy-done.9 = f32[16]{0:T(128)S(1)} copy-done((f32[16]{0:T(128)S(1)}, f32[16]{0:T(128)}, u32[]{:S(2)}) %copy-start.9) | copy-done | bytes 88
  12.3 1.0 %copy-done.2 = bf16[2,128,1024]{2,1,0:T(8,128)(2,1)S(1)} copy-done((bf16[2,128,1024]{2,1,0:T(8,128)(2,1)S(1)}, bf16[2,128,1024]{2,1,0:T(8,128)(2,1)}, u32[]{:S(2)}) %copy-start.2) | copy-done | bytes 524312
  13.3 2.9 %shard_map.140 = (f32[2,128,1024]{2,1,0:T(8,128)S(1)}, f32[2,128,1024]{2,1,0:T(8,128)S(1)}) custom-call(bf16[2,128,1024]{2,1,0:T(8,128)(2,1)S(1)} %copy-done, bf16[2,128,1024]{2,1,0:T(8,128)(2,1)S(1)} %copy-done.2, bf16[2,128,256]{2,1,0:T(8,128)(2,1)S(1)} %copy-done.3, bf16[2,128,256]{2,1,0:T(8,128)(2,1)S(1)} %copy-done.4, f32[2,16,128]{2,1,0:T(8,128)S(1)} %copy-done.6, ...), custom_call_target="tpu_custom_call" | custom-call | tf_op jit(solution)/shard_map/pallas_call | solution.py:495
  16.2 8.4 %collective-permute-done.near.rest_1_ = bf16[928,256]{1,0:T(8,128)(2,1)S(1)} collective-permute-done((bf16[928,256]{1,0:T(8,128)(2,1)}, bf16[928,256]{1,0:T(8,128)(2,1)S(1)}, u32[]{:S(2)}, u32[]{:S(2)}) %collective-permute-start) | collective-permute-done | bytes 475168 | tf_op jit(solution)/shard_map/ppermute | solution.py:461
  24.6 0.8 %shard_map.142.rest_4_ = bf16[256,256]{1,0:T(8,128)(2,1)S(1)} custom-call(s32[19]{0:T(128)S(1)} %copy-done.7, bf16[2,128,1024]{2,1,0:T(8,128)(2,1)S(1)} %copy-done, bf16[928,256]{1,0:T(8,128)(2,1)S(1)} %collective-permute-done.near.rest_1_, f32[2,128,1024]{2,1,0:T(8,128)S(1)} %get-tuple-element.23.after.ez), custom_call_target="tpu_custom_call" | custom-call | tf_op jit(solution)/shard_map/pallas_call | solution.py:508
  25.4 3.1 %collective-permute-start.4 = (bf16[256,256]{1,0:T(8,128)(2,1)S(1)}, bf16[256,256]{1,0:T(8,128)(2,1)S(1)}, u32[]{:S(2)}, u32[]{:S(2)}) collective-permute-start(bf16[256,256]{1,0:T(8,128)(2,1)S(1)} %shard_map.142.rest_4_), channel_id=1, source_target_pairs={{0,8},{4,12},{8,0},{12,4},{1,9},{5,13},{9,1},{13,5},{2,10},{6,14},... | collective-permute-start | bytes 393224 | tf_op jit(solution)/shard_map/ppermute | solution.py:461
  28.6 4.0 %collective-permute-done.2.rest_3_.rest_1_ = bf16[416,256]{1,0:T(8,128)(2,1)S(1)} collective-permute-done((bf16[416,256]{1,0:T(8,128)(2,1)}, bf16[416,256]{1,0:T(8,128)(2,1)S(1)}, u32[]{:S(2)}, u32[]{:S(2)}) %collective-permute-start.2) | collective-permute-done | bytes 213024 | tf_op jit(solution)/shard_map/ppermute | solution.py:461
  32.6 1.0 %shard_map.143 = (bf16[192,256]{1,0:T(8,128)(2,1)S(1)}, f32[2,16,128]{2,1,0:T(8,128)S(1)}, f32[2,16,128]{2,1,0:T(8,128)S(1)}) custom-call(s32[19]{0:T(128)S(1)} %copy-done.7, bf16[160,256]{1,0:T(8,128)(2,1)S(1)} %copy-done.5, bf16[928,256]{1,0:T(8,128)(2,1)S(1)} %collective-permute-done.near.rest_1_, ...), custom_call_target="tpu_custom_call" | custom-call | tf_op jit(solution)/shard_map/pallas_call | solution.py:516
  33.6 1.6 %collective-permute-start.3 = (bf16[192,256]{1,0:T(8,128)(2,1)S(1)}, bf16[192,256]{1,0:T(8,128)(2,1)S(1)}, u32[]{:S(2)}, u32[]{:S(2)}) collective-permute-start(bf16[192,256]{1,0:T(8,128)(2,1)S(1)} %get-tuple-element.28.mine), channel_id=1, source_target_pairs={{0,2},{2,0},{1,3},{3,1},{4,6},{6,4},{5,7},{7,5},{8,10},{10,8},{9,1... | collective-permute-start | bytes 294920 | tf_op jit(solution)/shard_map/ppermute | solution.py:465
  35.2 1.6 %shard_map.144 = (f32[128,1024]{1,0:T(8,128)S(1)}, f32[64,1024]{1,0:T(8,128)S(1)}, f32[2,16,256]{2,1,0:T(8,128)S(1)}) custom-call(s32[19]{0:T(128)S(1)} %copy-done.7, f32[2,16,128]{2,1,0:T(8,128)S(1)} %get-tuple-element.29.dts, f32[3,16]{1,0:T(4,128)S(1)} %pad_maximum_fusion.params), custom_call_target="tpu_custom_call" | custom-call | tf_op jit(solution)/shard_map/pallas_call | solution.py:527
  37.0 1.3 %collective-permute-done.3.other = bf16[192,256]{1,0:T(8,128)(2,1)S(1)} collective-permute-done((bf16[192,256]{1,0:T(8,128)(2,1)S(1)}, bf16[192,256]{1,0:T(8,128)(2,1)S(1)}, u32[]{:S(2)}, u32[]{:S(2)}) %collective-permute-start.3) | collective-permute-done | bytes 98336 | tf_op jit(solution)/shard_map/ppermute | solution.py:465
  38.3 0.8 %shard_map.147.rest_4_ = bf16[64,1024]{1,0:T(8,128)(2,1)S(1)} custom-call(s32[19]{0:T(128)S(1)} %copy-done.7, bf16[1024,256]{1,0:T(8,128)(2,1)S(1)} %bitcast.7, bf16[192,256]{1,0:T(8,128)(2,1)S(1)} %get-tuple-element.28.mine, bf16[192,256]{1,0:T(8,128)(2,1)S(1)} %collective-permute-done.3.other, f32[8,128]{1,0:T(8,128)S(1)} %shard_map.146.token, ...), custom_call_target="tpu_custom_call" | custom-call | tf_op jit(solution)/shard_map/pallas_call | solution.py:533
  39.1 2.4 %collective-permute-start.9 = (bf16[64,1024]{1,0:T(8,128)(2,1)S(1)}, bf16[64,1024]{1,0:T(8,128)(2,1)S(1)}, u32[]{:S(2)}, u32[]{:S(2)}) collective-permute-start(bf16[64,1024]{1,0:T(8,128)(2,1)S(1)} %shard_map.147.rest_4_), channel_id=1, source_target_pairs={{0,8},{4,12},{8,0},{12,4},{1,9},{5,13},{9,1},{13,5},{2,10},{6,14},... | collective-permute-start | bytes 393224 | tf_op jit(solution)/shard_map/ppermute | solution.py:461
  41.6 2.6 %shard_map.145 = (bf16[1024,256]{1,0:T(8,128)(2,1)S(1)}, bf16[256,256]{1,0:T(8,128)(2,1)S(1)}, bf16[64,1024]{1,0:T(8,128)(2,1)S(1)}, bf16[64,1024]{1,0:T(8,128)(...) custom-call(s32[19]{0:T(128)S(1)} %copy-done.7, bf16[1024,256]{1,0:T(8,128)(2,1)S(1)} %bitcast.8, ...), custom_call_target="tpu_custom_call" | custom-call | tf_op jit(solution)/shard_map/pallas_call | solution.py:537
  44.2 2.1 %collective-permute-start.5 = (bf16[64,1024]{1,0:T(8,128)(2,1)S(1)}, bf16[64,1024]{1,0:T(8,128)(2,1)S(1)}, u32[]{:S(2)}, u32[]{:S(2)}) collective-permute-start(bf16[64,1024]{1,0:T(8,128)(2,1)S(1)} %get-tuple-element.33), channel_id=1, source_target_pairs={{0,4},{4,0},{8,12},{12,8},{1,5},{5,1},{9,13},{13,9},{2,6},{6,2},{1... | collective-permute-start | bytes 393224 | tf_op jit(solution)/shard_map/ppermute | solution.py:461
  46.3 0.6 collective-permute-start.6
  46.9 1.9 %collective-permute-start.7 = (bf16[64,1024]{1,0:T(8,128)(2,1)S(1)}, bf16[64,1024]{1,0:T(8,128)(2,1)S(1)}, u32[]{:S(2)}, u32[]{:S(2)}) collective-permute-start(bf16[64,1024]{1,0:T(8,128)(2,1)S(1)} %get-tuple-element.35), channel_id=1, source_target_pairs={{0,12},{4,8},{8,4},{12,0},{1,13},{5,9},{9,5},{13,1},{2,14},{6,10},... | collective-permute-start | bytes 393224 | tf_op jit(solution)/shard_map/ppermute | solution.py:461
  48.8 1.0 %collective-permute-start.10 = (bf16[64,1024]{1,0:T(8,128)(2,1)S(1)}, bf16[64,1024]{1,0:T(8,128)(2,1)S(1)}, u32[]{:S(2)}, u32[]{:S(2)}) collective-permute-start(bf16[64,1024]{1,0:T(8,128)(2,1)S(1)} %collective-permute-done.9.rest_6_), channel_id=1, source_target_pairs={{0,4},{4,0},{8,12},{12,8},{1,5},{5,1},{9,13},{13,9},{2,6},{6,2},{1... | collective-permute-start | bytes 393224 | tf_op jit(solution)/shard_map/ppermute | solution.py:461
  49.9 3.6 %collective-permute-done.5.rest_1_ = bf16[64,1024]{1,0:T(8,128)(2,1)S(1)} collective-permute-done((bf16[64,1024]{1,0:T(8,128)(2,1)S(1)}, bf16[64,1024]{1,0:T(8,128)(2,1)S(1)}, u32[]{:S(2)}, u32[]{:S(2)}) %collective-permute-start.5) | collective-permute-done | bytes 131104 | tf_op jit(solution)/shard_map/ppermute | solution.py:461
  53.6 2.1 %collective-permute-done.6.rest_2_ = bf16[64,1024]{1,0:T(8,128)(2,1)S(1)} collective-permute-done((bf16[64,1024]{1,0:T(8,128)(2,1)S(1)}, bf16[64,1024]{1,0:T(8,128)(2,1)S(1)}, u32[]{:S(2)}, u32[]{:S(2)}) %collective-permute-start.6) | collective-permute-done | bytes 131104 | tf_op jit(solution)/shard_map/ppermute | solution.py:461
  55.7 1.0 %collective-permute-done.7.rest_3_ = bf16[64,1024]{1,0:T(8,128)(2,1)S(1)} collective-permute-done((bf16[64,1024]{1,0:T(8,128)(2,1)S(1)}, bf16[64,1024]{1,0:T(8,128)(2,1)S(1)}, u32[]{:S(2)}, u32[]{:S(2)}) %collective-permute-start.7) | collective-permute-done | bytes 131104 | tf_op jit(solution)/shard_map/ppermute | solution.py:461
  56.7 0.7 %collective-permute-done.10.rest_7_ = bf16[64,1024]{1,0:T(8,128)(2,1)S(1)} collective-permute-done((bf16[64,1024]{1,0:T(8,128)(2,1)S(1)}, bf16[64,1024]{1,0:T(8,128)(2,1)S(1)}, u32[]{:S(2)}, u32[]{:S(2)}) %collective-permute-start.10) | collective-permute-done | bytes 131104 | tf_op jit(solution)/shard_map/ppermute | solution.py:461
  57.4 1.4 %shard_map.148 = (f32[2,128,1024]{2,1,0:T(8,128)S(1)}, f32[2,128]{1,0:T(2,128)S(1)}) custom-call(s32[19]{0:T(128)S(1)} %copy-done.7, f32[2,128,1024]{2,1,0:T(8,128)S(1)} %get-tuple-element.22.yz, f32[2,128,1024]{2,1,0:T(8,128)S(1)} %get-tuple-element.23.after.ez, bf16[64,1024]{1,0:T(8,128)(2,1)S(1)} %get-tuple-element.32.rest_0_, ...), custom_call_target="tpu_custom_call" | custom-call | tf_op jit(solution)/shard_map/pallas_call | solution.py:560
  58.9 1.6 %collective-permute-start.11 = (f32[2,128]{1,0:T(2,128)S(1)}, f32[2,128]{1,0:T(2,128)S(1)}, u32[]{:S(2)}, u32[]{:S(2)}) collective-permute-start(f32[2,128]{1,0:T(2,128)S(1)} %get-tuple-element.37.own), channel_id=1, source_target_pairs={{0,2},{2,0},{1,3},{3,1},{4,6},{6,4},{5,7},{7,5},{8,10},{10,8},{9,1... | collective-permute-start | bytes 3080 | tf_op jit(solution)/shard_map/ppermute | solution.py:465
  60.4 1.7 %shard_map.150 = bf16[1024,256]{1,0:T(8,128)(2,1)} custom-call(s32[19]{0:T(128)S(1)} %copy-done.7, bf16[192,256]{1,0:T(8,128)(2,1)S(1)} %get-tuple-element.28.mine, bf16[192,256]{1,0:T(8,128)(2,1)S(1)} %collective-permute-done.3.other, f32[64,1024]{1,0:T(8,128)S(1)} %get-tuple-element.39.share, f32[2,16,256]{2,1,0:T(8,128)S(1)} %get-tuple-element.31.decays, ...), custom_call_target="tpu_custom_call" | custom-call | tf_op jit(solution)/shard_map/pallas_call | solution.py:554
  62.1 0.4 collective-permute-done.11.other
  62.5 1.6 %shard_map.149 = bf16[2,128,1024]{2,1,0:T(8,128)(2,1)} custom-call(s32[19]{0:T(128)S(1)} %copy-done.7, f32[2,128,1024]{2,1,0:T(8,128)S(1)} %get-tuple-element.36.gated, f32[2,128]{1,0:T(2,128)S(1)} %get-tuple-element.37.own, f32[2,128]{1,0:T(2,128)S(1)} %collective-permute-done.11.other, bf16[1,1024]{1,0:T(2,128)(2,1)S(1)} %broadcast_in_dim.9.gain, ...), custom_call_target="tpu_custom_call" | custom-call | tf_op jit(solution)/shard_map/pallas_call | solution.py:572
  (32 shorter events, 0.5 us)
Async XLA Ops:
  0.6 11.6 %copy-start = (bf16[2,128,1024]{2,1,0:T(8,128)(2,1)S(1)}, bf16[2,128,1024]{2,1,0:T(8,128)(2,1)}, u32[]{:S(2)}) copy-start(bf16[2,128,1024]{2,1,0:T(8,128)(2,1)} %x.3) | copy-start | bytes 1572868
  2.8 9.5 %copy-start.3 = (bf16[2,128,256]{2,1,0:T(8,128)(2,1)S(1)}, bf16[2,128,256]{2,1,0:T(8,128)(2,1)}, u32[]{:S(2)}) copy-start(bf16[2,128,256]{2,1,0:T(8,128)(2,1)} %b.1) | copy-start | bytes 393220
  2.8 9.5 %copy-start.4 = (bf16[2,128,256]{2,1,0:T(8,128)(2,1)S(1)}, bf16[2,128,256]{2,1,0:T(8,128)(2,1)}, u32[]{:S(2)}) copy-start(bf16[2,128,256]{2,1,0:T(8,128)(2,1)} %c.1) | copy-start | bytes 393220
  2.8 9.5 %copy-start.6 = (f32[2,16,128]{2,1,0:T(8,128)S(1)}, f32[2,16,128]{2,1,0:T(8,128)}, u32[]{:S(2)}) copy-start(f32[2,16,128]{2,1,0:T(8,128)} %dt.1) | copy-start | bytes 49156
  5.9 18.7 %collective-permute-start = (bf16[928,256]{1,0:T(8,128)(2,1)}, bf16[928,256]{1,0:T(8,128)(2,1)S(1)}, u32[]{:S(2)}, u32[]{:S(2)}) collective-permute-start(bf16[928,256]{1,0:T(8,128)(2,1)} %get-tuple-element.25), channel_id=1, source_target_pairs={{0,4},{4,0},{8,12},{12,8},{1,5},{5,1},{9,13},{13,9},{2,6},{6,2},{1... | collective-permute-start | bytes 1425416 | tf_op jit(solution)/shard_map/ppermute | solution.py:461
  9.0 19.6 %collective-permute-start.1 = (bf16[416,256]{1,0:T(8,128)(2,1)}, bf16[416,256]{1,0:T(8,128)(2,1)S(1)}, u32[]{:S(2)}, u32[]{:S(2)}) collective-permute-start(bf16[416,256]{1,0:T(8,128)(2,1)} %get-tuple-element.26), channel_id=1, source_target_pairs={{0,8},{4,12},{8,0},{12,4},{1,9},{5,13},{9,1},{13,5},{2,10},{6,14},... | collective-permute-start | bytes 638984 | tf_op jit(solution)/shard_map/ppermute | solution.py:461
  11.5 21.1 %collective-permute-start.2 = (bf16[416,256]{1,0:T(8,128)(2,1)}, bf16[416,256]{1,0:T(8,128)(2,1)S(1)}, u32[]{:S(2)}, u32[]{:S(2)}) collective-permute-start(bf16[416,256]{1,0:T(8,128)(2,1)} %get-tuple-element.27), channel_id=1, source_target_pairs={{0,12},{4,8},{8,4},{12,0},{1,13},{5,9},{9,5},{13,1},{2,14},{6,10},... | collective-permute-start | bytes 638984 | tf_op jit(solution)/shard_map/ppermute | solution.py:461
  11.6 0.7 %copy-start.9 = (f32[16]{0:T(128)S(1)}, f32[16]{0:T(128)}, u32[]{:S(2)}) copy-start(f32[16]{0:T(128)} %param.20) | copy-start | bytes 196
  11.6 0.7 %copy-start.10 = (f32[16]{0:T(128)S(1)}, f32[16]{0:T(128)}, u32[]{:S(2)}) copy-start(f32[16]{0:T(128)} %param.19) | copy-start | bytes 196
  11.6 0.7 %copy-start.11 = (f32[16]{0:T(128)S(1)}, f32[16]{0:T(128)}, u32[]{:S(2)}) copy-start(f32[16]{0:T(128)} %param.18) | copy-start | bytes 196
  12.3 1.0 %copy-start.2 = (bf16[2,128,1024]{2,1,0:T(8,128)(2,1)S(1)}, bf16[2,128,1024]{2,1,0:T(8,128)(2,1)}, u32[]{:S(2)}) copy-start(bf16[2,128,1024]{2,1,0:T(8,128)(2,1)} %z_in.1) | copy-start | bytes 1572868
  16.2 8.4 %copy-start.7 = (s32[19]{0:T(128)S(1)}, s32[19]{0:T(128)}, u32[]{:S(2)}) copy-start(s32[19]{0:T(128)} %concatenate.3.tab) | copy-start | bytes 232
  24.6 8.0 %copy-start.5 = (bf16[160,256]{1,0:T(8,128)(2,1)S(1)}, bf16[160,256]{1,0:T(8,128)(2,1)}, u32[]{:S(2)}) copy-start(bf16[160,256]{1,0:T(8,128)(2,1)} %get-tuple-element.24.rest_0_) | copy-start | bytes 245764
  25.4 11.6 %collective-permute-start.4 = (bf16[256,256]{1,0:T(8,128)(2,1)S(1)}, bf16[256,256]{1,0:T(8,128)(2,1)S(1)}, u32[]{:S(2)}, u32[]{:S(2)}) collective-permute-start(bf16[256,256]{1,0:T(8,128)(2,1)S(1)} %shard_map.142.rest_4_), channel_id=1, source_target_pairs={{0,8},{4,12},{8,0},{12,4},{1,9},{5,13},{9,1},{13,5},{2,10},{6,14},... | collective-permute-start | bytes 393224 | tf_op jit(solution)/shard_map/ppermute | solution.py:461
  32.6 5.7 %copy-start.1 = (bf16[1,16,64,256]{3,2,1,0:T(8,128)(2,1)S(1)}, bf16[1,16,64,256]{3,2,1,0:T(8,128)(2,1)}, u32[]{:S(2)}) copy-start(bf16[1,16,64,256]{3,2,1,0:T(8,128)(2,1)} %param.22) | copy-start | bytes 1572868
  33.6 4.7 %collective-permute-start.3 = (bf16[192,256]{1,0:T(8,128)(2,1)S(1)}, bf16[192,256]{1,0:T(8,128)(2,1)S(1)}, u32[]{:S(2)}, u32[]{:S(2)}) collective-permute-start(bf16[192,256]{1,0:T(8,128)(2,1)S(1)} %get-tuple-element.28.mine), channel_id=1, source_target_pairs={{0,2},{2,0},{1,3},{3,1},{4,6},{6,4},{5,7},{7,5},{8,10},{10,8},{9,1... | collective-permute-start | bytes 294920 | tf_op jit(solution)/shard_map/ppermute | solution.py:465
  39.1 9.6 %collective-permute-start.9 = (bf16[64,1024]{1,0:T(8,128)(2,1)S(1)}, bf16[64,1024]{1,0:T(8,128)(2,1)S(1)}, u32[]{:S(2)}, u32[]{:S(2)}) collective-permute-start(bf16[64,1024]{1,0:T(8,128)(2,1)S(1)} %shard_map.147.rest_4_), channel_id=1, source_target_pairs={{0,8},{4,12},{8,0},{12,4},{1,9},{5,13},{9,1},{13,5},{2,10},{6,14},... | collective-permute-start | bytes 393224 | tf_op jit(solution)/shard_map/ppermute | solution.py:461
  41.6 8.4 %collective-permute-start.8 = (bf16[64,1024]{1,0:T(8,128)(2,1)S(1)}, bf16[64,1024]{1,0:T(8,128)(2,1)S(1)}, u32[]{:S(2)}, u32[]{:S(2)}) collective-permute-start(bf16[64,1024]{1,0:T(8,128)(2,1)S(1)} %shard_map.147.rest_4_), channel_id=1, source_target_pairs={{0,4},{4,0},{8,12},{12,8},{1,5},{5,1},{9,13},{13,9},{2,6},{6,2},{1... | collective-permute-start | bytes 393224 | tf_op jit(solution)/shard_map/ppermute | solution.py:461
  44.2 9.3 %collective-permute-start.5 = (bf16[64,1024]{1,0:T(8,128)(2,1)S(1)}, bf16[64,1024]{1,0:T(8,128)(2,1)S(1)}, u32[]{:S(2)}, u32[]{:S(2)}) collective-permute-start(bf16[64,1024]{1,0:T(8,128)(2,1)S(1)} %get-tuple-element.33), channel_id=1, source_target_pairs={{0,4},{4,0},{8,12},{12,8},{1,5},{5,1},{9,13},{13,9},{2,6},{6,2},{1... | collective-permute-start | bytes 393224 | tf_op jit(solution)/shard_map/ppermute | solution.py:461
  46.3 9.4 %collective-permute-start.6 = (bf16[64,1024]{1,0:T(8,128)(2,1)S(1)}, bf16[64,1024]{1,0:T(8,128)(2,1)S(1)}, u32[]{:S(2)}, u32[]{:S(2)}) collective-permute-start(bf16[64,1024]{1,0:T(8,128)(2,1)S(1)} %get-tuple-element.34), channel_id=1, source_target_pairs={{0,8},{4,12},{8,0},{12,4},{1,9},{5,13},{9,1},{13,5},{2,10},{6,14},... | collective-permute-start | bytes 393224 | tf_op jit(solution)/shard_map/ppermute | solution.py:461
  46.9 9.8 %collective-permute-start.7 = (bf16[64,1024]{1,0:T(8,128)(2,1)S(1)}, bf16[64,1024]{1,0:T(8,128)(2,1)S(1)}, u32[]{:S(2)}, u32[]{:S(2)}) collective-permute-start(bf16[64,1024]{1,0:T(8,128)(2,1)S(1)} %get-tuple-element.35), channel_id=1, source_target_pairs={{0,12},{4,8},{8,4},{12,0},{1,13},{5,9},{9,5},{13,1},{2,14},{6,10},... | collective-permute-start | bytes 393224 | tf_op jit(solution)/shard_map/ppermute | solution.py:461
  48.8 8.7 %collective-permute-start.10 = (bf16[64,1024]{1,0:T(8,128)(2,1)S(1)}, bf16[64,1024]{1,0:T(8,128)(2,1)S(1)}, u32[]{:S(2)}, u32[]{:S(2)}) collective-permute-start(bf16[64,1024]{1,0:T(8,128)(2,1)S(1)} %collective-permute-done.9.rest_6_), channel_id=1, source_target_pairs={{0,4},{4,0},{8,12},{12,8},{1,5},{5,1},{9,13},{13,9},{2,6},{6,2},{1... | collective-permute-start | bytes 393224 | tf_op jit(solution)/shard_map/ppermute | solution.py:461
  57.4 3.0 %copy-start.8 = (bf16[1024]{0:T(1024)(128)(2,1)S(1)}, bf16[1024]{0:T(1024)(128)(2,1)}, u32[]{:S(2)}) copy-start(bf16[1024]{0:T(1024)(128)(2,1)} %param.21) | copy-start | bytes 6148
  58.9 3.6 %collective-permute-start.11 = (f32[2,128]{1,0:T(2,128)S(1)}, f32[2,128]{1,0:T(2,128)S(1)}, u32[]{:S(2)}, u32[]{:S(2)}) collective-permute-start(f32[2,128]{1,0:T(2,128)S(1)} %get-tuple-element.37.own), channel_id=1, source_target_pairs={{0,2},{2,0},{1,3},{3,1},{4,6},{6,4},{5,7},{7,5},{8,10},{10,8},{9,1... | collective-permute-start | bytes 3080 | tf_op jit(solution)/shard_map/ppermute | solution.py:465

commit v4 on v3

--- a/solution.py
+++ b/solution.py
@@ -116,46 +116,46 @@
     return ref.at[pl.ds(ref.shape[0] - size + start, size if count is None else count)]
 
 
-def send_part(peers, tab, x_in, b, c, dt, own, near, *rest):
-    far = rest[: peers - 2]
-    dtv, packed, x, bc, sem, in_sem = rest[peers - 2 :]
+def send_part(peers, x_in, b, c, dt, owner, lens, own, near, *rest):
+    outs = (own, near, *rest[: peers - 2])
+    dtv, x, bc, table, length, sem = rest[peers - 2 :]
     slots, rows, width = x.shape
     heads = dt.shape[1]
-    t = Table(tab, peers, slots)
+    dp = lax.axis_index("dp")
+    odd = lax.axis_index("head") % 2
     copies = Copies(sem)
-    first = Copies(in_sem.at[pl.ds(0, 1)])
-    first(dt, dtv)
-    second = Copies(in_sem.at[pl.ds(1, 2)])
-    second(x_in, x)
-    second(b, bc, t.odd == 0)
-    second(c, bc, t.odd != 0, again=True)
-    outs = [own, near] + list(far)
-    size = rows + 2 * heads
-    first.wait()
-    length = jnp.full((heads, rows), t.length.astype(F32)).astype(BF16)
-    for j in range(slots):
+    copies(owner, table)
+    copies(lens, length)
+    copies(dt, dtv)
+    copies(x_in, x)
+    copies(b, bc, odd == 0)
+    copies(c, bc, odd != 0, again=True)
+    copies.wait()
+    t = Table([lax.axis_index("sess"), odd, length[0]], peers, slots)
+    t.owner = lambda i: table[dp, i]
+    count = jnp.full((heads, rows), t.length.astype(F32)).astype(BF16)
+    picks = [t.slot(k) for k in range(peers)]
+
+    def put(out, index, j, start):
+        for g, lanes in enumerate(spans(width)):
+            at = (index * (width // 256) + g) * HALF
+            out[at : at + HALF] = x[j, start : start + HALF, lanes]
+
+    for k in list(range(2, peers)) + [1, 0]:
+        out, j = outs[k], picks[k]
+        at = out.shape[0] - rows - 2 * heads
+        out[at : at + rows] = bc[j]
         value = dtv[j]
         high = value.astype(BF16)
         value = value - high.astype(F32)
         middle = value.astype(BF16)
         low = (value - middle.astype(F32)).astype(BF16)
-        packed[j, :heads, :rows] = high
-        packed[j, :heads, rows:] = middle
-        packed[j, heads:, :rows] = low
-        packed[j, heads:, rows:] = length
-    second.wait()
+        out[at + rows : at + rows + heads] = jnp.concatenate([high, middle], axis=1)
+        out[at + rows + heads :] = jnp.concatenate([low, count], axis=1)
+        if k:
+            put(out, 0, j, 0)
     for m in range(peers // 2):
-        for src, dst in from_rows(x, t.slot(1 ^ 2 * m), HALF, chunk(near, m + 1, width)):
-            copies(src, dst)
-    for k in range(peers):
-        j = t.slot(k)
-        copies(bc.at[j], tail_of(outs[k], size, 0, rows))
-        if k:
-            for src, dst in from_rows(x, j, 0, chunk(outs[k], 0, width)):
-                copies(src, dst)
-    for k in range(peers):
-        copies(packed.at[t.slot(k)], tail_of(outs[k], size, rows, 2 * heads))
-    copies.wait()
+        put(near, m + 1, picks[1 ^ 2 * m], HALF)
 
 
 def forward_part(peers, slots, tab, x, near, after, *rest):
@@ -478,18 +478,17 @@
     own, near, *sends = call(
         bind(send_part),
         [packed(tail), packed((1 + half) * piece + tail)] + [packed(piece + tail)] * (peers - 2),
-        [SMEM, HBM, HBM, HBM, HBM],
-        [ANY] * peers,
-        [
+        [HBM] * 6,
+        scratch=[
             scratch(*dt_raw.shape, dtype=F32),
-            scratch(slots, 2 * heads, state),
             scratch(*x_rows.shape),
             scratch(*b.shape),
-            dma((half + peers - 1) * count + 2 * peers),
-            dma(3),
+            pltpu.SMEM(slot_owner.shape, jnp.int32),
+            pltpu.SMEM(lengths.shape, jnp.int32),
+            dma(5),
         ],
         limit=60,
-    )(tab, x_rows, b, c, dt_raw)
+    )(x_rows, b, c, dt_raw, slot_owner, lengths)
     near = far(near, 1)
     sends = [far(value, k + 2) for k, value in enumerate(sends)]
     yz, ez = call(

time: 64.6 us -> 62.1 us (0.961)
  waiting for transfers between devices: 22 us -> 19.6 us
  local copies, waits for them, and re-layouts: 2.39 us -> 4.33 us
  Pallas kernels: 17.4 us -> 16.2 us
  other arithmetic: 0.8 us -> 0.1 us
    unnamed x24 -> x26, local copies, waits for them, and re-layouts: 1.75 us -> 4.24 us
    ppermute x10, waiting for transfers between devices: 20.3 us -> 17.9 us  [far(): return lax.ppermute(value, 'sess', [(i, i ^ k) for i in range(peers)])]
    pallas_call x1, Pallas kernels: 3.06 us -> 2.11 us  [per_device(): call(bind(send_part), [packed(tail), packed((1 + half) * piece + tail)] +...]
    reduce_sum x1, other arithmetic: 0.78 us -> 0.09 us  [own_row(): return jnp.sum(jnp.where(mine, table, 0), axis=0)]
where the time goes in v4:
time: 62.1 us; the launch traced here: 61.8 us
  starting transfers between devices  20.1 us (32%)
  waiting for transfers between devices  19.6 us (32%)
  Pallas kernels  16.2 us (26%)
  local copies, waits for them, and re-layouts  4.33 us (7%)
  between operations  1.47 us (2%)
    ppermute x10, waiting for transfers between devices, far(): return lax.ppermute(value, 'sess', [(i, i ^ k) for i in range(peers)])  17.9 us
    ppermute x10, starting transfers between devices, far(): return lax.ppermute(value, 'sess', [(i, i ^ k) for i in range(peers)])  17 us
    unnamed x26, local copies, waits for them, and re-layouts  4.24 us
    ppermute x2, starting transfers between devices, swapped(): return lax.ppermute(value, 'head', [(i, i ^ 1) for i in range(count)])  3.11 us
    pallas_call x1, Pallas kernels, per_device(): call(block_part, [shape(x_rows.shape, F32)] * 2, [HBM] * 5 + [VMEM], scra...  2.88 us
    pallas_call x1, Pallas kernels, per_device(): call(bind(late_part, slots), [shape((width, state), BF16), packed(piece)]...  2.38 us
    pallas_call x1, Pallas kernels, per_device(): call(bind(send_part), [packed(tail), packed((1 + half) * piece + tail)] +...  2.11 us
    ppermute x2, waiting for transfers between devices, swapped(): return lax.ppermute(value, 'head', [(i, i ^ 1) for i in range(count)])  1.71 us
  transfers between devices with their start and end apart: 12, of which 10 were waited for; matrix products, arithmetic and copies ran while one was open for 0% of the time, Pallas kernels for 16%

profile of v4, /device:TPU:0, one launch (start us, length us, event | category | flops | bytes accessed | tf_op | source)
XLA Modules:
  0.0 61.8 jit_solution(9963458953609518060)
XLA Ops:
  1.3 2.1 %shard_map.141 = (bf16[160,256]{1,0:T(8,128)(2,1)}, bf16[928,256]{1,0:T(8,128)(2,1)}, bf16[416,256]{1,0:T(8,128)(2,1)}, bf16[416,256]{1,0:T(8,128)(2,1)}) custom-call(bf16[2,128,1024]{2,1,0:T(8,128)(2,1)} %x.3, bf16[2,128,256]{2,1,0:T(8,128)(2,1)} %b.1, bf16[2,128,256]{2,1,0:T(8,128)(2,1)} %c.1, f32[2,16,128]{2,1,0:T(8,128)} %dt.1, s32[2,8]{1,0:T(2,128)} %owner.1, ...), custom_call_target="tpu_custom_call" | custom-call | tf_op jit(solution)/shard_map/pallas_call | solution.py:478
  3.5 3.1 %collective-permute-start = (bf16[928,256]{1,0:T(8,128)(2,1)}, bf16[928,256]{1,0:T(8,128)(2,1)S(1)}, u32[]{:S(2)}, u32[]{:S(2)}) collective-permute-start(bf16[928,256]{1,0:T(8,128)(2,1)} %get-tuple-element.25), channel_id=1, source_target_pairs={{0,4},{4,0},{8,12},{12,8},{1,5},{5,1},{9,13},{13,9},{2,6},{6,2},{1... | collective-permute-start | bytes 1425416 | tf_op jit(solution)/shard_map/ppermute | solution.py:461
  6.6 2.6 %collective-permute-start.1 = (bf16[416,256]{1,0:T(8,128)(2,1)}, bf16[416,256]{1,0:T(8,128)(2,1)S(1)}, u32[]{:S(2)}, u32[]{:S(2)}) collective-permute-start(bf16[416,256]{1,0:T(8,128)(2,1)} %get-tuple-element.26), channel_id=1, source_target_pairs={{0,8},{4,12},{8,0},{12,4},{1,9},{5,13},{9,1},{13,5},{2,10},{6,14},... | collective-permute-start | bytes 638984 | tf_op jit(solution)/shard_map/ppermute | solution.py:461
  9.2 0.6 %copy-done.10 = f32[16]{0:T(128)S(1)} copy-done((f32[16]{0:T(128)S(1)}, f32[16]{0:T(128)}, u32[]{:S(2)}) %copy-start.10) | copy-done | bytes 88
  9.9 1.0 %copy-done.2 = bf16[2,128,1024]{2,1,0:T(8,128)(2,1)S(1)} copy-done((bf16[2,128,1024]{2,1,0:T(8,128)(2,1)S(1)}, bf16[2,128,1024]{2,1,0:T(8,128)(2,1)}, u32[]{:S(2)}) %copy-start.2) | copy-done | bytes 524312
  11.0 0.9 %copy-done.3 = bf16[2,128,256]{2,1,0:T(8,128)(2,1)S(1)} copy-done((bf16[2,128,256]{2,1,0:T(8,128)(2,1)S(1)}, bf16[2,128,256]{2,1,0:T(8,128)(2,1)}, u32[]{:S(2)}) %copy-start.3) | copy-done | bytes 131096
  11.9 0.9 %copy-done.4 = bf16[2,128,256]{2,1,0:T(8,128)(2,1)S(1)} copy-done((bf16[2,128,256]{2,1,0:T(8,128)(2,1)S(1)}, bf16[2,128,256]{2,1,0:T(8,128)(2,1)}, u32[]{:S(2)}) %copy-start.4) | copy-done | bytes 131096
  12.8 2.9 %shard_map.140 = (f32[2,128,1024]{2,1,0:T(8,128)S(1)}, f32[2,128,1024]{2,1,0:T(8,128)S(1)}) custom-call(bf16[2,128,1024]{2,1,0:T(8,128)(2,1)S(1)} %copy-done, bf16[2,128,1024]{2,1,0:T(8,128)(2,1)S(1)} %copy-done.2, bf16[2,128,256]{2,1,0:T(8,128)(2,1)S(1)} %copy-done.3, bf16[2,128,256]{2,1,0:T(8,128)(2,1)S(1)} %copy-done.4, f32[2,16,128]{2,1,0:T(8,128)S(1)} %copy-done.6, ...), custom_call_target="tpu_custom_call" | custom-call | tf_op jit(solution)/shard_map/pallas_call | solution.py:494
  15.7 0.6 %copy-done.7 = s32[2,8]{1,0:T(2,128)S(1)} copy-done((s32[2,8]{1,0:T(2,128)S(1)}, s32[2,8]{1,0:T(2,128)}, u32[]{:S(2)}) %copy-start.7) | copy-done | bytes 88
  16.5 5.7 %collective-permute-done.near.rest_1_ = bf16[928,256]{1,0:T(8,128)(2,1)S(1)} collective-permute-done((bf16[928,256]{1,0:T(8,128)(2,1)}, bf16[928,256]{1,0:T(8,128)(2,1)S(1)}, u32[]{:S(2)}, u32[]{:S(2)}) %collective-permute-start) | collective-permute-done | bytes 475168 | tf_op jit(solution)/shard_map/ppermute | solution.py:461
  22.2 0.6 %shard_map.142.rest_4_ = bf16[256,256]{1,0:T(8,128)(2,1)S(1)} custom-call(s32[19]{0:T(128)S(1)} %concatenate.3.tab, bf16[2,128,1024]{2,1,0:T(8,128)(2,1)S(1)} %copy-done, bf16[928,256]{1,0:T(8,128)(2,1)S(1)} %collective-permute-done.near.rest_1_, f32[2,128,1024]{2,1,0:T(8,128)S(1)} %get-tuple-element.23.after.ez), custom_call_target="tpu_custom_call" | custom-call | tf_op jit(solution)/shard_map/pallas_call | solution.py:507
  22.8 3.1 %collective-permute-start.4 = (bf16[256,256]{1,0:T(8,128)(2,1)S(1)}, bf16[256,256]{1,0:T(8,128)(2,1)S(1)}, u32[]{:S(2)}, u32[]{:S(2)}) collective-permute-start(bf16[256,256]{1,0:T(8,128)(2,1)S(1)} %shard_map.142.rest_4_), channel_id=1, source_target_pairs={{0,8},{4,12},{8,0},{12,4},{1,9},{5,13},{9,1},{13,5},{2,10},{6,14},... | collective-permute-start | bytes 393224 | tf_op jit(solution)/shard_map/ppermute | solution.py:461
  26.0 4.2 %collective-permute-done.2.rest_3_.rest_1_ = bf16[416,256]{1,0:T(8,128)(2,1)S(1)} collective-permute-done((bf16[416,256]{1,0:T(8,128)(2,1)}, bf16[416,256]{1,0:T(8,128)(2,1)S(1)}, u32[]{:S(2)}, u32[]{:S(2)}) %collective-permute-start.2) | collective-permute-done | bytes 213024 | tf_op jit(solution)/shard_map/ppermute | solution.py:461
  30.2 1.0 %shard_map.143 = (bf16[192,256]{1,0:T(8,128)(2,1)S(1)}, f32[2,16,128]{2,1,0:T(8,128)S(1)}, f32[2,16,128]{2,1,0:T(8,128)S(1)}) custom-call(s32[19]{0:T(128)S(1)} %concatenate.3.tab, bf16[160,256]{1,0:T(8,128)(2,1)S(1)} %copy-done.5, bf16[928,256]{1,0:T(8,128)(2,1)S(1)} %collective-permute-done.near.rest_1_, ...), custom_call_target="tpu_custom_call" | custom-call | tf_op jit(solution)/shard_map/pallas_call | solution.py:515
  31.2 1.6 %collective-permute-start.3 = (bf16[192,256]{1,0:T(8,128)(2,1)S(1)}, bf16[192,256]{1,0:T(8,128)(2,1)S(1)}, u32[]{:S(2)}, u32[]{:S(2)}) collective-permute-start(bf16[192,256]{1,0:T(8,128)(2,1)S(1)} %get-tuple-element.28.mine), channel_id=1, source_target_pairs={{0,2},{2,0},{1,3},{3,1},{4,6},{6,4},{5,7},{7,5},{8,10},{10,8},{9,1... | collective-permute-start | bytes 294920 | tf_op jit(solution)/shard_map/ppermute | solution.py:465
  32.8 1.6 %shard_map.144 = (f32[128,1024]{1,0:T(8,128)S(1)}, f32[64,1024]{1,0:T(8,128)S(1)}, f32[2,16,256]{2,1,0:T(8,128)S(1)}) custom-call(s32[19]{0:T(128)S(1)} %concatenate.3.tab, f32[2,16,128]{2,1,0:T(8,128)S(1)} %get-tuple-element.29.dts, f32[3,16]{1,0:T(4,128)S(1)} %pad_maximum_fusion.params), custom_call_target="tpu_custom_call" | custom-call | tf_op jit(solution)/shard_map/pallas_call | solution.py:526
  34.6 1.3 %collective-permute-done.3.other = bf16[192,256]{1,0:T(8,128)(2,1)S(1)} collective-permute-done((bf16[192,256]{1,0:T(8,128)(2,1)S(1)}, bf16[192,256]{1,0:T(8,128)(2,1)S(1)}, u32[]{:S(2)}, u32[]{:S(2)}) %collective-permute-start.3) | collective-permute-done | bytes 98336 | tf_op jit(solution)/shard_map/ppermute | solution.py:465
  35.9 0.8 %shard_map.147.rest_4_ = bf16[64,1024]{1,0:T(8,128)(2,1)S(1)} custom-call(s32[19]{0:T(128)S(1)} %concatenate.3.tab, bf16[1024,256]{1,0:T(8,128)(2,1)S(1)} %bitcast.7, bf16[192,256]{1,0:T(8,128)(2,1)S(1)} %get-tuple-element.28.mine, bf16[192,256]{1,0:T(8,128)(2,1)S(1)} %collective-permute-done.3.other, f32[8,128]{1,0:T(8,128)S(1)} %shard_map.146.token, ...), custom_call_target="tpu_custom_call" | custom-call | tf_op jit(solution)/shard_map/pallas_call | solution.py:532
  36.7 2.4 %collective-permute-start.9 = (bf16[64,1024]{1,0:T(8,128)(2,1)S(1)}, bf16[64,1024]{1,0:T(8,128)(2,1)S(1)}, u32[]{:S(2)}, u32[]{:S(2)}) collective-permute-start(bf16[64,1024]{1,0:T(8,128)(2,1)S(1)} %shard_map.147.rest_4_), channel_id=1, source_target_pairs={{0,8},{4,12},{8,0},{12,4},{1,9},{5,13},{9,1},{13,5},{2,10},{6,14},... | collective-permute-start | bytes 393224 | tf_op jit(solution)/shard_map/ppermute | solution.py:461
  39.2 2.4 %shard_map.145 = (bf16[1024,256]{1,0:T(8,128)(2,1)S(1)}, bf16[256,256]{1,0:T(8,128)(2,1)S(1)}, bf16[64,1024]{1,0:T(8,128)(2,1)S(1)}, bf16[64,1024]{1,0:T(8,128)(...) custom-call(s32[19]{0:T(128)S(1)} %concatenate.3.tab, bf16[1024,256]{1,0:T(8,128)(2,1)S(1)} %bitcast.8, ...), custom_call_target="tpu_custom_call" | custom-call | tf_op jit(solution)/shard_map/pallas_call | solution.py:536
  41.6 2.2 %collective-permute-start.5 = (bf16[64,1024]{1,0:T(8,128)(2,1)S(1)}, bf16[64,1024]{1,0:T(8,128)(2,1)S(1)}, u32[]{:S(2)}, u32[]{:S(2)}) collective-permute-start(bf16[64,1024]{1,0:T(8,128)(2,1)S(1)} %get-tuple-element.33), channel_id=1, source_target_pairs={{0,4},{4,0},{8,12},{12,8},{1,5},{5,1},{9,13},{13,9},{2,6},{6,2},{1... | collective-permute-start | bytes 393224 | tf_op jit(solution)/shard_map/ppermute | solution.py:461
  43.8 0.4 collective-permute-start.6
  44.2 2.0 %collective-permute-start.7 = (bf16[64,1024]{1,0:T(8,128)(2,1)S(1)}, bf16[64,1024]{1,0:T(8,128)(2,1)S(1)}, u32[]{:S(2)}, u32[]{:S(2)}) collective-permute-start(bf16[64,1024]{1,0:T(8,128)(2,1)S(1)} %get-tuple-element.35), channel_id=1, source_target_pairs={{0,12},{4,8},{8,4},{12,0},{1,13},{5,9},{9,5},{13,1},{2,14},{6,10},... | collective-permute-start | bytes 393224 | tf_op jit(solution)/shard_map/ppermute | solution.py:461
  46.2 1.0 %collective-permute-start.10 = (bf16[64,1024]{1,0:T(8,128)(2,1)S(1)}, bf16[64,1024]{1,0:T(8,128)(2,1)S(1)}, u32[]{:S(2)}, u32[]{:S(2)}) collective-permute-start(bf16[64,1024]{1,0:T(8,128)(2,1)S(1)} %collective-permute-done.9.rest_6_), channel_id=1, source_target_pairs={{0,4},{4,0},{8,12},{12,8},{1,5},{5,1},{9,13},{13,9},{2,6},{6,2},{1... | collective-permute-start | bytes 393224 | tf_op jit(solution)/shard_map/ppermute | solution.py:461
  47.5 3.7 %collective-permute-done.5.rest_1_ = bf16[64,1024]{1,0:T(8,128)(2,1)S(1)} collective-permute-done((bf16[64,1024]{1,0:T(8,128)(2,1)S(1)}, bf16[64,1024]{1,0:T(8,128)(2,1)S(1)}, u32[]{:S(2)}, u32[]{:S(2)}) %collective-permute-start.5) | collective-permute-done | bytes 131104 | tf_op jit(solution)/shard_map/ppermute | solution.py:461
  51.2 2.1 %collective-permute-done.6.rest_2_ = bf16[64,1024]{1,0:T(8,128)(2,1)S(1)} collective-permute-done((bf16[64,1024]{1,0:T(8,128)(2,1)S(1)}, bf16[64,1024]{1,0:T(8,128)(2,1)S(1)}, u32[]{:S(2)}, u32[]{:S(2)}) %collective-permute-start.6) | collective-permute-done | bytes 131104 | tf_op jit(solution)/shard_map/ppermute | solution.py:461
  53.3 1.0 %collective-permute-done.7.rest_3_ = bf16[64,1024]{1,0:T(8,128)(2,1)S(1)} collective-permute-done((bf16[64,1024]{1,0:T(8,128)(2,1)S(1)}, bf16[64,1024]{1,0:T(8,128)(2,1)S(1)}, u32[]{:S(2)}, u32[]{:S(2)}) %collective-permute-start.7) | collective-permute-done | bytes 131104 | tf_op jit(solution)/shard_map/ppermute | solution.py:461
  54.3 0.7 %collective-permute-done.10.rest_7_ = bf16[64,1024]{1,0:T(8,128)(2,1)S(1)} collective-permute-done((bf16[64,1024]{1,0:T(8,128)(2,1)S(1)}, bf16[64,1024]{1,0:T(8,128)(2,1)S(1)}, u32[]{:S(2)}, u32[]{:S(2)}) %collective-permute-start.10) | collective-permute-done | bytes 131104 | tf_op jit(solution)/shard_map/ppermute | solution.py:461
  55.0 1.6 %shard_map.148 = (f32[2,128,1024]{2,1,0:T(8,128)S(1)}, f32[2,128]{1,0:T(2,128)S(1)}) custom-call(s32[19]{0:T(128)S(1)} %concatenate.3.tab, f32[2,128,1024]{2,1,0:T(8,128)S(1)} %get-tuple-element.22.yz, f32[2,128,1024]{2,1,0:T(8,128)S(1)} %get-tuple-element.23.after.ez, bf16[64,1024]{1,0:T(8,128)(2,1)S(1)} %get-tuple-element.32.rest_0_, ...), custom_call_target="tpu_custom_call" | custom-call | tf_op jit(solution)/shard_map/pallas_call | solution.py:559
  56.6 1.6 %collective-permute-start.11 = (f32[2,128]{1,0:T(2,128)S(1)}, f32[2,128]{1,0:T(2,128)S(1)}, u32[]{:S(2)}, u32[]{:S(2)}) collective-permute-start(f32[2,128]{1,0:T(2,128)S(1)} %get-tuple-element.37.own), channel_id=1, source_target_pairs={{0,2},{2,0},{1,3},{3,1},{4,6},{6,4},{5,7},{7,5},{8,10},{10,8},{9,1... | collective-permute-start | bytes 3080 | tf_op jit(solution)/shard_map/ppermute | solution.py:465
  58.2 1.7 %shard_map.150 = bf16[1024,256]{1,0:T(8,128)(2,1)} custom-call(s32[19]{0:T(128)S(1)} %concatenate.3.tab, bf16[192,256]{1,0:T(8,128)(2,1)S(1)} %get-tuple-element.28.mine, bf16[192,256]{1,0:T(8,128)(2,1)S(1)} %collective-permute-done.3.other, f32[64,1024]{1,0:T(8,128)S(1)} %get-tuple-element.39.share, f32[2,16,256]{2,1,0:T(8,128)S(1)} %get-tuple-element.31.decays, ...), custom_call_target="tpu_custom_call" | custom-call | tf_op jit(solution)/shard_map/pallas_call | solution.py:553
  60.2 1.6 %shard_map.149 = bf16[2,128,1024]{2,1,0:T(8,128)(2,1)} custom-call(s32[19]{0:T(128)S(1)} %concatenate.3.tab, f32[2,128,1024]{2,1,0:T(8,128)S(1)} %get-tuple-element.36.gated, f32[2,128]{1,0:T(2,128)S(1)} %get-tuple-element.37.own, f32[2,128]{1,0:T(2,128)S(1)} %collective-permute-done.11.other, bf16[1,1024]{1,0:T(2,128)(2,1)S(1)} %broadcast_in_dim.9.gain, ...), custom_call_target="tpu_custom_call" | custom-call | tf_op jit(solution)/shard_map/pallas_call | solution.py:571
  (34 shorter events, 1.2 us)
Async XLA Ops:
  0.6 9.2 %copy-start = (bf16[2,128,1024]{2,1,0:T(8,128)(2,1)S(1)}, bf16[2,128,1024]{2,1,0:T(8,128)(2,1)}, u32[]{:S(2)}) copy-start(bf16[2,128,1024]{2,1,0:T(8,128)(2,1)} %x.3) | copy-start | bytes 1572868
  3.5 18.7 %collective-permute-start = (bf16[928,256]{1,0:T(8,128)(2,1)}, bf16[928,256]{1,0:T(8,128)(2,1)S(1)}, u32[]{:S(2)}, u32[]{:S(2)}) collective-permute-start(bf16[928,256]{1,0:T(8,128)(2,1)} %get-tuple-element.25), channel_id=1, source_target_pairs={{0,4},{4,0},{8,12},{12,8},{1,5},{5,1},{9,13},{13,9},{2,6},{6,2},{1... | collective-permute-start | bytes 1425416 | tf_op jit(solution)/shard_map/ppermute | solution.py:461
  6.6 19.4 %collective-permute-start.1 = (bf16[416,256]{1,0:T(8,128)(2,1)}, bf16[416,256]{1,0:T(8,128)(2,1)S(1)}, u32[]{:S(2)}, u32[]{:S(2)}) collective-permute-start(bf16[416,256]{1,0:T(8,128)(2,1)} %get-tuple-element.26), channel_id=1, source_target_pairs={{0,8},{4,12},{8,0},{12,4},{1,9},{5,13},{9,1},{13,5},{2,10},{6,14},... | collective-permute-start | bytes 638984 | tf_op jit(solution)/shard_map/ppermute | solution.py:461
  9.1 21.1 %collective-permute-start.2 = (bf16[416,256]{1,0:T(8,128)(2,1)}, bf16[416,256]{1,0:T(8,128)(2,1)S(1)}, u32[]{:S(2)}, u32[]{:S(2)}) collective-permute-start(bf16[416,256]{1,0:T(8,128)(2,1)} %get-tuple-element.27), channel_id=1, source_target_pairs={{0,12},{4,8},{8,4},{12,0},{1,13},{5,9},{9,5},{13,1},{2,14},{6,10},... | collective-permute-start | bytes 638984 | tf_op jit(solution)/shard_map/ppermute | solution.py:461
  9.1 0.8 %copy-start.6 = (f32[2,16,128]{2,1,0:T(8,128)S(1)}, f32[2,16,128]{2,1,0:T(8,128)}, u32[]{:S(2)}) copy-start(f32[2,16,128]{2,1,0:T(8,128)} %dt.1) | copy-start | bytes 49156
  9.1 0.7 %copy-start.10 = (f32[16]{0:T(128)S(1)}, f32[16]{0:T(128)}, u32[]{:S(2)}) copy-start(f32[16]{0:T(128)} %param.20) | copy-start | bytes 196
  9.1 0.7 %copy-start.11 = (f32[16]{0:T(128)S(1)}, f32[16]{0:T(128)}, u32[]{:S(2)}) copy-start(f32[16]{0:T(128)} %param.19) | copy-start | bytes 196
  9.2 0.7 %copy-start.12 = (f32[16]{0:T(128)S(1)}, f32[16]{0:T(128)}, u32[]{:S(2)}) copy-start(f32[16]{0:T(128)} %param.18) | copy-start | bytes 196
  9.9 1.0 %copy-start.2 = (bf16[2,128,1024]{2,1,0:T(8,128)(2,1)S(1)}, bf16[2,128,1024]{2,1,0:T(8,128)(2,1)}, u32[]{:S(2)}) copy-start(bf16[2,128,1024]{2,1,0:T(8,128)(2,1)} %z_in.1) | copy-start | bytes 1572868
  11.0 0.9 %copy-start.3 = (bf16[2,128,256]{2,1,0:T(8,128)(2,1)S(1)}, bf16[2,128,256]{2,1,0:T(8,128)(2,1)}, u32[]{:S(2)}) copy-start(bf16[2,128,256]{2,1,0:T(8,128)(2,1)} %b.1) | copy-start | bytes 393220
  11.9 0.9 %copy-start.4 = (bf16[2,128,256]{2,1,0:T(8,128)(2,1)S(1)}, bf16[2,128,256]{2,1,0:T(8,128)(2,1)}, u32[]{:S(2)}) copy-start(bf16[2,128,256]{2,1,0:T(8,128)(2,1)} %c.1) | copy-start | bytes 393220
  12.8 2.9 %copy-start.9 = (s32[2,8]{1,0:T(2,128)S(1)}, s32[2,8]{1,0:T(2,128)}, u32[]{:S(2)}) copy-start(s32[2,8]{1,0:T(2,128)} %param.25) | copy-start | bytes 196
  15.7 0.7 %copy-start.7 = (s32[2,8]{1,0:T(2,128)S(1)}, s32[2,8]{1,0:T(2,128)}, u32[]{:S(2)}) copy-start(s32[2,8]{1,0:T(2,128)} %owner.1) | copy-start | bytes 196
  22.2 8.0 %copy-start.5 = (bf16[160,256]{1,0:T(8,128)(2,1)S(1)}, bf16[160,256]{1,0:T(8,128)(2,1)}, u32[]{:S(2)}) copy-start(bf16[160,256]{1,0:T(8,128)(2,1)} %get-tuple-element.24.rest_0_) | copy-start | bytes 245764
  22.8 11.7 %collective-permute-start.4 = (bf16[256,256]{1,0:T(8,128)(2,1)S(1)}, bf16[256,256]{1,0:T(8,128)(2,1)S(1)}, u32[]{:S(2)}, u32[]{:S(2)}) collective-permute-start(bf16[256,256]{1,0:T(8,128)(2,1)S(1)} %shard_map.142.rest_4_), channel_id=1, source_target_pairs={{0,8},{4,12},{8,0},{12,4},{1,9},{5,13},{9,1},{13,5},{2,10},{6,14},... | collective-permute-start | bytes 393224 | tf_op jit(solution)/shard_map/ppermute | solution.py:461
  30.2 5.7 %copy-start.1 = (bf16[1,16,64,256]{3,2,1,0:T(8,128)(2,1)S(1)}, bf16[1,16,64,256]{3,2,1,0:T(8,128)(2,1)}, u32[]{:S(2)}) copy-start(bf16[1,16,64,256]{3,2,1,0:T(8,128)(2,1)} %param.22) | copy-start | bytes 1572868
  31.2 4.7 %collective-permute-start.3 = (bf16[192,256]{1,0:T(8,128)(2,1)S(1)}, bf16[192,256]{1,0:T(8,128)(2,1)S(1)}, u32[]{:S(2)}, u32[]{:S(2)}) collective-permute-start(bf16[192,256]{1,0:T(8,128)(2,1)S(1)} %get-tuple-element.28.mine), channel_id=1, source_target_pairs={{0,2},{2,0},{1,3},{3,1},{4,6},{6,4},{5,7},{7,5},{8,10},{10,8},{9,1... | collective-permute-start | bytes 294920 | tf_op jit(solution)/shard_map/ppermute | solution.py:465
  36.7 9.5 %collective-permute-start.9 = (bf16[64,1024]{1,0:T(8,128)(2,1)S(1)}, bf16[64,1024]{1,0:T(8,128)(2,1)S(1)}, u32[]{:S(2)}, u32[]{:S(2)}) collective-permute-start(bf16[64,1024]{1,0:T(8,128)(2,1)S(1)} %shard_map.147.rest_4_), channel_id=1, source_target_pairs={{0,8},{4,12},{8,0},{12,4},{1,9},{5,13},{9,1},{13,5},{2,10},{6,14},... | collective-permute-start | bytes 393224 | tf_op jit(solution)/shard_map/ppermute | solution.py:461
  39.2 8.4 %collective-permute-start.8 = (bf16[64,1024]{1,0:T(8,128)(2,1)S(1)}, bf16[64,1024]{1,0:T(8,128)(2,1)S(1)}, u32[]{:S(2)}, u32[]{:S(2)}) collective-permute-start(bf16[64,1024]{1,0:T(8,128)(2,1)S(1)} %shard_map.147.rest_4_), channel_id=1, source_target_pairs={{0,4},{4,0},{8,12},{12,8},{1,5},{5,1},{9,13},{13,9},{2,6},{6,2},{1... | collective-permute-start | bytes 393224 | tf_op jit(solution)/shard_map/ppermute | solution.py:461
  41.6 9.6 %collective-permute-start.5 = (bf16[64,1024]{1,0:T(8,128)(2,1)S(1)}, bf16[64,1024]{1,0:T(8,128)(2,1)S(1)}, u32[]{:S(2)}, u32[]{:S(2)}) collective-permute-start(bf16[64,1024]{1,0:T(8,128)(2,1)S(1)} %get-tuple-element.33), channel_id=1, source_target_pairs={{0,4},{4,0},{8,12},{12,8},{1,5},{5,1},{9,13},{13,9},{2,6},{6,2},{1... | collective-permute-start | bytes 393224 | tf_op jit(solution)/shard_map/ppermute | solution.py:461
  43.8 9.6 %collective-permute-start.6 = (bf16[64,1024]{1,0:T(8,128)(2,1)S(1)}, bf16[64,1024]{1,0:T(8,128)(2,1)S(1)}, u32[]{:S(2)}, u32[]{:S(2)}) collective-permute-start(bf16[64,1024]{1,0:T(8,128)(2,1)S(1)} %get-tuple-element.34), channel_id=1, source_target_pairs={{0,8},{4,12},{8,0},{12,4},{1,9},{5,13},{9,1},{13,5},{2,10},{6,14},... | collective-permute-start | bytes 393224 | tf_op jit(solution)/shard_map/ppermute | solution.py:461
  44.2 10.1 %collective-permute-start.7 = (bf16[64,1024]{1,0:T(8,128)(2,1)S(1)}, bf16[64,1024]{1,0:T(8,128)(2,1)S(1)}, u32[]{:S(2)}, u32[]{:S(2)}) collective-permute-start(bf16[64,1024]{1,0:T(8,128)(2,1)S(1)} %get-tuple-element.35), channel_id=1, source_target_pairs={{0,12},{4,8},{8,4},{12,0},{1,13},{5,9},{9,5},{13,1},{2,14},{6,10},... | collective-permute-start | bytes 393224 | tf_op jit(solution)/shard_map/ppermute | solution.py:461
  46.2 8.8 %collective-permute-start.10 = (bf16[64,1024]{1,0:T(8,128)(2,1)S(1)}, bf16[64,1024]{1,0:T(8,128)(2,1)S(1)}, u32[]{:S(2)}, u32[]{:S(2)}) collective-permute-start(bf16[64,1024]{1,0:T(8,128)(2,1)S(1)} %collective-permute-done.9.rest_6_), channel_id=1, source_target_pairs={{0,4},{4,0},{8,12},{12,8},{1,5},{5,1},{9,13},{13,9},{2,6},{6,2},{1... | collective-permute-start | bytes 393224 | tf_op jit(solution)/shard_map/ppermute | solution.py:461
  55.0 3.1 %copy-start.8 = (bf16[1024]{0:T(1024)(128)(2,1)S(1)}, bf16[1024]{0:T(1024)(128)(2,1)}, u32[]{:S(2)}) copy-start(bf16[1024]{0:T(1024)(128)(2,1)} %param.21) | copy-start | bytes 6148
  56.6 3.6 %collective-permute-start.11 = (f32[2,128]{1,0:T(2,128)S(1)}, f32[2,128]{1,0:T(2,128)S(1)}, u32[]{:S(2)}, u32[]{:S(2)}) collective-permute-start(f32[2,128]{1,0:T(2,128)S(1)} %get-tuple-element.37.own), channel_id=1, source_target_pairs={{0,2},{2,0},{1,3},{3,1},{4,6},{6,4},{5,7},{7,5},{8,10},{10,8},{9,1... | collective-permute-start | bytes 3080 | tf_op jit(solution)/shard_map/ppermute | solution.py:465

commit v5 on v4

--- a/solution.py
+++ b/solution.py
@@ -96,6 +96,17 @@
         self.started = []
 
 
+def gather(sem, dst, choices):
+    for pred, pairs in choices:
+
+        @pl.when(pred)
+        def _():
+            for src, part in pairs:
+                pltpu.make_async_copy(src, part, sem).start()
+
+    return pltpu.make_async_copy(dst, dst, sem).wait
+
+
 def spans(width):
     return [slice(g * 256, (g + 1) * 256) for g in range(width // 256)]
 
@@ -117,8 +128,9 @@
 
 
 def send_part(peers, x_in, b, c, dt, owner, lens, own, near, *rest):
-    outs = (own, near, *rest[: peers - 2])
-    dtv, x, bc, table, length, sem = rest[peers - 2 :]
+    smalls = (own, near, *rest[: peers - 2])
+    outs = (own, near, *rest[peers - 2 : 2 * peers - 4])
+    dtv, x, bc, table, length, sem = rest[2 * peers - 4 :]
     slots, rows, width = x.shape
     heads = dt.shape[1]
     dp = lax.axis_index("dp")
@@ -142,7 +154,7 @@
             out[at : at + HALF] = x[j, start : start + HALF, lanes]
 
     for k in list(range(2, peers)) + [1, 0]:
-        out, j = outs[k], picks[k]
+        out, j = smalls[k], picks[k]
         at = out.shape[0] - rows - 2 * heads
         out[at : at + rows] = bc[j]
         value = dtv[j]
@@ -153,7 +165,7 @@
         out[at + rows : at + rows + heads] = jnp.concatenate([high, middle], axis=1)
         out[at + rows + heads :] = jnp.concatenate([low, count], axis=1)
         if k:
-            put(out, 0, j, 0)
+            put(outs[k], 0, j, 0)
     for m in range(peers // 2):
         put(near, m + 1, picks[1 ^ 2 * m], HALF)
 
@@ -162,13 +174,17 @@
     outs, sem = rest[:-1], rest[-1]
     rows, width = x.shape[1:]
     t = Table(tab, peers, slots)
-    copies = Copies(sem)
     for m in range(1, peers // 2):
-        at = t.holder(2 * m, 0)
-        copies(chunk(near, m + 1, width), outs[m - 1], at == 1)
-        for g, (src, dst) in enumerate(from_rows(x, t.slot(2 * m), HALF, outs[m - 1])):
-            copies(src, dst, at == 0, again=not g)
-    copies.wait()
+        out, at = outs[m - 1], t.holder(2 * m, 0)
+        wait = gather(
+            sem.at[m - 1],
+            out,
+            [
+                (at == 0, from_rows(x, t.slot(2 * m), HALF, out)),
+                (at == 1, [(chunk(near, m + 1, width), out)]),
+            ],
+        )
+        pl.when(at < 2)(wait)
 
 
 def pick_part(peers, slots, heads, tab, *rest):
@@ -177,17 +193,19 @@
     rows = mine.shape[0] - HALF
     size = rows + 2 * heads
     t = Table(tab, peers, slots)
-    copies = Copies(sem)
+    waits = []
     for part in range(2):
-        at = t.holder(0, part)
-        for k in range(peers):
-            copies(tail_of(got[k], size), tails.at[part], at == k, again=k > 0)
+        at, out = t.holder(0, part), tails.at[part]
+        choices = [(at == k, [(tail_of(got[k], size), out)]) for k in range(peers)]
+        waits.append(gather(sem.at[part], out, choices))
     for j in range(slots):
-        for k in range(peers):
-            copies(
-                tail_of(got[k], size, rows + heads, heads), counts.at[j], t.far(j) == k, again=k > 0
-            )
-    copies.wait()
+        at, out = t.far(j), counts.at[j]
+        choices = [
+            (at == k, [(tail_of(got[k], size, rows + heads, heads), out)]) for k in range(peers)
+        ]
+        waits.append(gather(sem.at[2 + j], out, choices))
+    for wait in waits:
+        wait()
     mine[:rows] = tails[0, :rows]
     mine[rows:] = tails[1, :HALF]
     for part in range(2):
@@ -198,7 +216,8 @@
         lens[j] = counts[j, :, rows:].astype(F32)
 
 
-def touch_part(value, out):
+def touch_part(*refs):
+    out = refs[-1]
     out[...] = jnp.zeros(out.shape, out.dtype)
 
 
@@ -289,21 +308,20 @@
     size = width // heads
     t = Table(tab, peers, slots)
     k0, k1, j = t.holder(0, 0), t.holder(0, 1), t.slot(0)
-    loads = Copies(sem)
-    others = Copies(sem.at[pl.ds(2 * width // 256, width // 256 + 2)])
-    straight = [(1, chunk(near, 0, width))] + [
-        (k, chunk(far[k - 2], 0, width)) for k in range(2, peers)
-    ]
-    for g, (src, dst) in enumerate(from_rows(x, j, HALF, high)):
-        loads(src, dst, k0 == 0)
-    loads(chunk(near, 1, width), high, k0 == 1, again=True)
-    for m in range(1, half):
-        loads(onward[m - 1], high, k0 // 2 == m, again=True)
-    for at, out, use in ((k0, low, loads), (k1, second, others)):
-        for g, (src, dst) in enumerate(from_rows(x, j, 0, out)):
-            use(src, dst, at == 0)
-        for k, src in straight:
-            use(src, out, at == k, again=True)
+    upper = (
+        [(k0 == 0, from_rows(x, j, HALF, high)), (k0 == 1, [(chunk(near, 1, width), high)])]
+        + [(k0 // 2 == m, [(onward[m - 1], high)]) for m in range(1, half)]
+    )
+    straight = [near] + list(far)
+
+    def lower(at, out):
+        return [(at == 0, from_rows(x, j, 0, out))] + [
+            (at == k, [(chunk(straight[k - 1], 0, width), out)]) for k in range(1, peers)
+        ]
+
+    got_high = gather(sem.at[0], high, upper)
+    got_low = gather(sem.at[1], low, lower(k0, low))
+    got_second = gather(sem.at[2], second, lower(k1, second))
 
     @pl.when(t.odd == 0)
     def _():
@@ -317,7 +335,8 @@
 
     for lanes in spans(width):
         car0[:, lanes] = dot(cs[:HALF], cache[lanes], (1, 1)).astype(BF16)
-    loads.wait()
+    got_low()
+    got_high()
     for g, lanes in enumerate(spans(width)):
         at = slice(g * HALF, (g + 1) * HALF)
         xv = jnp.concatenate([low[at], high[at]], axis=0).astype(F32)
@@ -330,12 +349,14 @@
                 + local[q * size : (q + 1) * size]
             ).astype(BF16)
         car1[:, lanes] = dot(cs[rows:], late[lanes], (1, 1)).astype(BF16)
-    others.wait()
-    stores = Copies(sem)
-    for at, src in ((k0, car0), (k1, car1)):
-        for k in range(peers):
-            stores(src, cars[k], at == k, again=k > 0)
-    stores.wait()
+    got_second()
+    waits = []
+    for flag, at, src in ((0, k0, car0), (1, k1, car1)):
+        choices = [(at == k, [(src, cars[k])]) for k in range(peers)]
+        gather(sem.at[flag], src, choices)
+        waits.append(pltpu.make_async_copy(src, cars[0], sem.at[flag]).wait)
+    for wait in waits:
+        wait()
 
 
 def final_part(peers, slots, tab, mine, other, share, decays, late, second, final, bs):
@@ -372,17 +393,19 @@
     t = Table(tab, peers, slots)
     waits = []
     for j in range(slots):
-        copies = Copies(sem.at[j])
         early = t.late(t.me * slots + j) == 0
-        for k in range(peers):
-            copies(cars[k], got.at[j, pl.ds(0, HALF)], t.far(j) == k, again=k > 0)
-        for k in range(peers):
-            copies(
-                uppers[k], got.at[j, pl.ds(HALF, HALF)], (t.far(j) == k) & early, again=k > 0
-            )
-        waits.append(copies)
-    for j in range(slots):
-        waits[j].wait()
+        low, high = got.at[j, pl.ds(0, HALF)], got.at[j, pl.ds(HALF, HALF)]
+        at = t.far(j)
+        first = gather(sem.at[j, 0], low, [(at == k, [(cars[k], low)]) for k in range(peers)])
+        second = gather(
+            sem.at[j, 1],
+            high,
+            [((at == k) & early, [(uppers[k], high)]) for k in range(peers)],
+        )
+        waits.append((early, first, second))
+    for j, (early, first, second) in enumerate(waits):
+        first()
+        pl.when(early)(second)
         total = jnp.zeros((rows, 128), F32)
         for p in range(width // 128):
             lanes = slice(p * 128, (p + 1) * 128)
@@ -392,10 +415,11 @@
         squares[j : j + 1] = jnp.sum(jnp.transpose(total), axis=0, keepdims=True)
 
 
-def norm_part(peers, tab, gated, own, other, gain, lens, mixed):
+def norm_part(peers, tab, gated, own, other, gain, lens, mixed, out, sem):
     slots, rows, width = gated.shape
     t = Table(tab, peers, slots)
     row = iota((rows, 128), 0).astype(F32)
+    copies = Copies(sem)
     for j in range(slots):
         late = t.late(t.me * slots + j)
         live = row + (late * rows).astype(F32) < lens[j][:1]
@@ -404,7 +428,9 @@
         for p in range(width // 128):
             lanes = slice(p * 128, (p + 1) * 128)
             value = gated[j, :, lanes] * inverse * gain[:, lanes].astype(F32)
-            mixed[j, :, lanes] = jnp.where(live, value, 0.0).astype(BF16)
+            out[j, :, lanes] = jnp.where(live, value, 0.0).astype(BF16)
+        copies(out.at[j], mixed.at[j])
+    copies.wait()
 
 
 def call(kernel, outs, in_specs, out_specs=None, scratch=(), limit=24, cost=0):
@@ -475,9 +501,11 @@
     tail = rows + 2 * heads
     packed = lambda size: shape((size, 256), BF16)
     upper_rows = shape((HALF, width), BF16)
-    own, near, *sends = call(
+    own, near, *rest = call(
         bind(send_part),
-        [packed(tail), packed((1 + half) * piece + tail)] + [packed(piece + tail)] * (peers - 2),
+        [packed(tail), packed((1 + half) * piece + tail)]
+        + [packed(tail)] * (peers - 2)
+        + [packed(piece)] * (peers - 2),
         [HBM] * 6,
         scratch=[
             scratch(*dt_raw.shape, dtype=F32),
@@ -490,7 +518,8 @@
         limit=60,
     )(x_rows, b, c, dt_raw, slot_owner, lengths)
     near = far(near, 1)
-    sends = [far(value, k + 2) for k, value in enumerate(sends)]
+    smalls = [far(value, k + 2) for k, value in enumerate(rest[: peers - 2])]
+    sends = [far(value, k + 2) for k, value in enumerate(rest[peers - 2 :])]
     yz, ez = call(
         block_part,
         [shape(x_rows.shape, F32)] * 2,
@@ -509,7 +538,7 @@
         [packed(piece)] * (half - 1),
         [SMEM, HBM, ANY, ANY],
         [ANY] * (half - 1),
-        [dma((half - 1) * count)],
+        [dma(half - 1)],
     )(tab, x_rows, near, ez)
     onward = [far(value, 2 * (m + 1)) for m, value in enumerate(passing)]
     mine, dts, lens = call(
@@ -521,14 +550,14 @@
         ],
         [SMEM] + [ANY] * (peers + 1),
         scratch=[scratch(2, tail, 256), scratch(slots, heads, 256), dma(2 + slots)],
-    )(tab, own, near, *sends, passing[0])
+    )(tab, own, near, *smalls, passing[0])
     other = swapped(mine)
     share0, share1, decays = call(
         bind(share_part, slots),
         [shape((rows, width), F32), shape((HALF, width), F32), shape((2, heads, 256), F32)],
         [SMEM, VMEM, VMEM],
     )(tab, dts, params)
-    token = call(touch_part, shape((8, 128), F32), [ANY], cost=40_000_000)(onward[0])
+    token = call(touch_part, shape((8, 128), F32), [ANY] * (peers - 2), cost=40_000_000)(*sends)
     upper = call(
         bind(early_part, slots), upper_rows, [SMEM, VMEM, VMEM, VMEM, ANY, ANY]
     )(tab, cache, mine, other, token, decays)
@@ -545,7 +574,7 @@
             scratch(HALF, width),
             scratch(rows, state),
             scratch(rows + HALF, state),
-            dma(3 * count + 2),
+            dma(3),
         ],
     )(tab, cache, mine, other, share0, decays, x_rows, near, *sends, *onward)
     cars = {0: cars[0]} | {k: far(cars[k], k) for k in list(range(2, peers)) + [1]}
@@ -568,7 +597,7 @@
         *[cars[k] for k in range(peers)],
         *[uppers[k] for k in range(peers)],
     )
-    mixed_rows = call(bind(norm_part), shape(x_rows.shape, BF16), [SMEM] + [VMEM] * 5)(
+    mixed_rows = call(bind(norm_part), shape(x_rows.shape, BF16), [SMEM] + [VMEM] * 5, ANY, [scratch(*x_rows.shape), dma(slots)])(
         tab, gated, squares, swapped(squares), norm_gain[None], lens
     )
     return (mixed_rows, final.reshape(cache_state.shape))

time: 62.1 us -> 60.8 us (0.979)
  waiting for transfers between devices: 19.6 us -> 11.4 us
  starting transfers between devices: 20.1 us -> 26 us
    ppermute x10 -> x12, waiting for transfers between devices: 17.9 us -> 10.2 us  [far(): return lax.ppermute(value, 'sess', [(i, i ^ k) for i in range(peers)])]
    ppermute x10 -> x12, starting transfers between devices: 17 us -> 23.7 us  [far(): return lax.ppermute(value, 'sess', [(i, i ^ k) for i in range(peers)])]
    ppermute x2, starting transfers between devices: 3.11 us -> 2.32 us  [swapped(): return lax.ppermute(value, 'head', [(i, i ^ 1) for i in range(count)])]
    pallas_call x1, Pallas kernels: 1.01 us -> 1.67 us  [per_device(): call(bind(pick_part, slots, heads), [shape((rows + HALF, state), BF16), s...]
  transfers between devices with their start and end apart: 12 -> 14, of which waited for: 10 -> 5; matrix products, arithmetic and copies ran while one was open for 0% -> 0% of each run, Pallas kernels for 16% -> 19%
where the time goes in v5:
time: 60.8 us; the launch traced here: 59.9 us
  starting transfers between devices  26 us (43%)
  Pallas kernels  16.8 us (28%)
  waiting for transfers between devices  11.4 us (19%)
  local copies, waits for them, and re-layouts  4.07 us (7%)
  between operations  1.51 us (2%)
    ppermute x12, starting transfers between devices, far(): return lax.ppermute(value, 'sess', [(i, i ^ k) for i in range(peers)])  23.7 us
    ppermute x12, waiting for transfers between devices, far(): return lax.ppermute(value, 'sess', [(i, i ^ k) for i in range(peers)])  10.2 us
    unnamed x26, local copies, waits for them, and re-layouts  3.99 us
    pallas_call x1, Pallas kernels, per_device(): call(block_part, [shape(x_rows.shape, F32)] * 2, [HBM] * 5 + [VMEM], scra...  2.87 us
    ppermute x2, starting transfers between devices, swapped(): return lax.ppermute(value, 'head', [(i, i ^ 1) for i in range(count)])  2.32 us
    pallas_call x1, Pallas kernels, per_device(): call(bind(late_part, slots), [shape((width, state), BF16), packed(piece)]...  2.25 us
    pallas_call x1, Pallas kernels, per_device(): call(bind(send_part), [packed(tail), packed((1 + half) * piece + tail)] +...  2.16 us
    pallas_call x1, Pallas kernels, per_device(): call(bind(final_part, slots), shape((width, state), BF16), [SMEM] + [VMEM...  1.69 us
  transfers between devices with their start and end apart: 14, of which 5 were waited for; matrix products, arithmetic and copies ran while one was open for 0% of the time, Pallas kernels for 19%

profile of v5, /device:TPU:0, one launch (start us, length us, event | category | flops | bytes accessed | tf_op | source)
XLA Modules:
  0.0 59.9 jit_solution(13674695336191403493)
XLA Ops:
  1.4 2.2 %shard_map.141 = (bf16[160,256]{1,0:T(8,128)(2,1)}, bf16[928,256]{1,0:T(8,128)(2,1)}, bf16[160,256]{1,0:T(8,128)(2,1)}, bf16[160,256]{1,0:T(8,128)(2,1)}, bf16[2...) custom-call(bf16[2,128,1024]{2,1,0:T(8,128)(2,1)} %x.3, bf16[2,128,256]{2,1,0:T(8,128)(2,1)} %b.1, bf16[2,128,256]{2,1,0:T(8,128)(2,1)} %c.1, ...), custom_call_target="tpu_custom_call" | custom-call | tf_op jit(solution)/shard_map/pallas_call | solution.py:504
  3.5 3.1 %collective-permute-start = (bf16[928,256]{1,0:T(8,128)(2,1)}, bf16[928,256]{1,0:T(8,128)(2,1)S(1)}, u32[]{:S(2)}, u32[]{:S(2)}) collective-permute-start(bf16[928,256]{1,0:T(8,128)(2,1)} %get-tuple-element.27), channel_id=1, source_target_pairs={{0,4},{4,0},{8,12},{12,8},{1,5},{5,1},{9,13},{13,9},{2,6},{6,2},{1... | collective-permute-start | bytes 1425416 | tf_op jit(solution)/shard_map/ppermute | solution.py:487
  6.6 2.6 %collective-permute-start.1 = (bf16[160,256]{1,0:T(8,128)(2,1)}, bf16[160,256]{1,0:T(8,128)(2,1)}, u32[]{:S(2)}, u32[]{:S(2)}) collective-permute-start(bf16[160,256]{1,0:T(8,128)(2,1)} %get-tuple-element.28), channel_id=1, source_target_pairs={{0,8},{4,12},{8,0},{12,4},{1,9},{5,13},{9,1},{13,5},{2,10},{6,14},... | collective-permute-start | bytes 245768 | tf_op jit(solution)/shard_map/ppermute | solution.py:487
  9.2 1.9 %collective-permute-start.4 = (bf16[256,256]{1,0:T(8,128)(2,1)}, bf16[256,256]{1,0:T(8,128)(2,1)S(1)}, u32[]{:S(2)}, u32[]{:S(2)}) collective-permute-start(bf16[256,256]{1,0:T(8,128)(2,1)} %get-tuple-element.34), channel_id=1, source_target_pairs={{0,8},{4,12},{8,0},{12,4},{1,9},{5,13},{9,1},{13,5},{2,10},{6,14},... | collective-permute-start | bytes 393224 | tf_op jit(solution)/shard_map/ppermute | solution.py:487
  11.1 1.9 %collective-permute-start.5 = (bf16[256,256]{1,0:T(8,128)(2,1)}, bf16[256,256]{1,0:T(8,128)(2,1)S(1)}, u32[]{:S(2)}, u32[]{:S(2)}) collective-permute-start(bf16[256,256]{1,0:T(8,128)(2,1)} %get-tuple-element.35), channel_id=1, source_target_pairs={{0,12},{4,8},{8,4},{12,0},{1,13},{5,9},{9,5},{13,1},{2,14},{6,10},... | collective-permute-start | bytes 393224 | tf_op jit(solution)/shard_map/ppermute | solution.py:487
  13.0 0.7 %copy-done.7 = s32[2,8]{1,0:T(2,128)S(1)} copy-done((s32[2,8]{1,0:T(2,128)S(1)}, s32[2,8]{1,0:T(2,128)}, u32[]{:S(2)}) %copy-start.7) | copy-done | bytes 88
  13.8 0.6 %copy-done.10 = f32[16]{0:T(128)S(1)} copy-done((f32[16]{0:T(128)S(1)}, f32[16]{0:T(128)}, u32[]{:S(2)}) %copy-start.10) | copy-done | bytes 88
  14.5 0.7 %copy-done.6 = f32[2,16,128]{2,1,0:T(8,128)S(1)} copy-done((f32[2,16,128]{2,1,0:T(8,128)S(1)}, f32[2,16,128]{2,1,0:T(8,128)}, u32[]{:S(2)}) %copy-start.6) | copy-done | bytes 16408
  15.2 1.0 %copy-done.2 = bf16[2,128,1024]{2,1,0:T(8,128)(2,1)S(1)} copy-done((bf16[2,128,1024]{2,1,0:T(8,128)(2,1)S(1)}, bf16[2,128,1024]{2,1,0:T(8,128)(2,1)}, u32[]{:S(2)}) %copy-start.2) | copy-done | bytes 524312
  16.3 0.9 %copy-done.4 = bf16[2,128,256]{2,1,0:T(8,128)(2,1)S(1)} copy-done((bf16[2,128,256]{2,1,0:T(8,128)(2,1)S(1)}, bf16[2,128,256]{2,1,0:T(8,128)(2,1)}, u32[]{:S(2)}) %copy-start.4) | copy-done | bytes 131096
  17.2 2.9 %shard_map.140 = (f32[2,128,1024]{2,1,0:T(8,128)S(1)}, f32[2,128,1024]{2,1,0:T(8,128)S(1)}) custom-call(bf16[2,128,1024]{2,1,0:T(8,128)(2,1)S(1)} %copy-done, bf16[2,128,1024]{2,1,0:T(8,128)(2,1)S(1)} %copy-done.2, bf16[2,128,256]{2,1,0:T(8,128)(2,1)S(1)} %copy-done.3, bf16[2,128,256]{2,1,0:T(8,128)(2,1)S(1)} %copy-done.4, f32[2,16,128]{2,1,0:T(8,128)S(1)} %copy-done.6, ...), custom_call_target="tpu_custom_call" | custom-call | tf_op jit(solution)/shard_map/pallas_call | solution.py:523
  20.1 3.4 %collective-permute-done.near.rest_1_ = bf16[928,256]{1,0:T(8,128)(2,1)S(1)} collective-permute-done((bf16[928,256]{1,0:T(8,128)(2,1)}, bf16[928,256]{1,0:T(8,128)(2,1)S(1)}, u32[]{:S(2)}, u32[]{:S(2)}) %collective-permute-start) | collective-permute-done | bytes 475168 | tf_op jit(solution)/shard_map/ppermute | solution.py:487
  23.5 0.8 %shard_map.142.rest_4_ = bf16[256,256]{1,0:T(8,128)(2,1)S(1)} custom-call(s32[19]{0:T(128)S(1)} %concatenate.3.tab, bf16[2,128,1024]{2,1,0:T(8,128)(2,1)S(1)} %copy-done, bf16[928,256]{1,0:T(8,128)(2,1)S(1)} %collective-permute-done.near.rest_1_, f32[2,128,1024]{2,1,0:T(8,128)S(1)} %get-tuple-element.25.after.ez), custom_call_target="tpu_custom_call" | custom-call | tf_op jit(solution)/shard_map/pallas_call | solution.py:536
  24.3 0.4 collective-permute-done.2.rest_3_
  24.6 1.7 %shard_map.143 = (bf16[192,256]{1,0:T(8,128)(2,1)S(1)}, f32[2,16,128]{2,1,0:T(8,128)S(1)}, f32[2,16,128]{2,1,0:T(8,128)S(1)}) custom-call(s32[19]{0:T(128)S(1)} %concatenate.3.tab, bf16[160,256]{1,0:T(8,128)(2,1)S(1)} %copy-done.5, bf16[928,256]{1,0:T(8,128)(2,1)S(1)} %collective-permute-done.near.rest_1_, bf16[160,256]{1,0:T(8,128)(2,1)} %collective-permute-done.1.rest_2_, ...), custom_call_target="tpu_custom_call" | custom-call | tf_op jit(solution)/shard_map/pallas_call | solution.py:544
  26.3 1.6 %collective-permute-start.3 = (bf16[192,256]{1,0:T(8,128)(2,1)S(1)}, bf16[192,256]{1,0:T(8,128)(2,1)S(1)}, u32[]{:S(2)}, u32[]{:S(2)}) collective-permute-start(bf16[192,256]{1,0:T(8,128)(2,1)S(1)} %get-tuple-element.30.mine), channel_id=1, source_target_pairs={{0,2},{2,0},{1,3},{3,1},{4,6},{6,4},{5,7},{7,5},{8,10},{10,8},{9,1... | collective-permute-start | bytes 294920 | tf_op jit(solution)/shard_map/ppermute | solution.py:491
  27.9 3.1 %collective-permute-start.6 = (bf16[256,256]{1,0:T(8,128)(2,1)S(1)}, bf16[256,256]{1,0:T(8,128)(2,1)S(1)}, u32[]{:S(2)}, u32[]{:S(2)}) collective-permute-start(bf16[256,256]{1,0:T(8,128)(2,1)S(1)} %shard_map.142.rest_4_), channel_id=1, source_target_pairs={{0,8},{4,12},{8,0},{12,4},{1,9},{5,13},{9,1},{13,5},{2,10},{6,14},... | collective-permute-start | bytes 393224 | tf_op jit(solution)/shard_map/ppermute | solution.py:487
  31.1 1.6 %shard_map.144 = (f32[128,1024]{1,0:T(8,128)S(1)}, f32[64,1024]{1,0:T(8,128)S(1)}, f32[2,16,256]{2,1,0:T(8,128)S(1)}) custom-call(s32[19]{0:T(128)S(1)} %concatenate.3.tab, f32[2,16,128]{2,1,0:T(8,128)S(1)} %get-tuple-element.31.dts, f32[3,16]{1,0:T(4,128)S(1)} %pad_maximum_fusion.params), custom_call_target="tpu_custom_call" | custom-call | tf_op jit(solution)/shard_map/pallas_call | solution.py:555
  32.7 0.8 %shard_map.147.rest_4_ = bf16[64,1024]{1,0:T(8,128)(2,1)S(1)} custom-call(s32[19]{0:T(128)S(1)} %concatenate.3.tab, bf16[1024,256]{1,0:T(8,128)(2,1)S(1)} %bitcast.7, bf16[192,256]{1,0:T(8,128)(2,1)S(1)} %get-tuple-element.30.mine, bf16[192,256]{1,0:T(8,128)(2,1)S(1)} %collective-permute-done.3.other, f32[8,128]{1,0:T(8,128)S(1)} %shard_map.146.token, ...), custom_call_target="tpu_custom_call" | custom-call | tf_op jit(solution)/shard_map/pallas_call | solution.py:561
  33.5 1.6 %collective-permute-start.11 = (bf16[64,1024]{1,0:T(8,128)(2,1)S(1)}, bf16[64,1024]{1,0:T(8,128)(2,1)S(1)}, u32[]{:S(2)}, u32[]{:S(2)}) collective-permute-start(bf16[64,1024]{1,0:T(8,128)(2,1)S(1)} %shard_map.147.rest_4_), channel_id=1, source_target_pairs={{0,8},{4,12},{8,0},{12,4},{1,9},{5,13},{9,1},{13,5},{2,10},{6,14},... | collective-permute-start | bytes 393224 | tf_op jit(solution)/shard_map/ppermute | solution.py:487
  35.1 4.2 %collective-permute-start.10 = (bf16[64,1024]{1,0:T(8,128)(2,1)S(1)}, bf16[64,1024]{1,0:T(8,128)(2,1)S(1)}, u32[]{:S(2)}, u32[]{:S(2)}) collective-permute-start(bf16[64,1024]{1,0:T(8,128)(2,1)S(1)} %shard_map.147.rest_4_), channel_id=1, source_target_pairs={{0,4},{4,0},{8,12},{12,8},{1,5},{5,1},{9,13},{13,9},{2,6},{6,2},{1... | collective-permute-start | bytes 393224 | tf_op jit(solution)/shard_map/ppermute | solution.py:487
  39.3 2.3 %shard_map.145 = (bf16[1024,256]{1,0:T(8,128)(2,1)S(1)}, bf16[256,256]{1,0:T(8,128)(2,1)S(1)}, bf16[64,1024]{1,0:T(8,128)(2,1)S(1)}, bf16[64,1024]{1,0:T(8,128)(...) custom-call(s32[19]{0:T(128)S(1)} %concatenate.3.tab, bf16[1024,256]{1,0:T(8,128)(2,1)S(1)} %bitcast.8, ...), custom_call_target="tpu_custom_call" | custom-call | tf_op jit(solution)/shard_map/pallas_call | solution.py:565
  41.5 1.1 %collective-permute-start.7 = (bf16[64,1024]{1,0:T(8,128)(2,1)S(1)}, bf16[64,1024]{1,0:T(8,128)(2,1)S(1)}, u32[]{:S(2)}, u32[]{:S(2)}) collective-permute-start(bf16[64,1024]{1,0:T(8,128)(2,1)S(1)} %get-tuple-element.37), channel_id=1, source_target_pairs={{0,4},{4,0},{8,12},{12,8},{1,5},{5,1},{9,13},{13,9},{2,6},{6,2},{1... | collective-permute-start | bytes 393224 | tf_op jit(solution)/shard_map/ppermute | solution.py:487
  42.7 3.6 %collective-permute-start.8 = (bf16[64,1024]{1,0:T(8,128)(2,1)S(1)}, bf16[64,1024]{1,0:T(8,128)(2,1)S(1)}, u32[]{:S(2)}, u32[]{:S(2)}) collective-permute-start(bf16[64,1024]{1,0:T(8,128)(2,1)S(1)} %get-tuple-element.38), channel_id=1, source_target_pairs={{0,8},{4,12},{8,0},{12,4},{1,9},{5,13},{9,1},{13,5},{2,10},{6,14},... | collective-permute-start | bytes 393224 | tf_op jit(solution)/shard_map/ppermute | solution.py:487
  46.2 0.6 collective-permute-start.12
  46.8 3.3 %collective-permute-done.7.rest_1_ = bf16[64,1024]{1,0:T(8,128)(2,1)S(1)} collective-permute-done((bf16[64,1024]{1,0:T(8,128)(2,1)S(1)}, bf16[64,1024]{1,0:T(8,128)(2,1)S(1)}, u32[]{:S(2)}, u32[]{:S(2)}) %collective-permute-start.7) | collective-permute-done | bytes 131104 | tf_op jit(solution)/shard_map/ppermute | solution.py:487
  50.1 3.1 %collective-permute-done.9.rest_3_ = bf16[64,1024]{1,0:T(8,128)(2,1)S(1)} collective-permute-done((bf16[64,1024]{1,0:T(8,128)(2,1)S(1)}, bf16[64,1024]{1,0:T(8,128)(2,1)S(1)}, u32[]{:S(2)}, u32[]{:S(2)}) %collective-permute-start.9) | collective-permute-done | bytes 131104 | tf_op jit(solution)/shard_map/ppermute | solution.py:487
  53.2 1.5 %shard_map.148 = (f32[2,128,1024]{2,1,0:T(8,128)S(1)}, f32[2,128]{1,0:T(2,128)S(1)}) custom-call(s32[19]{0:T(128)S(1)} %concatenate.3.tab, f32[2,128,1024]{2,1,0:T(8,128)S(1)} %get-tuple-element.24.yz, f32[2,128,1024]{2,1,0:T(8,128)S(1)} %get-tuple-element.25.after.ez, bf16[64,1024]{1,0:T(8,128)(2,1)S(1)} %get-tuple-element.36.rest_0_, ...), custom_call_target="tpu_custom_call" | custom-call | tf_op jit(solution)/shard_map/pallas_call | solution.py:588
  54.7 0.7 %collective-permute-start.13 = (f32[2,128]{1,0:T(2,128)S(1)}, f32[2,128]{1,0:T(2,128)S(1)}, u32[]{:S(2)}, u32[]{:S(2)}) collective-permute-start(f32[2,128]{1,0:T(2,128)S(1)} %get-tuple-element.41.own), channel_id=1, source_target_pairs={{0,2},{2,0},{1,3},{3,1},{4,6},{6,4},{5,7},{7,5},{8,10},{10,8},{9,1... | collective-permute-start | bytes 3080 | tf_op jit(solution)/shard_map/ppermute | solution.py:491
  55.5 1.7 %shard_map.150 = bf16[1024,256]{1,0:T(8,128)(2,1)} custom-call(s32[19]{0:T(128)S(1)} %concatenate.3.tab, bf16[192,256]{1,0:T(8,128)(2,1)S(1)} %get-tuple-element.30.mine, bf16[192,256]{1,0:T(8,128)(2,1)S(1)} %collective-permute-done.3.other, f32[64,1024]{1,0:T(8,128)S(1)} %get-tuple-element.43.share, f32[2,16,256]{2,1,0:T(8,128)S(1)} %get-tuple-element.33.decays, ...), custom_call_target="tpu_custom_call" | custom-call | tf_op jit(solution)/shard_map/pallas_call | solution.py:582
  57.2 1.2 %collective-permute-done.13.other = f32[2,128]{1,0:T(2,128)S(1)} collective-permute-done((f32[2,128]{1,0:T(2,128)S(1)}, f32[2,128]{1,0:T(2,128)S(1)}, u32[]{:S(2)}, u32[]{:S(2)}) %collective-permute-start.13) | collective-permute-done | bytes 1056 | tf_op jit(solution)/shard_map/ppermute | solution.py:491
  58.4 1.6 %shard_map.149 = bf16[2,128,1024]{2,1,0:T(8,128)(2,1)} custom-call(s32[19]{0:T(128)S(1)} %concatenate.3.tab, f32[2,128,1024]{2,1,0:T(8,128)S(1)} %get-tuple-element.40.gated, f32[2,128]{1,0:T(2,128)S(1)} %get-tuple-element.41.own, f32[2,128]{1,0:T(2,128)S(1)} %collective-permute-done.13.other, bf16[1,1024]{1,0:T(2,128)(2,1)S(1)} %broadcast_in_dim.9.gain, ...), custom_call_target="tpu_custom_call" | custom-call | tf_op jit(solution)/shard_map/pallas_call | solution.py:600
  (38 shorter events, 0.3 us)
Async XLA Ops:
  0.6 13.9 %copy-start = (bf16[2,128,1024]{2,1,0:T(8,128)(2,1)S(1)}, bf16[2,128,1024]{2,1,0:T(8,128)(2,1)}, u32[]{:S(2)}) copy-start(bf16[2,128,1024]{2,1,0:T(8,128)(2,1)} %x.3) | copy-start | bytes 1572868
  1.3 13.2 %copy-start.3 = (bf16[2,128,256]{2,1,0:T(8,128)(2,1)S(1)}, bf16[2,128,256]{2,1,0:T(8,128)(2,1)}, u32[]{:S(2)}) copy-start(bf16[2,128,256]{2,1,0:T(8,128)(2,1)} %b.1) | copy-start | bytes 393220
  3.5 20.0 %collective-permute-start = (bf16[928,256]{1,0:T(8,128)(2,1)}, bf16[928,256]{1,0:T(8,128)(2,1)S(1)}, u32[]{:S(2)}, u32[]{:S(2)}) collective-permute-start(bf16[928,256]{1,0:T(8,128)(2,1)} %get-tuple-element.27), channel_id=1, source_target_pairs={{0,4},{4,0},{8,12},{12,8},{1,5},{5,1},{9,13},{13,9},{2,6},{6,2},{1... | collective-permute-start | bytes 1425416 | tf_op jit(solution)/shard_map/ppermute | solution.py:487
  6.6 17.6 %collective-permute-start.1 = (bf16[160,256]{1,0:T(8,128)(2,1)}, bf16[160,256]{1,0:T(8,128)(2,1)}, u32[]{:S(2)}, u32[]{:S(2)}) collective-permute-start(bf16[160,256]{1,0:T(8,128)(2,1)} %get-tuple-element.28), channel_id=1, source_target_pairs={{0,8},{4,12},{8,0},{12,4},{1,9},{5,13},{9,1},{13,5},{2,10},{6,14},... | collective-permute-start | bytes 245768 | tf_op jit(solution)/shard_map/ppermute | solution.py:487
  9.2 15.4 %collective-permute-start.2 = (bf16[160,256]{1,0:T(8,128)(2,1)}, bf16[160,256]{1,0:T(8,128)(2,1)}, u32[]{:S(2)}, u32[]{:S(2)}) collective-permute-start(bf16[160,256]{1,0:T(8,128)(2,1)} %get-tuple-element.29), channel_id=1, source_target_pairs={{0,12},{4,8},{8,4},{12,0},{1,13},{5,9},{9,5},{13,1},{2,14},{6,10},... | collective-permute-start | bytes 245768 | tf_op jit(solution)/shard_map/ppermute | solution.py:487
  9.2 3.8 %copy-start.9 = (s32[2,8]{1,0:T(2,128)S(1)}, s32[2,8]{1,0:T(2,128)}, u32[]{:S(2)}) copy-start(s32[2,8]{1,0:T(2,128)} %param.25) | copy-start | bytes 196
  9.2 21.9 %collective-permute-start.4 = (bf16[256,256]{1,0:T(8,128)(2,1)}, bf16[256,256]{1,0:T(8,128)(2,1)S(1)}, u32[]{:S(2)}, u32[]{:S(2)}) collective-permute-start(bf16[256,256]{1,0:T(8,128)(2,1)} %get-tuple-element.34), channel_id=1, source_target_pairs={{0,8},{4,12},{8,0},{12,4},{1,9},{5,13},{9,1},{13,5},{2,10},{6,14},... | collective-permute-start | bytes 393224 | tf_op jit(solution)/shard_map/ppermute | solution.py:487
  11.1 20.0 %collective-permute-start.5 = (bf16[256,256]{1,0:T(8,128)(2,1)}, bf16[256,256]{1,0:T(8,128)(2,1)S(1)}, u32[]{:S(2)}, u32[]{:S(2)}) collective-permute-start(bf16[256,256]{1,0:T(8,128)(2,1)} %get-tuple-element.35), channel_id=1, source_target_pairs={{0,12},{4,8},{8,4},{12,0},{1,13},{5,9},{9,5},{13,1},{2,14},{6,10},... | collective-permute-start | bytes 393224 | tf_op jit(solution)/shard_map/ppermute | solution.py:487
  13.0 0.7 %copy-start.7 = (s32[2,8]{1,0:T(2,128)S(1)}, s32[2,8]{1,0:T(2,128)}, u32[]{:S(2)}) copy-start(s32[2,8]{1,0:T(2,128)} %owner.1) | copy-start | bytes 196
  13.8 0.7 %copy-start.10 = (f32[16]{0:T(128)S(1)}, f32[16]{0:T(128)}, u32[]{:S(2)}) copy-start(f32[16]{0:T(128)} %param.20) | copy-start | bytes 196
  13.8 0.7 %copy-start.11 = (f32[16]{0:T(128)S(1)}, f32[16]{0:T(128)}, u32[]{:S(2)}) copy-start(f32[16]{0:T(128)} %param.19) | copy-start | bytes 196
  13.8 0.7 %copy-start.12 = (f32[16]{0:T(128)S(1)}, f32[16]{0:T(128)}, u32[]{:S(2)}) copy-start(f32[16]{0:T(128)} %param.18) | copy-start | bytes 196
  14.5 0.7 %copy-start.6 = (f32[2,16,128]{2,1,0:T(8,128)S(1)}, f32[2,16,128]{2,1,0:T(8,128)}, u32[]{:S(2)}) copy-start(f32[2,16,128]{2,1,0:T(8,128)} %dt.1) | copy-start | bytes 49156
  15.2 1.0 %copy-start.2 = (bf16[2,128,1024]{2,1,0:T(8,128)(2,1)S(1)}, bf16[2,128,1024]{2,1,0:T(8,128)(2,1)}, u32[]{:S(2)}) copy-start(bf16[2,128,1024]{2,1,0:T(8,128)(2,1)} %z_in.1) | copy-start | bytes 1572868
  16.3 0.9 %copy-start.4 = (bf16[2,128,256]{2,1,0:T(8,128)(2,1)S(1)}, bf16[2,128,256]{2,1,0:T(8,128)(2,1)}, u32[]{:S(2)}) copy-start(bf16[2,128,256]{2,1,0:T(8,128)(2,1)} %c.1) | copy-start | bytes 393220
  23.5 1.2 %copy-start.5 = (bf16[160,256]{1,0:T(8,128)(2,1)S(1)}, bf16[160,256]{1,0:T(8,128)(2,1)}, u32[]{:S(2)}) copy-start(bf16[160,256]{1,0:T(8,128)(2,1)} %get-tuple-element.26.rest_0_) | copy-start | bytes 245764
  24.6 8.0 %copy-start.1 = (bf16[1,16,64,256]{3,2,1,0:T(8,128)(2,1)S(1)}, bf16[1,16,64,256]{3,2,1,0:T(8,128)(2,1)}, u32[]{:S(2)}) copy-start(bf16[1,16,64,256]{3,2,1,0:T(8,128)(2,1)} %param.22) | copy-start | bytes 1572868
  26.3 6.3 %collective-permute-start.3 = (bf16[192,256]{1,0:T(8,128)(2,1)S(1)}, bf16[192,256]{1,0:T(8,128)(2,1)S(1)}, u32[]{:S(2)}, u32[]{:S(2)}) collective-permute-start(bf16[192,256]{1,0:T(8,128)(2,1)S(1)} %get-tuple-element.30.mine), channel_id=1, source_target_pairs={{0,2},{2,0},{1,3},{3,1},{4,6},{6,4},{5,7},{7,5},{8,10},{10,8},{9,1... | collective-permute-start | bytes 294920 | tf_op jit(solution)/shard_map/ppermute | solution.py:491
  27.9 11.3 %collective-permute-start.6 = (bf16[256,256]{1,0:T(8,128)(2,1)S(1)}, bf16[256,256]{1,0:T(8,128)(2,1)S(1)}, u32[]{:S(2)}, u32[]{:S(2)}) collective-permute-start(bf16[256,256]{1,0:T(8,128)(2,1)S(1)} %shard_map.142.rest_4_), channel_id=1, source_target_pairs={{0,8},{4,12},{8,0},{12,4},{1,9},{5,13},{9,1},{13,5},{2,10},{6,14},... | collective-permute-start | bytes 393224 | tf_op jit(solution)/shard_map/ppermute | solution.py:487
  33.5 12.7 %collective-permute-start.11 = (bf16[64,1024]{1,0:T(8,128)(2,1)S(1)}, bf16[64,1024]{1,0:T(8,128)(2,1)S(1)}, u32[]{:S(2)}, u32[]{:S(2)}) collective-permute-start(bf16[64,1024]{1,0:T(8,128)(2,1)S(1)} %shard_map.147.rest_4_), channel_id=1, source_target_pairs={{0,8},{4,12},{8,0},{12,4},{1,9},{5,13},{9,1},{13,5},{2,10},{6,14},... | collective-permute-start | bytes 393224 | tf_op jit(solution)/shard_map/ppermute | solution.py:487
  35.1 11.7 %collective-permute-start.10 = (bf16[64,1024]{1,0:T(8,128)(2,1)S(1)}, bf16[64,1024]{1,0:T(8,128)(2,1)S(1)}, u32[]{:S(2)}, u32[]{:S(2)}) collective-permute-start(bf16[64,1024]{1,0:T(8,128)(2,1)S(1)} %shard_map.147.rest_4_), channel_id=1, source_target_pairs={{0,4},{4,0},{8,12},{12,8},{1,5},{5,1},{9,13},{13,9},{2,6},{6,2},{1... | collective-permute-start | bytes 393224 | tf_op jit(solution)/shard_map/ppermute | solution.py:487
  41.5 8.6 %collective-permute-start.7 = (bf16[64,1024]{1,0:T(8,128)(2,1)S(1)}, bf16[64,1024]{1,0:T(8,128)(2,1)S(1)}, u32[]{:S(2)}, u32[]{:S(2)}) collective-permute-start(bf16[64,1024]{1,0:T(8,128)(2,1)S(1)} %get-tuple-element.37), channel_id=1, source_target_pairs={{0,4},{4,0},{8,12},{12,8},{1,5},{5,1},{9,13},{13,9},{2,6},{6,2},{1... | collective-permute-start | bytes 393224 | tf_op jit(solution)/shard_map/ppermute | solution.py:487
  42.7 7.5 %collective-permute-start.8 = (bf16[64,1024]{1,0:T(8,128)(2,1)S(1)}, bf16[64,1024]{1,0:T(8,128)(2,1)S(1)}, u32[]{:S(2)}, u32[]{:S(2)}) collective-permute-start(bf16[64,1024]{1,0:T(8,128)(2,1)S(1)} %get-tuple-element.38), channel_id=1, source_target_pairs={{0,8},{4,12},{8,0},{12,4},{1,9},{5,13},{9,1},{13,5},{2,10},{6,14},... | collective-permute-start | bytes 393224 | tf_op jit(solution)/shard_map/ppermute | solution.py:487
  46.2 7.0 %collective-permute-start.9 = (bf16[64,1024]{1,0:T(8,128)(2,1)S(1)}, bf16[64,1024]{1,0:T(8,128)(2,1)S(1)}, u32[]{:S(2)}, u32[]{:S(2)}) collective-permute-start(bf16[64,1024]{1,0:T(8,128)(2,1)S(1)} %get-tuple-element.39), channel_id=1, source_target_pairs={{0,12},{4,8},{8,4},{12,0},{1,13},{5,9},{9,5},{13,1},{2,14},{6,10},... | collective-permute-start | bytes 393224 | tf_op jit(solution)/shard_map/ppermute | solution.py:487
  46.2 7.0 %collective-permute-start.12 = (bf16[64,1024]{1,0:T(8,128)(2,1)S(1)}, bf16[64,1024]{1,0:T(8,128)(2,1)S(1)}, u32[]{:S(2)}, u32[]{:S(2)}) collective-permute-start(bf16[64,1024]{1,0:T(8,128)(2,1)S(1)} %collective-permute-done.11.rest_6_), channel_id=1, source_target_pairs={{0,4},{4,0},{8,12},{12,8},{1,5},{5,1},{9,13},{13,9},{2,6},{6,2},{1... | collective-permute-start | bytes 393224 | tf_op jit(solution)/shard_map/ppermute | solution.py:487
  53.2 2.2 %copy-start.8 = (bf16[1024]{0:T(1024)(128)(2,1)S(1)}, bf16[1024]{0:T(1024)(128)(2,1)}, u32[]{:S(2)}) copy-start(bf16[1024]{0:T(1024)(128)(2,1)} %param.21) | copy-start | bytes 6148
  54.7 3.6 %collective-permute-start.13 = (f32[2,128]{1,0:T(2,128)S(1)}, f32[2,128]{1,0:T(2,128)S(1)}, u32[]{:S(2)}, u32[]{:S(2)}) collective-permute-start(f32[2,128]{1,0:T(2,128)S(1)} %get-tuple-element.41.own), channel_id=1, source_target_pairs={{0,2},{2,0},{1,3},{3,1},{4,6},{6,4},{5,7},{7,5},{8,10},{10,8},{9,1... | collective-permute-start | bytes 3080 | tf_op jit(solution)/shard_map/ppermute | solution.py:491

commit v6 on v5

--- a/solution.py
+++ b/solution.py
@@ -287,7 +287,7 @@
             ez[s, :, lanes] = decay * gate
 
 
-def early_part(peers, slots, tab, cache, mine, other, token, decays, upper):
+def early_part(peers, slots, tab, cache, mine, other, token, upper):
     def work(cs):
         for lanes in spans(cache.shape[0]):
             upper[:, lanes] = dot(cs[HALF : 2 * HALF], cache[lanes], (1, 1)).astype(BF16)
@@ -559,8 +559,8 @@
     )(tab, dts, params)
     token = call(touch_part, shape((8, 128), F32), [ANY] * (peers - 2), cost=40_000_000)(*sends)
     upper = call(
-        bind(early_part, slots), upper_rows, [SMEM, VMEM, VMEM, VMEM, ANY, ANY]
-    )(tab, cache, mine, other, token, decays)
+        bind(early_part, slots), upper_rows, [SMEM, VMEM, VMEM, VMEM, ANY]
+    )(tab, cache, mine, other, token)
     uppers = {2 * m: far(upper, 2 * m) if m else upper for m in range(half)}
     late, second, *cars = call(
         bind(late_part, slots),

time: 60.8 us -> 61.3 us (level)
  starting transfers between devices: 26 us -> 27.6 us
  waiting for transfers between devices: 11.4 us -> 10.7 us
    ppermute x2, starting transfers between devices: 2.32 us -> 3.15 us  [swapped(): return lax.ppermute(value, 'head', [(i, i ^ 1) for i in range(count)])]
    ppermute x2, waiting for transfers between devices: 1.22 us -> 0.39 us  [swapped(): return lax.ppermute(value, 'head', [(i, i ^ 1) for i in range(count)])]
    ppermute x12, starting transfers between devices: 23.7 us -> 24.4 us  [far(): return lax.ppermute(value, 'sess', [(i, i ^ k) for i in range(peers)])]
  transfers between devices with their start and end apart: 14 -> 14, of which waited for: 5 -> 6; matrix products, arithmetic and copies ran while one was open for 0% -> 0% of each run, Pallas kernels for 19% -> 19%
where the time goes in v6:
time: 61.3 us; the launch traced here: 60.7 us
  starting transfers between devices  27.6 us (45%)
  Pallas kernels  16.7 us (27%)
  waiting for transfers between devices  10.7 us (17%)
  local copies, waits for them, and re-layouts  4.07 us (7%)
  between operations  1.51 us (2%)
    ppermute x12, starting transfers between devices, far(): return lax.ppermute(value, 'sess', [(i, i ^ k) for i in range(peers)])  24.4 us
    ppermute x12, waiting for transfers between devices, far(): return lax.ppermute(value, 'sess', [(i, i ^ k) for i in range(peers)])  10.3 us
    unnamed x26, local copies, waits for them, and re-layouts  3.99 us
    ppermute x2, starting transfers between devices, swapped(): return lax.ppermute(value, 'head', [(i, i ^ 1) for i in range(count)])  3.15 us
    pallas_call x1, Pallas kernels, per_device(): call(block_part, [shape(x_rows.shape, F32)] * 2, [HBM] * 5 + [VMEM], scra...  2.87 us
    pallas_call x1, Pallas kernels, per_device(): call(bind(late_part, slots), [shape((width, state), BF16), packed(piece)]...  2.37 us
    pallas_call x1, Pallas kernels, per_device(): call(bind(send_part), [packed(tail), packed((1 + half) * piece + tail)] +...  2.16 us
    pallas_call x1, Pallas kernels, per_device(): call(bind(final_part, slots), shape((width, state), BF16), [SMEM] + [VMEM...  1.68 us
  transfers between devices with their start and end apart: 14, of which 6 were waited for; matrix products, arithmetic and copies ran while one was open for 0% of the time, Pallas kernels for 19%

profile of v6, /device:TPU:0, one launch (start us, length us, event | category | flops | bytes accessed | tf_op | source)
XLA Modules:
  0.0 60.7 jit_solution(1833340590074633440)
XLA Ops:
  1.4 2.2 %shard_map.141 = (bf16[160,256]{1,0:T(8,128)(2,1)}, bf16[928,256]{1,0:T(8,128)(2,1)}, bf16[160,256]{1,0:T(8,128)(2,1)}, bf16[160,256]{1,0:T(8,128)(2,1)}, bf16[2...) custom-call(bf16[2,128,1024]{2,1,0:T(8,128)(2,1)} %x.3, bf16[2,128,256]{2,1,0:T(8,128)(2,1)} %b.1, bf16[2,128,256]{2,1,0:T(8,128)(2,1)} %c.1, ...), custom_call_target="tpu_custom_call" | custom-call | tf_op jit(solution)/shard_map/pallas_call | solution.py:504
  3.5 3.1 %collective-permute-start = (bf16[928,256]{1,0:T(8,128)(2,1)}, bf16[928,256]{1,0:T(8,128)(2,1)S(1)}, u32[]{:S(2)}, u32[]{:S(2)}) collective-permute-start(bf16[928,256]{1,0:T(8,128)(2,1)} %get-tuple-element.27), channel_id=1, source_target_pairs={{0,4},{4,0},{8,12},{12,8},{1,5},{5,1},{9,13},{13,9},{2,6},{6,2},{1... | collective-permute-start | bytes 1425416 | tf_op jit(solution)/shard_map/ppermute | solution.py:487
  6.6 2.6 %collective-permute-start.1 = (bf16[160,256]{1,0:T(8,128)(2,1)}, bf16[160,256]{1,0:T(8,128)(2,1)}, u32[]{:S(2)}, u32[]{:S(2)}) collective-permute-start(bf16[160,256]{1,0:T(8,128)(2,1)} %get-tuple-element.28), channel_id=1, source_target_pairs={{0,8},{4,12},{8,0},{12,4},{1,9},{5,13},{9,1},{13,5},{2,10},{6,14},... | collective-permute-start | bytes 245768 | tf_op jit(solution)/shard_map/ppermute | solution.py:487
  9.2 1.9 %collective-permute-start.4 = (bf16[256,256]{1,0:T(8,128)(2,1)}, bf16[256,256]{1,0:T(8,128)(2,1)S(1)}, u32[]{:S(2)}, u32[]{:S(2)}) collective-permute-start(bf16[256,256]{1,0:T(8,128)(2,1)} %get-tuple-element.34), channel_id=1, source_target_pairs={{0,8},{4,12},{8,0},{12,4},{1,9},{5,13},{9,1},{13,5},{2,10},{6,14},... | collective-permute-start | bytes 393224 | tf_op jit(solution)/shard_map/ppermute | solution.py:487
  11.1 1.9 %collective-permute-start.5 = (bf16[256,256]{1,0:T(8,128)(2,1)}, bf16[256,256]{1,0:T(8,128)(2,1)S(1)}, u32[]{:S(2)}, u32[]{:S(2)}) collective-permute-start(bf16[256,256]{1,0:T(8,128)(2,1)} %get-tuple-element.35), channel_id=1, source_target_pairs={{0,12},{4,8},{8,4},{12,0},{1,13},{5,9},{9,5},{13,1},{2,14},{6,10},... | collective-permute-start | bytes 393224 | tf_op jit(solution)/shard_map/ppermute | solution.py:487
  13.0 0.7 %copy-done.7 = s32[2,8]{1,0:T(2,128)S(1)} copy-done((s32[2,8]{1,0:T(2,128)S(1)}, s32[2,8]{1,0:T(2,128)}, u32[]{:S(2)}) %copy-start.7) | copy-done | bytes 88
  13.8 0.6 %copy-done.10 = f32[16]{0:T(128)S(1)} copy-done((f32[16]{0:T(128)S(1)}, f32[16]{0:T(128)}, u32[]{:S(2)}) %copy-start.10) | copy-done | bytes 88
  14.5 0.7 %copy-done.6 = f32[2,16,128]{2,1,0:T(8,128)S(1)} copy-done((f32[2,16,128]{2,1,0:T(8,128)S(1)}, f32[2,16,128]{2,1,0:T(8,128)}, u32[]{:S(2)}) %copy-start.6) | copy-done | bytes 16408
  15.2 1.0 %copy-done.2 = bf16[2,128,1024]{2,1,0:T(8,128)(2,1)S(1)} copy-done((bf16[2,128,1024]{2,1,0:T(8,128)(2,1)S(1)}, bf16[2,128,1024]{2,1,0:T(8,128)(2,1)}, u32[]{:S(2)}) %copy-start.2) | copy-done | bytes 524312
  16.3 0.9 %copy-done.4 = bf16[2,128,256]{2,1,0:T(8,128)(2,1)S(1)} copy-done((bf16[2,128,256]{2,1,0:T(8,128)(2,1)S(1)}, bf16[2,128,256]{2,1,0:T(8,128)(2,1)}, u32[]{:S(2)}) %copy-start.4) | copy-done | bytes 131096
  17.2 2.9 %shard_map.140 = (f32[2,128,1024]{2,1,0:T(8,128)S(1)}, f32[2,128,1024]{2,1,0:T(8,128)S(1)}) custom-call(bf16[2,128,1024]{2,1,0:T(8,128)(2,1)S(1)} %copy-done, bf16[2,128,1024]{2,1,0:T(8,128)(2,1)S(1)} %copy-done.2, bf16[2,128,256]{2,1,0:T(8,128)(2,1)S(1)} %copy-done.3, bf16[2,128,256]{2,1,0:T(8,128)(2,1)S(1)} %copy-done.4, f32[2,16,128]{2,1,0:T(8,128)S(1)} %copy-done.6, ...), custom_call_target="tpu_custom_call" | custom-call | tf_op jit(solution)/shard_map/pallas_call | solution.py:523
  20.1 3.4 %collective-permute-done.near.rest_1_ = bf16[928,256]{1,0:T(8,128)(2,1)S(1)} collective-permute-done((bf16[928,256]{1,0:T(8,128)(2,1)}, bf16[928,256]{1,0:T(8,128)(2,1)S(1)}, u32[]{:S(2)}, u32[]{:S(2)}) %collective-permute-start) | collective-permute-done | bytes 475168 | tf_op jit(solution)/shard_map/ppermute | solution.py:487
  23.5 0.6 shard_map.142.rest_4_
  24.1 0.6 collective-permute-done.2.rest_3_
  24.6 1.6 %shard_map.143 = (bf16[192,256]{1,0:T(8,128)(2,1)S(1)}, f32[2,16,128]{2,1,0:T(8,128)S(1)}, f32[2,16,128]{2,1,0:T(8,128)S(1)}) custom-call(s32[19]{0:T(128)S(1)} %concatenate.3.tab, bf16[160,256]{1,0:T(8,128)(2,1)S(1)} %copy-done.5, bf16[928,256]{1,0:T(8,128)(2,1)S(1)} %collective-permute-done.near.rest_1_, bf16[160,256]{1,0:T(8,128)(2,1)} %collective-permute-done.1.rest_2_, ...), custom_call_target="tpu_custom_call" | custom-call | tf_op jit(solution)/shard_map/pallas_call | solution.py:544
  26.3 1.6 %collective-permute-start.3 = (bf16[192,256]{1,0:T(8,128)(2,1)S(1)}, bf16[192,256]{1,0:T(8,128)(2,1)S(1)}, u32[]{:S(2)}, u32[]{:S(2)}) collective-permute-start(bf16[192,256]{1,0:T(8,128)(2,1)S(1)} %get-tuple-element.30.mine), channel_id=1, source_target_pairs={{0,2},{2,0},{1,3},{3,1},{4,6},{6,4},{5,7},{7,5},{8,10},{10,8},{9,1... | collective-permute-start | bytes 294920 | tf_op jit(solution)/shard_map/ppermute | solution.py:491
  27.9 3.3 %collective-permute-start.6 = (bf16[256,256]{1,0:T(8,128)(2,1)S(1)}, bf16[256,256]{1,0:T(8,128)(2,1)S(1)}, u32[]{:S(2)}, u32[]{:S(2)}) collective-permute-start(bf16[256,256]{1,0:T(8,128)(2,1)S(1)} %shard_map.142.rest_4_), channel_id=1, source_target_pairs={{0,8},{4,12},{8,0},{12,4},{1,9},{5,13},{9,1},{13,5},{2,10},{6,14},... | collective-permute-start | bytes 393224 | tf_op jit(solution)/shard_map/ppermute | solution.py:487
  31.2 0.8 %shard_map.147.rest_4_ = bf16[64,1024]{1,0:T(8,128)(2,1)S(1)} custom-call(s32[19]{0:T(128)S(1)} %concatenate.3.tab, bf16[1024,256]{1,0:T(8,128)(2,1)S(1)} %bitcast.7, bf16[192,256]{1,0:T(8,128)(2,1)S(1)} %get-tuple-element.30.mine, bf16[192,256]{1,0:T(8,128)(2,1)S(1)} %collective-permute-done.3.other, f32[8,128]{1,0:T(8,128)S(1)} %shard_map.146.token), custom_call_target="tpu_custom_call" | custom-call | tf_op jit(solution)/shard_map/pallas_call | solution.py:561
  32.0 3.2 %collective-permute-start.11 = (bf16[64,1024]{1,0:T(8,128)(2,1)S(1)}, bf16[64,1024]{1,0:T(8,128)(2,1)S(1)}, u32[]{:S(2)}, u32[]{:S(2)}) collective-permute-start(bf16[64,1024]{1,0:T(8,128)(2,1)S(1)} %shard_map.147.rest_4_), channel_id=1, source_target_pairs={{0,8},{4,12},{8,0},{12,4},{1,9},{5,13},{9,1},{13,5},{2,10},{6,14},... | collective-permute-start | bytes 393224 | tf_op jit(solution)/shard_map/ppermute | solution.py:487
  35.2 1.6 %shard_map.144 = (f32[128,1024]{1,0:T(8,128)S(1)}, f32[64,1024]{1,0:T(8,128)S(1)}, f32[2,16,256]{2,1,0:T(8,128)S(1)}) custom-call(s32[19]{0:T(128)S(1)} %concatenate.3.tab, f32[2,16,128]{2,1,0:T(8,128)S(1)} %get-tuple-element.31.dts, f32[3,16]{1,0:T(4,128)S(1)} %pad_maximum_fusion.params), custom_call_target="tpu_custom_call" | custom-call | tf_op jit(solution)/shard_map/pallas_call | solution.py:555
  36.8 4.0 %collective-permute-start.10 = (bf16[64,1024]{1,0:T(8,128)(2,1)S(1)}, bf16[64,1024]{1,0:T(8,128)(2,1)S(1)}, u32[]{:S(2)}, u32[]{:S(2)}) collective-permute-start(bf16[64,1024]{1,0:T(8,128)(2,1)S(1)} %shard_map.147.rest_4_), channel_id=1, source_target_pairs={{0,4},{4,0},{8,12},{12,8},{1,5},{5,1},{9,13},{13,9},{2,6},{6,2},{1... | collective-permute-start | bytes 393224 | tf_op jit(solution)/shard_map/ppermute | solution.py:487
  40.8 2.4 %shard_map.145 = (bf16[1024,256]{1,0:T(8,128)(2,1)S(1)}, bf16[256,256]{1,0:T(8,128)(2,1)S(1)}, bf16[64,1024]{1,0:T(8,128)(2,1)S(1)}, bf16[64,1024]{1,0:T(8,128)(...) custom-call(s32[19]{0:T(128)S(1)} %concatenate.3.tab, bf16[1024,256]{1,0:T(8,128)(2,1)S(1)} %bitcast.8, ...), custom_call_target="tpu_custom_call" | custom-call | tf_op jit(solution)/shard_map/pallas_call | solution.py:565
  43.3 2.9 %collective-permute-start.8 = (bf16[64,1024]{1,0:T(8,128)(2,1)S(1)}, bf16[64,1024]{1,0:T(8,128)(2,1)S(1)}, u32[]{:S(2)}, u32[]{:S(2)}) collective-permute-start(bf16[64,1024]{1,0:T(8,128)(2,1)S(1)} %get-tuple-element.38), channel_id=1, source_target_pairs={{0,8},{4,12},{8,0},{12,4},{1,9},{5,13},{9,1},{13,5},{2,10},{6,14},... | collective-permute-start | bytes 393224 | tf_op jit(solution)/shard_map/ppermute | solution.py:487
  46.2 1.4 %collective-permute-start.9 = (bf16[64,1024]{1,0:T(8,128)(2,1)S(1)}, bf16[64,1024]{1,0:T(8,128)(2,1)S(1)}, u32[]{:S(2)}, u32[]{:S(2)}) collective-permute-start(bf16[64,1024]{1,0:T(8,128)(2,1)S(1)} %get-tuple-element.39), channel_id=1, source_target_pairs={{0,12},{4,8},{8,4},{12,0},{1,13},{5,9},{9,5},{13,1},{2,14},{6,10},... | collective-permute-start | bytes 393224 | tf_op jit(solution)/shard_map/ppermute | solution.py:487
  47.6 2.9 %collective-permute-done.7.rest_1_ = bf16[64,1024]{1,0:T(8,128)(2,1)S(1)} collective-permute-done((bf16[64,1024]{1,0:T(8,128)(2,1)S(1)}, bf16[64,1024]{1,0:T(8,128)(2,1)S(1)}, u32[]{:S(2)}, u32[]{:S(2)}) %collective-permute-start.7) | collective-permute-done | bytes 131104 | tf_op jit(solution)/shard_map/ppermute | solution.py:487
  50.5 2.5 %collective-permute-done.9.rest_3_ = bf16[64,1024]{1,0:T(8,128)(2,1)S(1)} collective-permute-done((bf16[64,1024]{1,0:T(8,128)(2,1)S(1)}, bf16[64,1024]{1,0:T(8,128)(2,1)S(1)}, u32[]{:S(2)}, u32[]{:S(2)}) %collective-permute-start.9) | collective-permute-done | bytes 131104 | tf_op jit(solution)/shard_map/ppermute | solution.py:487
  53.1 0.9 %collective-permute-done.12.rest_7_ = bf16[64,1024]{1,0:T(8,128)(2,1)S(1)} collective-permute-done((bf16[64,1024]{1,0:T(8,128)(2,1)S(1)}, bf16[64,1024]{1,0:T(8,128)(2,1)S(1)}, u32[]{:S(2)}, u32[]{:S(2)}) %collective-permute-start.12) | collective-permute-done | bytes 131104 | tf_op jit(solution)/shard_map/ppermute | solution.py:487
  54.0 1.5 %shard_map.148 = (f32[2,128,1024]{2,1,0:T(8,128)S(1)}, f32[2,128]{1,0:T(2,128)S(1)}) custom-call(s32[19]{0:T(128)S(1)} %concatenate.3.tab, f32[2,128,1024]{2,1,0:T(8,128)S(1)} %get-tuple-element.24.yz, f32[2,128,1024]{2,1,0:T(8,128)S(1)} %get-tuple-element.25.after.ez, bf16[64,1024]{1,0:T(8,128)(2,1)S(1)} %get-tuple-element.36.rest_0_, ...), custom_call_target="tpu_custom_call" | custom-call | tf_op jit(solution)/shard_map/pallas_call | solution.py:588
  55.5 1.6 %collective-permute-start.13 = (f32[2,128]{1,0:T(2,128)S(1)}, f32[2,128]{1,0:T(2,128)S(1)}, u32[]{:S(2)}, u32[]{:S(2)}) collective-permute-start(f32[2,128]{1,0:T(2,128)S(1)} %get-tuple-element.41.own), channel_id=1, source_target_pairs={{0,2},{2,0},{1,3},{3,1},{4,6},{6,4},{5,7},{7,5},{8,10},{10,8},{9,1... | collective-permute-start | bytes 3080 | tf_op jit(solution)/shard_map/ppermute | solution.py:491
  57.1 1.7 %shard_map.150 = bf16[1024,256]{1,0:T(8,128)(2,1)} custom-call(s32[19]{0:T(128)S(1)} %concatenate.3.tab, bf16[192,256]{1,0:T(8,128)(2,1)S(1)} %get-tuple-element.30.mine, bf16[192,256]{1,0:T(8,128)(2,1)S(1)} %collective-permute-done.3.other, f32[64,1024]{1,0:T(8,128)S(1)} %get-tuple-element.43.share, f32[2,16,256]{2,1,0:T(8,128)S(1)} %get-tuple-element.33.decays, ...), custom_call_target="tpu_custom_call" | custom-call | tf_op jit(solution)/shard_map/pallas_call | solution.py:582
  58.8 0.4 collective-permute-done.13.other
  59.1 1.6 %shard_map.149 = bf16[2,128,1024]{2,1,0:T(8,128)(2,1)} custom-call(s32[19]{0:T(128)S(1)} %concatenate.3.tab, f32[2,128,1024]{2,1,0:T(8,128)S(1)} %get-tuple-element.40.gated, f32[2,128]{1,0:T(2,128)S(1)} %get-tuple-element.41.own, f32[2,128]{1,0:T(2,128)S(1)} %collective-permute-done.13.other, bf16[1,1024]{1,0:T(2,128)(2,1)S(1)} %broadcast_in_dim.9.gain, ...), custom_call_target="tpu_custom_call" | custom-call | tf_op jit(solution)/shard_map/pallas_call | solution.py:600
  (38 shorter events, 0.4 us)
Async XLA Ops:
  0.6 13.9 %copy-start = (bf16[2,128,1024]{2,1,0:T(8,128)(2,1)S(1)}, bf16[2,128,1024]{2,1,0:T(8,128)(2,1)}, u32[]{:S(2)}) copy-start(bf16[2,128,1024]{2,1,0:T(8,128)(2,1)} %x.3) | copy-start | bytes 1572868
  1.3 13.2 %copy-start.3 = (bf16[2,128,256]{2,1,0:T(8,128)(2,1)S(1)}, bf16[2,128,256]{2,1,0:T(8,128)(2,1)}, u32[]{:S(2)}) copy-start(bf16[2,128,256]{2,1,0:T(8,128)(2,1)} %b.1) | copy-start | bytes 393220
  3.5 20.0 %collective-permute-start = (bf16[928,256]{1,0:T(8,128)(2,1)}, bf16[928,256]{1,0:T(8,128)(2,1)S(1)}, u32[]{:S(2)}, u32[]{:S(2)}) collective-permute-start(bf16[928,256]{1,0:T(8,128)(2,1)} %get-tuple-element.27), channel_id=1, source_target_pairs={{0,4},{4,0},{8,12},{12,8},{1,5},{5,1},{9,13},{13,9},{2,6},{6,2},{1... | collective-permute-start | bytes 1425416 | tf_op jit(solution)/shard_map/ppermute | solution.py:487
  6.6 17.5 %collective-permute-start.1 = (bf16[160,256]{1,0:T(8,128)(2,1)}, bf16[160,256]{1,0:T(8,128)(2,1)}, u32[]{:S(2)}, u32[]{:S(2)}) collective-permute-start(bf16[160,256]{1,0:T(8,128)(2,1)} %get-tuple-element.28), channel_id=1, source_target_pairs={{0,8},{4,12},{8,0},{12,4},{1,9},{5,13},{9,1},{13,5},{2,10},{6,14},... | collective-permute-start | bytes 245768 | tf_op jit(solution)/shard_map/ppermute | solution.py:487
  9.2 15.4 %collective-permute-start.2 = (bf16[160,256]{1,0:T(8,128)(2,1)}, bf16[160,256]{1,0:T(8,128)(2,1)}, u32[]{:S(2)}, u32[]{:S(2)}) collective-permute-start(bf16[160,256]{1,0:T(8,128)(2,1)} %get-tuple-element.29), channel_id=1, source_target_pairs={{0,12},{4,8},{8,4},{12,0},{1,13},{5,9},{9,5},{13,1},{2,14},{6,10},... | collective-permute-start | bytes 245768 | tf_op jit(solution)/shard_map/ppermute | solution.py:487
  9.2 3.8 %copy-start.9 = (s32[2,8]{1,0:T(2,128)S(1)}, s32[2,8]{1,0:T(2,128)}, u32[]{:S(2)}) copy-start(s32[2,8]{1,0:T(2,128)} %param.25) | copy-start | bytes 196
  9.2 22.0 %collective-permute-start.4 = (bf16[256,256]{1,0:T(8,128)(2,1)}, bf16[256,256]{1,0:T(8,128)(2,1)S(1)}, u32[]{:S(2)}, u32[]{:S(2)}) collective-permute-start(bf16[256,256]{1,0:T(8,128)(2,1)} %get-tuple-element.34), channel_id=1, source_target_pairs={{0,8},{4,12},{8,0},{12,4},{1,9},{5,13},{9,1},{13,5},{2,10},{6,14},... | collective-permute-start | bytes 393224 | tf_op jit(solution)/shard_map/ppermute | solution.py:487
  11.1 20.1 %collective-permute-start.5 = (bf16[256,256]{1,0:T(8,128)(2,1)}, bf16[256,256]{1,0:T(8,128)(2,1)S(1)}, u32[]{:S(2)}, u32[]{:S(2)}) collective-permute-start(bf16[256,256]{1,0:T(8,128)(2,1)} %get-tuple-element.35), channel_id=1, source_target_pairs={{0,12},{4,8},{8,4},{12,0},{1,13},{5,9},{9,5},{13,1},{2,14},{6,10},... | collective-permute-start | bytes 393224 | tf_op jit(solution)/shard_map/ppermute | solution.py:487
  13.0 0.7 %copy-start.7 = (s32[2,8]{1,0:T(2,128)S(1)}, s32[2,8]{1,0:T(2,128)}, u32[]{:S(2)}) copy-start(s32[2,8]{1,0:T(2,128)} %owner.1) | copy-start | bytes 196
  13.8 0.7 %copy-start.10 = (f32[16]{0:T(128)S(1)}, f32[16]{0:T(128)}, u32[]{:S(2)}) copy-start(f32[16]{0:T(128)} %param.20) | copy-start | bytes 196
  13.8 0.7 %copy-start.11 = (f32[16]{0:T(128)S(1)}, f32[16]{0:T(128)}, u32[]{:S(2)}) copy-start(f32[16]{0:T(128)} %param.19) | copy-start | bytes 196
  13.8 0.7 %copy-start.12 = (f32[16]{0:T(128)S(1)}, f32[16]{0:T(128)}, u32[]{:S(2)}) copy-start(f32[16]{0:T(128)} %param.18) | copy-start | bytes 196
  14.5 0.7 %copy-start.6 = (f32[2,16,128]{2,1,0:T(8,128)S(1)}, f32[2,16,128]{2,1,0:T(8,128)}, u32[]{:S(2)}) copy-start(f32[2,16,128]{2,1,0:T(8,128)} %dt.1) | copy-start | bytes 49156
  15.2 1.0 %copy-start.2 = (bf16[2,128,1024]{2,1,0:T(8,128)(2,1)S(1)}, bf16[2,128,1024]{2,1,0:T(8,128)(2,1)}, u32[]{:S(2)}) copy-start(bf16[2,128,1024]{2,1,0:T(8,128)(2,1)} %z_in.1) | copy-start | bytes 1572868
  16.3 0.9 %copy-start.4 = (bf16[2,128,256]{2,1,0:T(8,128)(2,1)S(1)}, bf16[2,128,256]{2,1,0:T(8,128)(2,1)}, u32[]{:S(2)}) copy-start(bf16[2,128,256]{2,1,0:T(8,128)(2,1)} %c.1) | copy-start | bytes 393220
  23.5 1.2 %copy-start.5 = (bf16[160,256]{1,0:T(8,128)(2,1)S(1)}, bf16[160,256]{1,0:T(8,128)(2,1)}, u32[]{:S(2)}) copy-start(bf16[160,256]{1,0:T(8,128)(2,1)} %get-tuple-element.26.rest_0_) | copy-start | bytes 245764
  24.6 6.5 %copy-start.1 = (bf16[1,16,64,256]{3,2,1,0:T(8,128)(2,1)S(1)}, bf16[1,16,64,256]{3,2,1,0:T(8,128)(2,1)}, u32[]{:S(2)}) copy-start(bf16[1,16,64,256]{3,2,1,0:T(8,128)(2,1)} %param.22) | copy-start | bytes 1572868
  26.3 4.9 %collective-permute-start.3 = (bf16[192,256]{1,0:T(8,128)(2,1)S(1)}, bf16[192,256]{1,0:T(8,128)(2,1)S(1)}, u32[]{:S(2)}, u32[]{:S(2)}) collective-permute-start(bf16[192,256]{1,0:T(8,128)(2,1)S(1)} %get-tuple-element.30.mine), channel_id=1, source_target_pairs={{0,2},{2,0},{1,3},{3,1},{4,6},{6,4},{5,7},{7,5},{8,10},{10,8},{9,1... | collective-permute-start | bytes 294920 | tf_op jit(solution)/shard_map/ppermute | solution.py:491
  27.9 12.9 %collective-permute-start.6 = (bf16[256,256]{1,0:T(8,128)(2,1)S(1)}, bf16[256,256]{1,0:T(8,128)(2,1)S(1)}, u32[]{:S(2)}, u32[]{:S(2)}) collective-permute-start(bf16[256,256]{1,0:T(8,128)(2,1)S(1)} %shard_map.142.rest_4_), channel_id=1, source_target_pairs={{0,8},{4,12},{8,0},{12,4},{1,9},{5,13},{9,1},{13,5},{2,10},{6,14},... | collective-permute-start | bytes 393224 | tf_op jit(solution)/shard_map/ppermute | solution.py:487
  32.0 15.6 %collective-permute-start.11 = (bf16[64,1024]{1,0:T(8,128)(2,1)S(1)}, bf16[64,1024]{1,0:T(8,128)(2,1)S(1)}, u32[]{:S(2)}, u32[]{:S(2)}) collective-permute-start(bf16[64,1024]{1,0:T(8,128)(2,1)S(1)} %shard_map.147.rest_4_), channel_id=1, source_target_pairs={{0,8},{4,12},{8,0},{12,4},{1,9},{5,13},{9,1},{13,5},{2,10},{6,14},... | collective-permute-start | bytes 393224 | tf_op jit(solution)/shard_map/ppermute | solution.py:487
  36.8 10.9 %collective-permute-start.10 = (bf16[64,1024]{1,0:T(8,128)(2,1)S(1)}, bf16[64,1024]{1,0:T(8,128)(2,1)S(1)}, u32[]{:S(2)}, u32[]{:S(2)}) collective-permute-start(bf16[64,1024]{1,0:T(8,128)(2,1)S(1)} %shard_map.147.rest_4_), channel_id=1, source_target_pairs={{0,4},{4,0},{8,12},{12,8},{1,5},{5,1},{9,13},{13,9},{2,6},{6,2},{1... | collective-permute-start | bytes 393224 | tf_op jit(solution)/shard_map/ppermute | solution.py:487
  43.2 7.4 %collective-permute-start.7 = (bf16[64,1024]{1,0:T(8,128)(2,1)S(1)}, bf16[64,1024]{1,0:T(8,128)(2,1)S(1)}, u32[]{:S(2)}, u32[]{:S(2)}) collective-permute-start(bf16[64,1024]{1,0:T(8,128)(2,1)S(1)} %get-tuple-element.37), channel_id=1, source_target_pairs={{0,4},{4,0},{8,12},{12,8},{1,5},{5,1},{9,13},{13,9},{2,6},{6,2},{1... | collective-permute-start | bytes 393224 | tf_op jit(solution)/shard_map/ppermute | solution.py:487
  43.3 7.3 %collective-permute-start.8 = (bf16[64,1024]{1,0:T(8,128)(2,1)S(1)}, bf16[64,1024]{1,0:T(8,128)(2,1)S(1)}, u32[]{:S(2)}, u32[]{:S(2)}) collective-permute-start(bf16[64,1024]{1,0:T(8,128)(2,1)S(1)} %get-tuple-element.38), channel_id=1, source_target_pairs={{0,8},{4,12},{8,0},{12,4},{1,9},{5,13},{9,1},{13,5},{2,10},{6,14},... | collective-permute-start | bytes 393224 | tf_op jit(solution)/shard_map/ppermute | solution.py:487
  46.2 6.9 %collective-permute-start.9 = (bf16[64,1024]{1,0:T(8,128)(2,1)S(1)}, bf16[64,1024]{1,0:T(8,128)(2,1)S(1)}, u32[]{:S(2)}, u32[]{:S(2)}) collective-permute-start(bf16[64,1024]{1,0:T(8,128)(2,1)S(1)} %get-tuple-element.39), channel_id=1, source_target_pairs={{0,12},{4,8},{8,4},{12,0},{1,13},{5,9},{9,5},{13,1},{2,14},{6,10},... | collective-permute-start | bytes 393224 | tf_op jit(solution)/shard_map/ppermute | solution.py:487
  47.6 6.4 %collective-permute-start.12 = (bf16[64,1024]{1,0:T(8,128)(2,1)S(1)}, bf16[64,1024]{1,0:T(8,128)(2,1)S(1)}, u32[]{:S(2)}, u32[]{:S(2)}) collective-permute-start(bf16[64,1024]{1,0:T(8,128)(2,1)S(1)} %collective-permute-done.11.rest_6_), channel_id=1, source_target_pairs={{0,4},{4,0},{8,12},{12,8},{1,5},{5,1},{9,13},{13,9},{2,6},{6,2},{1... | collective-permute-start | bytes 393224 | tf_op jit(solution)/shard_map/ppermute | solution.py:487
  54.0 3.1 %copy-start.8 = (bf16[1024]{0:T(1024)(128)(2,1)S(1)}, bf16[1024]{0:T(1024)(128)(2,1)}, u32[]{:S(2)}) copy-start(bf16[1024]{0:T(1024)(128)(2,1)} %param.21) | copy-start | bytes 6148
  55.5 3.6 %collective-permute-start.13 = (f32[2,128]{1,0:T(2,128)S(1)}, f32[2,128]{1,0:T(2,128)S(1)}, u32[]{:S(2)}, u32[]{:S(2)}) collective-permute-start(f32[2,128]{1,0:T(2,128)S(1)} %get-tuple-element.41.own), channel_id=1, source_target_pairs={{0,2},{2,0},{1,3},{3,1},{4,6},{6,4},{5,7},{7,5},{8,10},{10,8},{9,1... | collective-permute-start | bytes 3080 | tf_op jit(solution)/shard_map/ppermute | solution.py:491

commit v7 on v6

--- a/solution.py
+++ b/solution.py
@@ -388,28 +388,23 @@
 
 def gate_part(peers, tab, yz, ez, *rest):
     cars, uppers = rest[:peers], rest[peers : 2 * peers]
-    gated, squares, got, sem = rest[2 * peers :]
+    gated, squares = rest[2 * peers :]
     slots, rows, width = yz.shape
     t = Table(tab, peers, slots)
-    waits = []
+
+    def choose(at, refs, lanes):
+        out = refs[0][:, lanes].astype(F32)
+        for k in range(1, peers):
+            out = jnp.where(at == k, refs[k][:, lanes].astype(F32), out)
+        return out
+
     for j in range(slots):
-        early = t.late(t.me * slots + j) == 0
-        low, high = got.at[j, pl.ds(0, HALF)], got.at[j, pl.ds(HALF, HALF)]
         at = t.far(j)
-        first = gather(sem.at[j, 0], low, [(at == k, [(cars[k], low)]) for k in range(peers)])
-        second = gather(
-            sem.at[j, 1],
-            high,
-            [((at == k) & early, [(uppers[k], high)]) for k in range(peers)],
-        )
-        waits.append((early, first, second))
-    for j, (early, first, second) in enumerate(waits):
-        first()
-        pl.when(early)(second)
         total = jnp.zeros((rows, 128), F32)
         for p in range(width // 128):
             lanes = slice(p * 128, (p + 1) * 128)
-            value = yz[j, :, lanes] + ez[j, :, lanes] * got[j, :, lanes].astype(F32)
+            got = jnp.concatenate([choose(at, cars, lanes), choose(at, uppers, lanes)], axis=0)
+            value = yz[j, :, lanes] + ez[j, :, lanes] * got
             gated[j, :, lanes] = value
             total = total + value * value
         squares[j : j + 1] = jnp.sum(jnp.transpose(total), axis=0, keepdims=True)
@@ -588,8 +583,7 @@
     gated, squares = call(
         bind(gate_part),
         [shape(x_rows.shape, F32), shape((slots, rows), F32)],
-        [SMEM, VMEM, VMEM] + [ANY] * (2 * peers),
-        scratch=[scratch(slots, rows, width), dma(slots, 2)],
+        [SMEM] + [VMEM] * (2 + 2 * peers),
     )(
         tab,
         yz,

time: 61.3 us -> 60.5 us (0.987)
  no operation moved by 1% of the time
where the time goes in v7:
time: 60.5 us; the launch traced here: 60 us
  starting transfers between devices  27.5 us (45%)
  Pallas kernels  16.1 us (27%)
  waiting for transfers between devices  10.7 us (18%)
  local copies, waits for them, and re-layouts  4.07 us (7%)
  between operations  1.51 us (2%)
    ppermute x12, starting transfers between devices, far(): return lax.ppermute(value, 'sess', [(i, i ^ k) for i in range(peers)])  24.4 us
    ppermute x12, waiting for transfers between devices, far(): return lax.ppermute(value, 'sess', [(i, i ^ k) for i in range(peers)])  10.3 us
    unnamed x26, local copies, waits for them, and re-layouts  3.99 us
    ppermute x2, starting transfers between devices, swapped(): return lax.ppermute(value, 'head', [(i, i ^ 1) for i in range(count)])  3.15 us
    pallas_call x1, Pallas kernels, per_device(): call(block_part, [shape(x_rows.shape, F32)] * 2, [HBM] * 5 + [VMEM], scra...  2.87 us
    pallas_call x1, Pallas kernels, per_device(): call(bind(late_part, slots), [shape((width, state), BF16), packed(piece)]...  2.26 us
    pallas_call x1, Pallas kernels, per_device(): call(bind(send_part), [packed(tail), packed((1 + half) * piece + tail)] +...  2.16 us
    pallas_call x1, Pallas kernels, per_device(): call(bind(final_part, slots), shape((width, state), BF16), [SMEM] + [VMEM...  1.68 us
  transfers between devices with their start and end apart: 14, of which 6 were waited for; matrix products, arithmetic and copies ran while one was open for 0% of the time, Pallas kernels for 19%

profile of v7, /device:TPU:0, one launch (start us, length us, event | category | flops | bytes accessed | tf_op | source)
XLA Modules:
  0.0 60.0 jit_solution(15662075578876348164)
XLA Ops:
  1.4 2.2 %shard_map.141 = (bf16[160,256]{1,0:T(8,128)(2,1)}, bf16[928,256]{1,0:T(8,128)(2,1)}, bf16[160,256]{1,0:T(8,128)(2,1)}, bf16[160,256]{1,0:T(8,128)(2,1)}, bf16[2...) custom-call(bf16[2,128,1024]{2,1,0:T(8,128)(2,1)} %x.3, bf16[2,128,256]{2,1,0:T(8,128)(2,1)} %b.1, bf16[2,128,256]{2,1,0:T(8,128)(2,1)} %c.1, ...), custom_call_target="tpu_custom_call" | custom-call | tf_op jit(solution)/shard_map/pallas_call | solution.py:499
  3.5 3.1 %collective-permute-start = (bf16[928,256]{1,0:T(8,128)(2,1)}, bf16[928,256]{1,0:T(8,128)(2,1)S(1)}, u32[]{:S(2)}, u32[]{:S(2)}) collective-permute-start(bf16[928,256]{1,0:T(8,128)(2,1)} %get-tuple-element.27), channel_id=1, source_target_pairs={{0,4},{4,0},{8,12},{12,8},{1,5},{5,1},{9,13},{13,9},{2,6},{6,2},{1... | collective-permute-start | bytes 1425416 | tf_op jit(solution)/shard_map/ppermute | solution.py:482
  6.6 2.6 %collective-permute-start.1 = (bf16[160,256]{1,0:T(8,128)(2,1)}, bf16[160,256]{1,0:T(8,128)(2,1)}, u32[]{:S(2)}, u32[]{:S(2)}) collective-permute-start(bf16[160,256]{1,0:T(8,128)(2,1)} %get-tuple-element.28), channel_id=1, source_target_pairs={{0,8},{4,12},{8,0},{12,4},{1,9},{5,13},{9,1},{13,5},{2,10},{6,14},... | collective-permute-start | bytes 245768 | tf_op jit(solution)/shard_map/ppermute | solution.py:482
  9.2 1.9 %collective-permute-start.4 = (bf16[256,256]{1,0:T(8,128)(2,1)}, bf16[256,256]{1,0:T(8,128)(2,1)S(1)}, u32[]{:S(2)}, u32[]{:S(2)}) collective-permute-start(bf16[256,256]{1,0:T(8,128)(2,1)} %get-tuple-element.34), channel_id=1, source_target_pairs={{0,8},{4,12},{8,0},{12,4},{1,9},{5,13},{9,1},{13,5},{2,10},{6,14},... | collective-permute-start | bytes 393224 | tf_op jit(solution)/shard_map/ppermute | solution.py:482
  11.1 1.9 %collective-permute-start.5 = (bf16[256,256]{1,0:T(8,128)(2,1)}, bf16[256,256]{1,0:T(8,128)(2,1)S(1)}, u32[]{:S(2)}, u32[]{:S(2)}) collective-permute-start(bf16[256,256]{1,0:T(8,128)(2,1)} %get-tuple-element.35), channel_id=1, source_target_pairs={{0,12},{4,8},{8,4},{12,0},{1,13},{5,9},{9,5},{13,1},{2,14},{6,10},... | collective-permute-start | bytes 393224 | tf_op jit(solution)/shard_map/ppermute | solution.py:482
  13.0 0.7 %copy-done.7 = s32[2,8]{1,0:T(2,128)S(1)} copy-done((s32[2,8]{1,0:T(2,128)S(1)}, s32[2,8]{1,0:T(2,128)}, u32[]{:S(2)}) %copy-start.7) | copy-done | bytes 88
  13.8 0.6 %copy-done.10 = f32[16]{0:T(128)S(1)} copy-done((f32[16]{0:T(128)S(1)}, f32[16]{0:T(128)}, u32[]{:S(2)}) %copy-start.10) | copy-done | bytes 88
  14.5 0.7 %copy-done.6 = f32[2,16,128]{2,1,0:T(8,128)S(1)} copy-done((f32[2,16,128]{2,1,0:T(8,128)S(1)}, f32[2,16,128]{2,1,0:T(8,128)}, u32[]{:S(2)}) %copy-start.6) | copy-done | bytes 16408
  15.2 1.0 %copy-done.2 = bf16[2,128,1024]{2,1,0:T(8,128)(2,1)S(1)} copy-done((bf16[2,128,1024]{2,1,0:T(8,128)(2,1)S(1)}, bf16[2,128,1024]{2,1,0:T(8,128)(2,1)}, u32[]{:S(2)}) %copy-start.2) | copy-done | bytes 524312
  16.3 0.9 %copy-done.4 = bf16[2,128,256]{2,1,0:T(8,128)(2,1)S(1)} copy-done((bf16[2,128,256]{2,1,0:T(8,128)(2,1)S(1)}, bf16[2,128,256]{2,1,0:T(8,128)(2,1)}, u32[]{:S(2)}) %copy-start.4) | copy-done | bytes 131096
  17.2 2.9 %shard_map.140 = (f32[2,128,1024]{2,1,0:T(8,128)S(1)}, f32[2,128,1024]{2,1,0:T(8,128)S(1)}) custom-call(bf16[2,128,1024]{2,1,0:T(8,128)(2,1)S(1)} %copy-done, bf16[2,128,1024]{2,1,0:T(8,128)(2,1)S(1)} %copy-done.2, bf16[2,128,256]{2,1,0:T(8,128)(2,1)S(1)} %copy-done.3, bf16[2,128,256]{2,1,0:T(8,128)(2,1)S(1)} %copy-done.4, f32[2,16,128]{2,1,0:T(8,128)S(1)} %copy-done.6, ...), custom_call_target="tpu_custom_call" | custom-call | tf_op jit(solution)/shard_map/pallas_call | solution.py:518
  20.1 3.4 %collective-permute-done.near.rest_1_ = bf16[928,256]{1,0:T(8,128)(2,1)S(1)} collective-permute-done((bf16[928,256]{1,0:T(8,128)(2,1)}, bf16[928,256]{1,0:T(8,128)(2,1)S(1)}, u32[]{:S(2)}, u32[]{:S(2)}) %collective-permute-start) | collective-permute-done | bytes 475168 | tf_op jit(solution)/shard_map/ppermute | solution.py:482
  23.5 0.6 shard_map.142.rest_4_
  24.1 0.6 collective-permute-done.2.rest_3_
  24.6 1.7 %shard_map.143 = (bf16[192,256]{1,0:T(8,128)(2,1)S(1)}, f32[2,16,128]{2,1,0:T(8,128)S(1)}, f32[2,16,128]{2,1,0:T(8,128)S(1)}) custom-call(s32[19]{0:T(128)S(1)} %concatenate.3.tab, bf16[160,256]{1,0:T(8,128)(2,1)S(1)} %copy-done.5, bf16[928,256]{1,0:T(8,128)(2,1)S(1)} %collective-permute-done.near.rest_1_, bf16[160,256]{1,0:T(8,128)(2,1)} %collective-permute-done.1.rest_2_, ...), custom_call_target="tpu_custom_call" | custom-call | tf_op jit(solution)/shard_map/pallas_call | solution.py:539
  26.3 1.6 %collective-permute-start.3 = (bf16[192,256]{1,0:T(8,128)(2,1)S(1)}, bf16[192,256]{1,0:T(8,128)(2,1)S(1)}, u32[]{:S(2)}, u32[]{:S(2)}) collective-permute-start(bf16[192,256]{1,0:T(8,128)(2,1)S(1)} %get-tuple-element.30.mine), channel_id=1, source_target_pairs={{0,2},{2,0},{1,3},{3,1},{4,6},{6,4},{5,7},{7,5},{8,10},{10,8},{9,1... | collective-permute-start | bytes 294920 | tf_op jit(solution)/shard_map/ppermute | solution.py:486
  27.9 3.3 %collective-permute-start.6 = (bf16[256,256]{1,0:T(8,128)(2,1)S(1)}, bf16[256,256]{1,0:T(8,128)(2,1)S(1)}, u32[]{:S(2)}, u32[]{:S(2)}) collective-permute-start(bf16[256,256]{1,0:T(8,128)(2,1)S(1)} %shard_map.142.rest_4_), channel_id=1, source_target_pairs={{0,8},{4,12},{8,0},{12,4},{1,9},{5,13},{9,1},{13,5},{2,10},{6,14},... | collective-permute-start | bytes 393224 | tf_op jit(solution)/shard_map/ppermute | solution.py:482
  31.3 0.8 %shard_map.147.rest_4_ = bf16[64,1024]{1,0:T(8,128)(2,1)S(1)} custom-call(s32[19]{0:T(128)S(1)} %concatenate.3.tab, bf16[1024,256]{1,0:T(8,128)(2,1)S(1)} %bitcast.7, bf16[192,256]{1,0:T(8,128)(2,1)S(1)} %get-tuple-element.30.mine, bf16[192,256]{1,0:T(8,128)(2,1)S(1)} %collective-permute-done.3.other, f32[8,128]{1,0:T(8,128)S(1)} %shard_map.146.token), custom_call_target="tpu_custom_call" | custom-call | tf_op jit(solution)/shard_map/pallas_call | solution.py:556
  32.1 3.2 %collective-permute-start.11 = (bf16[64,1024]{1,0:T(8,128)(2,1)S(1)}, bf16[64,1024]{1,0:T(8,128)(2,1)S(1)}, u32[]{:S(2)}, u32[]{:S(2)}) collective-permute-start(bf16[64,1024]{1,0:T(8,128)(2,1)S(1)} %shard_map.147.rest_4_), channel_id=1, source_target_pairs={{0,8},{4,12},{8,0},{12,4},{1,9},{5,13},{9,1},{13,5},{2,10},{6,14},... | collective-permute-start | bytes 393224 | tf_op jit(solution)/shard_map/ppermute | solution.py:482
  35.2 1.6 %shard_map.144 = (f32[128,1024]{1,0:T(8,128)S(1)}, f32[64,1024]{1,0:T(8,128)S(1)}, f32[2,16,256]{2,1,0:T(8,128)S(1)}) custom-call(s32[19]{0:T(128)S(1)} %concatenate.3.tab, f32[2,16,128]{2,1,0:T(8,128)S(1)} %get-tuple-element.31.dts, f32[3,16]{1,0:T(4,128)S(1)} %pad_maximum_fusion.params), custom_call_target="tpu_custom_call" | custom-call | tf_op jit(solution)/shard_map/pallas_call | solution.py:550
  36.8 4.0 %collective-permute-start.10 = (bf16[64,1024]{1,0:T(8,128)(2,1)S(1)}, bf16[64,1024]{1,0:T(8,128)(2,1)S(1)}, u32[]{:S(2)}, u32[]{:S(2)}) collective-permute-start(bf16[64,1024]{1,0:T(8,128)(2,1)S(1)} %shard_map.147.rest_4_), channel_id=1, source_target_pairs={{0,4},{4,0},{8,12},{12,8},{1,5},{5,1},{9,13},{13,9},{2,6},{6,2},{1... | collective-permute-start | bytes 393224 | tf_op jit(solution)/shard_map/ppermute | solution.py:482
  40.8 2.3 %shard_map.145 = (bf16[1024,256]{1,0:T(8,128)(2,1)S(1)}, bf16[256,256]{1,0:T(8,128)(2,1)S(1)}, bf16[64,1024]{1,0:T(8,128)(2,1)S(1)}, bf16[64,1024]{1,0:T(8,128)(...) custom-call(s32[19]{0:T(128)S(1)} %concatenate.3.tab, bf16[1024,256]{1,0:T(8,128)(2,1)S(1)} %bitcast.8, ...), custom_call_target="tpu_custom_call" | custom-call | tf_op jit(solution)/shard_map/pallas_call | solution.py:560
  43.3 2.8 %collective-permute-start.8 = (bf16[64,1024]{1,0:T(8,128)(2,1)S(1)}, bf16[64,1024]{1,0:T(8,128)(2,1)S(1)}, u32[]{:S(2)}, u32[]{:S(2)}) collective-permute-start(bf16[64,1024]{1,0:T(8,128)(2,1)S(1)} %get-tuple-element.38), channel_id=1, source_target_pairs={{0,8},{4,12},{8,0},{12,4},{1,9},{5,13},{9,1},{13,5},{2,10},{6,14},... | collective-permute-start | bytes 393224 | tf_op jit(solution)/shard_map/ppermute | solution.py:482
  46.0 1.5 %collective-permute-start.9 = (bf16[64,1024]{1,0:T(8,128)(2,1)S(1)}, bf16[64,1024]{1,0:T(8,128)(2,1)S(1)}, u32[]{:S(2)}, u32[]{:S(2)}) collective-permute-start(bf16[64,1024]{1,0:T(8,128)(2,1)S(1)} %get-tuple-element.39), channel_id=1, source_target_pairs={{0,12},{4,8},{8,4},{12,0},{1,13},{5,9},{9,5},{13,1},{2,14},{6,10},... | collective-permute-start | bytes 393224 | tf_op jit(solution)/shard_map/ppermute | solution.py:482
  47.5 2.8 %collective-permute-done.7.rest_1_ = bf16[64,1024]{1,0:T(8,128)(2,1)S(1)} collective-permute-done((bf16[64,1024]{1,0:T(8,128)(2,1)S(1)}, bf16[64,1024]{1,0:T(8,128)(2,1)S(1)}, u32[]{:S(2)}, u32[]{:S(2)}) %collective-permute-start.7) | collective-permute-done | bytes 131104 | tf_op jit(solution)/shard_map/ppermute | solution.py:482
  50.3 2.7 %collective-permute-done.9.rest_3_ = bf16[64,1024]{1,0:T(8,128)(2,1)S(1)} collective-permute-done((bf16[64,1024]{1,0:T(8,128)(2,1)S(1)}, bf16[64,1024]{1,0:T(8,128)(2,1)S(1)}, u32[]{:S(2)}, u32[]{:S(2)}) %collective-permute-start.9) | collective-permute-done | bytes 131104 | tf_op jit(solution)/shard_map/ppermute | solution.py:482
  53.0 0.8 %collective-permute-done.12.rest_7_ = bf16[64,1024]{1,0:T(8,128)(2,1)S(1)} collective-permute-done((bf16[64,1024]{1,0:T(8,128)(2,1)S(1)}, bf16[64,1024]{1,0:T(8,128)(2,1)S(1)}, u32[]{:S(2)}, u32[]{:S(2)}) %collective-permute-start.12) | collective-permute-done | bytes 131104 | tf_op jit(solution)/shard_map/ppermute | solution.py:482
  53.9 0.9 %shard_map.148 = (f32[2,128,1024]{2,1,0:T(8,128)S(1)}, f32[2,128]{1,0:T(2,128)S(1)}) custom-call(s32[19]{0:T(128)S(1)} %concatenate.3.tab, f32[2,128,1024]{2,1,0:T(8,128)S(1)} %get-tuple-element.24.yz, f32[2,128,1024]{2,1,0:T(8,128)S(1)} %get-tuple-element.25.after.ez, bf16[64,1024]{1,0:T(8,128)(2,1)S(1)} %get-tuple-element.36.rest_0_, ...), custom_call_target="tpu_custom_call" | custom-call | tf_op jit(solution)/shard_map/pallas_call | solution.py:583
  54.8 1.6 %collective-permute-start.13 = (f32[2,128]{1,0:T(2,128)S(1)}, f32[2,128]{1,0:T(2,128)S(1)}, u32[]{:S(2)}, u32[]{:S(2)}) collective-permute-start(f32[2,128]{1,0:T(2,128)S(1)} %get-tuple-element.41.own), channel_id=1, source_target_pairs={{0,2},{2,0},{1,3},{3,1},{4,6},{6,4},{5,7},{7,5},{8,10},{10,8},{9,1... | collective-permute-start | bytes 3080 | tf_op jit(solution)/shard_map/ppermute | solution.py:486
  56.4 1.7 %shard_map.150 = bf16[1024,256]{1,0:T(8,128)(2,1)} custom-call(s32[19]{0:T(128)S(1)} %concatenate.3.tab, bf16[192,256]{1,0:T(8,128)(2,1)S(1)} %get-tuple-element.30.mine, bf16[192,256]{1,0:T(8,128)(2,1)S(1)} %collective-permute-done.3.other, f32[64,1024]{1,0:T(8,128)S(1)} %get-tuple-element.43.share, f32[2,16,256]{2,1,0:T(8,128)S(1)} %get-tuple-element.33.decays, ...), custom_call_target="tpu_custom_call" | custom-call | tf_op jit(solution)/shard_map/pallas_call | solution.py:577
  58.1 0.4 collective-permute-done.13.other
  58.5 1.6 %shard_map.149 = bf16[2,128,1024]{2,1,0:T(8,128)(2,1)} custom-call(s32[19]{0:T(128)S(1)} %concatenate.3.tab, f32[2,128,1024]{2,1,0:T(8,128)S(1)} %get-tuple-element.40.gated, f32[2,128]{1,0:T(2,128)S(1)} %get-tuple-element.41.own, f32[2,128]{1,0:T(2,128)S(1)} %collective-permute-done.13.other, bf16[1,1024]{1,0:T(2,128)(2,1)S(1)} %broadcast_in_dim.9.gain, ...), custom_call_target="tpu_custom_call" | custom-call | tf_op jit(solution)/shard_map/pallas_call | solution.py:594
  (38 shorter events, 0.5 us)
Async XLA Ops:
  0.6 13.9 %copy-start = (bf16[2,128,1024]{2,1,0:T(8,128)(2,1)S(1)}, bf16[2,128,1024]{2,1,0:T(8,128)(2,1)}, u32[]{:S(2)}) copy-start(bf16[2,128,1024]{2,1,0:T(8,128)(2,1)} %x.3) | copy-start | bytes 1572868
  1.3 13.2 %copy-start.3 = (bf16[2,128,256]{2,1,0:T(8,128)(2,1)S(1)}, bf16[2,128,256]{2,1,0:T(8,128)(2,1)}, u32[]{:S(2)}) copy-start(bf16[2,128,256]{2,1,0:T(8,128)(2,1)} %b.1) | copy-start | bytes 393220
  3.5 20.0 %collective-permute-start = (bf16[928,256]{1,0:T(8,128)(2,1)}, bf16[928,256]{1,0:T(8,128)(2,1)S(1)}, u32[]{:S(2)}, u32[]{:S(2)}) collective-permute-start(bf16[928,256]{1,0:T(8,128)(2,1)} %get-tuple-element.27), channel_id=1, source_target_pairs={{0,4},{4,0},{8,12},{12,8},{1,5},{5,1},{9,13},{13,9},{2,6},{6,2},{1... | collective-permute-start | bytes 1425416 | tf_op jit(solution)/shard_map/ppermute | solution.py:482
  6.6 17.5 %collective-permute-start.1 = (bf16[160,256]{1,0:T(8,128)(2,1)}, bf16[160,256]{1,0:T(8,128)(2,1)}, u32[]{:S(2)}, u32[]{:S(2)}) collective-permute-start(bf16[160,256]{1,0:T(8,128)(2,1)} %get-tuple-element.28), channel_id=1, source_target_pairs={{0,8},{4,12},{8,0},{12,4},{1,9},{5,13},{9,1},{13,5},{2,10},{6,14},... | collective-permute-start | bytes 245768 | tf_op jit(solution)/shard_map/ppermute | solution.py:482
  9.2 15.4 %collective-permute-start.2 = (bf16[160,256]{1,0:T(8,128)(2,1)}, bf16[160,256]{1,0:T(8,128)(2,1)}, u32[]{:S(2)}, u32[]{:S(2)}) collective-permute-start(bf16[160,256]{1,0:T(8,128)(2,1)} %get-tuple-element.29), channel_id=1, source_target_pairs={{0,12},{4,8},{8,4},{12,0},{1,13},{5,9},{9,5},{13,1},{2,14},{6,10},... | collective-permute-start | bytes 245768 | tf_op jit(solution)/shard_map/ppermute | solution.py:482
  9.2 3.8 %copy-start.9 = (s32[2,8]{1,0:T(2,128)S(1)}, s32[2,8]{1,0:T(2,128)}, u32[]{:S(2)}) copy-start(s32[2,8]{1,0:T(2,128)} %param.25) | copy-start | bytes 196
  9.2 22.0 %collective-permute-start.4 = (bf16[256,256]{1,0:T(8,128)(2,1)}, bf16[256,256]{1,0:T(8,128)(2,1)S(1)}, u32[]{:S(2)}, u32[]{:S(2)}) collective-permute-start(bf16[256,256]{1,0:T(8,128)(2,1)} %get-tuple-element.34), channel_id=1, source_target_pairs={{0,8},{4,12},{8,0},{12,4},{1,9},{5,13},{9,1},{13,5},{2,10},{6,14},... | collective-permute-start | bytes 393224 | tf_op jit(solution)/shard_map/ppermute | solution.py:482
  11.1 20.1 %collective-permute-start.5 = (bf16[256,256]{1,0:T(8,128)(2,1)}, bf16[256,256]{1,0:T(8,128)(2,1)S(1)}, u32[]{:S(2)}, u32[]{:S(2)}) collective-permute-start(bf16[256,256]{1,0:T(8,128)(2,1)} %get-tuple-element.35), channel_id=1, source_target_pairs={{0,12},{4,8},{8,4},{12,0},{1,13},{5,9},{9,5},{13,1},{2,14},{6,10},... | collective-permute-start | bytes 393224 | tf_op jit(solution)/shard_map/ppermute | solution.py:482
  13.0 0.7 %copy-start.7 = (s32[2,8]{1,0:T(2,128)S(1)}, s32[2,8]{1,0:T(2,128)}, u32[]{:S(2)}) copy-start(s32[2,8]{1,0:T(2,128)} %owner.1) | copy-start | bytes 196
  13.8 0.7 %copy-start.10 = (f32[16]{0:T(128)S(1)}, f32[16]{0:T(128)}, u32[]{:S(2)}) copy-start(f32[16]{0:T(128)} %param.20) | copy-start | bytes 196
  13.8 0.7 %copy-start.11 = (f32[16]{0:T(128)S(1)}, f32[16]{0:T(128)}, u32[]{:S(2)}) copy-start(f32[16]{0:T(128)} %param.19) | copy-start | bytes 196
  13.8 0.7 %copy-start.12 = (f32[16]{0:T(128)S(1)}, f32[16]{0:T(128)}, u32[]{:S(2)}) copy-start(f32[16]{0:T(128)} %param.18) | copy-start | bytes 196
  14.5 0.7 %copy-start.6 = (f32[2,16,128]{2,1,0:T(8,128)S(1)}, f32[2,16,128]{2,1,0:T(8,128)}, u32[]{:S(2)}) copy-start(f32[2,16,128]{2,1,0:T(8,128)} %dt.1) | copy-start | bytes 49156
  15.2 1.0 %copy-start.2 = (bf16[2,128,1024]{2,1,0:T(8,128)(2,1)S(1)}, bf16[2,128,1024]{2,1,0:T(8,128)(2,1)}, u32[]{:S(2)}) copy-start(bf16[2,128,1024]{2,1,0:T(8,128)(2,1)} %z_in.1) | copy-start | bytes 1572868
  16.3 0.9 %copy-start.4 = (bf16[2,128,256]{2,1,0:T(8,128)(2,1)S(1)}, bf16[2,128,256]{2,1,0:T(8,128)(2,1)}, u32[]{:S(2)}) copy-start(bf16[2,128,256]{2,1,0:T(8,128)(2,1)} %c.1) | copy-start | bytes 393220
  23.5 1.2 %copy-start.5 = (bf16[160,256]{1,0:T(8,128)(2,1)S(1)}, bf16[160,256]{1,0:T(8,128)(2,1)}, u32[]{:S(2)}) copy-start(bf16[160,256]{1,0:T(8,128)(2,1)} %get-tuple-element.26.rest_0_) | copy-start | bytes 245764
  24.6 6.6 %copy-start.1 = (bf16[1,16,64,256]{3,2,1,0:T(8,128)(2,1)S(1)}, bf16[1,16,64,256]{3,2,1,0:T(8,128)(2,1)}, u32[]{:S(2)}) copy-start(bf16[1,16,64,256]{3,2,1,0:T(8,128)(2,1)} %param.22) | copy-start | bytes 1572868
  26.3 4.9 %collective-permute-start.3 = (bf16[192,256]{1,0:T(8,128)(2,1)S(1)}, bf16[192,256]{1,0:T(8,128)(2,1)S(1)}, u32[]{:S(2)}, u32[]{:S(2)}) collective-permute-start(bf16[192,256]{1,0:T(8,128)(2,1)S(1)} %get-tuple-element.30.mine), channel_id=1, source_target_pairs={{0,2},{2,0},{1,3},{3,1},{4,6},{6,4},{5,7},{7,5},{8,10},{10,8},{9,1... | collective-permute-start | bytes 294920 | tf_op jit(solution)/shard_map/ppermute | solution.py:486
  27.9 12.9 %collective-permute-start.6 = (bf16[256,256]{1,0:T(8,128)(2,1)S(1)}, bf16[256,256]{1,0:T(8,128)(2,1)S(1)}, u32[]{:S(2)}, u32[]{:S(2)}) collective-permute-start(bf16[256,256]{1,0:T(8,128)(2,1)S(1)} %shard_map.142.rest_4_), channel_id=1, source_target_pairs={{0,8},{4,12},{8,0},{12,4},{1,9},{5,13},{9,1},{13,5},{2,10},{6,14},... | collective-permute-start | bytes 393224 | tf_op jit(solution)/shard_map/ppermute | solution.py:482
  32.1 15.4 %collective-permute-start.11 = (bf16[64,1024]{1,0:T(8,128)(2,1)S(1)}, bf16[64,1024]{1,0:T(8,128)(2,1)S(1)}, u32[]{:S(2)}, u32[]{:S(2)}) collective-permute-start(bf16[64,1024]{1,0:T(8,128)(2,1)S(1)} %shard_map.147.rest_4_), channel_id=1, source_target_pairs={{0,8},{4,12},{8,0},{12,4},{1,9},{5,13},{9,1},{13,5},{2,10},{6,14},... | collective-permute-start | bytes 393224 | tf_op jit(solution)/shard_map/ppermute | solution.py:482
  36.8 10.7 %collective-permute-start.10 = (bf16[64,1024]{1,0:T(8,128)(2,1)S(1)}, bf16[64,1024]{1,0:T(8,128)(2,1)S(1)}, u32[]{:S(2)}, u32[]{:S(2)}) collective-permute-start(bf16[64,1024]{1,0:T(8,128)(2,1)S(1)} %shard_map.147.rest_4_), channel_id=1, source_target_pairs={{0,4},{4,0},{8,12},{12,8},{1,5},{5,1},{9,13},{13,9},{2,6},{6,2},{1... | collective-permute-start | bytes 393224 | tf_op jit(solution)/shard_map/ppermute | solution.py:482
  43.0 7.3 %collective-permute-start.7 = (bf16[64,1024]{1,0:T(8,128)(2,1)S(1)}, bf16[64,1024]{1,0:T(8,128)(2,1)S(1)}, u32[]{:S(2)}, u32[]{:S(2)}) collective-permute-start(bf16[64,1024]{1,0:T(8,128)(2,1)S(1)} %get-tuple-element.37), channel_id=1, source_target_pairs={{0,4},{4,0},{8,12},{12,8},{1,5},{5,1},{9,13},{13,9},{2,6},{6,2},{1... | collective-permute-start | bytes 393224 | tf_op jit(solution)/shard_map/ppermute | solution.py:482
  43.3 7.1 %collective-permute-start.8 = (bf16[64,1024]{1,0:T(8,128)(2,1)S(1)}, bf16[64,1024]{1,0:T(8,128)(2,1)S(1)}, u32[]{:S(2)}, u32[]{:S(2)}) collective-permute-start(bf16[64,1024]{1,0:T(8,128)(2,1)S(1)} %get-tuple-element.38), channel_id=1, source_target_pairs={{0,8},{4,12},{8,0},{12,4},{1,9},{5,13},{9,1},{13,5},{2,10},{6,14},... | collective-permute-start | bytes 393224 | tf_op jit(solution)/shard_map/ppermute | solution.py:482
  46.0 7.0 %collective-permute-start.9 = (bf16[64,1024]{1,0:T(8,128)(2,1)S(1)}, bf16[64,1024]{1,0:T(8,128)(2,1)S(1)}, u32[]{:S(2)}, u32[]{:S(2)}) collective-permute-start(bf16[64,1024]{1,0:T(8,128)(2,1)S(1)} %get-tuple-element.39), channel_id=1, source_target_pairs={{0,12},{4,8},{8,4},{12,0},{1,13},{5,9},{9,5},{13,1},{2,14},{6,10},... | collective-permute-start | bytes 393224 | tf_op jit(solution)/shard_map/ppermute | solution.py:482
  47.5 6.4 %collective-permute-start.12 = (bf16[64,1024]{1,0:T(8,128)(2,1)S(1)}, bf16[64,1024]{1,0:T(8,128)(2,1)S(1)}, u32[]{:S(2)}, u32[]{:S(2)}) collective-permute-start(bf16[64,1024]{1,0:T(8,128)(2,1)S(1)} %collective-permute-done.11.rest_6_), channel_id=1, source_target_pairs={{0,4},{4,0},{8,12},{12,8},{1,5},{5,1},{9,13},{13,9},{2,6},{6,2},{1... | collective-permute-start | bytes 393224 | tf_op jit(solution)/shard_map/ppermute | solution.py:482
  53.9 2.5 %copy-start.8 = (bf16[1024]{0:T(1024)(128)(2,1)S(1)}, bf16[1024]{0:T(1024)(128)(2,1)}, u32[]{:S(2)}) copy-start(bf16[1024]{0:T(1024)(128)(2,1)} %param.21) | copy-start | bytes 6148
  54.8 3.6 %collective-permute-start.13 = (f32[2,128]{1,0:T(2,128)S(1)}, f32[2,128]{1,0:T(2,128)S(1)}, u32[]{:S(2)}, u32[]{:S(2)}) collective-permute-start(f32[2,128]{1,0:T(2,128)S(1)} %get-tuple-element.41.own), channel_id=1, source_target_pairs={{0,2},{2,0},{1,3},{3,1},{4,6},{6,4},{5,7},{7,5},{8,10},{10,8},{9,1... | collective-permute-start | bytes 3080 | tf_op jit(solution)/shard_map/ppermute | solution.py:486

commit v8 on v7

--- a/solution.py
+++ b/solution.py
@@ -302,26 +302,32 @@
     far, onward = rest[: peers - 2], rest[peers - 2 : peers - 3 + half]
     rest = rest[peers - 3 + half :]
     late, second, cars = rest[0], rest[1], rest[2 : peers + 2]
-    low, high, car0, car1, bs, cs, sem = rest[peers + 2 :]
+    car0, car1, bs, cs, sem = rest[peers + 2 :]
     rows, width = share.shape
     heads = decays.shape[1]
     size = width // heads
     t = Table(tab, peers, slots)
     k0, k1, j = t.holder(0, 0), t.holder(0, 1), t.slot(0)
-    upper = (
-        [(k0 == 0, from_rows(x, j, HALF, high)), (k0 == 1, [(chunk(near, 1, width), high)])]
-        + [(k0 // 2 == m, [(onward[m - 1], high)]) for m in range(1, half)]
-    )
     straight = [near] + list(far)
-
-    def lower(at, out):
-        return [(at == 0, from_rows(x, j, 0, out))] + [
-            (at == k, [(chunk(straight[k - 1], 0, width), out)]) for k in range(1, peers)
+    count = width // 256
+
+    def one_of(values):
+        out = values[0][1]
+        for pred, value in values[1:]:
+            out = jnp.where(pred, value, out)
+        return out
+
+    def low(at, g, lanes):
+        rest = [(at == k, straight[k - 1][g * HALF : (g + 1) * HALF].astype(F32)) for k in range(1, peers)]
+        return one_of([(None, x[j, :HALF, lanes].astype(F32))] + rest)
+
+    def high(g, lanes):
+        rest = [(k0 == 1, near[(count + g) * HALF : (count + g + 1) * HALF].astype(F32))]
+        rest += [
+            (k0 // 2 == m, onward[m - 1][g * HALF : (g + 1) * HALF].astype(F32))
+            for m in range(1, half)
         ]
-
-    got_high = gather(sem.at[0], high, upper)
-    got_low = gather(sem.at[1], low, lower(k0, low))
-    got_second = gather(sem.at[2], second, lower(k1, second))
+        return one_of([(None, x[j, HALF:, lanes].astype(F32))] + rest)
 
     @pl.when(t.odd == 0)
     def _():
@@ -335,11 +341,9 @@
 
     for lanes in spans(width):
         car0[:, lanes] = dot(cs[:HALF], cache[lanes], (1, 1)).astype(BF16)
-    got_low()
-    got_high()
     for g, lanes in enumerate(spans(width)):
-        at = slice(g * HALF, (g + 1) * HALF)
-        xv = jnp.concatenate([low[at], high[at]], axis=0).astype(F32)
+        second[g * HALF : (g + 1) * HALF] = low(k1, g, lanes).astype(BF16)
+        xv = jnp.concatenate([low(k0, g, lanes), high(g, lanes)], axis=0)
         local = dot((xv * share[:, lanes]).astype(BF16), bs[...], (0, 0)).astype(BF16).astype(F32)
         for q in range(256 // size):
             h = g * (256 // size) + q
@@ -349,7 +353,6 @@
                 + local[q * size : (q + 1) * size]
             ).astype(BF16)
         car1[:, lanes] = dot(cs[rows:], late[lanes], (1, 1)).astype(BF16)
-    got_second()
     waits = []
     for flag, at, src in ((0, k0, car0), (1, k1, car1)):
         choices = [(at == k, [(src, cars[k])]) for k in range(peers)]
@@ -560,11 +563,9 @@
     late, second, *cars = call(
         bind(late_part, slots),
         [shape((width, state), BF16), packed(piece)] + [upper_rows] * peers,
-        [SMEM] + [VMEM] * 5 + [HBM] + [ANY] * (peers + half - 2),
+        [SMEM] + [VMEM] * (5 + 1 + peers + half - 2),
         [VMEM, VMEM] + [ANY] * peers,
         [
-            scratch(piece, 256),
-            scratch(piece, 256),
             scratch(HALF, width),
             scratch(HALF, width),
             scratch(rows, state),

time: 60.5 us -> 60 us (level)
  transfers between devices with their start and end apart: 14 -> 14, of which waited for: 6 -> 6; matrix products, arithmetic and copies ran while one was open for 0% -> 0% of each run, Pallas kernels for 19% -> 18%
where the time goes in v8:
time: 60 us; the launch traced here: 59.7 us
  starting transfers between devices  27.6 us (46%)
  Pallas kernels  15.7 us (26%)
  waiting for transfers between devices  10.7 us (18%)
  local copies, waits for them, and re-layouts  4.07 us (7%)
  between operations  1.51 us (3%)
    ppermute x12, starting transfers between devices, far(): return lax.ppermute(value, 'sess', [(i, i ^ k) for i in range(peers)])  24.5 us
    ppermute x12, waiting for transfers between devices, far(): return lax.ppermute(value, 'sess', [(i, i ^ k) for i in range(peers)])  10.3 us
    unnamed x26, local copies, waits for them, and re-layouts  3.99 us
    ppermute x2, starting transfers between devices, swapped(): return lax.ppermute(value, 'head', [(i, i ^ 1) for i in range(count)])  3.15 us
    pallas_call x1, Pallas kernels, per_device(): call(block_part, [shape(x_rows.shape, F32)] * 2, [HBM] * 5 + [VMEM], scra...  2.87 us
    pallas_call x1, Pallas kernels, per_device(): call(bind(send_part), [packed(tail), packed((1 + half) * piece + tail)] +...  2.16 us
    pallas_call x1, Pallas kernels, per_device(): call(bind(late_part, slots), [shape((width, state), BF16), packed(piece)]...  1.8 us
    pallas_call x1, Pallas kernels, per_device(): call(bind(final_part, slots), shape((width, state), BF16), [SMEM] + [VMEM...  1.68 us
  transfers between devices with their start and end apart: 14, of which 6 were waited for; matrix products, arithmetic and copies ran while one was open for 0% of the time, Pallas kernels for 18%

profile of v8, /device:TPU:0, one launch (start us, length us, event | category | flops | bytes accessed | tf_op | source)
XLA Modules:
  0.0 59.7 jit_solution(5080897534133986716)
XLA Ops:
  1.4 2.2 %shard_map.141 = (bf16[160,256]{1,0:T(8,128)(2,1)}, bf16[928,256]{1,0:T(8,128)(2,1)}, bf16[160,256]{1,0:T(8,128)(2,1)}, bf16[160,256]{1,0:T(8,128)(2,1)}, bf16[2...) custom-call(bf16[2,128,1024]{2,1,0:T(8,128)(2,1)} %x.3, bf16[2,128,256]{2,1,0:T(8,128)(2,1)} %b.1, bf16[2,128,256]{2,1,0:T(8,128)(2,1)} %c.1, ...), custom_call_target="tpu_custom_call" | custom-call | tf_op jit(solution)/shard_map/pallas_call | solution.py:502
  3.5 3.1 %collective-permute-start = (bf16[928,256]{1,0:T(8,128)(2,1)}, bf16[928,256]{1,0:T(8,128)(2,1)S(1)}, u32[]{:S(2)}, u32[]{:S(2)}) collective-permute-start(bf16[928,256]{1,0:T(8,128)(2,1)} %get-tuple-element.27), channel_id=1, source_target_pairs={{0,4},{4,0},{8,12},{12,8},{1,5},{5,1},{9,13},{13,9},{2,6},{6,2},{1... | collective-permute-start | bytes 1425416 | tf_op jit(solution)/shard_map/ppermute | solution.py:485
  6.6 2.6 %collective-permute-start.1 = (bf16[160,256]{1,0:T(8,128)(2,1)}, bf16[160,256]{1,0:T(8,128)(2,1)}, u32[]{:S(2)}, u32[]{:S(2)}) collective-permute-start(bf16[160,256]{1,0:T(8,128)(2,1)} %get-tuple-element.28), channel_id=1, source_target_pairs={{0,8},{4,12},{8,0},{12,4},{1,9},{5,13},{9,1},{13,5},{2,10},{6,14},... | collective-permute-start | bytes 245768 | tf_op jit(solution)/shard_map/ppermute | solution.py:485
  9.2 1.9 %collective-permute-start.4 = (bf16[256,256]{1,0:T(8,128)(2,1)}, bf16[256,256]{1,0:T(8,128)(2,1)S(1)}, u32[]{:S(2)}, u32[]{:S(2)}) collective-permute-start(bf16[256,256]{1,0:T(8,128)(2,1)} %get-tuple-element.34), channel_id=1, source_target_pairs={{0,8},{4,12},{8,0},{12,4},{1,9},{5,13},{9,1},{13,5},{2,10},{6,14},... | collective-permute-start | bytes 393224 | tf_op jit(solution)/shard_map/ppermute | solution.py:485
  11.1 1.9 %collective-permute-start.5 = (bf16[256,256]{1,0:T(8,128)(2,1)}, bf16[256,256]{1,0:T(8,128)(2,1)S(1)}, u32[]{:S(2)}, u32[]{:S(2)}) collective-permute-start(bf16[256,256]{1,0:T(8,128)(2,1)} %get-tuple-element.35), channel_id=1, source_target_pairs={{0,12},{4,8},{8,4},{12,0},{1,13},{5,9},{9,5},{13,1},{2,14},{6,10},... | collective-permute-start | bytes 393224 | tf_op jit(solution)/shard_map/ppermute | solution.py:485
  13.0 0.7 %copy-done.7 = s32[2,8]{1,0:T(2,128)S(1)} copy-done((s32[2,8]{1,0:T(2,128)S(1)}, s32[2,8]{1,0:T(2,128)}, u32[]{:S(2)}) %copy-start.7) | copy-done | bytes 88
  13.8 0.6 %copy-done.10 = f32[16]{0:T(128)S(1)} copy-done((f32[16]{0:T(128)S(1)}, f32[16]{0:T(128)}, u32[]{:S(2)}) %copy-start.10) | copy-done | bytes 88
  14.5 0.7 %copy-done.6 = f32[2,16,128]{2,1,0:T(8,128)S(1)} copy-done((f32[2,16,128]{2,1,0:T(8,128)S(1)}, f32[2,16,128]{2,1,0:T(8,128)}, u32[]{:S(2)}) %copy-start.6) | copy-done | bytes 16408
  15.2 1.0 %copy-done.2 = bf16[2,128,1024]{2,1,0:T(8,128)(2,1)S(1)} copy-done((bf16[2,128,1024]{2,1,0:T(8,128)(2,1)S(1)}, bf16[2,128,1024]{2,1,0:T(8,128)(2,1)}, u32[]{:S(2)}) %copy-start.2) | copy-done | bytes 524312
  16.3 0.9 %copy-done.4 = bf16[2,128,256]{2,1,0:T(8,128)(2,1)S(1)} copy-done((bf16[2,128,256]{2,1,0:T(8,128)(2,1)S(1)}, bf16[2,128,256]{2,1,0:T(8,128)(2,1)}, u32[]{:S(2)}) %copy-start.4) | copy-done | bytes 131096
  17.2 2.9 %shard_map.140 = (f32[2,128,1024]{2,1,0:T(8,128)S(1)}, f32[2,128,1024]{2,1,0:T(8,128)S(1)}) custom-call(bf16[2,128,1024]{2,1,0:T(8,128)(2,1)S(1)} %copy-done, bf16[2,128,1024]{2,1,0:T(8,128)(2,1)S(1)} %copy-done.2, bf16[2,128,256]{2,1,0:T(8,128)(2,1)S(1)} %copy-done.3, bf16[2,128,256]{2,1,0:T(8,128)(2,1)S(1)} %copy-done.4, f32[2,16,128]{2,1,0:T(8,128)S(1)} %copy-done.6, ...), custom_call_target="tpu_custom_call" | custom-call | tf_op jit(solution)/shard_map/pallas_call | solution.py:521
  20.1 3.4 %collective-permute-done.near.rest_1_ = bf16[928,256]{1,0:T(8,128)(2,1)S(1)} collective-permute-done((bf16[928,256]{1,0:T(8,128)(2,1)}, bf16[928,256]{1,0:T(8,128)(2,1)S(1)}, u32[]{:S(2)}, u32[]{:S(2)}) %collective-permute-start) | collective-permute-done | bytes 475168 | tf_op jit(solution)/shard_map/ppermute | solution.py:485
  23.5 0.6 %shard_map.142.rest_4_ = bf16[256,256]{1,0:T(8,128)(2,1)S(1)} custom-call(s32[19]{0:T(128)S(1)} %concatenate.3.tab, bf16[2,128,1024]{2,1,0:T(8,128)(2,1)S(1)} %copy-done, bf16[928,256]{1,0:T(8,128)(2,1)S(1)} %collective-permute-done.near.rest_1_, f32[2,128,1024]{2,1,0:T(8,128)S(1)} %get-tuple-element.25.after.ez), custom_call_target="tpu_custom_call" | custom-call | tf_op jit(solution)/shard_map/pallas_call | solution.py:534
  24.1 0.6 collective-permute-done.2.rest_3_
  24.6 1.7 %shard_map.143 = (bf16[192,256]{1,0:T(8,128)(2,1)S(1)}, f32[2,16,128]{2,1,0:T(8,128)S(1)}, f32[2,16,128]{2,1,0:T(8,128)S(1)}) custom-call(s32[19]{0:T(128)S(1)} %concatenate.3.tab, bf16[160,256]{1,0:T(8,128)(2,1)S(1)} %copy-done.5, bf16[928,256]{1,0:T(8,128)(2,1)S(1)} %collective-permute-done.near.rest_1_, bf16[160,256]{1,0:T(8,128)(2,1)} %collective-permute-done.1.rest_2_, ...), custom_call_target="tpu_custom_call" | custom-call | tf_op jit(solution)/shard_map/pallas_call | solution.py:542
  26.3 1.6 %collective-permute-start.3 = (bf16[192,256]{1,0:T(8,128)(2,1)S(1)}, bf16[192,256]{1,0:T(8,128)(2,1)S(1)}, u32[]{:S(2)}, u32[]{:S(2)}) collective-permute-start(bf16[192,256]{1,0:T(8,128)(2,1)S(1)} %get-tuple-element.30.mine), channel_id=1, source_target_pairs={{0,2},{2,0},{1,3},{3,1},{4,6},{6,4},{5,7},{7,5},{8,10},{10,8},{9,1... | collective-permute-start | bytes 294920 | tf_op jit(solution)/shard_map/ppermute | solution.py:489
  27.9 3.3 %collective-permute-start.6 = (bf16[256,256]{1,0:T(8,128)(2,1)S(1)}, bf16[256,256]{1,0:T(8,128)(2,1)S(1)}, u32[]{:S(2)}, u32[]{:S(2)}) collective-permute-start(bf16[256,256]{1,0:T(8,128)(2,1)S(1)} %shard_map.142.rest_4_), channel_id=1, source_target_pairs={{0,8},{4,12},{8,0},{12,4},{1,9},{5,13},{9,1},{13,5},{2,10},{6,14},... | collective-permute-start | bytes 393224 | tf_op jit(solution)/shard_map/ppermute | solution.py:485
  31.3 0.8 %shard_map.147.rest_4_ = bf16[64,1024]{1,0:T(8,128)(2,1)S(1)} custom-call(s32[19]{0:T(128)S(1)} %concatenate.3.tab, bf16[1024,256]{1,0:T(8,128)(2,1)S(1)} %bitcast.7, bf16[192,256]{1,0:T(8,128)(2,1)S(1)} %get-tuple-element.30.mine, bf16[192,256]{1,0:T(8,128)(2,1)S(1)} %collective-permute-done.3.other, f32[8,128]{1,0:T(8,128)S(1)} %shard_map.146.token), custom_call_target="tpu_custom_call" | custom-call | tf_op jit(solution)/shard_map/pallas_call | solution.py:559
  32.1 3.2 %collective-permute-start.11 = (bf16[64,1024]{1,0:T(8,128)(2,1)S(1)}, bf16[64,1024]{1,0:T(8,128)(2,1)S(1)}, u32[]{:S(2)}, u32[]{:S(2)}) collective-permute-start(bf16[64,1024]{1,0:T(8,128)(2,1)S(1)} %shard_map.147.rest_4_), channel_id=1, source_target_pairs={{0,8},{4,12},{8,0},{12,4},{1,9},{5,13},{9,1},{13,5},{2,10},{6,14},... | collective-permute-start | bytes 393224 | tf_op jit(solution)/shard_map/ppermute | solution.py:485
  35.2 1.6 %shard_map.144 = (f32[128,1024]{1,0:T(8,128)S(1)}, f32[64,1024]{1,0:T(8,128)S(1)}, f32[2,16,256]{2,1,0:T(8,128)S(1)}) custom-call(s32[19]{0:T(128)S(1)} %concatenate.3.tab, f32[2,16,128]{2,1,0:T(8,128)S(1)} %get-tuple-element.31.dts, f32[3,16]{1,0:T(4,128)S(1)} %pad_maximum_fusion.params), custom_call_target="tpu_custom_call" | custom-call | tf_op jit(solution)/shard_map/pallas_call | solution.py:553
  36.8 4.1 %collective-permute-start.10 = (bf16[64,1024]{1,0:T(8,128)(2,1)S(1)}, bf16[64,1024]{1,0:T(8,128)(2,1)S(1)}, u32[]{:S(2)}, u32[]{:S(2)}) collective-permute-start(bf16[64,1024]{1,0:T(8,128)(2,1)S(1)} %shard_map.147.rest_4_), channel_id=1, source_target_pairs={{0,4},{4,0},{8,12},{12,8},{1,5},{5,1},{9,13},{13,9},{2,6},{6,2},{1... | collective-permute-start | bytes 393224 | tf_op jit(solution)/shard_map/ppermute | solution.py:485
  40.9 1.8 %shard_map.145 = (bf16[1024,256]{1,0:T(8,128)(2,1)S(1)}, bf16[256,256]{1,0:T(8,128)(2,1)S(1)}, bf16[64,1024]{1,0:T(8,128)(2,1)S(1)}, bf16[64,1024]{1,0:T(8,128)(...) custom-call(s32[19]{0:T(128)S(1)} %concatenate.3.tab, bf16[1024,256]{1,0:T(8,128)(2,1)S(1)} %bitcast.8, ...), custom_call_target="tpu_custom_call" | custom-call | tf_op jit(solution)/shard_map/pallas_call | solution.py:563
  42.8 3.0 %collective-permute-start.8 = (bf16[64,1024]{1,0:T(8,128)(2,1)S(1)}, bf16[64,1024]{1,0:T(8,128)(2,1)S(1)}, u32[]{:S(2)}, u32[]{:S(2)}) collective-permute-start(bf16[64,1024]{1,0:T(8,128)(2,1)S(1)} %get-tuple-element.38), channel_id=1, source_target_pairs={{0,8},{4,12},{8,0},{12,4},{1,9},{5,13},{9,1},{13,5},{2,10},{6,14},... | collective-permute-start | bytes 393224 | tf_op jit(solution)/shard_map/ppermute | solution.py:485
  45.8 1.3 %collective-permute-start.9 = (bf16[64,1024]{1,0:T(8,128)(2,1)S(1)}, bf16[64,1024]{1,0:T(8,128)(2,1)S(1)}, u32[]{:S(2)}, u32[]{:S(2)}) collective-permute-start(bf16[64,1024]{1,0:T(8,128)(2,1)S(1)} %get-tuple-element.39), channel_id=1, source_target_pairs={{0,12},{4,8},{8,4},{12,0},{1,13},{5,9},{9,5},{13,1},{2,14},{6,10},... | collective-permute-start | bytes 393224 | tf_op jit(solution)/shard_map/ppermute | solution.py:485
  47.2 3.0 %collective-permute-done.7.rest_1_ = bf16[64,1024]{1,0:T(8,128)(2,1)S(1)} collective-permute-done((bf16[64,1024]{1,0:T(8,128)(2,1)S(1)}, bf16[64,1024]{1,0:T(8,128)(2,1)S(1)}, u32[]{:S(2)}, u32[]{:S(2)}) %collective-permute-start.7) | collective-permute-done | bytes 131104 | tf_op jit(solution)/shard_map/ppermute | solution.py:485
  50.1 2.6 %collective-permute-done.9.rest_3_ = bf16[64,1024]{1,0:T(8,128)(2,1)S(1)} collective-permute-done((bf16[64,1024]{1,0:T(8,128)(2,1)S(1)}, bf16[64,1024]{1,0:T(8,128)(2,1)S(1)}, u32[]{:S(2)}, u32[]{:S(2)}) %collective-permute-start.9) | collective-permute-done | bytes 131104 | tf_op jit(solution)/shard_map/ppermute | solution.py:485
  52.7 0.8 %collective-permute-done.12.rest_7_ = bf16[64,1024]{1,0:T(8,128)(2,1)S(1)} collective-permute-done((bf16[64,1024]{1,0:T(8,128)(2,1)S(1)}, bf16[64,1024]{1,0:T(8,128)(2,1)S(1)}, u32[]{:S(2)}, u32[]{:S(2)}) %collective-permute-start.12) | collective-permute-done | bytes 131104 | tf_op jit(solution)/shard_map/ppermute | solution.py:485
  53.5 0.9 %shard_map.148 = (f32[2,128,1024]{2,1,0:T(8,128)S(1)}, f32[2,128]{1,0:T(2,128)S(1)}) custom-call(s32[19]{0:T(128)S(1)} %concatenate.3.tab, f32[2,128,1024]{2,1,0:T(8,128)S(1)} %get-tuple-element.24.yz, f32[2,128,1024]{2,1,0:T(8,128)S(1)} %get-tuple-element.25.after.ez, bf16[64,1024]{1,0:T(8,128)(2,1)S(1)} %get-tuple-element.36.rest_0_, ...), custom_call_target="tpu_custom_call" | custom-call | tf_op jit(solution)/shard_map/pallas_call | solution.py:584
  54.5 1.6 %collective-permute-start.13 = (f32[2,128]{1,0:T(2,128)S(1)}, f32[2,128]{1,0:T(2,128)S(1)}, u32[]{:S(2)}, u32[]{:S(2)}) collective-permute-start(f32[2,128]{1,0:T(2,128)S(1)} %get-tuple-element.41.own), channel_id=1, source_target_pairs={{0,2},{2,0},{1,3},{3,1},{4,6},{6,4},{5,7},{7,5},{8,10},{10,8},{9,1... | collective-permute-start | bytes 3080 | tf_op jit(solution)/shard_map/ppermute | solution.py:489
  56.0 1.7 %shard_map.150 = bf16[1024,256]{1,0:T(8,128)(2,1)} custom-call(s32[19]{0:T(128)S(1)} %concatenate.3.tab, bf16[192,256]{1,0:T(8,128)(2,1)S(1)} %get-tuple-element.30.mine, bf16[192,256]{1,0:T(8,128)(2,1)S(1)} %collective-permute-done.3.other, f32[64,1024]{1,0:T(8,128)S(1)} %get-tuple-element.43.share, f32[2,16,256]{2,1,0:T(8,128)S(1)} %get-tuple-element.33.decays, ...), custom_call_target="tpu_custom_call" | custom-call | tf_op jit(solution)/shard_map/pallas_call | solution.py:578
  57.7 0.4 collective-permute-done.13.other
  58.1 1.6 %shard_map.149 = bf16[2,128,1024]{2,1,0:T(8,128)(2,1)} custom-call(s32[19]{0:T(128)S(1)} %concatenate.3.tab, f32[2,128,1024]{2,1,0:T(8,128)S(1)} %get-tuple-element.40.gated, f32[2,128]{1,0:T(2,128)S(1)} %get-tuple-element.41.own, f32[2,128]{1,0:T(2,128)S(1)} %collective-permute-done.13.other, bf16[1,1024]{1,0:T(2,128)(2,1)S(1)} %broadcast_in_dim.9.gain, ...), custom_call_target="tpu_custom_call" | custom-call | tf_op jit(solution)/shard_map/pallas_call | solution.py:595
  (38 shorter events, 0.4 us)
Async XLA Ops:
  0.6 13.9 %copy-start = (bf16[2,128,1024]{2,1,0:T(8,128)(2,1)S(1)}, bf16[2,128,1024]{2,1,0:T(8,128)(2,1)}, u32[]{:S(2)}) copy-start(bf16[2,128,1024]{2,1,0:T(8,128)(2,1)} %x.3) | copy-start | bytes 1572868
  1.3 13.2 %copy-start.3 = (bf16[2,128,256]{2,1,0:T(8,128)(2,1)S(1)}, bf16[2,128,256]{2,1,0:T(8,128)(2,1)}, u32[]{:S(2)}) copy-start(bf16[2,128,256]{2,1,0:T(8,128)(2,1)} %b.1) | copy-start | bytes 393220
  3.5 20.0 %collective-permute-start = (bf16[928,256]{1,0:T(8,128)(2,1)}, bf16[928,256]{1,0:T(8,128)(2,1)S(1)}, u32[]{:S(2)}, u32[]{:S(2)}) collective-permute-start(bf16[928,256]{1,0:T(8,128)(2,1)} %get-tuple-element.27), channel_id=1, source_target_pairs={{0,4},{4,0},{8,12},{12,8},{1,5},{5,1},{9,13},{13,9},{2,6},{6,2},{1... | collective-permute-start | bytes 1425416 | tf_op jit(solution)/shard_map/ppermute | solution.py:485
  6.6 17.5 %collective-permute-start.1 = (bf16[160,256]{1,0:T(8,128)(2,1)}, bf16[160,256]{1,0:T(8,128)(2,1)}, u32[]{:S(2)}, u32[]{:S(2)}) collective-permute-start(bf16[160,256]{1,0:T(8,128)(2,1)} %get-tuple-element.28), channel_id=1, source_target_pairs={{0,8},{4,12},{8,0},{12,4},{1,9},{5,13},{9,1},{13,5},{2,10},{6,14},... | collective-permute-start | bytes 245768 | tf_op jit(solution)/shard_map/ppermute | solution.py:485
  9.2 15.4 %collective-permute-start.2 = (bf16[160,256]{1,0:T(8,128)(2,1)}, bf16[160,256]{1,0:T(8,128)(2,1)}, u32[]{:S(2)}, u32[]{:S(2)}) collective-permute-start(bf16[160,256]{1,0:T(8,128)(2,1)} %get-tuple-element.29), channel_id=1, source_target_pairs={{0,12},{4,8},{8,4},{12,0},{1,13},{5,9},{9,5},{13,1},{2,14},{6,10},... | collective-permute-start | bytes 245768 | tf_op jit(solution)/shard_map/ppermute | solution.py:485
  9.2 3.8 %copy-start.9 = (s32[2,8]{1,0:T(2,128)S(1)}, s32[2,8]{1,0:T(2,128)}, u32[]{:S(2)}) copy-start(s32[2,8]{1,0:T(2,128)} %param.25) | copy-start | bytes 196
  9.2 22.0 %collective-permute-start.4 = (bf16[256,256]{1,0:T(8,128)(2,1)}, bf16[256,256]{1,0:T(8,128)(2,1)S(1)}, u32[]{:S(2)}, u32[]{:S(2)}) collective-permute-start(bf16[256,256]{1,0:T(8,128)(2,1)} %get-tuple-element.34), channel_id=1, source_target_pairs={{0,8},{4,12},{8,0},{12,4},{1,9},{5,13},{9,1},{13,5},{2,10},{6,14},... | collective-permute-start | bytes 393224 | tf_op jit(solution)/shard_map/ppermute | solution.py:485
  11.1 20.1 %collective-permute-start.5 = (bf16[256,256]{1,0:T(8,128)(2,1)}, bf16[256,256]{1,0:T(8,128)(2,1)S(1)}, u32[]{:S(2)}, u32[]{:S(2)}) collective-permute-start(bf16[256,256]{1,0:T(8,128)(2,1)} %get-tuple-element.35), channel_id=1, source_target_pairs={{0,12},{4,8},{8,4},{12,0},{1,13},{5,9},{9,5},{13,1},{2,14},{6,10},... | collective-permute-start | bytes 393224 | tf_op jit(solution)/shard_map/ppermute | solution.py:485
  13.0 0.7 %copy-start.7 = (s32[2,8]{1,0:T(2,128)S(1)}, s32[2,8]{1,0:T(2,128)}, u32[]{:S(2)}) copy-start(s32[2,8]{1,0:T(2,128)} %owner.1) | copy-start | bytes 196
  13.8 0.7 %copy-start.10 = (f32[16]{0:T(128)S(1)}, f32[16]{0:T(128)}, u32[]{:S(2)}) copy-start(f32[16]{0:T(128)} %param.20) | copy-start | bytes 196
  13.8 0.7 %copy-start.11 = (f32[16]{0:T(128)S(1)}, f32[16]{0:T(128)}, u32[]{:S(2)}) copy-start(f32[16]{0:T(128)} %param.19) | copy-start | bytes 196
  13.8 0.7 %copy-start.12 = (f32[16]{0:T(128)S(1)}, f32[16]{0:T(128)}, u32[]{:S(2)}) copy-start(f32[16]{0:T(128)} %param.18) | copy-start | bytes 196
  14.5 0.7 %copy-start.6 = (f32[2,16,128]{2,1,0:T(8,128)S(1)}, f32[2,16,128]{2,1,0:T(8,128)}, u32[]{:S(2)}) copy-start(f32[2,16,128]{2,1,0:T(8,128)} %dt.1) | copy-start | bytes 49156
  15.2 1.0 %copy-start.2 = (bf16[2,128,1024]{2,1,0:T(8,128)(2,1)S(1)}, bf16[2,128,1024]{2,1,0:T(8,128)(2,1)}, u32[]{:S(2)}) copy-start(bf16[2,128,1024]{2,1,0:T(8,128)(2,1)} %z_in.1) | copy-start | bytes 1572868
  16.3 0.9 %copy-start.4 = (bf16[2,128,256]{2,1,0:T(8,128)(2,1)S(1)}, bf16[2,128,256]{2,1,0:T(8,128)(2,1)}, u32[]{:S(2)}) copy-start(bf16[2,128,256]{2,1,0:T(8,128)(2,1)} %c.1) | copy-start | bytes 393220
  23.5 1.2 %copy-start.5 = (bf16[160,256]{1,0:T(8,128)(2,1)S(1)}, bf16[160,256]{1,0:T(8,128)(2,1)}, u32[]{:S(2)}) copy-start(bf16[160,256]{1,0:T(8,128)(2,1)} %get-tuple-element.26.rest_0_) | copy-start | bytes 245764
  24.6 6.6 %copy-start.1 = (bf16[1,16,64,256]{3,2,1,0:T(8,128)(2,1)S(1)}, bf16[1,16,64,256]{3,2,1,0:T(8,128)(2,1)}, u32[]{:S(2)}) copy-start(bf16[1,16,64,256]{3,2,1,0:T(8,128)(2,1)} %param.22) | copy-start | bytes 1572868
  26.3 4.9 %collective-permute-start.3 = (bf16[192,256]{1,0:T(8,128)(2,1)S(1)}, bf16[192,256]{1,0:T(8,128)(2,1)S(1)}, u32[]{:S(2)}, u32[]{:S(2)}) collective-permute-start(bf16[192,256]{1,0:T(8,128)(2,1)S(1)} %get-tuple-element.30.mine), channel_id=1, source_target_pairs={{0,2},{2,0},{1,3},{3,1},{4,6},{6,4},{5,7},{7,5},{8,10},{10,8},{9,1... | collective-permute-start | bytes 294920 | tf_op jit(solution)/shard_map/ppermute | solution.py:489
  27.9 12.9 %collective-permute-start.6 = (bf16[256,256]{1,0:T(8,128)(2,1)S(1)}, bf16[256,256]{1,0:T(8,128)(2,1)S(1)}, u32[]{:S(2)}, u32[]{:S(2)}) collective-permute-start(bf16[256,256]{1,0:T(8,128)(2,1)S(1)} %shard_map.142.rest_4_), channel_id=1, source_target_pairs={{0,8},{4,12},{8,0},{12,4},{1,9},{5,13},{9,1},{13,5},{2,10},{6,14},... | collective-permute-start | bytes 393224 | tf_op jit(solution)/shard_map/ppermute | solution.py:485
  32.1 15.1 %collective-permute-start.11 = (bf16[64,1024]{1,0:T(8,128)(2,1)S(1)}, bf16[64,1024]{1,0:T(8,128)(2,1)S(1)}, u32[]{:S(2)}, u32[]{:S(2)}) collective-permute-start(bf16[64,1024]{1,0:T(8,128)(2,1)S(1)} %shard_map.147.rest_4_), channel_id=1, source_target_pairs={{0,8},{4,12},{8,0},{12,4},{1,9},{5,13},{9,1},{13,5},{2,10},{6,14},... | collective-permute-start | bytes 393224 | tf_op jit(solution)/shard_map/ppermute | solution.py:485
  36.8 10.3 %collective-permute-start.10 = (bf16[64,1024]{1,0:T(8,128)(2,1)S(1)}, bf16[64,1024]{1,0:T(8,128)(2,1)S(1)}, u32[]{:S(2)}, u32[]{:S(2)}) collective-permute-start(bf16[64,1024]{1,0:T(8,128)(2,1)S(1)} %shard_map.147.rest_4_), channel_id=1, source_target_pairs={{0,4},{4,0},{8,12},{12,8},{1,5},{5,1},{9,13},{13,9},{2,6},{6,2},{1... | collective-permute-start | bytes 393224 | tf_op jit(solution)/shard_map/ppermute | solution.py:485
  42.7 7.4 %collective-permute-start.7 = (bf16[64,1024]{1,0:T(8,128)(2,1)S(1)}, bf16[64,1024]{1,0:T(8,128)(2,1)S(1)}, u32[]{:S(2)}, u32[]{:S(2)}) collective-permute-start(bf16[64,1024]{1,0:T(8,128)(2,1)S(1)} %get-tuple-element.37), channel_id=1, source_target_pairs={{0,4},{4,0},{8,12},{12,8},{1,5},{5,1},{9,13},{13,9},{2,6},{6,2},{1... | collective-permute-start | bytes 393224 | tf_op jit(solution)/shard_map/ppermute | solution.py:485
  42.8 7.3 %collective-permute-start.8 = (bf16[64,1024]{1,0:T(8,128)(2,1)S(1)}, bf16[64,1024]{1,0:T(8,128)(2,1)S(1)}, u32[]{:S(2)}, u32[]{:S(2)}) collective-permute-start(bf16[64,1024]{1,0:T(8,128)(2,1)S(1)} %get-tuple-element.38), channel_id=1, source_target_pairs={{0,8},{4,12},{8,0},{12,4},{1,9},{5,13},{9,1},{13,5},{2,10},{6,14},... | collective-permute-start | bytes 393224 | tf_op jit(solution)/shard_map/ppermute | solution.py:485
  45.8 6.9 %collective-permute-start.9 = (bf16[64,1024]{1,0:T(8,128)(2,1)S(1)}, bf16[64,1024]{1,0:T(8,128)(2,1)S(1)}, u32[]{:S(2)}, u32[]{:S(2)}) collective-permute-start(bf16[64,1024]{1,0:T(8,128)(2,1)S(1)} %get-tuple-element.39), channel_id=1, source_target_pairs={{0,12},{4,8},{8,4},{12,0},{1,13},{5,9},{9,5},{13,1},{2,14},{6,10},... | collective-permute-start | bytes 393224 | tf_op jit(solution)/shard_map/ppermute | solution.py:485
  47.1 6.4 %collective-permute-start.12 = (bf16[64,1024]{1,0:T(8,128)(2,1)S(1)}, bf16[64,1024]{1,0:T(8,128)(2,1)S(1)}, u32[]{:S(2)}, u32[]{:S(2)}) collective-permute-start(bf16[64,1024]{1,0:T(8,128)(2,1)S(1)} %collective-permute-done.11.rest_6_), channel_id=1, source_target_pairs={{0,4},{4,0},{8,12},{12,8},{1,5},{5,1},{9,13},{13,9},{2,6},{6,2},{1... | collective-permute-start | bytes 393224 | tf_op jit(solution)/shard_map/ppermute | solution.py:485
  53.5 2.5 %copy-start.8 = (bf16[1024]{0:T(1024)(128)(2,1)S(1)}, bf16[1024]{0:T(1024)(128)(2,1)}, u32[]{:S(2)}) copy-start(bf16[1024]{0:T(1024)(128)(2,1)} %param.21) | copy-start | bytes 6148
  54.5 3.6 %collective-permute-start.13 = (f32[2,128]{1,0:T(2,128)S(1)}, f32[2,128]{1,0:T(2,128)S(1)}, u32[]{:S(2)}, u32[]{:S(2)}) collective-permute-start(f32[2,128]{1,0:T(2,128)S(1)} %get-tuple-element.41.own), channel_id=1, source_target_pairs={{0,2},{2,0},{1,3},{3,1},{4,6},{6,4},{5,7},{7,5},{8,10},{10,8},{9,1... | collective-permute-start | bytes 3080 | tf_op jit(solution)/shard_map/ppermute | solution.py:489

commit v9 on v8

--- a/solution.py
+++ b/solution.py
@@ -189,31 +189,28 @@
 
 def pick_part(peers, slots, heads, tab, *rest):
     got = rest[:peers]
-    mine, dts, lens, tails, counts, sem = rest[peers + 1 :]
+    mine, dts, lens = rest[peers + 1 :]
     rows = mine.shape[0] - HALF
     size = rows + 2 * heads
     t = Table(tab, peers, slots)
-    waits = []
-    for part in range(2):
-        at, out = t.holder(0, part), tails.at[part]
-        choices = [(at == k, [(tail_of(got[k], size), out)]) for k in range(peers)]
-        waits.append(gather(sem.at[part], out, choices))
+
+    def choose(at, start, count):
+        out = None
+        for k in range(peers):
+            base = got[k].shape[0] - size + start
+            value = got[k][base : base + count].astype(F32)
+            out = jnp.where(at == k, value, out) if k else value
+        return out
+
+    first, second = t.holder(0, 0), t.holder(0, 1)
+    mine[:rows] = choose(first, 0, rows).astype(BF16)
+    mine[rows:] = choose(second, 0, HALF).astype(BF16)
+    for part, at in ((0, first), (1, second)):
+        top = choose(at, rows, heads)
+        low = choose(at, rows + heads, heads)
+        dts[part] = top[:, :rows] + (top[:, rows:] + low[:, :rows])
     for j in range(slots):
-        at, out = t.far(j), counts.at[j]
-        choices = [
-            (at == k, [(tail_of(got[k], size, rows + heads, heads), out)]) for k in range(peers)
-        ]
-        waits.append(gather(sem.at[2 + j], out, choices))
-    for wait in waits:
-        wait()
-    mine[:rows] = tails[0, :rows]
-    mine[rows:] = tails[1, :HALF]
-    for part in range(2):
-        first = tails[part, rows : rows + heads].astype(F32)
-        second = tails[part, rows + heads :].astype(F32)
-        dts[part] = first[:, :rows] + (first[:, rows:] + second[:, :rows])
-    for j in range(slots):
-        lens[j] = counts[j, :, rows:].astype(F32)
+        lens[j] = choose(t.far(j), rows + heads, heads)[:, rows:]
 
 
 def touch_part(*refs):
@@ -546,8 +543,7 @@
             shape((2, heads, rows), F32),
             shape((slots, heads, rows), F32),
         ],
-        [SMEM] + [ANY] * (peers + 1),
-        scratch=[scratch(2, tail, 256), scratch(slots, heads, 256), dma(2 + slots)],
+        [SMEM] + [VMEM] * peers + [ANY],
     )(tab, own, near, *smalls, passing[0])
     other = swapped(mine)
     share0, share1, decays = call(

time: 60 us -> 59.4 us (0.990)
  no operation moved by 1% of the time
where the time goes in v9:
time: 59.4 us; the launch traced here: 59.1 us
  starting transfers between devices  27.7 us (47%)
  Pallas kernels  15.1 us (25%)
  waiting for transfers between devices  10.6 us (18%)
  local copies, waits for them, and re-layouts  4.07 us (7%)
  between operations  1.51 us (3%)
    ppermute x12, starting transfers between devices, far(): return lax.ppermute(value, 'sess', [(i, i ^ k) for i in range(peers)])  24.5 us
    ppermute x12, waiting for transfers between devices, far(): return lax.ppermute(value, 'sess', [(i, i ^ k) for i in range(peers)])  10.3 us
    unnamed x26, local copies, waits for them, and re-layouts  3.99 us
    ppermute x2, starting transfers between devices, swapped(): return lax.ppermute(value, 'head', [(i, i ^ 1) for i in range(count)])  3.15 us
    pallas_call x1, Pallas kernels, per_device(): call(block_part, [shape(x_rows.shape, F32)] * 2, [HBM] * 5 + [VMEM], scra...  2.87 us
    pallas_call x1, Pallas kernels, per_device(): call(bind(send_part), [packed(tail), packed((1 + half) * piece + tail)] +...  2.16 us
    pallas_call x1, Pallas kernels, per_device(): call(bind(late_part, slots), [shape((width, state), BF16), packed(piece)]...  1.8 us
    pallas_call x1, Pallas kernels, per_device(): call(bind(final_part, slots), shape((width, state), BF16), [SMEM] + [VMEM...  1.68 us
  transfers between devices with their start and end apart: 14, of which 6 were waited for; matrix products, arithmetic and copies ran while one was open for 0% of the time, Pallas kernels for 18%

profile of v9, /device:TPU:0, one launch (start us, length us, event | category | flops | bytes accessed | tf_op | source)
XLA Modules:
  0.0 59.1 jit_solution(5225363252711169253)
XLA Ops:
  1.4 2.2 %shard_map.141 = (bf16[160,256]{1,0:T(8,128)(2,1)}, bf16[928,256]{1,0:T(8,128)(2,1)}, bf16[160,256]{1,0:T(8,128)(2,1)}, bf16[160,256]{1,0:T(8,128)(2,1)}, bf16[2...) custom-call(bf16[2,128,1024]{2,1,0:T(8,128)(2,1)} %x.3, bf16[2,128,256]{2,1,0:T(8,128)(2,1)} %b.1, bf16[2,128,256]{2,1,0:T(8,128)(2,1)} %c.1, ...), custom_call_target="tpu_custom_call" | custom-call | tf_op jit(solution)/shard_map/pallas_call | solution.py:499
  3.5 3.1 %collective-permute-start = (bf16[928,256]{1,0:T(8,128)(2,1)}, bf16[928,256]{1,0:T(8,128)(2,1)S(1)}, u32[]{:S(2)}, u32[]{:S(2)}) collective-permute-start(bf16[928,256]{1,0:T(8,128)(2,1)} %get-tuple-element.27), channel_id=1, source_target_pairs={{0,4},{4,0},{8,12},{12,8},{1,5},{5,1},{9,13},{13,9},{2,6},{6,2},{1... | collective-permute-start | bytes 1425416 | tf_op jit(solution)/shard_map/ppermute | solution.py:482
  6.6 2.6 %collective-permute-start.1 = (bf16[160,256]{1,0:T(8,128)(2,1)}, bf16[160,256]{1,0:T(8,128)(2,1)}, u32[]{:S(2)}, u32[]{:S(2)}) collective-permute-start(bf16[160,256]{1,0:T(8,128)(2,1)} %get-tuple-element.28), channel_id=1, source_target_pairs={{0,8},{4,12},{8,0},{12,4},{1,9},{5,13},{9,1},{13,5},{2,10},{6,14},... | collective-permute-start | bytes 245768 | tf_op jit(solution)/shard_map/ppermute | solution.py:482
  9.2 1.9 %collective-permute-start.4 = (bf16[256,256]{1,0:T(8,128)(2,1)}, bf16[256,256]{1,0:T(8,128)(2,1)S(1)}, u32[]{:S(2)}, u32[]{:S(2)}) collective-permute-start(bf16[256,256]{1,0:T(8,128)(2,1)} %get-tuple-element.34), channel_id=1, source_target_pairs={{0,8},{4,12},{8,0},{12,4},{1,9},{5,13},{9,1},{13,5},{2,10},{6,14},... | collective-permute-start | bytes 393224 | tf_op jit(solution)/shard_map/ppermute | solution.py:482
  11.1 1.9 %collective-permute-start.5 = (bf16[256,256]{1,0:T(8,128)(2,1)}, bf16[256,256]{1,0:T(8,128)(2,1)S(1)}, u32[]{:S(2)}, u32[]{:S(2)}) collective-permute-start(bf16[256,256]{1,0:T(8,128)(2,1)} %get-tuple-element.35), channel_id=1, source_target_pairs={{0,12},{4,8},{8,4},{12,0},{1,13},{5,9},{9,5},{13,1},{2,14},{6,10},... | collective-permute-start | bytes 393224 | tf_op jit(solution)/shard_map/ppermute | solution.py:482
  13.0 0.7 %copy-done.7 = s32[2,8]{1,0:T(2,128)S(1)} copy-done((s32[2,8]{1,0:T(2,128)S(1)}, s32[2,8]{1,0:T(2,128)}, u32[]{:S(2)}) %copy-start.7) | copy-done | bytes 88
  13.8 0.6 %copy-done.10 = f32[16]{0:T(128)S(1)} copy-done((f32[16]{0:T(128)S(1)}, f32[16]{0:T(128)}, u32[]{:S(2)}) %copy-start.10) | copy-done | bytes 88
  14.5 0.7 %copy-done.6 = f32[2,16,128]{2,1,0:T(8,128)S(1)} copy-done((f32[2,16,128]{2,1,0:T(8,128)S(1)}, f32[2,16,128]{2,1,0:T(8,128)}, u32[]{:S(2)}) %copy-start.6) | copy-done | bytes 16408
  15.2 1.0 %copy-done.2 = bf16[2,128,1024]{2,1,0:T(8,128)(2,1)S(1)} copy-done((bf16[2,128,1024]{2,1,0:T(8,128)(2,1)S(1)}, bf16[2,128,1024]{2,1,0:T(8,128)(2,1)}, u32[]{:S(2)}) %copy-start.2) | copy-done | bytes 524312
  16.3 0.9 %copy-done.4 = bf16[2,128,256]{2,1,0:T(8,128)(2,1)S(1)} copy-done((bf16[2,128,256]{2,1,0:T(8,128)(2,1)S(1)}, bf16[2,128,256]{2,1,0:T(8,128)(2,1)}, u32[]{:S(2)}) %copy-start.4) | copy-done | bytes 131096
  17.2 2.9 %shard_map.140 = (f32[2,128,1024]{2,1,0:T(8,128)S(1)}, f32[2,128,1024]{2,1,0:T(8,128)S(1)}) custom-call(bf16[2,128,1024]{2,1,0:T(8,128)(2,1)S(1)} %copy-done, bf16[2,128,1024]{2,1,0:T(8,128)(2,1)S(1)} %copy-done.2, bf16[2,128,256]{2,1,0:T(8,128)(2,1)S(1)} %copy-done.3, bf16[2,128,256]{2,1,0:T(8,128)(2,1)S(1)} %copy-done.4, f32[2,16,128]{2,1,0:T(8,128)S(1)} %copy-done.6, ...), custom_call_target="tpu_custom_call" | custom-call | tf_op jit(solution)/shard_map/pallas_call | solution.py:518
  20.1 3.4 %collective-permute-done.near.rest_1_ = bf16[928,256]{1,0:T(8,128)(2,1)S(1)} collective-permute-done((bf16[928,256]{1,0:T(8,128)(2,1)}, bf16[928,256]{1,0:T(8,128)(2,1)S(1)}, u32[]{:S(2)}, u32[]{:S(2)}) %collective-permute-start) | collective-permute-done | bytes 475168 | tf_op jit(solution)/shard_map/ppermute | solution.py:482
  23.5 0.6 %shard_map.142.rest_4_ = bf16[256,256]{1,0:T(8,128)(2,1)S(1)} custom-call(s32[19]{0:T(128)S(1)} %concatenate.3.tab, bf16[2,128,1024]{2,1,0:T(8,128)(2,1)S(1)} %copy-done, bf16[928,256]{1,0:T(8,128)(2,1)S(1)} %collective-permute-done.near.rest_1_, f32[2,128,1024]{2,1,0:T(8,128)S(1)} %get-tuple-element.25.after.ez), custom_call_target="tpu_custom_call" | custom-call | tf_op jit(solution)/shard_map/pallas_call | solution.py:531
  24.1 0.5 collective-permute-done.2.rest_3_
  24.6 1.1 %shard_map.143 = (bf16[192,256]{1,0:T(8,128)(2,1)S(1)}, f32[2,16,128]{2,1,0:T(8,128)S(1)}, f32[2,16,128]{2,1,0:T(8,128)S(1)}) custom-call(s32[19]{0:T(128)S(1)} %concatenate.3.tab, bf16[160,256]{1,0:T(8,128)(2,1)S(1)} %copy-done.5, bf16[928,256]{1,0:T(8,128)(2,1)S(1)} %collective-permute-done.near.rest_1_, bf16[160,256]{1,0:T(8,128)(2,1)} %collective-permute-done.1.rest_2_, ...), custom_call_target="tpu_custom_call" | custom-call | tf_op jit(solution)/shard_map/pallas_call | solution.py:539
  25.8 1.6 %collective-permute-start.3 = (bf16[192,256]{1,0:T(8,128)(2,1)S(1)}, bf16[192,256]{1,0:T(8,128)(2,1)S(1)}, u32[]{:S(2)}, u32[]{:S(2)}) collective-permute-start(bf16[192,256]{1,0:T(8,128)(2,1)S(1)} %get-tuple-element.30.mine), channel_id=1, source_target_pairs={{0,2},{2,0},{1,3},{3,1},{4,6},{6,4},{5,7},{7,5},{8,10},{10,8},{9,1... | collective-permute-start | bytes 294920 | tf_op jit(solution)/shard_map/ppermute | solution.py:486
  27.4 3.3 %collective-permute-start.6 = (bf16[256,256]{1,0:T(8,128)(2,1)S(1)}, bf16[256,256]{1,0:T(8,128)(2,1)S(1)}, u32[]{:S(2)}, u32[]{:S(2)}) collective-permute-start(bf16[256,256]{1,0:T(8,128)(2,1)S(1)} %shard_map.142.rest_4_), channel_id=1, source_target_pairs={{0,8},{4,12},{8,0},{12,4},{1,9},{5,13},{9,1},{13,5},{2,10},{6,14},... | collective-permute-start | bytes 393224 | tf_op jit(solution)/shard_map/ppermute | solution.py:482
  30.7 0.8 %shard_map.147.rest_4_ = bf16[64,1024]{1,0:T(8,128)(2,1)S(1)} custom-call(s32[19]{0:T(128)S(1)} %concatenate.3.tab, bf16[1024,256]{1,0:T(8,128)(2,1)S(1)} %bitcast.7, bf16[192,256]{1,0:T(8,128)(2,1)S(1)} %get-tuple-element.30.mine, bf16[192,256]{1,0:T(8,128)(2,1)S(1)} %collective-permute-done.3.other, f32[8,128]{1,0:T(8,128)S(1)} %shard_map.146.token), custom_call_target="tpu_custom_call" | custom-call | tf_op jit(solution)/shard_map/pallas_call | solution.py:555
  31.5 3.2 %collective-permute-start.11 = (bf16[64,1024]{1,0:T(8,128)(2,1)S(1)}, bf16[64,1024]{1,0:T(8,128)(2,1)S(1)}, u32[]{:S(2)}, u32[]{:S(2)}) collective-permute-start(bf16[64,1024]{1,0:T(8,128)(2,1)S(1)} %shard_map.147.rest_4_), channel_id=1, source_target_pairs={{0,8},{4,12},{8,0},{12,4},{1,9},{5,13},{9,1},{13,5},{2,10},{6,14},... | collective-permute-start | bytes 393224 | tf_op jit(solution)/shard_map/ppermute | solution.py:482
  34.7 1.6 %shard_map.144 = (f32[128,1024]{1,0:T(8,128)S(1)}, f32[64,1024]{1,0:T(8,128)S(1)}, f32[2,16,256]{2,1,0:T(8,128)S(1)}) custom-call(s32[19]{0:T(128)S(1)} %concatenate.3.tab, f32[2,16,128]{2,1,0:T(8,128)S(1)} %get-tuple-element.31.dts, f32[3,16]{1,0:T(4,128)S(1)} %pad_maximum_fusion.params), custom_call_target="tpu_custom_call" | custom-call | tf_op jit(solution)/shard_map/pallas_call | solution.py:549
  36.2 4.1 %collective-permute-start.10 = (bf16[64,1024]{1,0:T(8,128)(2,1)S(1)}, bf16[64,1024]{1,0:T(8,128)(2,1)S(1)}, u32[]{:S(2)}, u32[]{:S(2)}) collective-permute-start(bf16[64,1024]{1,0:T(8,128)(2,1)S(1)} %shard_map.147.rest_4_), channel_id=1, source_target_pairs={{0,4},{4,0},{8,12},{12,8},{1,5},{5,1},{9,13},{13,9},{2,6},{6,2},{1... | collective-permute-start | bytes 393224 | tf_op jit(solution)/shard_map/ppermute | solution.py:482
  40.4 1.8 %shard_map.145 = (bf16[1024,256]{1,0:T(8,128)(2,1)S(1)}, bf16[256,256]{1,0:T(8,128)(2,1)S(1)}, bf16[64,1024]{1,0:T(8,128)(2,1)S(1)}, bf16[64,1024]{1,0:T(8,128)(...) custom-call(s32[19]{0:T(128)S(1)} %concatenate.3.tab, bf16[1024,256]{1,0:T(8,128)(2,1)S(1)} %bitcast.8, ...), custom_call_target="tpu_custom_call" | custom-call | tf_op jit(solution)/shard_map/pallas_call | solution.py:559
  42.3 3.0 %collective-permute-start.8 = (bf16[64,1024]{1,0:T(8,128)(2,1)S(1)}, bf16[64,1024]{1,0:T(8,128)(2,1)S(1)}, u32[]{:S(2)}, u32[]{:S(2)}) collective-permute-start(bf16[64,1024]{1,0:T(8,128)(2,1)S(1)} %get-tuple-element.38), channel_id=1, source_target_pairs={{0,8},{4,12},{8,0},{12,4},{1,9},{5,13},{9,1},{13,5},{2,10},{6,14},... | collective-permute-start | bytes 393224 | tf_op jit(solution)/shard_map/ppermute | solution.py:482
  45.3 1.3 %collective-permute-start.9 = (bf16[64,1024]{1,0:T(8,128)(2,1)S(1)}, bf16[64,1024]{1,0:T(8,128)(2,1)S(1)}, u32[]{:S(2)}, u32[]{:S(2)}) collective-permute-start(bf16[64,1024]{1,0:T(8,128)(2,1)S(1)} %get-tuple-element.39), channel_id=1, source_target_pairs={{0,12},{4,8},{8,4},{12,0},{1,13},{5,9},{9,5},{13,1},{2,14},{6,10},... | collective-permute-start | bytes 393224 | tf_op jit(solution)/shard_map/ppermute | solution.py:482
  46.6 2.9 %collective-permute-done.7.rest_1_ = bf16[64,1024]{1,0:T(8,128)(2,1)S(1)} collective-permute-done((bf16[64,1024]{1,0:T(8,128)(2,1)S(1)}, bf16[64,1024]{1,0:T(8,128)(2,1)S(1)}, u32[]{:S(2)}, u32[]{:S(2)}) %collective-permute-start.7) | collective-permute-done | bytes 131104 | tf_op jit(solution)/shard_map/ppermute | solution.py:482
  49.6 2.6 %collective-permute-done.9.rest_3_ = bf16[64,1024]{1,0:T(8,128)(2,1)S(1)} collective-permute-done((bf16[64,1024]{1,0:T(8,128)(2,1)S(1)}, bf16[64,1024]{1,0:T(8,128)(2,1)S(1)}, u32[]{:S(2)}, u32[]{:S(2)}) %collective-permute-start.9) | collective-permute-done | bytes 131104 | tf_op jit(solution)/shard_map/ppermute | solution.py:482
  52.2 0.8 %collective-permute-done.12.rest_7_ = bf16[64,1024]{1,0:T(8,128)(2,1)S(1)} collective-permute-done((bf16[64,1024]{1,0:T(8,128)(2,1)S(1)}, bf16[64,1024]{1,0:T(8,128)(2,1)S(1)}, u32[]{:S(2)}, u32[]{:S(2)}) %collective-permute-start.12) | collective-permute-done | bytes 131104 | tf_op jit(solution)/shard_map/ppermute | solution.py:482
  53.0 0.9 %shard_map.148 = (f32[2,128,1024]{2,1,0:T(8,128)S(1)}, f32[2,128]{1,0:T(2,128)S(1)}) custom-call(s32[19]{0:T(128)S(1)} %concatenate.3.tab, f32[2,128,1024]{2,1,0:T(8,128)S(1)} %get-tuple-element.24.yz, f32[2,128,1024]{2,1,0:T(8,128)S(1)} %get-tuple-element.25.after.ez, bf16[64,1024]{1,0:T(8,128)(2,1)S(1)} %get-tuple-element.36.rest_0_, ...), custom_call_target="tpu_custom_call" | custom-call | tf_op jit(solution)/shard_map/pallas_call | solution.py:580
  53.9 1.6 %collective-permute-start.13 = (f32[2,128]{1,0:T(2,128)S(1)}, f32[2,128]{1,0:T(2,128)S(1)}, u32[]{:S(2)}, u32[]{:S(2)}) collective-permute-start(f32[2,128]{1,0:T(2,128)S(1)} %get-tuple-element.41.own), channel_id=1, source_target_pairs={{0,2},{2,0},{1,3},{3,1},{4,6},{6,4},{5,7},{7,5},{8,10},{10,8},{9,1... | collective-permute-start | bytes 3080 | tf_op jit(solution)/shard_map/ppermute | solution.py:486
  55.5 1.7 %shard_map.150 = bf16[1024,256]{1,0:T(8,128)(2,1)} custom-call(s32[19]{0:T(128)S(1)} %concatenate.3.tab, bf16[192,256]{1,0:T(8,128)(2,1)S(1)} %get-tuple-element.30.mine, bf16[192,256]{1,0:T(8,128)(2,1)S(1)} %collective-permute-done.3.other, f32[64,1024]{1,0:T(8,128)S(1)} %get-tuple-element.43.share, f32[2,16,256]{2,1,0:T(8,128)S(1)} %get-tuple-element.33.decays, ...), custom_call_target="tpu_custom_call" | custom-call | tf_op jit(solution)/shard_map/pallas_call | solution.py:574
  57.2 0.4 collective-permute-done.13.other
  57.6 1.6 %shard_map.149 = bf16[2,128,1024]{2,1,0:T(8,128)(2,1)} custom-call(s32[19]{0:T(128)S(1)} %concatenate.3.tab, f32[2,128,1024]{2,1,0:T(8,128)S(1)} %get-tuple-element.40.gated, f32[2,128]{1,0:T(2,128)S(1)} %get-tuple-element.41.own, f32[2,128]{1,0:T(2,128)S(1)} %collective-permute-done.13.other, bf16[1,1024]{1,0:T(2,128)(2,1)S(1)} %broadcast_in_dim.9.gain, ...), custom_call_target="tpu_custom_call" | custom-call | tf_op jit(solution)/shard_map/pallas_call | solution.py:591
  (38 shorter events, 0.4 us)
Async XLA Ops:
  0.6 13.9 %copy-start = (bf16[2,128,1024]{2,1,0:T(8,128)(2,1)S(1)}, bf16[2,128,1024]{2,1,0:T(8,128)(2,1)}, u32[]{:S(2)}) copy-start(bf16[2,128,1024]{2,1,0:T(8,128)(2,1)} %x.3) | copy-start | bytes 1572868
  1.3 13.2 %copy-start.3 = (bf16[2,128,256]{2,1,0:T(8,128)(2,1)S(1)}, bf16[2,128,256]{2,1,0:T(8,128)(2,1)}, u32[]{:S(2)}) copy-start(bf16[2,128,256]{2,1,0:T(8,128)(2,1)} %b.1) | copy-start | bytes 393220
  3.5 20.0 %collective-permute-start = (bf16[928,256]{1,0:T(8,128)(2,1)}, bf16[928,256]{1,0:T(8,128)(2,1)S(1)}, u32[]{:S(2)}, u32[]{:S(2)}) collective-permute-start(bf16[928,256]{1,0:T(8,128)(2,1)} %get-tuple-element.27), channel_id=1, source_target_pairs={{0,4},{4,0},{8,12},{12,8},{1,5},{5,1},{9,13},{13,9},{2,6},{6,2},{1... | collective-permute-start | bytes 1425416 | tf_op jit(solution)/shard_map/ppermute | solution.py:482
  6.6 17.5 %collective-permute-start.1 = (bf16[160,256]{1,0:T(8,128)(2,1)}, bf16[160,256]{1,0:T(8,128)(2,1)}, u32[]{:S(2)}, u32[]{:S(2)}) collective-permute-start(bf16[160,256]{1,0:T(8,128)(2,1)} %get-tuple-element.28), channel_id=1, source_target_pairs={{0,8},{4,12},{8,0},{12,4},{1,9},{5,13},{9,1},{13,5},{2,10},{6,14},... | collective-permute-start | bytes 245768 | tf_op jit(solution)/shard_map/ppermute | solution.py:482
  9.2 15.4 %collective-permute-start.2 = (bf16[160,256]{1,0:T(8,128)(2,1)}, bf16[160,256]{1,0:T(8,128)(2,1)}, u32[]{:S(2)}, u32[]{:S(2)}) collective-permute-start(bf16[160,256]{1,0:T(8,128)(2,1)} %get-tuple-element.29), channel_id=1, source_target_pairs={{0,12},{4,8},{8,4},{12,0},{1,13},{5,9},{9,5},{13,1},{2,14},{6,10},... | collective-permute-start | bytes 245768 | tf_op jit(solution)/shard_map/ppermute | solution.py:482
  9.2 3.8 %copy-start.9 = (s32[2,8]{1,0:T(2,128)S(1)}, s32[2,8]{1,0:T(2,128)}, u32[]{:S(2)}) copy-start(s32[2,8]{1,0:T(2,128)} %param.25) | copy-start | bytes 196
  9.2 21.4 %collective-permute-start.4 = (bf16[256,256]{1,0:T(8,128)(2,1)}, bf16[256,256]{1,0:T(8,128)(2,1)S(1)}, u32[]{:S(2)}, u32[]{:S(2)}) collective-permute-start(bf16[256,256]{1,0:T(8,128)(2,1)} %get-tuple-element.34), channel_id=1, source_target_pairs={{0,8},{4,12},{8,0},{12,4},{1,9},{5,13},{9,1},{13,5},{2,10},{6,14},... | collective-permute-start | bytes 393224 | tf_op jit(solution)/shard_map/ppermute | solution.py:482
  11.1 19.5 %collective-permute-start.5 = (bf16[256,256]{1,0:T(8,128)(2,1)}, bf16[256,256]{1,0:T(8,128)(2,1)S(1)}, u32[]{:S(2)}, u32[]{:S(2)}) collective-permute-start(bf16[256,256]{1,0:T(8,128)(2,1)} %get-tuple-element.35), channel_id=1, source_target_pairs={{0,12},{4,8},{8,4},{12,0},{1,13},{5,9},{9,5},{13,1},{2,14},{6,10},... | collective-permute-start | bytes 393224 | tf_op jit(solution)/shard_map/ppermute | solution.py:482
  13.0 0.7 %copy-start.7 = (s32[2,8]{1,0:T(2,128)S(1)}, s32[2,8]{1,0:T(2,128)}, u32[]{:S(2)}) copy-start(s32[2,8]{1,0:T(2,128)} %owner.1) | copy-start | bytes 196
  13.8 0.7 %copy-start.10 = (f32[16]{0:T(128)S(1)}, f32[16]{0:T(128)}, u32[]{:S(2)}) copy-start(f32[16]{0:T(128)} %param.20) | copy-start | bytes 196
  13.8 0.7 %copy-start.11 = (f32[16]{0:T(128)S(1)}, f32[16]{0:T(128)}, u32[]{:S(2)}) copy-start(f32[16]{0:T(128)} %param.19) | copy-start | bytes 196
  13.8 0.7 %copy-start.12 = (f32[16]{0:T(128)S(1)}, f32[16]{0:T(128)}, u32[]{:S(2)}) copy-start(f32[16]{0:T(128)} %param.18) | copy-start | bytes 196
  14.5 0.7 %copy-start.6 = (f32[2,16,128]{2,1,0:T(8,128)S(1)}, f32[2,16,128]{2,1,0:T(8,128)}, u32[]{:S(2)}) copy-start(f32[2,16,128]{2,1,0:T(8,128)} %dt.1) | copy-start | bytes 49156
  15.2 1.0 %copy-start.2 = (bf16[2,128,1024]{2,1,0:T(8,128)(2,1)S(1)}, bf16[2,128,1024]{2,1,0:T(8,128)(2,1)}, u32[]{:S(2)}) copy-start(bf16[2,128,1024]{2,1,0:T(8,128)(2,1)} %z_in.1) | copy-start | bytes 1572868
  16.3 0.9 %copy-start.4 = (bf16[2,128,256]{2,1,0:T(8,128)(2,1)S(1)}, bf16[2,128,256]{2,1,0:T(8,128)(2,1)}, u32[]{:S(2)}) copy-start(bf16[2,128,256]{2,1,0:T(8,128)(2,1)} %c.1) | copy-start | bytes 393220
  23.5 1.2 %copy-start.5 = (bf16[160,256]{1,0:T(8,128)(2,1)S(1)}, bf16[160,256]{1,0:T(8,128)(2,1)}, u32[]{:S(2)}) copy-start(bf16[160,256]{1,0:T(8,128)(2,1)} %get-tuple-element.26.rest_0_) | copy-start | bytes 245764
  24.6 6.0 %copy-start.1 = (bf16[1,16,64,256]{3,2,1,0:T(8,128)(2,1)S(1)}, bf16[1,16,64,256]{3,2,1,0:T(8,128)(2,1)}, u32[]{:S(2)}) copy-start(bf16[1,16,64,256]{3,2,1,0:T(8,128)(2,1)} %param.22) | copy-start | bytes 1572868
  25.8 4.9 %collective-permute-start.3 = (bf16[192,256]{1,0:T(8,128)(2,1)S(1)}, bf16[192,256]{1,0:T(8,128)(2,1)S(1)}, u32[]{:S(2)}, u32[]{:S(2)}) collective-permute-start(bf16[192,256]{1,0:T(8,128)(2,1)S(1)} %get-tuple-element.30.mine), channel_id=1, source_target_pairs={{0,2},{2,0},{1,3},{3,1},{4,6},{6,4},{5,7},{7,5},{8,10},{10,8},{9,1... | collective-permute-start | bytes 294920 | tf_op jit(solution)/shard_map/ppermute | solution.py:486
  27.4 13.0 %collective-permute-start.6 = (bf16[256,256]{1,0:T(8,128)(2,1)S(1)}, bf16[256,256]{1,0:T(8,128)(2,1)S(1)}, u32[]{:S(2)}, u32[]{:S(2)}) collective-permute-start(bf16[256,256]{1,0:T(8,128)(2,1)S(1)} %shard_map.142.rest_4_), channel_id=1, source_target_pairs={{0,8},{4,12},{8,0},{12,4},{1,9},{5,13},{9,1},{13,5},{2,10},{6,14},... | collective-permute-start | bytes 393224 | tf_op jit(solution)/shard_map/ppermute | solution.py:482
  31.5 15.1 %collective-permute-start.11 = (bf16[64,1024]{1,0:T(8,128)(2,1)S(1)}, bf16[64,1024]{1,0:T(8,128)(2,1)S(1)}, u32[]{:S(2)}, u32[]{:S(2)}) collective-permute-start(bf16[64,1024]{1,0:T(8,128)(2,1)S(1)} %shard_map.147.rest_4_), channel_id=1, source_target_pairs={{0,8},{4,12},{8,0},{12,4},{1,9},{5,13},{9,1},{13,5},{2,10},{6,14},... | collective-permute-start | bytes 393224 | tf_op jit(solution)/shard_map/ppermute | solution.py:482
  36.2 10.4 %collective-permute-start.10 = (bf16[64,1024]{1,0:T(8,128)(2,1)S(1)}, bf16[64,1024]{1,0:T(8,128)(2,1)S(1)}, u32[]{:S(2)}, u32[]{:S(2)}) collective-permute-start(bf16[64,1024]{1,0:T(8,128)(2,1)S(1)} %shard_map.147.rest_4_), channel_id=1, source_target_pairs={{0,4},{4,0},{8,12},{12,8},{1,5},{5,1},{9,13},{13,9},{2,6},{6,2},{1... | collective-permute-start | bytes 393224 | tf_op jit(solution)/shard_map/ppermute | solution.py:482
  42.2 7.4 %collective-permute-start.7 = (bf16[64,1024]{1,0:T(8,128)(2,1)S(1)}, bf16[64,1024]{1,0:T(8,128)(2,1)S(1)}, u32[]{:S(2)}, u32[]{:S(2)}) collective-permute-start(bf16[64,1024]{1,0:T(8,128)(2,1)S(1)} %get-tuple-element.37), channel_id=1, source_target_pairs={{0,4},{4,0},{8,12},{12,8},{1,5},{5,1},{9,13},{13,9},{2,6},{6,2},{1... | collective-permute-start | bytes 393224 | tf_op jit(solution)/shard_map/ppermute | solution.py:482
  42.3 7.3 %collective-permute-start.8 = (bf16[64,1024]{1,0:T(8,128)(2,1)S(1)}, bf16[64,1024]{1,0:T(8,128)(2,1)S(1)}, u32[]{:S(2)}, u32[]{:S(2)}) collective-permute-start(bf16[64,1024]{1,0:T(8,128)(2,1)S(1)} %get-tuple-element.38), channel_id=1, source_target_pairs={{0,8},{4,12},{8,0},{12,4},{1,9},{5,13},{9,1},{13,5},{2,10},{6,14},... | collective-permute-start | bytes 393224 | tf_op jit(solution)/shard_map/ppermute | solution.py:482
  45.3 6.9 %collective-permute-start.9 = (bf16[64,1024]{1,0:T(8,128)(2,1)S(1)}, bf16[64,1024]{1,0:T(8,128)(2,1)S(1)}, u32[]{:S(2)}, u32[]{:S(2)}) collective-permute-start(bf16[64,1024]{1,0:T(8,128)(2,1)S(1)} %get-tuple-element.39), channel_id=1, source_target_pairs={{0,12},{4,8},{8,4},{12,0},{1,13},{5,9},{9,5},{13,1},{2,14},{6,10},... | collective-permute-start | bytes 393224 | tf_op jit(solution)/shard_map/ppermute | solution.py:482
  46.6 6.4 %collective-permute-start.12 = (bf16[64,1024]{1,0:T(8,128)(2,1)S(1)}, bf16[64,1024]{1,0:T(8,128)(2,1)S(1)}, u32[]{:S(2)}, u32[]{:S(2)}) collective-permute-start(bf16[64,1024]{1,0:T(8,128)(2,1)S(1)} %collective-permute-done.11.rest_6_), channel_id=1, source_target_pairs={{0,4},{4,0},{8,12},{12,8},{1,5},{5,1},{9,13},{13,9},{2,6},{6,2},{1... | collective-permute-start | bytes 393224 | tf_op jit(solution)/shard_map/ppermute | solution.py:482
  53.0 2.5 %copy-start.8 = (bf16[1024]{0:T(1024)(128)(2,1)S(1)}, bf16[1024]{0:T(1024)(128)(2,1)}, u32[]{:S(2)}) copy-start(bf16[1024]{0:T(1024)(128)(2,1)} %param.21) | copy-start | bytes 6148
  53.9 3.6 %collective-permute-start.13 = (f32[2,128]{1,0:T(2,128)S(1)}, f32[2,128]{1,0:T(2,128)S(1)}, u32[]{:S(2)}, u32[]{:S(2)}) collective-permute-start(f32[2,128]{1,0:T(2,128)S(1)} %get-tuple-element.41.own), channel_id=1, source_target_pairs={{0,2},{2,0},{1,3},{3,1},{4,6},{6,4},{5,7},{7,5},{8,10},{10,8},{9,1... | collective-permute-start | bytes 3080 | tf_op jit(solution)/shard_map/ppermute | solution.py:486
